TPU v7x, 32 devices: a whole 2x2x4 slice. The times are simulated.
32 devices in a mesh: groups: 2 (over y), slab: 4 (over z), sub: 4 (over x, core).
Axes of the slice: x: 2, y: 2, z: 4, core: 2. Of those that a mesh axis runs over, the one named last changes fastest.
Arguments:
- velocity: float32 [3, 64, 128, 512], P(None, ('groups', 'slab'), 'sub'), parts along dimension 1, may hold values from -6 to 6
- template: bfloat16 [64, 128, 512], P(('groups', 'slab'), 'sub'), parts along dimension 0, may hold values from -6 to 6
- moving: bfloat16 [64, 128, 512], P(('groups', 'slab'), 'sub'), parts along dimension 0, may hold values from -6 to 6
- stiffness: float32 [64, 128, 512], P(('groups', 'slab'), 'sub'), parts along dimension 0, may hold values from 0.25 to 4
- fetch_plane: int32 [64, 128, 4], P(('groups', 'slab'), 'sub'), parts along dimension 0, may hold values from 0 to 31, as said below
- tissue: int32 [64, 128, 4], P(('groups', 'slab'), 'sub'), parts along dimension 0, may hold values 0 or 1
Outputs:
- new_velocity: float32 [3, 64, 128, 512], P(None, ('groups', 'slab'), 'sub'), parts along dimension 1
- warped: bfloat16 [64, 128, 512], P(('groups', 'slab'), 'sub'), parts along dimension 0
There are 2 independent parts, one for each index of `groups`. A program takes and returns all parts, laid end to end along the dimension named above; each array names one. Nothing has to cross between parts.
Inputs may be any that keep to these rules, and one draw needn't show every extreme that they name: `fetch_plane`: take the blocks with z in [s*8, (s+1)*8) and y in [q*32, (q+1)*32) for any s and q: at most 512 of them name planes in one range [t*8, (t+1)*8), and in every draw one range t is named by exactly 512 blocks of every such group.
All inputs are finite; a program needn't handle non-finite values. No bound on the sum of `tissue` on one device may be relied on, other than what follows from the above.
Results may differ from a plain program's by a relative error of at most 0.001.
Values may be sent and summed in bfloat16 or wider, within the bound.
No kernel may reach another device: no remote copies, remote signals or barrier semaphores. Data moves between devices by JAX's collectives and lax.ppermute only.
A program may use at most 64 MiB of HBM per device.

v0:
```python
import jax
import jax.numpy as jnp
from jax import lax
from jax.sharding import PartitionSpec as P

BLOCK = 128


def extended(cells, sides, width):
    for axis, dim in sides:
        count = lax.axis_size(axis)
        head = lax.slice_in_dim(cells, 0, width, axis=dim)
        tail = lax.slice_in_dim(cells, cells.shape[dim] - width, cells.shape[dim], axis=dim)
        cells = jnp.concatenate(
            [
                lax.ppermute(tail, axis, [(i, (i + 1) % count) for i in range(count)]),
                cells,
                lax.ppermute(head, axis, [((i + 1) % count, i) for i in range(count)]),
            ],
            axis=dim,
        )
    return cells


def tables(length):
    wave_ids = jnp.arange(length, dtype=jnp.int32)
    phase = wave_ids[:, None] * wave_ids[None, :] % length
    angle = 2.0 * jnp.pi / length * phase.astype(jnp.float32)
    return (jnp.cos(angle), jnp.sin(angle))


def apply_along(values, matrix, axis_id):
    result = lax.dot_general(
        values,
        matrix,
        (((axis_id,), (0,)), ((), ())),
        precision=lax.Precision.HIGHEST,
        preferred_element_type=jnp.float32,
    )
    return jnp.moveaxis(result, -1, axis_id)


def forward_along(values_pair, axis_id):
    real_part, imag_part = values_pair
    cosine, sine = tables(real_part.shape[axis_id])
    return (
        apply_along(real_part, cosine, axis_id) + apply_along(imag_part, sine, axis_id),
        apply_along(imag_part, cosine, axis_id) - apply_along(real_part, sine, axis_id),
    )


def inverse_along(values_pair, axis_id):
    real_part, imag_part = values_pair
    length = real_part.shape[axis_id]
    cosine, sine = tables(length)
    scale = 1.0 / length
    return (
        (apply_along(real_part, cosine, axis_id) - apply_along(imag_part, sine, axis_id)) * scale,
        (apply_along(imag_part, cosine, axis_id) + apply_along(real_part, sine, axis_id)) * scale,
    )


def symbol_sq(length, first_id, span):
    wave_ids = first_id + jnp.arange(span, dtype=jnp.int32)
    signed = jnp.where(wave_ids < length // 2, wave_ids, wave_ids - length).astype(jnp.float32)
    wave = 2.0 * jnp.pi / length * signed
    return wave * wave


def local(velocity, template, moving, stiffness, fetch_plane, tissue):
    planes_dev, rows_dev, x_length = moving.shape
    blocks_x = x_length // BLOCK
    slabs = lax.axis_size("slab")
    subs = lax.axis_size("sub")
    my_slab = lax.axis_index("slab")
    my_sub = lax.axis_index("sub")
    per_dev = planes_dev * rows_dev * blocks_x
    capacity = 2 * per_dev // slabs
    source_plane = fetch_plane.reshape(-1)
    block_ids = jnp.arange(per_dev, dtype=jnp.int32)
    row_of = block_ids // blocks_x % rows_dev
    column_of = block_ids % blocks_x
    moving_rows = moving.reshape(per_dev, BLOCK)
    holder = source_plane // planes_dev
    within = (source_plane % planes_dev * rows_dev + row_of) * blocks_x + column_of
    matches = (holder[:, None] == jnp.arange(slabs, dtype=jnp.int32)[None, :]).astype(jnp.int32)
    earlier = jnp.sum((jnp.cumsum(matches, axis=0) - matches) * matches, axis=1)
    target = holder * capacity + earlier
    wanted = (
        jnp.zeros((slabs * capacity,), jnp.int32).at[target].set(within).reshape(slabs, capacity)
    )
    asked = lax.all_to_all(wanted, "slab", split_axis=0, concat_axis=0, tiled=True)
    fetched = moving_rows[asked.reshape(-1)].reshape(asked.shape + (BLOCK,))
    replies = lax.all_to_all(fetched, "slab", split_axis=0, concat_axis=0, tiled=True)
    warped_rows = replies.reshape(slabs * capacity, BLOCK)[target]
    warped = warped_rows.reshape(planes_dev, rows_dev, x_length)
    padded = extended(warped, (("slab", 0), ("sub", 1)), 1).astype(jnp.float32)
    image = padded[1:-1, 1:-1]
    grad_z = 0.5 * (padded[2:, 1:-1] - padded[:-2, 1:-1])
    grad_y = 0.5 * (padded[1:-1, 2:] - padded[1:-1, :-2])
    grad_x = 0.5 * (jnp.roll(image, -1, 2) - jnp.roll(image, 1, 2))
    residual = image - template.astype(jnp.float32)
    tissue_vox = jnp.repeat(tissue.astype(jnp.float32), BLOCK, axis=2)
    weight_field = tissue_vox * stiffness * residual
    force = jnp.stack([weight_field * grad_z, weight_field * grad_y, weight_field * grad_x])
    cos_x, sin_x = tables(x_length)
    real_part = apply_along(force, cos_x, 3)
    imag_part = -apply_along(force, sin_x, 3)
    moved = (
        lax.all_to_all(real_part, "sub", split_axis=3, concat_axis=2, tiled=True),
        lax.all_to_all(imag_part, "sub", split_axis=3, concat_axis=2, tiled=True),
    )
    moved = forward_along(moved, 2)
    moved = (
        lax.all_to_all(moved[0], "slab", split_axis=2, concat_axis=1, tiled=True),
        lax.all_to_all(moved[1], "slab", split_axis=2, concat_axis=1, tiled=True),
    )
    moved = forward_along(moved, 1)
    total_z = moved[0].shape[1]
    y_span = moved[0].shape[2]
    x_span = moved[0].shape[3]
    factor = 1.0 / (
        symbol_sq(total_z, 0, total_z)[:, None, None]
        + symbol_sq(y_span * slabs, my_slab * y_span, y_span)[None, :, None]
        + symbol_sq(x_span * subs, my_sub * x_span, x_span)[None, None, :]
        + 1.0 / 256.0
    )
    moved = (moved[0] * factor, moved[1] * factor)
    moved = inverse_along(moved, 1)
    moved = (
        lax.all_to_all(moved[0], "slab", split_axis=1, concat_axis=2, tiled=True),
        lax.all_to_all(moved[1], "slab", split_axis=1, concat_axis=2, tiled=True),
    )
    moved = inverse_along(moved, 2)
    real_part, imag_part = (
        lax.all_to_all(moved[0], "sub", split_axis=2, concat_axis=3, tiled=True),
        lax.all_to_all(moved[1], "sub", split_axis=2, concat_axis=3, tiled=True),
    )
    smoothed = (apply_along(real_part, cos_x, 3) - apply_along(imag_part, sin_x, 3)) * (
        1.0 / x_length
    )
    new_velocity = 0.5 * (velocity - smoothed)
    return (new_velocity, warped)


def solution(mesh):
    placed = (
        P(None, ("groups", "slab"), "sub", None),
        P(("groups", "slab"), "sub", None),
        P(("groups", "slab"), "sub", None),
        P(("groups", "slab"), "sub", None),
        P(("groups", "slab"), "sub", None),
        P(("groups", "slab"), "sub", None),
    )
    return jax.shard_map(
        local,
        mesh=mesh,
        in_specs=placed,
        out_specs=(P(None, ("groups", "slab"), "sub", None), P(("groups", "slab"), "sub", None)),
        check_vma=False,
    )
```

profile of v0, /device:TPU:0, one launch (start us, length us, event | category | flops | bytes accessed | tf_op | source)
XLA Modules:
  0.0 399.4 jit_solution(18127117719359659913)
XLA Ops:
  4.3 4.9 %scatter_custom_fusion = s32[2048]{0:T(1024)} fusion(s32[1024]{0:T(1024)S(1)} %bitcast.189, s32[1024]{0:T(1024)S(1)} %get-tuple-element.14, s32[]{:T(128)} %constant.128.clone.1), kind=kCustom, calls=%fused_computation.155 | custom fusion | bytes 8196 | tf_op jit(solution)/shard_map/scatter | solution.py:90
  9.2 6.3 %all-to-all-start = ((s32[4,1,512]{2,1,0:T(1,128)}), s32[4,1,512]{2,1,0:T(1,128)S(1)}, u32[]{:S(2)}, u32[]{:S(2)}) async-start(s32[4,1,512]{2,1,0:T(1,128)} %bitcast.4), calls=%async_computation | async-start | bytes 16384 | tf_op jit(solution)/shard_map/all_to_all | solution.py:92
  16.7 4.5 %all-to-all-done = s32[4,1,512]{2,1,0:T(1,128)S(1)} async-done(((s32[4,1,512]{2,1,0:T(1,128)}), s32[4,1,512]{2,1,0:T(1,128)S(1)}, u32[]{:S(2)}, u32[]{:S(2)}) %all-to-all-start) | async-done | bytes 8224 | tf_op jit(solution)/shard_map/all_to_all | solution.py:92
  21.2 8.1 %gather_fusion = bf16[2048,128]{1,0:T(8,128)(2,1)} fusion(bf16[1024,128]{1,0:T(8,128)(2,1)S(1)} %reshape.249, s32[2048]{0:T(1024)S(1)} %broadcast_clamp_fusion), kind=kCustom, calls=%fused_computation | custom fusion | bytes 1056768 | tf_op jit(solution)/shard_map/gather | solution.py:93
  29.2 3.5 all-to-all-start.1
  32.7 13.3 %all-to-all-done.1 = bf16[4,512,128]{2,1,0:T(8,128)(2,1)S(1)} async-done(((bf16[4,512,128]{2,1,0:T(8,128)(2,1)}), bf16[4,512,128]{2,1,0:T(8,128)(2,1)S(1)}, u32[]{:S(2)}, u32[]{:S(2)}) %all-to-all-start.1) | async-done | bytes 524320 | tf_op jit(solution)/shard_map/all_to_all | solution.py:94
  46.0 3.2 gather_fusion.1
  49.6 3.9 collective-permute-start.1
  53.4 1.6 collective-permute-done
  55.2 2.0 collective-permute-start.3
  61.5 6.5 %fusion.16 = f32[3,8,32,512]{3,2,1,0:T(8,128)S(1)} fusion(f32[1,8,32,512]{3,2,1,0:T(8,128)S(1)} %get-tuple-element.9, f32[1,8,32,512]{3,2,1,0:T(8,128)S(1)} %get-tuple-element.8, f32[1,8,32,512]{3,2,1,0:T(8,128)S(1)} %get-tuple-element.2), kind=kOutput, calls=%fused_computation.29 | convolution fusion | flops 2420375552 | bytes 3145728 | tf_op jit(solution)/shard_map/dot_general | solution.py:33
  68.0 4.2 %copy.76 = f32[3,8,32,512]{2,1,0,3:T(8,128)} copy(f32[3,8,32,512]{3,2,1,0:T(8,128)S(1)} %fusion.16) | data formatting | bytes 3145728 | tf_op jit(solution)/shard_map/dot_general | solution.py:33
  72.1 5.9 %reshape.293 = f32[4,1,98304]{2,1,0:T(1,128)} reshape(f32[512,3,8,32]{3,2,1,0:T(8,128)} %bitcast.165) | data formatting | bytes 3145728
  78.1 4.1 %all-to-all-start.2 = ((f32[4,1,98304]{2,1,0:T(1,128)}), f32[4,1,98304]{2,1,0:T(1,128)S(1)}, u32[]{:S(2)}, u32[]{:S(2)}) async-start(f32[4,1,98304]{2,1,0:T(1,128)} %reshape.293), calls=%async_computation.2 | async-start | bytes 3145728 | tf_op jit(solution)/shard_map/all_to_all | solution.py:110
  82.2 7.9 %convolution_negate_fusion = f32[3,8,32,512]{3,2,1,0:T(8,128)S(1)} fusion(f32[1,8,32,512]{3,2,1,0:T(8,128)} %copy-done.13, f32[1,8,32,512]{3,2,1,0:T(8,128)} %copy-done.12, f32[1,8,32,512]{3,2,1,0:T(8,128)} %copy-done.11), kind=kOutput, calls=%fused_computation.24 | convolution fusion | flops 2420768768 | bytes 3145728 | tf_op jit(solution)/shard_map/dot_general | solution.py:33
  90.0 4.2 %copy.80 = f32[3,8,32,512]{2,1,0,3:T(8,128)} copy(f32[3,8,32,512]{3,2,1,0:T(8,128)S(1)} %convolution_negate_fusion) | data formatting | bytes 3145728 | tf_op jit(solution)/shard_map/neg | solution.py:108
  94.2 5.9 %reshape.291 = f32[4,1,98304]{2,1,0:T(1,128)} reshape(f32[512,3,8,32]{3,2,1,0:T(8,128)} %bitcast.166) | data formatting | bytes 3145728
  100.1 2.0 all-to-all-done.2
  102.2 4.5 %all-to-all-start.3 = ((f32[4,1,98304]{2,1,0:T(1,128)}), f32[4,1,98304]{2,1,0:T(1,128)}, u32[]{:S(2)}, u32[]{:S(2)}) async-start(f32[4,1,98304]{2,1,0:T(1,128)} %reshape.291), calls=%async_computation.3 | async-start | bytes 3145728 | tf_op jit(solution)/shard_map/all_to_all | solution.py:111
  107.3 5.2 %reduce.3 = f32[4,98304]{1,0:T(4,128)S(1)} reduce(f32[4,1,98304]{2,1,0:T(1,128)S(1)} %all-to-all-done.2, f32[]{:T(128)} %broadcast.468), dimensions={1}, to_apply=%all_to_all.116.reduce_sub_computation | reduce | bytes 3145732 | tf_op jit(solution)/shard_map/all_to_all | solution.py:110
  112.5 4.8 %reshape.294 = f32[512,3,8,32]{3,2,1,0:T(8,128)} reshape(f32[4,98304]{1,0:T(4,128)S(1)} %reduce.3) | data formatting | bytes 3145728
  117.4 4.6 %copy.122 = f32[3,8,32,4,128]{4,3,2,1,0:T(4,128)S(1)} copy(f32[3,8,32,4,128]{2,1,0,4,3:T(8,128)} %bitcast.167) | data formatting | bytes 3145728 | tf_op jit(solution)/shard_map/all_to_all | solution.py:110
  122.2 4.6 %all-to-all-done.3 = f32[4,1,98304]{2,1,0:T(1,128)} async-done(((f32[4,1,98304]{2,1,0:T(1,128)}), f32[4,1,98304]{2,1,0:T(1,128)}, u32[]{:S(2)}, u32[]{:S(2)}) %all-to-all-start.3) | async-done | bytes 1572896 | tf_op jit(solution)/shard_map/all_to_all | solution.py:111
  126.8 6.2 %reduce.2 = f32[4,98304]{1,0:T(4,128)S(1)} reduce(f32[4,1,98304]{2,1,0:T(1,128)} %all-to-all-done.3, f32[]{:T(128)} %broadcast.468), dimensions={1}, to_apply=%all_to_all.120.reduce_sub_computation | reduce | bytes 3145732 | tf_op jit(solution)/shard_map/all_to_all | solution.py:111
  133.0 4.8 %reshape.292 = f32[512,3,8,32]{3,2,1,0:T(8,128)} reshape(f32[4,98304]{1,0:T(4,128)S(1)} %reduce.2) | data formatting | bytes 3145728
  137.9 4.7 %copy.123 = f32[3,8,32,4,128]{4,3,2,1,0:T(4,128)S(1)} copy(f32[3,8,32,4,128]{2,1,0,4,3:T(8,128)} %bitcast.168) | data formatting | bytes 3145728 | tf_op jit(solution)/shard_map/all_to_all | solution.py:111
  142.7 2.8 fusion.56
  145.6 2.8 subtract_bitcast_fusion
  148.3 1.6 copy.89
  149.9 5.8 %all-to-all-start.5 = ((f32[3,8,128,128]{3,1,0,2:T(8,128)}), f32[3,8,128,128]{3,1,0,2:T(8,128)S(1)}, u32[]{:S(2)}, u32[]{:S(2)}) async-start(f32[3,8,128,128]{3,1,0,2:T(8,128)} %copy.89), calls=%async_computation.5 | async-start | bytes 3145728 | tf_op jit(solution)/shard_map/all_to_all | solution.py:116
  155.7 2.8 fusion.58
  158.6 2.8 add_bitcast_fusion
  161.4 1.7 copy.84
  163.0 29.4 %all-to-all-done.5 = f32[3,8,128,128]{3,1,0,2:T(8,128)S(1)} async-done(((f32[3,8,128,128]{3,1,0,2:T(8,128)}), f32[3,8,128,128]{3,1,0,2:T(8,128)S(1)}, u32[]{:S(2)}, u32[]{:S(2)}) %all-to-all-start.5) | async-done | bytes 1572896 | tf_op jit(solution)/shard_map/all_to_all | solution.py:116
  192.5 3.7 all-to-all-start.4
  197.3 2.7 fusion
  200.0 2.7 fusion.2
  202.7 29.9 %all-to-all-done.4 = f32[3,8,128,128]{3,1,0,2:T(8,128)S(1)} async-done(((f32[3,8,128,128]{3,1,0,2:T(8,128)}), f32[3,8,128,128]{3,1,0,2:T(8,128)S(1)}, u32[]{:S(2)}, u32[]{:S(2)}) %all-to-all-start.4) | async-done | bytes 1572896 | tf_op jit(solution)/shard_map/all_to_all | solution.py:115
  232.6 3.1 bitcast_multiply_fusion
  237.3 1.7 bitcast_multiply_fusion.1
  239.0 1.6 multiply_bitcast_fusion.2
  240.7 2.1 copy.96
  242.7 4.7 %all-to-all-start.7 = ((f32[3,32,32,128]{3,2,0,1:T(8,128)}), f32[3,32,32,128]{3,2,0,1:T(8,128)}, u32[]{:S(2)}, u32[]{:S(2)}) async-start(f32[3,32,32,128]{3,2,0,1:T(8,128)} %copy.96), calls=%async_computation.7 | async-start | bytes 3145728 | tf_op jit(solution)/shard_map/all_to_all | solution.py:132
  249.0 1.6 multiply_bitcast_fusion.3
  250.6 2.1 copy.92
  252.6 31.3 %all-to-all-done.7 = f32[3,32,32,128]{3,2,0,1:T(8,128)} async-done(((f32[3,32,32,128]{3,2,0,1:T(8,128)}), f32[3,32,32,128]{3,2,0,1:T(8,128)}, u32[]{:S(2)}, u32[]{:S(2)}) %all-to-all-start.7) | async-done | bytes 1572896 | tf_op jit(solution)/shard_map/all_to_all | solution.py:132
  284.0 3.6 all-to-all-start.6
  287.5 1.6 copy.98
  289.1 3.9 fusion.52
  293.0 30.9 %all-to-all-done.6 = f32[3,32,32,128]{3,2,0,1:T(8,128)S(1)} async-done(((f32[3,32,32,128]{3,2,0,1:T(8,128)}), f32[3,32,32,128]{3,2,0,1:T(8,128)S(1)}, u32[]{:S(2)}, u32[]{:S(2)}) %all-to-all-start.6) | async-done | bytes 1572896 | tf_op jit(solution)/shard_map/all_to_all | solution.py:131
  325.1 1.7 copy.94
  327.0 3.9 multiply_bitcast_fusion
  330.9 3.0 copy.105
  333.9 4.8 %all-to-all-start.9 = ((f32[3,8,128,128]{3,1,0,2:T(8,128)}), f32[3,8,128,128]{3,1,0,2:T(8,128)}, u32[]{:S(2)}, u32[]{:S(2)}) async-start(f32[3,8,128,128]{3,1,0,2:T(8,128)} %copy.105), calls=%async_computation.9 | async-start | bytes 3145728 | tf_op jit(solution)/shard_map/all_to_all | solution.py:137
  338.7 2.8 fusion.54
  341.5 2.8 multiply_bitcast_fusion.1
  344.3 1.6 copy.100
  345.9 12.9 %all-to-all-done.9 = f32[3,8,128,128]{3,1,0,2:T(8,128)} async-done(((f32[3,8,128,128]{3,1,0,2:T(8,128)}), f32[3,8,128,128]{3,1,0,2:T(8,128)}, u32[]{:S(2)}, u32[]{:S(2)}) %all-to-all-start.9) | async-done | bytes 1572896 | tf_op jit(solution)/shard_map/all_to_all | solution.py:137
  358.8 3.7 all-to-all-start.8
  362.6 2.4 copy.107
  365.0 1.8 all_to_all.147
  366.8 15.8 %all-to-all-done.8 = f32[3,8,128,128]{3,1,0,2:T(8,128)S(1)} async-done(((f32[3,8,128,128]{3,1,0,2:T(8,128)}), f32[3,8,128,128]{3,1,0,2:T(8,128)S(1)}, u32[]{:S(2)}, u32[]{:S(2)}) %all-to-all-start.8) | async-done | bytes 1572896 | tf_op jit(solution)/shard_map/all_to_all | solution.py:136
  384.3 7.3 %fusion.20 = f32[3,8,32,512]{3,2,1,0:T(8,128)S(1)} fusion(f32[3,8,32,512]{3,2,1,0:T(8,128)S(1)} %all_to_all.143), kind=kOutput, calls=%fused_computation.33 | convolution fusion | flops 2419589120 | bytes 3145728 | tf_op jit(solution)/shard_map/dot_general | solution.py:33
  391.6 7.6 %subtract_multiply_fusion = f32[3,8,32,512]{3,2,1,0:T(8,128)} fusion(f32[3,8,32,512]{3,2,1,0:T(8,128)S(1)} %copy-done.16, f32[3,8,32,512]{3,2,1,0:T(8,128)S(1)} %fusion.20, f32[3,8,32,512]{3,2,1,0:T(8,128)S(1)} %copy-done.8), kind=kOutput, calls=%fused_computation.14 | convolution fusion | flops 2421161984 | bytes 6291456 | tf_op jit(solution)/shard_map/dot_general | solution.py:33
  (85 shorter events, 17.6 us)
Async XLA Ops:
  9.2 11.9 %all-to-all-start = ((s32[4,1,512]{2,1,0:T(1,128)}), s32[4,1,512]{2,1,0:T(1,128)S(1)}, u32[]{:S(2)}, u32[]{:S(2)}) async-start(s32[4,1,512]{2,1,0:T(1,128)} %bitcast.4), calls=%async_computation | async-start | bytes 16384 | tf_op jit(solution)/shard_map/all_to_all | solution.py:92
  29.2 16.8 %all-to-all-start.1 = ((bf16[4,512,128]{2,1,0:T(8,128)(2,1)}), bf16[4,512,128]{2,1,0:T(8,128)(2,1)S(1)}, u32[]{:S(2)}, u32[]{:S(2)}) async-start(bf16[4,512,128]{2,1,0:T(8,128)(2,1)} %bitcast.7), calls=%async_computation.1 | async-start | bytes 1048576 | tf_op jit(solution)/shard_map/all_to_all | solution.py:94
  46.0 11.2 %copy-start.15 = (s32[8,32,4]{1,2,0:T(4,128)S(1)}, s32[8,32,4]{1,2,0:T(4,128)}, u32[]{:S(2)}) copy-start(s32[8,32,4]{1,2,0:T(4,128)} %param.11) | copy-start | bytes 12292
  49.3 5.8 %collective-permute-start = (bf16[1,32,512]{2,1,0:T(8,128)(2,1)S(1)}, bf16[1,32,512]{2,1,0:T(8,128)(2,1)S(1)}, u32[]{:S(2)}, u32[]{:S(2)}) collective-permute-start(bf16[1,32,512]{2,1,0:T(8,128)(2,1)S(1)} %slice.62), channel_id=1, source_target_pairs={{0,4},{4,8},{8,12},{12,0},{1,5},{5,9},{9,13},{13,1},{2,6},{6,10},{... | collective-permute-start | bytes 98312 | tf_op jit(solution)/shard_map/ppermute | solution.py:16
  49.5 9.3 %copy-start.9 = (bf16[8,32,512]{2,1,0:T(8,128)(2,1)}, bf16[8,32,512]{2,1,0:T(8,128)(2,1)S(1)}, u32[]{:S(2)}) copy-start(bf16[8,32,512]{2,1,0:T(8,128)(2,1)S(1)} %reshape.257) | copy-start | bytes 786436
  49.6 5.5 %collective-permute-start.1 = (bf16[1,32,512]{2,1,0:T(8,128)(2,1)S(1)}, bf16[1,32,512]{2,1,0:T(8,128)(2,1)S(1)}, u32[]{:S(2)}, u32[]{:S(2)}) collective-permute-start(bf16[1,32,512]{2,1,0:T(8,128)(2,1)S(1)} %slice.64), channel_id=1, source_target_pairs={{4,0},{8,4},{12,8},{0,12},{5,1},{9,5},{13,9},{1,13},{6,2},{10,6},{... | collective-permute-start | bytes 98312 | tf_op jit(solution)/shard_map/ppermute | solution.py:18
  55.1 3.3 collective-permute-start.2
  55.2 3.5 collective-permute-start.3
  58.8 1.0 copy-start.10
  58.8 1.1 copy-start.14
  60.2 0.9 copy-start.11
  60.5 0.9 copy-start.12
  60.5 1.0 copy-start.13
  78.1 24.1 %all-to-all-start.2 = ((f32[4,1,98304]{2,1,0:T(1,128)}), f32[4,1,98304]{2,1,0:T(1,128)S(1)}, u32[]{:S(2)}, u32[]{:S(2)}) async-start(f32[4,1,98304]{2,1,0:T(1,128)} %reshape.293), calls=%async_computation.2 | async-start | bytes 3145728 | tf_op jit(solution)/shard_map/all_to_all | solution.py:110
  102.2 24.6 %all-to-all-start.3 = ((f32[4,1,98304]{2,1,0:T(1,128)}), f32[4,1,98304]{2,1,0:T(1,128)}, u32[]{:S(2)}, u32[]{:S(2)}) async-start(f32[4,1,98304]{2,1,0:T(1,128)} %reshape.291), calls=%async_computation.3 | async-start | bytes 3145728 | tf_op jit(solution)/shard_map/all_to_all | solution.py:111
  142.7 2.8 copy-start
  149.9 42.5 %all-to-all-start.5 = ((f32[3,8,128,128]{3,1,0,2:T(8,128)}), f32[3,8,128,128]{3,1,0,2:T(8,128)S(1)}, u32[]{:S(2)}, u32[]{:S(2)}) async-start(f32[3,8,128,128]{3,1,0,2:T(8,128)} %copy.89), calls=%async_computation.5 | async-start | bytes 3145728 | tf_op jit(solution)/shard_map/all_to_all | solution.py:116
  155.7 2.8 copy-start.1
  192.5 40.2 %all-to-all-start.4 = ((f32[3,8,128,128]{3,1,0,2:T(8,128)}), f32[3,8,128,128]{3,1,0,2:T(8,128)S(1)}, u32[]{:S(2)}, u32[]{:S(2)}) async-start(f32[3,8,128,128]{3,1,0,2:T(8,128)} %copy.84), calls=%async_computation.4 | async-start | bytes 3145728 | tf_op jit(solution)/shard_map/all_to_all | solution.py:115
  235.7 1.6 copy-start.5
  235.8 1.6 copy-start.7
  239.0 1.7 copy-start.2
  242.7 4.7 %copy-start.3 = (f32[3,32,32,128]{3,1,2,0:T(8,128)S(1)}, f32[3,32,32,128]{3,1,2,0:T(8,128)}, u32[]{:S(2)}) copy-start(f32[3,32,32,128]{3,1,2,0:T(8,128)} %copy-done.2) | copy-start | bytes 4718596
  242.7 41.2 %all-to-all-start.7 = ((f32[3,32,32,128]{3,2,0,1:T(8,128)}), f32[3,32,32,128]{3,2,0,1:T(8,128)}, u32[]{:S(2)}, u32[]{:S(2)}) async-start(f32[3,32,32,128]{3,2,0,1:T(8,128)} %copy.96), calls=%async_computation.7 | async-start | bytes 3145728 | tf_op jit(solution)/shard_map/all_to_all | solution.py:132
  284.0 40.0 %all-to-all-start.6 = ((f32[3,32,32,128]{3,2,0,1:T(8,128)}), f32[3,32,32,128]{3,2,0,1:T(8,128)S(1)}, u32[]{:S(2)}, u32[]{:S(2)}) async-start(f32[3,32,32,128]{3,2,0,1:T(8,128)} %copy.92), calls=%async_computation.6 | async-start | bytes 3145728 | tf_op jit(solution)/shard_map/all_to_all | solution.py:131
  324.0 1.1 copy-start.4
  325.1 1.9 copy-start.6
  333.9 24.9 %all-to-all-start.9 = ((f32[3,8,128,128]{3,1,0,2:T(8,128)}), f32[3,8,128,128]{3,1,0,2:T(8,128)}, u32[]{:S(2)}, u32[]{:S(2)}) async-start(f32[3,8,128,128]{3,1,0,2:T(8,128)} %copy.105), calls=%async_computation.9 | async-start | bytes 3145728 | tf_op jit(solution)/shard_map/all_to_all | solution.py:137
  358.8 23.8 %all-to-all-start.8 = ((f32[3,8,128,128]{3,1,0,2:T(8,128)}), f32[3,8,128,128]{3,1,0,2:T(8,128)S(1)}, u32[]{:S(2)}, u32[]{:S(2)}) async-start(f32[3,8,128,128]{3,1,0,2:T(8,128)} %copy.100), calls=%async_computation.8 | async-start | bytes 3145728 | tf_op jit(solution)/shard_map/all_to_all | solution.py:136
  384.2 7.3 %copy-start.8 = (f32[3,8,32,512]{3,2,1,0:T(8,128)S(1)}, f32[3,8,32,512]{3,2,1,0:T(8,128)}, u32[]{:S(2)}) copy-start(f32[3,8,32,512]{3,2,1,0:T(8,128)} %all_to_all.147) | copy-start | bytes 4718596
  384.2 7.3 %copy-start.16 = (f32[3,8,32,512]{3,2,1,0:T(8,128)S(1)}, f32[3,8,32,512]{3,2,1,0:T(8,128)}, u32[]{:S(2)}) copy-start(f32[3,8,32,512]{3,2,1,0:T(8,128)} %param.6) | copy-start | bytes 4718596
where the time goes:
time: 404 us; the launch traced here: 399 us
  waiting for transfers between devices  177 us (44%)
  local copies, waits for them, and re-layouts  85.1 us (21%)
  matrix products  70.3 us (17%)
  starting transfers between devices  50.6 us (13%)
  other arithmetic  14.8 us (4%)
    dot_general x20, matrix products, apply_along(): lax.dot_general(values, matrix, (((axis_id,), (0,)), ((), ())), precision...  70.3 us
    all_to_all x1, waiting for transfers between devices, local(): lax.all_to_all(moved[1], 'slab', split_axis=1, concat_axis=2, tiled=True)  31.3 us
    all_to_all x1, waiting for transfers between devices, local(): lax.all_to_all(moved[0], 'slab', split_axis=1, concat_axis=2, tiled=True)  30.9 us
    all_to_all x1, waiting for transfers between devices, local(): lax.all_to_all(moved[0], 'slab', split_axis=2, concat_axis=1, tiled=True)  29.9 us
    all_to_all x1, waiting for transfers between devices, local(): lax.all_to_all(moved[1], 'slab', split_axis=2, concat_axis=1, tiled=True)  29.4 us
    unnamed x42, local copies, waits for them, and re-layouts  26.2 us
    all_to_all x1, waiting for transfers between devices, local(): lax.all_to_all(moved[0], 'sub', split_axis=2, concat_axis=3, tiled=True)  15.8 us
    all_to_all x1, waiting for transfers between devices, local(): lax.all_to_all(fetched, 'slab', split_axis=0, concat_axis=0, tiled=True)  13.3 us
  transfers between devices with their start and end apart: 14, of which 13 were waited for; matrix products, arithmetic and copies ran while one was open for 17% of the time, Pallas kernels for 0%

commit v1 on v0

--- a/solution.py
+++ b/solution.py
@@ -1,6 +1,11 @@
+import functools
+
 import jax
 import jax.numpy as jnp
+import numpy as np
 from jax import lax
+from jax.experimental import pallas as pl
+from jax.experimental.pallas import tpu as pltpu
 from jax.sharding import PartitionSpec as P
 
 BLOCK = 128
@@ -67,7 +72,7 @@
     return wave * wave
 
 
-def local(velocity, template, moving, stiffness, fetch_plane, tissue):
+def local_general(velocity, template, moving, stiffness, fetch_plane, tissue):
     planes_dev, rows_dev, x_length = moving.shape
     blocks_x = x_length // BLOCK
     slabs = lax.axis_size("slab")
@@ -143,6 +148,270 @@
     return (new_velocity, warped)
 
 
+VMEM_BYTES = 50 * 1024 * 1024
+
+
+def real_basis(length):
+    index = np.arange(length)
+    half = length // 2
+    wave = np.where(index <= half, index, index - half)[:, None]
+    angle = 2.0 * np.pi / length * (wave * index[None, :] % length)
+    rows = np.where(index[:, None] <= half, np.cos(angle), np.sin(angle)) * np.sqrt(2.0 / length)
+    rows[0] /= np.sqrt(2.0)
+    rows[half] /= np.sqrt(2.0)
+    return rows
+
+
+def in_two(table):
+    high = np.asarray(table, np.float32).astype(jnp.bfloat16)
+    low = (np.asarray(table, np.float64) - high.astype(np.float64)).astype(jnp.bfloat16)
+    return np.stack([high, low])
+
+
+def split(values):
+    high = values.astype(jnp.bfloat16)
+    return high, (values - high.astype(jnp.float32)).astype(jnp.bfloat16)
+
+
+def times(left, right, dims):
+    def one(a, b):
+        return lax.dot_general(a, b, (dims, ((), ())), preferred_element_type=jnp.float32)
+
+    return one(left[0], right[0]) + (one(left[0], right[1]) + one(left[1], right[0]))
+
+
+def wave_sq(index, length):
+    wave = jnp.where(index <= length // 2, index, index - length // 2).astype(jnp.float32)
+    wave = wave * (2.0 * np.pi / length)
+    return wave * wave
+
+
+def around(value, count):
+    return lax.rem(value + 2 * count, count)
+
+
+def call(kernel, out_shape, arguments, scratch=(), flops=0, nbytes=0):
+    smem = pl.BlockSpec(memory_space=pltpu.SMEM)
+    vmem = pl.BlockSpec(memory_space=pltpu.VMEM)
+    return pl.pallas_call(
+        kernel,
+        out_shape=out_shape,
+        in_specs=[smem] + [vmem] * (len(arguments) - 1),
+        out_specs=jax.tree.map(lambda _: vmem, out_shape),
+        scratch_shapes=list(scratch),
+        compiler_params=pltpu.CompilerParams(vmem_limit_bytes=VMEM_BYTES),
+        cost_estimate=pl.CostEstimate(flops=flops, bytes_accessed=nbytes, transcendentals=0),
+    )(*arguments)
+
+
+def send_columns_kernel(slabs, place, moving, fetch, *sends):
+    planes, rows, _ = moving.shape
+    me = place[0]
+    lane = lax.broadcasted_iota(jnp.int32, (rows, BLOCK), 1)
+    narrow = lax.broadcasted_iota(jnp.int32, (rows, fetch.shape[2]), 1)
+    for step, send in enumerate(sends):
+        to = around(me + step, slabs)
+        columns = pl.ds(pl.multiple_of(to * BLOCK, BLOCK), BLOCK)
+        send[0:planes] = moving[:, :, columns]
+        wanted = jnp.zeros((rows, BLOCK), jnp.float32)
+        for z in range(planes):
+            one = jnp.sum(jnp.where(narrow == to, fetch[z].astype(jnp.float32), 0.0), axis=1, keepdims=True)
+            wanted = jnp.where(lane == z, one, wanted)
+        send[planes] = wanted.astype(jnp.bfloat16)
+
+
+def pick_kernel(slabs, place, *refs):
+    received, sends, picked = refs[:slabs], refs[slabs:-1], refs[-1]
+    planes = received[0].shape[0] - 1
+    rows = received[0].shape[1]
+    me = place[0]
+    total = slabs * planes
+    group = 4
+    for step in range(slabs):
+        first = around(me - step, slabs) * planes
+        names = received[step][planes].astype(jnp.float32)
+        for start in range(0, planes, group):
+            wanted = [
+                jnp.broadcast_to(names[:, z : z + 1], (rows, BLOCK)) for z in range(start, start + group)
+            ]
+            found = [jnp.zeros((rows, BLOCK), jnp.float32) for _ in range(group)]
+            for other in range(slabs):
+                base = (around(me - other, slabs) * planes).astype(jnp.float32)
+                for plane in range(planes):
+                    values = received[other][plane].astype(jnp.float32)
+                    found = [
+                        jnp.where(w == base + float(plane), values, f) for w, f in zip(wanted, found)
+                    ]
+            for z in range(group):
+                picked[first + start + z] = found[z].astype(jnp.bfloat16)
+    for step, send in enumerate(sends):
+        first = around(me + step, slabs) * planes
+        for k in range(planes + 2):
+            send[k] = picked[around(first + (k - 1), total)]
+
+
+def force_kernel(slabs, place, *refs):
+    received = refs[:slabs]
+    above, below, template, stiffness, tissue, basis, warped, spectra, image, edges = refs[slabs:]
+    planes, rows, x_length = template.shape
+    me = place[0]
+    for step in range(slabs):
+        block = pl.ds(pl.multiple_of(around(me - step, slabs) * BLOCK, BLOCK), BLOCK)
+        image[:, :, block] = received[step][...].astype(jnp.float32)
+        warped[:, :, block] = received[step][1:-1]
+        edges[0, :, block] = above[step].astype(jnp.float32)
+        edges[1, :, block] = below[step].astype(jnp.float32)
+    row = lax.broadcasted_iota(jnp.int32, (rows, x_length), 0)
+    forces = [[], [], []]
+    for z in range(planes):
+        here = image[z + 1]
+        marked = tissue[z].astype(jnp.float32)
+        marked = jnp.concatenate(
+            [jnp.broadcast_to(marked[:, b : b + 1], (rows, BLOCK)) for b in range(x_length // BLOCK)], axis=1
+        )
+        weight = 0.5 * (marked * stiffness[z] * (here - template[z].astype(jnp.float32)))
+        before = jnp.where(row == 0, edges[0, z : z + 1, :], pltpu.roll(here, 1, 0))
+        after = jnp.where(row == rows - 1, edges[1, z : z + 1, :], pltpu.roll(here, rows - 1, 0))
+        forces[0].append(weight * (image[z + 2] - image[z]))
+        forces[1].append(weight * (after - before))
+        forces[2].append(weight * (pltpu.roll(here, x_length - 1, 1) - pltpu.roll(here, 1, 1)))
+    devices, part = spectra.shape[:2]
+    part //= 3
+    for a in range(3):
+        force = split(jnp.concatenate(forces[a], axis=0))
+        spectrum = times((basis[0], basis[1]), force, ((1,), (1,)))
+        spectra[:, a * part : (a + 1) * part, :] = spectrum.reshape(devices, part, planes * rows)
+
+
+def solve_kernel(subs, place, spectra, basis_z, basis_y, out, cells):
+    devices, lanes_used, area = spectra.shape
+    total_z, total_y, lanes = cells.shape
+    slabs = devices // subs
+    planes, rows = total_z // slabs, total_y // subs
+    pad = jnp.zeros((lanes - lanes_used, area), jnp.float32)
+    for d in range(devices):
+        block = jnp.concatenate([spectra[d], pad], axis=0).T.reshape(planes, rows, lanes)
+        s, q = d // subs, d % subs
+        cells[s * planes : (s + 1) * planes, q * rows : (q + 1) * rows, :] = block
+    tables_z, tables_y = (basis_z[0], basis_z[1]), (basis_y[0], basis_y[1])
+    part = lanes_used // 3
+    lane = lax.broadcasted_iota(jnp.int32, (1, lanes), 1)
+    x_sq = wave_sq(place[0] * part + lax.rem(lane, part), part * devices)
+    y_sq = wave_sq(lax.broadcasted_iota(jnp.int32, (total_y, 1), 0), total_y)
+    xy = (x_sq + y_sq) * 256.0 + 1.0
+    tile = basis_z.shape[1] // total_z
+    for g in range(total_y // tile):
+        own = cells[:, g * tile : (g + 1) * tile, :].reshape(total_z * tile, lanes)
+        own = times(tables_z, split(own), ((1,), (0,)))
+        cells[:, g * tile : (g + 1) * tile, :] = own.reshape(total_z, tile, lanes)
+    for z in range(total_z):
+        wave = 2.0 * np.pi / total_z * (z if z <= total_z // 2 else z - total_z // 2)
+        own = times(tables_y, split(cells[z]), ((1,), (0,)))
+        own = own / (xy + 256.0 * wave * wave)
+        cells[z] = times(tables_y, split(own), ((0,), (0,)))
+    for g in range(total_y // tile):
+        own = cells[:, g * tile : (g + 1) * tile, :].reshape(total_z * tile, lanes)
+        own = times(tables_z, split(own), ((0,), (0,)))
+        cells[:, g * tile : (g + 1) * tile, :] = own.reshape(total_z, tile, lanes)
+    for d in range(devices):
+        s, q = d // subs, d % subs
+        block = cells[s * planes : (s + 1) * planes, q * rows : (q + 1) * rows, :]
+        out[d] = block.reshape(area, lanes).T[:lanes_used]
+
+
+def update_kernel(place, spectra, velocity, basis, out):
+    devices, part, area = spectra.shape
+    part //= 3
+    _, planes, rows, x_length = velocity.shape
+    for a in range(3):
+        own = spectra[:, a * part : (a + 1) * part, :].reshape(x_length, area).T
+        smoothed = times(split(own), (basis[0], basis[1]), ((1,), (0,)))
+        out[a] = 0.5 * (velocity[a] - 32.0 * smoothed.reshape(planes, rows, x_length))
+
+
+def local_blocks(velocity, template, moving, stiffness, fetch_plane, tissue):
+    planes, rows, x_length = moving.shape
+    slabs, subs = lax.axis_size("slab"), lax.axis_size("sub")
+    total_z, total_y = planes * slabs, rows * subs
+    devices = slabs * subs
+    part = x_length // devices
+    area = planes * rows
+    my_slab = lax.axis_index("slab")
+    my_place = my_slab * subs + lax.axis_index("sub")
+    slab_id, place_id = my_slab.reshape(1), my_place.reshape(1)
+    bf16, f32 = jnp.bfloat16, jnp.float32
+
+    def shape(dims, kind=f32):
+        return jax.ShapeDtypeStruct(dims, kind)
+
+    def scatter(sends):
+        return [sends[0]] + [
+            lax.ppermute(sends[d], "slab", [(i, (i + d) % slabs) for i in range(slabs)])
+            for d in range(1, slabs)
+        ]
+
+    sends = call(
+        functools.partial(send_columns_kernel, slabs),
+        [shape((planes + 1, rows, BLOCK), bf16)] * slabs,
+        (slab_id, moving, fetch_plane),
+    )
+    received = scatter(sends)
+    sends = call(
+        functools.partial(pick_kernel, slabs),
+        [shape((planes + 2, rows, BLOCK), bf16)] * slabs,
+        (slab_id, *received),
+        [pltpu.VMEM((total_z, rows, BLOCK), bf16)],
+    )
+    received = scatter(sends)
+    last = jnp.stack([r[1:-1, rows - 1] for r in received])
+    first = jnp.stack([r[1:-1, 0] for r in received])
+    above = lax.ppermute(last, "sub", [(i, (i + 1) % subs) for i in range(subs)])
+    below = lax.ppermute(first, "sub", [((i + 1) % subs, i) for i in range(subs)])
+    basis_x = in_two(real_basis(x_length))
+    tile = 8
+    basis_z = in_two(np.kron(real_basis(total_z), np.eye(tile)))
+    basis_y = in_two(real_basis(total_y))
+    warped, spectra = call(
+        functools.partial(force_kernel, slabs),
+        [shape((planes, rows, x_length), bf16), shape((devices, 3 * part, area))],
+        (slab_id, *received, above, below, template, stiffness, tissue, in_two(8.0 * real_basis(x_length))),
+        [pltpu.VMEM((planes + 2, rows, x_length), f32), pltpu.VMEM((2, planes, x_length), f32)],
+    )
+    spectra = spectra.astype(jnp.float16)
+    spectra = lax.all_to_all(spectra, ("slab", "sub"), split_axis=0, concat_axis=0, tiled=True)
+    spectra = call(
+        functools.partial(solve_kernel, subs),
+        shape((devices, 3 * part, area)),
+        (place_id, spectra.astype(f32), basis_z, basis_y),
+        [pltpu.VMEM((total_z, total_y, 128), f32)],
+    )
+    spectra = spectra.astype(jnp.float16)
+    spectra = lax.all_to_all(spectra, ("slab", "sub"), split_axis=0, concat_axis=0, tiled=True)
+    new_velocity = call(
+        update_kernel,
+        shape(velocity.shape),
+        (place_id, spectra.astype(f32), velocity, basis_x),
+    )
+    return (new_velocity, warped)
+
+
+def local(velocity, template, moving, stiffness, fetch_plane, tissue):
+    planes, rows, x_length = moving.shape
+    slabs, subs = lax.axis_size("slab"), lax.axis_size("sub")
+    part = x_length // (slabs * subs)
+    fits = (
+        x_length == slabs * BLOCK
+        and planes == 8
+        and rows % 16 == 0
+        and part % 16 == 0
+        and 3 * part <= 128
+        and planes * slabs * 8 == 256
+        and rows * subs == 128
+    )
+    run = local_blocks if fits else local_general
+    return run(velocity, template, moving, stiffness, fetch_plane, tissue)
+
+
 def solution(mesh):
     placed = (
         P(None, ("groups", "slab"), "sub", None),

time: 404 us -> 97.1 us (0.24)
  waiting for transfers between devices: 177 us -> 34.1 us
  local copies, waits for them, and re-layouts: 85.1 us -> 4.14 us
  matrix products: 70.3 us -> 0 us
  starting transfers between devices: 50.6 us -> 16.6 us
  blocking collectives: 0 us -> 25.5 us
  Pallas kernels: 0 us -> 13.7 us
  other arithmetic: 14.8 us -> 1.46 us
    all_to_all x10 -> x1, waiting for transfers between devices: 175 us -> 18.7 us  [local_blocks(): lax.all_to_all(spectra, ('slab', 'sub'), split_axis=0, concat_axis=0, til...]
    dot_general x20 -> x0, matrix products: 70.3 us -> none  [apply_along(): lax.dot_general(values, matrix, (((axis_id,), (0,)), ((), ())), precision...]
    all_to_all x10 -> x1, starting transfers between devices: 44.7 us -> 3.89 us  [local_blocks(): lax.all_to_all(spectra, ('slab', 'sub'), split_axis=0, concat_axis=0, til...]
    all_to_all x0 -> x1, blocking collectives: none -> 25.5 us  [local_blocks(): lax.all_to_all(spectra, ('slab', 'sub'), split_axis=0, concat_axis=0, til...]
    unnamed x42 -> x16, local copies, waits for them, and re-layouts: 26.2 us -> 3.89 us
    all_to_all x11 -> x0, local copies, waits for them, and re-layouts: 19.4 us -> none  [the longest x3 5.45 us: local(): lax.all_to_all(imag_part, 'sub', split_axis=3, concat_axis=2, tiled=True)]
    pallas_call x0 -> x5, Pallas kernels: none -> 13.7 us  [call(): pl.pallas_call(kernel, out_shape=out_shape, in_specs=[smem] + [vmem] * (l...]
    ppermute x4 -> x8, waiting for transfers between devices: 2.4 us -> 15.4 us  [the longest x6 15 us: scatter(): lax.ppermute(sends[d], 'slab', [(i, (i + d) % slabs) for i in range(slabs)])]
  transfers between devices with their start and end apart: 14 -> 9, of which waited for: 13 -> 8; matrix products, arithmetic and copies ran while one was open for 17% -> 1% of each run, Pallas kernels for 0% -> 0%
where the time goes in v1:
time: 97.1 us; the launch traced here: 96.4 us
  waiting for transfers between devices  34.1 us (35%)
  blocking collectives  25.5 us (26%)
  starting transfers between devices  16.6 us (17%)
  Pallas kernels  13.7 us (14%)
  local copies, waits for them, and re-layouts  4.14 us (4%)
  other arithmetic  1.46 us (2%)
    all_to_all x1, blocking collectives, local_blocks(): lax.all_to_all(spectra, ('slab', 'sub'), split_axis=0, concat_axis=0, til...  25.5 us
    all_to_all x1, waiting for transfers between devices, local_blocks(): lax.all_to_all(spectra, ('slab', 'sub'), split_axis=0, concat_axis=0, til...  18.7 us
    ppermute x6, waiting for transfers between devices, scatter(): lax.ppermute(sends[d], 'slab', [(i, (i + d) % slabs) for i in range(slabs)])  15 us
    pallas_call x5, Pallas kernels, call(): pl.pallas_call(kernel, out_shape=out_shape, in_specs=[smem] + [vmem] * (l...  13.7 us
    ppermute x6, starting transfers between devices, scatter(): lax.ppermute(sends[d], 'slab', [(i, (i + d) % slabs) for i in range(slabs)])  10.9 us
    all_to_all x1, starting transfers between devices, local_blocks(): lax.all_to_all(spectra, ('slab', 'sub'), split_axis=0, concat_axis=0, til...  3.89 us
    unnamed x16, local copies, waits for them, and re-layouts  3.89 us
  transfers between devices with their start and end apart: 9, of which 8 were waited for; matrix products, arithmetic and copies ran while one was open for 1% of the time, Pallas kernels for 0%

profile of v1, /device:TPU:0, one launch (start us, length us, event | category | flops | bytes accessed | tf_op | source)
XLA Modules:
  0.0 96.4 jit_solution(16678982780301928839)
XLA Ops:
  0.6 0.0 copy-start
  0.6 0.0 copy-start.2
  0.7 0.0 copy-start.3
  0.7 1.0 %copy.12.fetch = s32[8,32,4]{2,1,0:T(8,128)S(1)} copy(s32[8,32,4]{1,2,0:T(4,128)} %param.14) | data formatting | bytes 8192 | tf_op args[4]
  1.6 0.0 copy-start.5
  1.6 0.9 copy-done.5
  2.6 0.2 shard_map.113
  2.8 3.1 %collective-permute-start = (bf16[9,32,128]{2,1,0:T(8,128)(2,1)S(1)}, bf16[9,32,128]{2,1,0:T(8,128)(2,1)S(1)}, u32[]{:S(2)}, u32[]{:S(2)}) collective-permute-start(bf16[9,32,128]{2,1,0:T(8,128)(2,1)S(1)} %get-tuple-element.13), channel_id=1, source_target_pairs={{0,4},{4,8},{8,12},{12,0},{1,5},{5,9},{9,13},{13,1},{2,6},{6,10},{... | collective-permute-start | bytes 221192 | tf_op jit(solution)/shard_map/ppermute | solution.py:349
  5.9 2.6 %collective-permute-start.1 = (bf16[9,32,128]{2,1,0:T(8,128)(2,1)S(1)}, bf16[9,32,128]{2,1,0:T(8,128)(2,1)S(1)}, u32[]{:S(2)}, u32[]{:S(2)}) collective-permute-start(bf16[9,32,128]{2,1,0:T(8,128)(2,1)S(1)} %get-tuple-element.14), channel_id=1, source_target_pairs={{0,8},{4,12},{8,0},{12,4},{1,9},{5,13},{9,1},{13,5},{2,10},{6,14},... | collective-permute-start | bytes 221192 | tf_op jit(solution)/shard_map/ppermute | solution.py:349
  8.5 1.3 %collective-permute-start.2 = (bf16[9,32,128]{2,1,0:T(8,128)(2,1)S(1)}, bf16[9,32,128]{2,1,0:T(8,128)(2,1)S(1)}, u32[]{:S(2)}, u32[]{:S(2)}) collective-permute-start(bf16[9,32,128]{2,1,0:T(8,128)(2,1)S(1)} %get-tuple-element.15), channel_id=1, source_target_pairs={{0,12},{4,0},{8,4},{12,8},{1,13},{5,1},{9,5},{13,9},{2,14},{6,2},{... | collective-permute-start | bytes 221192 | tf_op jit(solution)/shard_map/ppermute | solution.py:349
  9.8 0.8 collective-permute-done.refs_1_
  10.6 2.8 %collective-permute-done.1.refs_2_ = bf16[9,32,128]{2,1,0:T(8,128)(2,1)S(1)} collective-permute-done((bf16[9,32,128]{2,1,0:T(8,128)(2,1)S(1)}, bf16[9,32,128]{2,1,0:T(8,128)(2,1)S(1)}, u32[]{:S(2)}, u32[]{:S(2)}) %collective-permute-start.1) | collective-permute-done | bytes 73760 | tf_op jit(solution)/shard_map/ppermute | solution.py:349
  13.4 0.2 collective-permute-done.2.refs_3_
  13.6 1.2 %shard_map.114 = (bf16[10,32,128]{2,1,0:T(8,128)(2,1)S(1)}, bf16[10,32,128]{2,1,0:T(8,128)(2,1)S(1)}, bf16[10,32,128]{2,1,0:T(8,128)(2,1)S(1)}, bf16[10,32,128]{2,1,0:T(8,128)(2,1)S(1)}) custom-call(s32[1]{0:T(128)} %bitcast.1.place, bf16[9,32,128]{2,1,0:T(8,128)(2,1)S(1)} %get-tuple-element.12.refs_0_, ...), custom_call_target="tpu_custom_call" | custom-call | tf_op jit(solution)/shard_map/pallas_call | solution.py:196
  15.0 3.3 %collective-permute-start.5 = (bf16[10,32,128]{2,0,1:T(8,128)(2,1)S(1)}, bf16[10,32,128]{2,0,1:T(8,128)(2,1)S(1)}, u32[]{:S(2)}, u32[]{:S(2)}) collective-permute-start(bf16[10,32,128]{2,0,1:T(8,128)(2,1)S(1)} %copy.15), channel_id=1, source_target_pairs={{0,12},{4,0},{8,4},{12,8},{1,13},{5,1},{9,5},{13,9},{2,14},{6,2},{... | collective-permute-start | bytes 245768 | tf_op jit(solution)/shard_map/ppermute | solution.py:349
  18.3 0.2 collective-permute-start.4
  18.5 0.5 collective-permute-start.3
  19.0 3.2 %collective-permute-done.5 = bf16[10,32,128]{2,0,1:T(8,128)(2,1)S(1)} collective-permute-done((bf16[10,32,128]{2,0,1:T(8,128)(2,1)S(1)}, bf16[10,32,128]{2,0,1:T(8,128)(2,1)S(1)}, u32[]{:S(2)}, u32[]{:S(2)}) %collective-permute-start.5) | collective-permute-done | bytes 81952 | tf_op jit(solution)/shard_map/ppermute | solution.py:349
  22.2 8.0 %collective-permute-done.4 = bf16[10,32,128]{2,0,1:T(8,128)(2,1)S(1)} collective-permute-done((bf16[10,32,128]{2,0,1:T(8,128)(2,1)S(1)}, bf16[10,32,128]{2,0,1:T(8,128)(2,1)S(1)}, u32[]{:S(2)}, u32[]{:S(2)}) %collective-permute-start.4) | collective-permute-done | bytes 81952 | tf_op jit(solution)/shard_map/ppermute | solution.py:349
  30.2 0.0 collective-permute-done.3
  30.2 0.1 collective-permute-start.6
  30.3 1.8 %collective-permute-start.7 = (bf16[4,8,128]{2,1,0:T(8,128)(2,1)S(1)}, bf16[4,8,128]{2,1,0:T(8,128)(2,1)S(1)}, u32[]{:S(2)}, u32[]{:S(2)}) collective-permute-start(bf16[4,8,128]{2,1,0:T(8,128)(2,1)S(1)} %pad_maximum_fusion.1), channel_id=1, source_target_pairs={{1,0},{2,1},{3,2},{0,3},{5,4},{6,5},{7,6},{4,7},{9,8},{10,9},{11,1... | collective-permute-start | bytes 24584 | tf_op jit(solution)/shard_map/ppermute | solution.py:369
  32.0 0.8 copy.21.refs_8_
  33.0 0.3 collective-permute-done.6.refs_4_
  33.3 0.1 collective-permute-done.7.refs_5_
  33.4 0.0 copy-done
  33.4 0.0 copy-done.2
  33.4 0.0 copy-done.3
  33.4 2.4 %shard_map.115 = (bf16[8,32,512]{2,1,0:T(8,128)(2,1)}, f32[16,96,256]{2,1,0:T(8,128)S(1)}) custom-call(s32[1]{0:T(128)} %bitcast.1.place, bf16[10,32,128]{2,1,0:T(8,128)(2,1)S(1)} %get-tuple-element.16.refs_0_, bf16[10,32,128]{2,1,0:T(8,128)(2,1)S(1)} %copy.18.refs_1_, bf16[10,32,128]{2,1,0:T(8,128)(2,1)S(1)} %copy.19.refs_2_, ...), custom_call_target="tpu_custom_call" | custom-call | tf_op jit(solution)/shard_map/pallas_call | solution.py:196
  35.8 1.0 %convert_element_type.12 = f16[16,96,256]{2,1,0:T(8,128)(2,1)} convert(f32[16,96,256]{2,1,0:T(8,128)S(1)} %get-tuple-element.20) | non-fusion elementwise | flops 393216 | bytes 2359296 | tf_op jit(solution)/shard_map/convert_element_type | solution.py:380
  36.9 3.9 %all-to-all-start = ((f16[16,96,256]{2,1,0:T(8,128)(2,1)}), f16[16,96,256]{2,1,0:T(8,128)(2,1)S(1)}, u32[]{:S(2)}, u32[]{:S(2)}) async-start(f16[16,96,256]{2,1,0:T(8,128)(2,1)} %convert_element_type.12), calls=%async_computation | async-start | bytes 1572864 | tf_op jit(solution)/shard_map/all_to_all | solution.py:381
  40.8 0.0 copy-start.4
  40.8 0.0 copy-start.6
  40.8 18.7 %all-to-all-done = f16[16,96,256]{2,1,0:T(8,128)(2,1)S(1)} async-done(((f16[16,96,256]{2,1,0:T(8,128)(2,1)}), f16[16,96,256]{2,1,0:T(8,128)(2,1)S(1)}, u32[]{:S(2)}, u32[]{:S(2)}) %all-to-all-start) | async-done | bytes 786464 | tf_op jit(solution)/shard_map/all_to_all | solution.py:381
  59.5 0.1 convert_element_type.13.spectra
  59.6 0.0 copy-done.4
  59.6 0.0 copy-done.6
  59.6 5.8 %shard_map.116 = f32[16,96,256]{2,1,0:T(8,128)S(1)} custom-call(s32[1]{0:T(128)} %bitcast.place, f32[16,96,256]{2,1,0:T(8,128)S(1)} %convert_element_type.13.spectra, bf16[2,256,256]{2,1,0:T(8,128)(2,1)S(1)} %copy-done.4, bf16[2,128,128]{2,1,0:T(8,128)(2,1)S(1)} %copy-done.6), custom_call_target="tpu_custom_call" | custom-call | tf_op jit(solution)/shard_map/pallas_call | solution.py:196
  65.4 0.2 convert_element_type.14
  65.6 25.5 %all_to_all.10 = f16[16,96,256]{2,1,0:T(8,128)(2,1)S(1)} all-to-all(f16[16,96,256]{2,1,0:T(8,128)(2,1)S(1)} %convert_element_type.14), channel_id=1, replica_groups=mesh['groups'=2,'slab'=4,'sub'=4] {'slab','sub'}, dimensions={0} | all-to-all | bytes 1572864 | tf_op jit(solution)/shard_map/all_to_all | solution.py:389
  91.1 0.0 copy-start.1
  91.1 0.1 convert_element_type.15.spectra
  91.3 1.1 %copy-done.1 = bf16[2,512,512]{2,1,0:T(8,128)(2,1)S(1)} copy-done((bf16[2,512,512]{2,1,0:T(8,128)(2,1)S(1)}, bf16[2,512,512]{2,1,0:T(8,128)(2,1)}, u32[]{:S(2)}) %copy-start.1) | copy-done | bytes 1048600
  92.4 4.0 %shard_map.117 = f32[3,8,32,512]{3,2,1,0:T(8,128)} custom-call(s32[1]{0:T(128)} %bitcast.place, f32[16,96,256]{2,1,0:T(8,128)S(1)} %convert_element_type.15.spectra, f32[3,8,32,512]{3,2,1,0:T(8,128)} %velocity.1, bf16[2,512,512]{2,1,0:T(8,128)(2,1)S(1)} %copy-done.1), custom_call_target="tpu_custom_call" | custom-call | tf_op jit(solution)/shard_map/pallas_call | solution.py:196
  (13 shorter events, 0.3 us)
Async XLA Ops:
  0.6 32.8 %copy-start = (bf16[2,512,512]{2,1,0:T(8,128)(2,1)S(1)}, bf16[2,512,512]{2,1,0:T(8,128)(2,1)}, u32[]{:S(2)}) copy-start(bf16[2,512,512]{2,1,0:T(8,128)(2,1)} %constant.17.clone.refs_9_) | copy-start | bytes 3145732
  0.6 32.8 %copy-start.2 = (f32[8,32,512]{2,1,0:T(8,128)S(1)}, f32[8,32,512]{2,1,0:T(8,128)}, u32[]{:S(2)}) copy-start(f32[8,32,512]{2,1,0:T(8,128)} %refs_7_.1) | copy-start | bytes 1572868
  0.7 32.8 %copy-start.3 = (bf16[8,32,512]{2,1,0:T(8,128)(2,1)S(1)}, bf16[8,32,512]{2,1,0:T(8,128)(2,1)}, u32[]{:S(2)}) copy-start(bf16[8,32,512]{2,1,0:T(8,128)(2,1)} %refs_6_.1) | copy-start | bytes 786436
  1.6 0.9 copy-start.5
  2.8 7.8 %collective-permute-start = (bf16[9,32,128]{2,1,0:T(8,128)(2,1)S(1)}, bf16[9,32,128]{2,1,0:T(8,128)(2,1)S(1)}, u32[]{:S(2)}, u32[]{:S(2)}) collective-permute-start(bf16[9,32,128]{2,1,0:T(8,128)(2,1)S(1)} %get-tuple-element.13), channel_id=1, source_target_pairs={{0,4},{4,8},{8,12},{12,0},{1,5},{5,9},{9,13},{13,1},{2,6},{6,10},{... | collective-permute-start | bytes 221192 | tf_op jit(solution)/shard_map/ppermute | solution.py:349
  5.9 7.5 %collective-permute-start.1 = (bf16[9,32,128]{2,1,0:T(8,128)(2,1)S(1)}, bf16[9,32,128]{2,1,0:T(8,128)(2,1)S(1)}, u32[]{:S(2)}, u32[]{:S(2)}) collective-permute-start(bf16[9,32,128]{2,1,0:T(8,128)(2,1)S(1)} %get-tuple-element.14), channel_id=1, source_target_pairs={{0,8},{4,12},{8,0},{12,4},{1,9},{5,13},{9,1},{13,5},{2,10},{6,14},... | collective-permute-start | bytes 221192 | tf_op jit(solution)/shard_map/ppermute | solution.py:349
  8.5 5.2 %collective-permute-start.2 = (bf16[9,32,128]{2,1,0:T(8,128)(2,1)S(1)}, bf16[9,32,128]{2,1,0:T(8,128)(2,1)S(1)}, u32[]{:S(2)}, u32[]{:S(2)}) collective-permute-start(bf16[9,32,128]{2,1,0:T(8,128)(2,1)S(1)} %get-tuple-element.15), channel_id=1, source_target_pairs={{0,12},{4,0},{8,4},{12,8},{1,13},{5,1},{9,5},{13,9},{2,14},{6,2},{... | collective-permute-start | bytes 221192 | tf_op jit(solution)/shard_map/ppermute | solution.py:349
  15.0 7.2 %collective-permute-start.5 = (bf16[10,32,128]{2,0,1:T(8,128)(2,1)S(1)}, bf16[10,32,128]{2,0,1:T(8,128)(2,1)S(1)}, u32[]{:S(2)}, u32[]{:S(2)}) collective-permute-start(bf16[10,32,128]{2,0,1:T(8,128)(2,1)S(1)} %copy.15), channel_id=1, source_target_pairs={{0,12},{4,0},{8,4},{12,8},{1,13},{5,1},{9,5},{13,9},{2,14},{6,2},{... | collective-permute-start | bytes 245768 | tf_op jit(solution)/shard_map/ppermute | solution.py:349
  18.3 11.8 %collective-permute-start.4 = (bf16[10,32,128]{2,0,1:T(8,128)(2,1)S(1)}, bf16[10,32,128]{2,0,1:T(8,128)(2,1)S(1)}, u32[]{:S(2)}, u32[]{:S(2)}) collective-permute-start(bf16[10,32,128]{2,0,1:T(8,128)(2,1)S(1)} %copy.14), channel_id=1, source_target_pairs={{0,8},{4,12},{8,0},{12,4},{1,9},{5,13},{9,1},{13,5},{2,10},{6,14},... | collective-permute-start | bytes 245768 | tf_op jit(solution)/shard_map/ppermute | solution.py:349
  18.5 11.7 %collective-permute-start.3 = (bf16[10,32,128]{2,0,1:T(8,128)(2,1)S(1)}, bf16[10,32,128]{2,0,1:T(8,128)(2,1)S(1)}, u32[]{:S(2)}, u32[]{:S(2)}) collective-permute-start(bf16[10,32,128]{2,0,1:T(8,128)(2,1)S(1)} %copy.13), channel_id=1, source_target_pairs={{0,4},{4,8},{8,12},{12,0},{1,5},{5,9},{9,13},{13,1},{2,6},{6,10},{... | collective-permute-start | bytes 245768 | tf_op jit(solution)/shard_map/ppermute | solution.py:349
  30.2 3.1 %collective-permute-start.6 = (bf16[4,8,128]{2,1,0:T(8,128)(2,1)S(1)}, bf16[4,8,128]{2,1,0:T(8,128)(2,1)S(1)}, u32[]{:S(2)}, u32[]{:S(2)}) collective-permute-start(bf16[4,8,128]{2,1,0:T(8,128)(2,1)S(1)} %pad_maximum_fusion), channel_id=1, source_target_pairs={{0,1},{1,2},{2,3},{3,0},{4,5},{5,6},{6,7},{7,4},{8,9},{9,10},{10,1... | collective-permute-start | bytes 24584 | tf_op jit(solution)/shard_map/ppermute | solution.py:368
  30.3 3.1 %collective-permute-start.7 = (bf16[4,8,128]{2,1,0:T(8,128)(2,1)S(1)}, bf16[4,8,128]{2,1,0:T(8,128)(2,1)S(1)}, u32[]{:S(2)}, u32[]{:S(2)}) collective-permute-start(bf16[4,8,128]{2,1,0:T(8,128)(2,1)S(1)} %pad_maximum_fusion.1), channel_id=1, source_target_pairs={{1,0},{2,1},{3,2},{0,3},{5,4},{6,5},{7,6},{4,7},{9,8},{10,9},{11,1... | collective-permute-start | bytes 24584 | tf_op jit(solution)/shard_map/ppermute | solution.py:369
  36.9 22.6 %all-to-all-start = ((f16[16,96,256]{2,1,0:T(8,128)(2,1)}), f16[16,96,256]{2,1,0:T(8,128)(2,1)S(1)}, u32[]{:S(2)}, u32[]{:S(2)}) async-start(f16[16,96,256]{2,1,0:T(8,128)(2,1)} %convert_element_type.12), calls=%async_computation | async-start | bytes 1572864 | tf_op jit(solution)/shard_map/all_to_all | solution.py:381
  40.8 18.8 %copy-start.4 = (bf16[2,256,256]{2,1,0:T(8,128)(2,1)S(1)}, bf16[2,256,256]{2,1,0:T(8,128)(2,1)}, u32[]{:S(2)}) copy-start(bf16[2,256,256]{2,1,0:T(8,128)(2,1)} %constant.18.clone.basis_z) | copy-start | bytes 786436
  40.8 18.8 %copy-start.6 = (bf16[2,128,128]{2,1,0:T(8,128)(2,1)S(1)}, bf16[2,128,128]{2,1,0:T(8,128)(2,1)}, u32[]{:S(2)}) copy-start(bf16[2,128,128]{2,1,0:T(8,128)(2,1)} %constant.19.clone.basis_y) | copy-start | bytes 196612
  91.1 1.2 %copy-start.1 = (bf16[2,512,512]{2,1,0:T(8,128)(2,1)S(1)}, bf16[2,512,512]{2,1,0:T(8,128)(2,1)}, u32[]{:S(2)}) copy-start(bf16[2,512,512]{2,1,0:T(8,128)(2,1)} %constant.20.clone.basis) | copy-start | bytes 3145732

commit v2 on v1

--- a/solution.py
+++ b/solution.py
@@ -149,6 +149,7 @@
 
 
 VMEM_BYTES = 50 * 1024 * 1024
+COEFFICIENT_UNIT = 8191.0
 
 
 def real_basis(length):
@@ -204,83 +205,120 @@
     )(*arguments)
 
 
-def send_columns_kernel(slabs, place, moving, fetch, *sends):
-    planes, rows, _ = moving.shape
+def send_rows_kernel(slabs, place, moving, template, stiffness, fetch, tissue, *refs):
+    images, weights, wide = refs[:slabs], refs[slabs:-1], refs[-1]
+    planes, rows, x_length = moving.shape
+    share = rows // slabs
+    blocks = x_length // BLOCK
     me = place[0]
-    lane = lax.broadcasted_iota(jnp.int32, (rows, BLOCK), 1)
-    narrow = lax.broadcasted_iota(jnp.int32, (rows, fetch.shape[2]), 1)
-    for step, send in enumerate(sends):
-        to = around(me + step, slabs)
-        columns = pl.ds(pl.multiple_of(to * BLOCK, BLOCK), BLOCK)
-        send[0:planes] = moving[:, :, columns]
-        wanted = jnp.zeros((rows, BLOCK), jnp.float32)
-        for z in range(planes):
-            one = jnp.sum(jnp.where(narrow == to, fetch[z].astype(jnp.float32), 0.0), axis=1, keepdims=True)
-            wanted = jnp.where(lane == z, one, wanted)
-        send[planes] = wanted.astype(jnp.bfloat16)
-
-
-def pick_kernel(slabs, place, *refs):
-    received, sends, picked = refs[:slabs], refs[slabs:-1], refs[-1]
-    planes = received[0].shape[0] - 1
-    rows = received[0].shape[1]
+
+    def by_row(ref):
+        cells = jnp.concatenate([ref[z].astype(jnp.float32) for z in range(planes)], axis=0)
+        cells = jnp.concatenate([cells, jnp.zeros((cells.shape[0], BLOCK - rows), jnp.float32)], axis=1)
+        cells = jnp.concatenate([cells, jnp.zeros((BLOCK - cells.shape[0], BLOCK), jnp.float32)], axis=0)
+        return cells.T[:rows]
+
+    names, marks = by_row(fetch), by_row(tissue)
+    wide[3 * planes, :, 0:BLOCK] = names
+    for z in range(planes):
+        wide[z] = moving[z].astype(jnp.float32)
+        wide[planes + z] = template[z].astype(jnp.float32)
+        marked = jnp.concatenate(
+            [
+                jnp.broadcast_to(marks[:, z * blocks + b : z * blocks + b + 1], (rows, BLOCK))
+                for b in range(blocks)
+            ],
+            axis=1,
+        )
+        wide[2 * planes + z] = marked * stiffness[z] * COEFFICIENT_UNIT + 0.5
+    for step in range(slabs):
+        part = pl.ds(pl.multiple_of(around(me + step, slabs) * share, share), share)
+        for z in range(0, 2 * planes, 2):
+            both = jnp.concatenate([wide[z, part, :], wide[z + 1, part, :]], axis=0)
+            images[step][z * share : (z + 2) * share] = both.astype(jnp.bfloat16)
+        asked = jnp.concatenate([wide[3 * planes, part, 0:BLOCK]] * blocks, axis=1)
+        images[step][2 * planes * share : (2 * planes + 1) * share] = asked.astype(jnp.bfloat16)
+        for z in range(0, planes, 2):
+            both = jnp.concatenate([wide[2 * planes + z, part, :], wide[2 * planes + z + 1, part, :]], axis=0)
+            weights[step][z * share : (z + 2) * share] = both.astype(jnp.int32).astype(jnp.int16)
+
+
+def pick_kernel(slabs, planes, place, *refs):
+    received, sends = refs[:slabs], refs[slabs : 2 * slabs]
+    image, residual, first, last, edges = refs[2 * slabs :]
+    total, share, x_length = image.shape
+    blocks = x_length // BLOCK
     me = place[0]
-    total = slabs * planes
-    group = 4
+    group = 2
     for step in range(slabs):
-        first = around(me - step, slabs) * planes
-        names = received[step][planes].astype(jnp.float32)
+        base = around(me - step, slabs) * planes
+        names = received[step][2 * planes * share : (2 * planes + 1) * share, 0:BLOCK].astype(jnp.float32)
         for start in range(0, planes, group):
             wanted = [
-                jnp.broadcast_to(names[:, z : z + 1], (rows, BLOCK)) for z in range(start, start + group)
+                jnp.concatenate(
+                    [
+                        jnp.broadcast_to(names[:, z * blocks + b : z * blocks + b + 1], (share, BLOCK))
+                        for b in range(blocks)
+                    ],
+                    axis=1,
+                )
+                for z in range(start, start + group)
             ]
-            found = [jnp.zeros((rows, BLOCK), jnp.float32) for _ in range(group)]
+            found = [jnp.zeros((share, x_length), jnp.float32) for _ in range(group)]
             for other in range(slabs):
-                base = (around(me - other, slabs) * planes).astype(jnp.float32)
-                for plane in range(planes):
-                    values = received[other][plane].astype(jnp.float32)
-                    found = [
-                        jnp.where(w == base + float(plane), values, f) for w, f in zip(wanted, found)
-                    ]
-            for z in range(group):
-                picked[first + start + z] = found[z].astype(jnp.bfloat16)
+                name = (around(me - other, slabs) * planes).astype(jnp.float32)
+                for plane in range(0, planes, 2):
+                    both = received[other][plane * share : (plane + 2) * share].astype(jnp.float32)
+                    for k in range(2):
+                        values = both[k * share : (k + 1) * share]
+                        found = [
+                            jnp.where(w == name + float(plane + k), values, f) for w, f in zip(wanted, found)
+                        ]
+            both = received[step][(planes + start) * share : (planes + start + 2) * share].astype(jnp.float32)
+            for k in range(group):
+                z = base + (start + k)
+                image[z] = found[k]
+                residual[z] = found[k] - both[k * share : (k + 1) * share]
+                edges[0, pl.ds(z, 1), :] = found[k][0:1]
+                edges[1, pl.ds(z, 1), :] = found[k][share - 1 : share]
+    first[...] = edges[0].astype(jnp.bfloat16)
+    last[...] = edges[1].astype(jnp.bfloat16)
     for step, send in enumerate(sends):
-        first = around(me + step, slabs) * planes
-        for k in range(planes + 2):
-            send[k] = picked[around(first + (k - 1), total)]
+        base = around(me + step, slabs) * planes
+        for z in range(0, planes, 2):
+            both = jnp.concatenate([image[base + z], image[base + (z + 1)]], axis=0)
+            send[z * share : (z + 2) * share] = both.astype(jnp.bfloat16)
 
 
 def force_kernel(slabs, place, *refs):
-    received = refs[:slabs]
-    above, below, template, stiffness, tissue, basis, warped, spectra, image, edges = refs[slabs:]
-    planes, rows, x_length = template.shape
+    weights = refs[:slabs]
+    above, below, image, residual, basis_x, basis_z, spectra, edges, force = refs[slabs:]
+    total, share, x_length = image.shape
+    planes = total // slabs
     me = place[0]
+    edges[0] = above[...].astype(jnp.float32)
+    edges[1] = below[...].astype(jnp.float32)
+    row = lax.broadcasted_iota(jnp.int32, (share, x_length), 0)
     for step in range(slabs):
-        block = pl.ds(pl.multiple_of(around(me - step, slabs) * BLOCK, BLOCK), BLOCK)
-        image[:, :, block] = received[step][...].astype(jnp.float32)
-        warped[:, :, block] = received[step][1:-1]
-        edges[0, :, block] = above[step].astype(jnp.float32)
-        edges[1, :, block] = below[step].astype(jnp.float32)
-    row = lax.broadcasted_iota(jnp.int32, (rows, x_length), 0)
-    forces = [[], [], []]
-    for z in range(planes):
-        here = image[z + 1]
-        marked = tissue[z].astype(jnp.float32)
-        marked = jnp.concatenate(
-            [jnp.broadcast_to(marked[:, b : b + 1], (rows, BLOCK)) for b in range(x_length // BLOCK)], axis=1
-        )
-        weight = 0.5 * (marked * stiffness[z] * (here - template[z].astype(jnp.float32)))
-        before = jnp.where(row == 0, edges[0, z : z + 1, :], pltpu.roll(here, 1, 0))
-        after = jnp.where(row == rows - 1, edges[1, z : z + 1, :], pltpu.roll(here, rows - 1, 0))
-        forces[0].append(weight * (image[z + 2] - image[z]))
-        forces[1].append(weight * (after - before))
-        forces[2].append(weight * (pltpu.roll(here, x_length - 1, 1) - pltpu.roll(here, 1, 1)))
+        base = around(me - step, slabs) * planes
+        for start in range(0, planes, 2):
+            both = weights[step][start * share : (start + 2) * share].astype(jnp.int32).astype(jnp.float32)
+            for k in range(2):
+                z = base + (start + k)
+                here = image[z]
+                weight = both[k * share : (k + 1) * share] * (residual[z] * (0.5 / COEFFICIENT_UNIT))
+                before = jnp.where(row == 0, edges[0, pl.ds(z, 1), :], pltpu.roll(here, 1, 0))
+                after = jnp.where(row == share - 1, edges[1, pl.ds(z, 1), :], pltpu.roll(here, share - 1, 0))
+                force[0, z] = weight * (image[around(z + 1, total)] - image[around(z - 1, total)])
+                force[1, z] = weight * (after - before)
+                force[2, z] = weight * (pltpu.roll(here, x_length - 1, 1) - pltpu.roll(here, 1, 1))
     devices, part = spectra.shape[:2]
     part //= 3
     for a in range(3):
-        force = split(jnp.concatenate(forces[a], axis=0))
-        spectrum = times((basis[0], basis[1]), force, ((1,), (1,)))
-        spectra[:, a * part : (a + 1) * part, :] = spectrum.reshape(devices, part, planes * rows)
+        own = split(force[a].reshape(total * share, x_length))
+        own = split(times((basis_z[0], basis_z[1]), own, ((1,), (0,))))
+        own = times((basis_x[0], basis_x[1]), own, ((1,), (1,)))
+        spectra[:, a * part : (a + 1) * part, :] = own.reshape(devices, part, total * share)
 
 
 def solve_kernel(subs, place, spectra, basis_z, basis_y, out, cells):
@@ -288,54 +326,70 @@
     total_z, total_y, lanes = cells.shape
     slabs = devices // subs
     planes, rows = total_z // slabs, total_y // subs
+    share = rows // slabs
     pad = jnp.zeros((lanes - lanes_used, area), jnp.float32)
     for d in range(devices):
-        block = jnp.concatenate([spectra[d], pad], axis=0).T.reshape(planes, rows, lanes)
         s, q = d // subs, d % subs
-        cells[s * planes : (s + 1) * planes, q * rows : (q + 1) * rows, :] = block
+        block = jnp.concatenate([spectra[d], pad], axis=0).T.reshape(total_z, share, lanes)
+        cells[:, q * rows + s * share : q * rows + (s + 1) * share, :] = block
     tables_z, tables_y = (basis_z[0], basis_z[1]), (basis_y[0], basis_y[1])
     part = lanes_used // 3
     lane = lax.broadcasted_iota(jnp.int32, (1, lanes), 1)
     x_sq = wave_sq(place[0] * part + lax.rem(lane, part), part * devices)
     y_sq = wave_sq(lax.broadcasted_iota(jnp.int32, (total_y, 1), 0), total_y)
     xy = (x_sq + y_sq) * 256.0 + 1.0
-    tile = basis_z.shape[1] // total_z
-    for g in range(total_y // tile):
-        own = cells[:, g * tile : (g + 1) * tile, :].reshape(total_z * tile, lanes)
-        own = times(tables_z, split(own), ((1,), (0,)))
-        cells[:, g * tile : (g + 1) * tile, :] = own.reshape(total_z, tile, lanes)
-    for z in range(total_z):
-        wave = 2.0 * np.pi / total_z * (z if z <= total_z // 2 else z - total_z // 2)
-        own = times(tables_y, split(cells[z]), ((1,), (0,)))
-        own = own / (xy + 256.0 * wave * wave)
-        cells[z] = times(tables_y, split(own), ((0,), (0,)))
-    for g in range(total_y // tile):
-        own = cells[:, g * tile : (g + 1) * tile, :].reshape(total_z * tile, lanes)
+    for z in range(0, total_z, 2):
+        own = jnp.concatenate([cells[z], cells[z + 1]], axis=1)
+        own = times(tables_y, split(own), ((1,), (0,)))
+        scale = []
+        for k in range(2):
+            wave = 2.0 * np.pi / total_z * (z + k if z + k <= total_z // 2 else z + k - total_z // 2)
+            scale.append(xy + 256.0 * wave * wave)
+        own = own / jnp.concatenate(scale, axis=1)
+        own = times(tables_y, split(own), ((0,), (0,)))
+        cells[z] = own[:, :lanes]
+        cells[z + 1] = own[:, lanes:]
+    for g in range(0, total_y, 2 * share):
+        own = jnp.concatenate(
+            [cells[:, y : y + share, :].reshape(area, lanes) for y in (g, g + share)], axis=1
+        )
         own = times(tables_z, split(own), ((0,), (0,)))
-        cells[:, g * tile : (g + 1) * tile, :] = own.reshape(total_z, tile, lanes)
+        cells[:, g : g + share, :] = own[:, :lanes].reshape(total_z, share, lanes)
+        cells[:, g + share : g + 2 * share, :] = own[:, lanes:].reshape(total_z, share, lanes)
     for d in range(devices):
         s, q = d // subs, d % subs
         block = cells[s * planes : (s + 1) * planes, q * rows : (q + 1) * rows, :]
         out[d] = block.reshape(area, lanes).T[:lanes_used]
 
 
-def update_kernel(place, spectra, velocity, basis, out):
+def update_kernel(slabs, place, spectra, velocity, basis, *refs):
+    received, (out, warped, wide) = refs[:slabs], refs[slabs:]
     devices, part, area = spectra.shape
     part //= 3
     _, planes, rows, x_length = velocity.shape
+    share = rows // slabs
+    for step in range(slabs):
+        place_of = pl.ds(pl.multiple_of(around(place[0] - step, slabs) * share, share), share)
+        for z in range(0, planes, 2):
+            both = received[step][z * share : (z + 2) * share].astype(jnp.float32)
+            wide[z, place_of, :] = both[:share]
+            wide[z + 1, place_of, :] = both[share:]
+    warped[...] = wide[...].astype(jnp.bfloat16)
     for a in range(3):
         own = spectra[:, a * part : (a + 1) * part, :].reshape(x_length, area).T
         smoothed = times(split(own), (basis[0], basis[1]), ((1,), (0,)))
         out[a] = 0.5 * (velocity[a] - 32.0 * smoothed.reshape(planes, rows, x_length))
 
 
-def local_blocks(velocity, template, moving, stiffness, fetch_plane, tissue):
+def local_rows(velocity, template, moving, stiffness, fetch_plane, tissue):
     planes, rows, x_length = moving.shape
     slabs, subs = lax.axis_size("slab"), lax.axis_size("sub")
     total_z, total_y = planes * slabs, rows * subs
     devices = slabs * subs
     part = x_length // devices
     area = planes * rows
+    share = rows // slabs
+    both_axes = ("slab", "sub")
     my_slab = lax.axis_index("slab")
     my_place = my_slab * subs + lax.axis_index("sub")
     slab_id, place_id = my_slab.reshape(1), my_place.reshape(1)
@@ -350,49 +404,56 @@
             for d in range(1, slabs)
         ]
 
+    def exchange(values):
+        values = values.astype(jnp.float16)
+        return lax.all_to_all(values, both_axes, split_axis=0, concat_axis=0, tiled=True)
+
+    images = shape(((2 * planes + 1) * share, x_length), bf16)
+    weights = shape((planes * share, x_length), jnp.int16)
     sends = call(
-        functools.partial(send_columns_kernel, slabs),
-        [shape((planes + 1, rows, BLOCK), bf16)] * slabs,
-        (slab_id, moving, fetch_plane),
-    )
-    received = scatter(sends)
-    sends = call(
-        functools.partial(pick_kernel, slabs),
-        [shape((planes + 2, rows, BLOCK), bf16)] * slabs,
-        (slab_id, *received),
-        [pltpu.VMEM((total_z, rows, BLOCK), bf16)],
-    )
-    received = scatter(sends)
-    last = jnp.stack([r[1:-1, rows - 1] for r in received])
-    first = jnp.stack([r[1:-1, 0] for r in received])
-    above = lax.ppermute(last, "sub", [(i, (i + 1) % subs) for i in range(subs)])
-    below = lax.ppermute(first, "sub", [((i + 1) % subs, i) for i in range(subs)])
-    basis_x = in_two(real_basis(x_length))
-    tile = 8
-    basis_z = in_two(np.kron(real_basis(total_z), np.eye(tile)))
-    basis_y = in_two(real_basis(total_y))
-    warped, spectra = call(
+        functools.partial(send_rows_kernel, slabs),
+        [images] * slabs + [weights] * slabs,
+        (slab_id, moving, template, stiffness, fetch_plane.swapaxes(1, 2), tissue.swapaxes(1, 2)),
+        [pltpu.VMEM((3 * planes + 1, rows, x_length), f32)],
+    )
+    images, weights = scatter(sends[:slabs]), scatter(sends[slabs:])
+    *sends, image, residual, first, last = call(
+        functools.partial(pick_kernel, slabs, planes),
+        [shape((planes * share, x_length), bf16)] * slabs
+        + [shape((total_z, share, x_length))] * 2
+        + [shape((total_z, x_length), bf16)] * 2,
+        (slab_id, *images),
+        [pltpu.VMEM((2, total_z, x_length), f32)],
+    )
+    ring = [s * subs + q for q in range(subs) for s in range(slabs)]
+    onward = [(ring[i], ring[(i + 1) % devices]) for i in range(devices)]
+    above = lax.ppermute(last, both_axes, onward)
+    below = lax.ppermute(first, both_axes, [(b, a) for a, b in onward])
+    basis_z = in_two(np.kron(real_basis(total_z), np.eye(share)))
+    spectra = call(
         functools.partial(force_kernel, slabs),
-        [shape((planes, rows, x_length), bf16), shape((devices, 3 * part, area))],
-        (slab_id, *received, above, below, template, stiffness, tissue, in_two(8.0 * real_basis(x_length))),
-        [pltpu.VMEM((planes + 2, rows, x_length), f32), pltpu.VMEM((2, planes, x_length), f32)],
-    )
-    spectra = spectra.astype(jnp.float16)
-    spectra = lax.all_to_all(spectra, ("slab", "sub"), split_axis=0, concat_axis=0, tiled=True)
+        shape((devices, 3 * part, area)),
+        (slab_id, *weights, above, below, image, residual, in_two(8.0 * real_basis(x_length)), basis_z),
+        [pltpu.VMEM((2, total_z, x_length), f32), pltpu.VMEM((3, total_z, share, x_length), f32)],
+    )
+    spectra = exchange(spectra)
+    spectra, sends = lax.optimization_barrier((spectra, sends))
+    warped = scatter(sends)
     spectra = call(
         functools.partial(solve_kernel, subs),
         shape((devices, 3 * part, area)),
-        (place_id, spectra.astype(f32), basis_z, basis_y),
+        (place_id, spectra.astype(f32), basis_z, in_two(real_basis(total_y))),
         [pltpu.VMEM((total_z, total_y, 128), f32)],
     )
-    spectra = spectra.astype(jnp.float16)
-    spectra = lax.all_to_all(spectra, ("slab", "sub"), split_axis=0, concat_axis=0, tiled=True)
-    new_velocity = call(
-        update_kernel,
-        shape(velocity.shape),
-        (place_id, spectra.astype(f32), velocity, basis_x),
-    )
-    return (new_velocity, warped)
+    spectra = exchange(spectra)
+    return tuple(
+        call(
+            functools.partial(update_kernel, slabs),
+            [shape(velocity.shape), shape(moving.shape, bf16)],
+            (slab_id, spectra.astype(f32), velocity, in_two(real_basis(x_length)), *warped),
+            [pltpu.VMEM((planes, rows, x_length), f32)],
+        )
+    )
 
 
 def local(velocity, template, moving, stiffness, fetch_plane, tissue):
@@ -400,15 +461,15 @@
     slabs, subs = lax.axis_size("slab"), lax.axis_size("sub")
     part = x_length // (slabs * subs)
     fits = (
-        x_length == slabs * BLOCK
-        and planes == 8
-        and rows % 16 == 0
-        and part % 16 == 0
-        and 3 * part <= 128
+        planes == 8
+        and rows == 8 * slabs
+        and part % 8 == 0
+        and 3 * part <= BLOCK
         and planes * slabs * 8 == 256
-        and rows * subs == 128
-    )
-    run = local_blocks if fits else local_general
+        and rows * subs == BLOCK
+        and planes * (x_length // BLOCK) <= BLOCK
+    )
+    run = local_rows if fits else local_general
     return run(velocity, template, moving, stiffness, fetch_plane, tissue)
 
 

time: 97.1 us -> 103 us (1.061)
  blocking collectives: 25.5 us -> 0 us
  starting transfers between devices: 16.6 us -> 32 us
  waiting for transfers between devices: 34.1 us -> 48.5 us
  other arithmetic: 1.46 us -> 3.71 us
    all_to_all x1 -> x0, blocking collectives: 25.5 us -> none  [local_blocks(): lax.all_to_all(spectra, ('slab', 'sub'), split_axis=0, concat_axis=0, til...]
    all_to_all x1 -> x2, waiting for transfers between devices: 18.7 us -> 32.1 us  [exchange(): lax.all_to_all(values, both_axes, split_axis=0, concat_axis=0, tiled=True)]
    all_to_all x1 -> x2, starting transfers between devices: 3.89 us -> 10.8 us  [exchange(): lax.all_to_all(values, both_axes, split_axis=0, concat_axis=0, tiled=True)]
    ppermute x6 -> x9, starting transfers between devices: 10.9 us -> 15.9 us  [scatter(): lax.ppermute(sends[d], 'slab', [(i, (i + d) % slabs) for i in range(slabs)])]
    ppermute x2, starting transfers between devices: 1.83 us -> 5.31 us  [the longest x1 4.81 us: local_rows(): above = lax.ppermute(last, both_axes, onward)]
    ppermute x2, waiting for transfers between devices: 0.44 us -> 3.75 us  [the longest x1 2.23 us: local_rows(): below = lax.ppermute(first, both_axes, [(b, a) for a, b in onward])]
    ppermute x6 -> x9, waiting for transfers between devices: 15 us -> 12.7 us  [scatter(): lax.ppermute(sends[d], 'slab', [(i, (i + d) % slabs) for i in range(slabs)])]
    convert_element_type x4, other arithmetic: 1.45 us -> 3.71 us  [the longest x2 3.48 us: exchange(): values = values.astype(jnp.float16)]
  transfers between devices with their start and end apart: 9 -> 13, of which waited for: 8 -> 9; matrix products, arithmetic and copies ran while one was open for 1% -> 0% of each run, Pallas kernels for 0% -> 1%
where the time goes in v2:
time: 103 us
  waiting for transfers between devices  48.5 us (47%)
  starting transfers between devices  32 us (31%)
  Pallas kernels  13.2 us (13%)
  local copies, waits for them, and re-layouts  4.49 us (4%)
  other arithmetic  3.71 us (4%)
    all_to_all x2, waiting for transfers between devices, exchange(): lax.all_to_all(values, both_axes, split_axis=0, concat_axis=0, tiled=True)  32.1 us
    ppermute x9, starting transfers between devices, scatter(): lax.ppermute(sends[d], 'slab', [(i, (i + d) % slabs) for i in range(slabs)])  15.9 us
    pallas_call x5, Pallas kernels, call(): pl.pallas_call(kernel, out_shape=out_shape, in_specs=[smem] + [vmem] * (l...  13.2 us
    ppermute x9, waiting for transfers between devices, scatter(): lax.ppermute(sends[d], 'slab', [(i, (i + d) % slabs) for i in range(slabs)])  12.7 us
    all_to_all x2, starting transfers between devices, exchange(): lax.all_to_all(values, both_axes, split_axis=0, concat_axis=0, tiled=True)  10.8 us
    ppermute x1, starting transfers between devices, local_rows(): above = lax.ppermute(last, both_axes, onward)  4.81 us
    unnamed x18, local copies, waits for them, and re-layouts  4.49 us
    convert_element_type x2, other arithmetic, exchange(): values = values.astype(jnp.float16)  3.48 us
  transfers between devices with their start and end apart: 13, of which 9 were waited for; matrix products, arithmetic and copies ran while one was open for 0% of the time, Pallas kernels for 1%

profile of v2, /device:TPU:0, one launch (start us, length us, event | category | flops | bytes accessed | tf_op | source)
XLA Modules:
  0.0 102.7 jit_solution(10773659921292737244)
XLA Ops:
  0.6 0.0 copy-start.2
  0.6 0.0 copy-start.1
  0.7 0.0 copy-start.3
  0.7 1.1 %copy-done.3 = f32[8,32,512]{2,1,0:T(8,128)S(1)} copy-done((f32[8,32,512]{2,1,0:T(8,128)S(1)}, f32[8,32,512]{2,1,0:T(8,128)}, u32[]{:S(2)}) %copy-start.3) | copy-done | bytes 524312
  1.8 0.0 copy-start.4
  1.8 0.9 copy-done.4
  2.8 0.0 copy-start.5
  2.8 0.9 copy-done.5
  3.7 0.0 copy-start.7
  3.7 0.7 copy-done.7
  4.4 0.0 copy-start.8
  4.4 0.7 copy-done.8
  5.1 0.5 shard_map.113
  5.7 3.1 %collective-permute-start.3 = (bf16[136,512]{1,0:T(8,128)(2,1)S(1)}, bf16[136,512]{1,0:T(8,128)(2,1)S(1)}, u32[]{:S(2)}, u32[]{:S(2)}) collective-permute-start(bf16[136,512]{1,0:T(8,128)(2,1)S(1)} %get-tuple-element.28), channel_id=1, source_target_pairs={{0,4},{4,8},{8,12},{12,0},{1,5},{5,9},{9,13},{13,1},{2,6},{6,10},{... | collective-permute-start | bytes 417800 | tf_op jit(solution)/shard_map/ppermute | solution.py:403
  8.8 2.6 %collective-permute-start.4 = (bf16[136,512]{1,0:T(8,128)(2,1)S(1)}, bf16[136,512]{1,0:T(8,128)(2,1)S(1)}, u32[]{:S(2)}, u32[]{:S(2)}) collective-permute-start(bf16[136,512]{1,0:T(8,128)(2,1)S(1)} %get-tuple-element.29), channel_id=1, source_target_pairs={{0,8},{4,12},{8,0},{12,4},{1,9},{5,13},{9,1},{13,5},{2,10},{6,14},... | collective-permute-start | bytes 417800 | tf_op jit(solution)/shard_map/ppermute | solution.py:403
  11.4 1.4 %collective-permute-start.5 = (bf16[136,512]{1,0:T(8,128)(2,1)S(1)}, bf16[136,512]{1,0:T(8,128)(2,1)S(1)}, u32[]{:S(2)}, u32[]{:S(2)}) collective-permute-start(bf16[136,512]{1,0:T(8,128)(2,1)S(1)} %get-tuple-element.30), channel_id=1, source_target_pairs={{0,12},{4,0},{8,4},{12,8},{1,13},{5,1},{9,5},{13,9},{2,14},{6,2},{... | collective-permute-start | bytes 417800 | tf_op jit(solution)/shard_map/ppermute | solution.py:403
  12.7 0.7 collective-permute-start
  13.4 0.3 collective-permute-start.1
  13.7 1.7 %collective-permute-done.3.refs_1_ = bf16[136,512]{1,0:T(8,128)(2,1)S(1)} collective-permute-done((bf16[136,512]{1,0:T(8,128)(2,1)S(1)}, bf16[136,512]{1,0:T(8,128)(2,1)S(1)}, u32[]{:S(2)}, u32[]{:S(2)}) %collective-permute-start.3) | collective-permute-done | bytes 139296 | tf_op jit(solution)/shard_map/ppermute | solution.py:403
  15.4 2.1 %collective-permute-start.2 = (s16[64,512]{1,0:T(8,128)(2,1)S(1)}, s16[64,512]{1,0:T(8,128)(2,1)S(1)}, u32[]{:S(2)}, u32[]{:S(2)}) collective-permute-start(s16[64,512]{1,0:T(8,128)(2,1)S(1)} %get-tuple-element.26), channel_id=1, source_target_pairs={{0,12},{4,0},{8,4},{12,8},{1,13},{5,1},{9,5},{13,9},{2,14},{6,2},{... | collective-permute-start | bytes 196616 | tf_op jit(solution)/shard_map/ppermute | solution.py:403
  17.5 3.9 %collective-permute-done.4.refs_2_ = bf16[136,512]{1,0:T(8,128)(2,1)S(1)} collective-permute-done((bf16[136,512]{1,0:T(8,128)(2,1)S(1)}, bf16[136,512]{1,0:T(8,128)(2,1)S(1)}, u32[]{:S(2)}, u32[]{:S(2)}) %collective-permute-start.4) | collective-permute-done | bytes 139296 | tf_op jit(solution)/shard_map/ppermute | solution.py:403
  21.4 0.8 collective-permute-done.5.refs_3_
  22.2 1.5 %shard_map.114 = (bf16[64,512]{1,0:T(8,128)(2,1)S(1)}, bf16[64,512]{1,0:T(8,128)(2,1)S(1)}, bf16[64,512]{1,0:T(8,128)(2,1)S(1)}, bf16[64,512]{1,0:T(8,128)(2,1)S...) custom-call(s32[1]{0:T(128)} %bitcast.place, ...), custom_call_target="tpu_custom_call" | custom-call | tf_op jit(solution)/shard_map/pallas_call | solution.py:197
  23.7 4.8 %collective-permute-start.6 = (bf16[32,512]{1,0:T(8,128)(2,1)S(1)}, bf16[32,512]{1,0:T(8,128)(2,1)S(1)}, u32[]{:S(2)}, u32[]{:S(2)}) collective-permute-start(bf16[32,512]{1,0:T(8,128)(2,1)S(1)} %get-tuple-element.31), channel_id=1, source_target_pairs={{0,4},{4,8},{8,12},{12,1},{1,5},{5,9},{9,13},{13,2},{2,6},{6,10},{... | collective-permute-start | bytes 98312 | tf_op jit(solution)/shard_map/ppermute | solution.py:430
  28.5 0.5 collective-permute-start.7
  29.0 0.0 collective-permute-done.refs_1_
  29.0 0.0 collective-permute-done.1.refs_2_
  29.0 0.0 collective-permute-done.2.refs_3_
  29.0 1.5 %collective-permute-done.6.refs_4_ = bf16[32,512]{1,0:T(8,128)(2,1)S(1)} collective-permute-done((bf16[32,512]{1,0:T(8,128)(2,1)S(1)}, bf16[32,512]{1,0:T(8,128)(2,1)S(1)}, u32[]{:S(2)}, u32[]{:S(2)}) %collective-permute-start.6) | collective-permute-done | bytes 32800 | tf_op jit(solution)/shard_map/ppermute | solution.py:430
  30.5 2.2 %collective-permute-done.7.refs_5_ = bf16[32,512]{1,0:T(8,128)(2,1)S(1)} collective-permute-done((bf16[32,512]{1,0:T(8,128)(2,1)S(1)}, bf16[32,512]{1,0:T(8,128)(2,1)S(1)}, u32[]{:S(2)}, u32[]{:S(2)}) %collective-permute-start.7) | collective-permute-done | bytes 32800 | tf_op jit(solution)/shard_map/ppermute | solution.py:431
  32.7 0.0 copy-done.2
  32.7 0.0 copy-done.1
  32.7 3.7 %shard_map.115 = f32[16,96,256]{2,1,0:T(8,128)} custom-call(s32[1]{0:T(128)} %bitcast.place, s16[64,512]{1,0:T(8,128)(2,1)S(1)} %get-tuple-element.23.refs_0_, s16[64,512]{1,0:T(8,128)(2,1)S(1)} %collective-permute-done.refs_1_, s16[64,512]{1,0:T(8,128)(2,1)S(1)} %collective-permute-done.1.refs_2_, s16[64,512]{1,0:T(8,128)(2,1)S(1)} %collective-permute-done.2.refs_3_, ...), custom_call_target="tpu_custom_call" | custom-call | tf_op jit(solution)/shard_map/pallas_call | solution.py:197
  36.5 2.4 %convert_element_type.12 = f16[16,96,256]{2,1,0:T(8,128)(2,1)} convert(f32[16,96,256]{2,1,0:T(8,128)} %shard_map.115) | non-fusion elementwise | flops 393216 | bytes 2359296 | tf_op jit(solution)/shard_map/convert_element_type | solution.py:408
  38.9 5.3 %all-to-all-start = ((f16[16,96,256]{2,1,0:T(8,128)(2,1)}), f16[16,96,256]{2,1,0:T(8,128)(2,1)S(1)}, u32[]{:S(2)}, u32[]{:S(2)}) async-start(f16[16,96,256]{2,1,0:T(8,128)(2,1)} %convert_element_type.12), calls=%async_computation | async-start | bytes 1572864 | tf_op jit(solution)/shard_map/all_to_all | solution.py:409
  44.3 0.0 copy-start.6
  44.3 18.7 %all-to-all-done = f16[16,96,256]{2,1,0:T(8,128)(2,1)S(1)} async-done(((f16[16,96,256]{2,1,0:T(8,128)(2,1)}), f16[16,96,256]{2,1,0:T(8,128)(2,1)S(1)}, u32[]{:S(2)}, u32[]{:S(2)}) %all-to-all-start) | async-done | bytes 786464 | tf_op jit(solution)/shard_map/all_to_all | solution.py:409
  63.0 0.1 convert_element_type.13.spectra
  63.1 0.0 copy-done.6
  63.1 3.3 %shard_map.116 = f32[16,96,256]{2,1,0:T(8,128)S(1)} custom-call(s32[1]{0:T(128)} %bitcast.1.place, f32[16,96,256]{2,1,0:T(8,128)S(1)} %convert_element_type.13.spectra, bf16[2,256,256]{2,1,0:T(8,128)(2,1)S(1)} %copy-done.2, bf16[2,128,128]{2,1,0:T(8,128)(2,1)S(1)} %copy-done.6), custom_call_target="tpu_custom_call" | custom-call | tf_op jit(solution)/shard_map/pallas_call | solution.py:197
  66.4 1.0 %convert_element_type.14 = f16[16,96,256]{2,1,0:T(8,128)(2,1)} convert(f32[16,96,256]{2,1,0:T(8,128)S(1)} %shard_map.116) | non-fusion elementwise | flops 393216 | bytes 2359296 | tf_op jit(solution)/shard_map/convert_element_type | solution.py:408
  67.5 5.5 %all-to-all-start.1 = ((f16[16,96,256]{2,1,0:T(8,128)(2,1)}), f16[16,96,256]{2,1,0:T(8,128)(2,1)S(1)}, u32[]{:S(2)}, u32[]{:S(2)}) async-start(f16[16,96,256]{2,1,0:T(8,128)(2,1)} %convert_element_type.14), calls=%async_computation.1 | async-start | bytes 1572864 | tf_op jit(solution)/shard_map/all_to_all | solution.py:409
  73.0 0.0 copy-start
  73.0 2.0 %collective-permute-start.8 = (bf16[64,512]{1,0:T(8,128)(2,1)S(1)}, bf16[64,512]{1,0:T(8,128)(2,1)S(1)}, u32[]{:S(2)}, u32[]{:S(2)}) collective-permute-start(bf16[64,512]{1,0:T(8,128)(2,1)S(1)} %get-tuple-element.41), channel_id=1, source_target_pairs={{0,4},{4,8},{8,12},{12,0},{1,5},{5,9},{9,13},{13,1},{2,6},{6,10},{... | collective-permute-start | bytes 196616 | tf_op jit(solution)/shard_map/ppermute | solution.py:403
  75.0 2.4 %collective-permute-start.9 = (bf16[64,512]{1,0:T(8,128)(2,1)S(1)}, bf16[64,512]{1,0:T(8,128)(2,1)S(1)}, u32[]{:S(2)}, u32[]{:S(2)}) collective-permute-start(bf16[64,512]{1,0:T(8,128)(2,1)S(1)} %get-tuple-element.42), channel_id=1, source_target_pairs={{0,8},{4,12},{8,0},{12,4},{1,9},{5,13},{9,1},{13,5},{2,10},{6,14},... | collective-permute-start | bytes 196616 | tf_op jit(solution)/shard_map/ppermute | solution.py:403
  77.3 1.5 %collective-permute-start.10 = (bf16[64,512]{1,0:T(8,128)(2,1)S(1)}, bf16[64,512]{1,0:T(8,128)(2,1)S(1)}, u32[]{:S(2)}, u32[]{:S(2)}) collective-permute-start(bf16[64,512]{1,0:T(8,128)(2,1)S(1)} %get-tuple-element.43), channel_id=1, source_target_pairs={{0,12},{4,0},{8,4},{12,8},{1,13},{5,1},{9,5},{13,9},{2,14},{6,2},{... | collective-permute-start | bytes 196616 | tf_op jit(solution)/shard_map/ppermute | solution.py:403
  78.8 13.4 %all-to-all-done.1 = f16[16,96,256]{2,1,0:T(8,128)(2,1)S(1)} async-done(((f16[16,96,256]{2,1,0:T(8,128)(2,1)}), f16[16,96,256]{2,1,0:T(8,128)(2,1)S(1)}, u32[]{:S(2)}, u32[]{:S(2)}) %all-to-all-start.1) | async-done | bytes 786464 | tf_op jit(solution)/shard_map/all_to_all | solution.py:409
  92.2 0.1 convert_element_type.15.spectra
  92.3 0.4 collective-permute-done.8.refs_1_
  92.7 5.9 %collective-permute-done.9.refs_2_ = bf16[64,512]{1,0:T(8,128)(2,1)S(1)} collective-permute-done((bf16[64,512]{1,0:T(8,128)(2,1)S(1)}, bf16[64,512]{1,0:T(8,128)(2,1)S(1)}, u32[]{:S(2)}, u32[]{:S(2)}) %collective-permute-start.9) | collective-permute-done | bytes 65568 | tf_op jit(solution)/shard_map/ppermute | solution.py:403
  98.6 0.0 collective-permute-done.10.refs_3_
  98.6 0.0 copy-done
  98.6 4.1 %shard_map.117 = (f32[3,8,32,512]{3,2,1,0:T(8,128)}, bf16[8,32,512]{2,1,0:T(8,128)(2,1)}) custom-call(s32[1]{0:T(128)} %bitcast.place, f32[16,96,256]{2,1,0:T(8,128)S(1)} %convert_element_type.15.spectra, f32[3,8,32,512]{3,2,1,0:T(8,128)} %velocity.1, bf16[2,512,512]{2,1,0:T(8,128)(2,1)S(1)} %copy-done, bf16[64,512]{1,0:T(8,128)(2,1)S(1)} %get-tuple-element.40.refs_0_, ...), custom_call_target="tpu_custom_call" | custom-call | tf_op jit(solution)/shard_map/pallas_call | solution.py:197
Async XLA Ops:
  0.6 32.1 %copy-start.2 = (bf16[2,256,256]{2,1,0:T(8,128)(2,1)S(1)}, bf16[2,256,256]{2,1,0:T(8,128)(2,1)}, u32[]{:S(2)}) copy-start(bf16[2,256,256]{2,1,0:T(8,128)(2,1)} %constant.18.clone.refs_9_.basis_z) | copy-start | bytes 786436
  0.6 32.1 %copy-start.1 = (bf16[2,512,512]{2,1,0:T(8,128)(2,1)S(1)}, bf16[2,512,512]{2,1,0:T(8,128)(2,1)}, u32[]{:S(2)}) copy-start(bf16[2,512,512]{2,1,0:T(8,128)(2,1)} %constant.17.clone.refs_8_) | copy-start | bytes 3145732
  0.7 1.1 %copy-start.3 = (f32[8,32,512]{2,1,0:T(8,128)S(1)}, f32[8,32,512]{2,1,0:T(8,128)}, u32[]{:S(2)}) copy-start(f32[8,32,512]{2,1,0:T(8,128)} %stiffness.1) | copy-start | bytes 1572868
  1.8 0.9 copy-start.4
  2.8 0.9 copy-start.5
  3.7 0.7 copy-start.7
  4.4 0.7 copy-start.8
  5.7 9.7 %collective-permute-start.3 = (bf16[136,512]{1,0:T(8,128)(2,1)S(1)}, bf16[136,512]{1,0:T(8,128)(2,1)S(1)}, u32[]{:S(2)}, u32[]{:S(2)}) collective-permute-start(bf16[136,512]{1,0:T(8,128)(2,1)S(1)} %get-tuple-element.28), channel_id=1, source_target_pairs={{0,4},{4,8},{8,12},{12,0},{1,5},{5,9},{9,13},{13,1},{2,6},{6,10},{... | collective-permute-start | bytes 417800 | tf_op jit(solution)/shard_map/ppermute | solution.py:403
  8.8 12.6 %collective-permute-start.4 = (bf16[136,512]{1,0:T(8,128)(2,1)S(1)}, bf16[136,512]{1,0:T(8,128)(2,1)S(1)}, u32[]{:S(2)}, u32[]{:S(2)}) collective-permute-start(bf16[136,512]{1,0:T(8,128)(2,1)S(1)} %get-tuple-element.29), channel_id=1, source_target_pairs={{0,8},{4,12},{8,0},{12,4},{1,9},{5,13},{9,1},{13,5},{2,10},{6,14},... | collective-permute-start | bytes 417800 | tf_op jit(solution)/shard_map/ppermute | solution.py:403
  11.4 10.8 %collective-permute-start.5 = (bf16[136,512]{1,0:T(8,128)(2,1)S(1)}, bf16[136,512]{1,0:T(8,128)(2,1)S(1)}, u32[]{:S(2)}, u32[]{:S(2)}) collective-permute-start(bf16[136,512]{1,0:T(8,128)(2,1)S(1)} %get-tuple-element.30), channel_id=1, source_target_pairs={{0,12},{4,0},{8,4},{12,8},{1,13},{5,1},{9,5},{13,9},{2,14},{6,2},{... | collective-permute-start | bytes 417800 | tf_op jit(solution)/shard_map/ppermute | solution.py:403
  12.7 16.3 %collective-permute-start = (s16[64,512]{1,0:T(8,128)(2,1)S(1)}, s16[64,512]{1,0:T(8,128)(2,1)S(1)}, u32[]{:S(2)}, u32[]{:S(2)}) collective-permute-start(s16[64,512]{1,0:T(8,128)(2,1)S(1)} %get-tuple-element.24), channel_id=1, source_target_pairs={{0,4},{4,8},{8,12},{12,0},{1,5},{5,9},{9,13},{13,1},{2,6},{6,10},{... | collective-permute-start | bytes 196616 | tf_op jit(solution)/shard_map/ppermute | solution.py:403
  13.4 15.6 %collective-permute-start.1 = (s16[64,512]{1,0:T(8,128)(2,1)S(1)}, s16[64,512]{1,0:T(8,128)(2,1)S(1)}, u32[]{:S(2)}, u32[]{:S(2)}) collective-permute-start(s16[64,512]{1,0:T(8,128)(2,1)S(1)} %get-tuple-element.25), channel_id=1, source_target_pairs={{0,8},{4,12},{8,0},{12,4},{1,9},{5,13},{9,1},{13,5},{2,10},{6,14},... | collective-permute-start | bytes 196616 | tf_op jit(solution)/shard_map/ppermute | solution.py:403
  15.4 13.6 %collective-permute-start.2 = (s16[64,512]{1,0:T(8,128)(2,1)S(1)}, s16[64,512]{1,0:T(8,128)(2,1)S(1)}, u32[]{:S(2)}, u32[]{:S(2)}) collective-permute-start(s16[64,512]{1,0:T(8,128)(2,1)S(1)} %get-tuple-element.26), channel_id=1, source_target_pairs={{0,12},{4,0},{8,4},{12,8},{1,13},{5,1},{9,5},{13,9},{2,14},{6,2},{... | collective-permute-start | bytes 196616 | tf_op jit(solution)/shard_map/ppermute | solution.py:403
  23.7 6.8 %collective-permute-start.6 = (bf16[32,512]{1,0:T(8,128)(2,1)S(1)}, bf16[32,512]{1,0:T(8,128)(2,1)S(1)}, u32[]{:S(2)}, u32[]{:S(2)}) collective-permute-start(bf16[32,512]{1,0:T(8,128)(2,1)S(1)} %get-tuple-element.31), channel_id=1, source_target_pairs={{0,4},{4,8},{8,12},{12,1},{1,5},{5,9},{9,13},{13,2},{2,6},{6,10},{... | collective-permute-start | bytes 98312 | tf_op jit(solution)/shard_map/ppermute | solution.py:430
  28.5 4.3 %collective-permute-start.7 = (bf16[32,512]{1,0:T(8,128)(2,1)S(1)}, bf16[32,512]{1,0:T(8,128)(2,1)S(1)}, u32[]{:S(2)}, u32[]{:S(2)}) collective-permute-start(bf16[32,512]{1,0:T(8,128)(2,1)S(1)} %get-tuple-element.32), channel_id=1, source_target_pairs={{4,0},{8,4},{12,8},{1,12},{5,1},{9,5},{13,9},{2,13},{6,2},{10,6},{... | collective-permute-start | bytes 98312 | tf_op jit(solution)/shard_map/ppermute | solution.py:431
  38.9 24.1 %all-to-all-start = ((f16[16,96,256]{2,1,0:T(8,128)(2,1)}), f16[16,96,256]{2,1,0:T(8,128)(2,1)S(1)}, u32[]{:S(2)}, u32[]{:S(2)}) async-start(f16[16,96,256]{2,1,0:T(8,128)(2,1)} %convert_element_type.12), calls=%async_computation | async-start | bytes 1572864 | tf_op jit(solution)/shard_map/all_to_all | solution.py:409
  44.3 18.8 %copy-start.6 = (bf16[2,128,128]{2,1,0:T(8,128)(2,1)S(1)}, bf16[2,128,128]{2,1,0:T(8,128)(2,1)}, u32[]{:S(2)}) copy-start(bf16[2,128,128]{2,1,0:T(8,128)(2,1)} %constant.19.clone.basis_y) | copy-start | bytes 196612
  67.5 24.7 %all-to-all-start.1 = ((f16[16,96,256]{2,1,0:T(8,128)(2,1)}), f16[16,96,256]{2,1,0:T(8,128)(2,1)S(1)}, u32[]{:S(2)}, u32[]{:S(2)}) async-start(f16[16,96,256]{2,1,0:T(8,128)(2,1)} %convert_element_type.14), calls=%async_computation.1 | async-start | bytes 1572864 | tf_op jit(solution)/shard_map/all_to_all | solution.py:409
  73.0 25.6 %copy-start = (bf16[2,512,512]{2,1,0:T(8,128)(2,1)S(1)}, bf16[2,512,512]{2,1,0:T(8,128)(2,1)}, u32[]{:S(2)}) copy-start(bf16[2,512,512]{2,1,0:T(8,128)(2,1)} %constant.20.clone.basis) | copy-start | bytes 3145732
  73.0 19.7 %collective-permute-start.8 = (bf16[64,512]{1,0:T(8,128)(2,1)S(1)}, bf16[64,512]{1,0:T(8,128)(2,1)S(1)}, u32[]{:S(2)}, u32[]{:S(2)}) collective-permute-start(bf16[64,512]{1,0:T(8,128)(2,1)S(1)} %get-tuple-element.41), channel_id=1, source_target_pairs={{0,4},{4,8},{8,12},{12,0},{1,5},{5,9},{9,13},{13,1},{2,6},{6,10},{... | collective-permute-start | bytes 196616 | tf_op jit(solution)/shard_map/ppermute | solution.py:403
  75.0 23.6 %collective-permute-start.9 = (bf16[64,512]{1,0:T(8,128)(2,1)S(1)}, bf16[64,512]{1,0:T(8,128)(2,1)S(1)}, u32[]{:S(2)}, u32[]{:S(2)}) collective-permute-start(bf16[64,512]{1,0:T(8,128)(2,1)S(1)} %get-tuple-element.42), channel_id=1, source_target_pairs={{0,8},{4,12},{8,0},{12,4},{1,9},{5,13},{9,1},{13,5},{2,10},{6,14},... | collective-permute-start | bytes 196616 | tf_op jit(solution)/shard_map/ppermute | solution.py:403
  77.3 21.3 %collective-permute-start.10 = (bf16[64,512]{1,0:T(8,128)(2,1)S(1)}, bf16[64,512]{1,0:T(8,128)(2,1)S(1)}, u32[]{:S(2)}, u32[]{:S(2)}) collective-permute-start(bf16[64,512]{1,0:T(8,128)(2,1)S(1)} %get-tuple-element.43), channel_id=1, source_target_pairs={{0,12},{4,0},{8,4},{12,8},{1,13},{5,1},{9,5},{13,9},{2,14},{6,2},{... | collective-permute-start | bytes 196616 | tf_op jit(solution)/shard_map/ppermute | solution.py:403

commit v3 on v2

--- a/solution.py
+++ b/solution.py
@@ -148,7 +148,7 @@
     return (new_velocity, warped)
 
 
-VMEM_BYTES = 50 * 1024 * 1024
+VMEM_BYTES = 24 * 1024 * 1024
 COEFFICIENT_UNIT = 8191.0
 
 
@@ -191,13 +191,18 @@
     return lax.rem(value + 2 * count, count)
 
 
-def call(kernel, out_shape, arguments, scratch=(), flops=0, nbytes=0):
-    smem = pl.BlockSpec(memory_space=pltpu.SMEM)
+def call(kernel, out_shape, *arguments, scratch=(), flops=0):
+    places = [
+        pl.BlockSpec(memory_space=pl.ANY if isinstance(a, tuple) else pltpu.SMEM if a.ndim == 1 else pltpu.VMEM)
+        for a in arguments
+    ]
+    arguments = [a[0] if isinstance(a, tuple) else a for a in arguments]
     vmem = pl.BlockSpec(memory_space=pltpu.VMEM)
+    nbytes = sum(a.size * a.dtype.itemsize for a in arguments + jax.tree.leaves(out_shape))
     return pl.pallas_call(
         kernel,
         out_shape=out_shape,
-        in_specs=[smem] + [vmem] * (len(arguments) - 1),
+        in_specs=places,
         out_specs=jax.tree.map(lambda _: vmem, out_shape),
         scratch_shapes=list(scratch),
         compiler_params=pltpu.CompilerParams(vmem_limit_bytes=VMEM_BYTES),
@@ -205,24 +210,50 @@
     )(*arguments)
 
 
-def send_rows_kernel(slabs, place, moving, template, stiffness, fetch, tissue, *refs):
-    images, weights, wide = refs[:slabs], refs[slabs:-1], refs[-1]
-    planes, rows, x_length = moving.shape
+def fetch_all(pairs, done):
+    copies = [pltpu.make_async_copy(src, dst, done.at[k]) for k, (src, dst) in enumerate(pairs)]
+    for copy in copies:
+        copy.start()
+    for copy in copies:
+        copy.wait()
+
+
+def by_row(ref, rows):
+    cells = jnp.concatenate([ref[z].astype(jnp.float32) for z in range(ref.shape[0])], axis=0)
+    cells = jnp.concatenate([cells, jnp.zeros((cells.shape[0], BLOCK - rows), jnp.float32)], axis=1)
+    cells = jnp.concatenate([cells, jnp.zeros((BLOCK - cells.shape[0], BLOCK), jnp.float32)], axis=0)
+    return cells.T[:rows]
+
+
+def names_at(fetch, row):
+    planes, blocks, rows = fetch.shape
+    lane = lax.broadcasted_iota(jnp.int32, (planes, rows), 1)
+    wide = []
+    for b in range(blocks):
+        own = jnp.concatenate([fetch[z, b : b + 1, :] for z in range(planes)], axis=0).astype(jnp.float32)
+        own = jnp.sum(jnp.where(lane == row, own, 0.0), axis=1, keepdims=True)
+        wide.append(jnp.broadcast_to(own, (planes, BLOCK)))
+    return jnp.concatenate(wide, axis=1)
+
+
+def edge_rows_kernel(moving_in, fetch_in, first, last, moving, fetch, done):
+    fetch_all([(moving_in, moving), (fetch_in, fetch)], done)
+    planes, rows, _ = moving.shape
+    for row, out in ((0, first), (rows - 1, last)):
+        own = jnp.concatenate(
+            [moving[z].astype(jnp.float32)[row : row + 1] for z in range(planes)], axis=0
+        )
+        out[...] = jnp.concatenate([own, names_at(fetch, row)], axis=0).astype(jnp.bfloat16)
+
+
+def send_weights_kernel(slabs, place, stiffness_in, tissue_in, *refs):
+    weights, (wide, stiffness, tissue, done) = refs[:slabs], refs[slabs:]
+    fetch_all([(stiffness_in, stiffness), (tissue_in, tissue)], done)
+    planes, rows, x_length = stiffness.shape
     share = rows // slabs
     blocks = x_length // BLOCK
-    me = place[0]
-
-    def by_row(ref):
-        cells = jnp.concatenate([ref[z].astype(jnp.float32) for z in range(planes)], axis=0)
-        cells = jnp.concatenate([cells, jnp.zeros((cells.shape[0], BLOCK - rows), jnp.float32)], axis=1)
-        cells = jnp.concatenate([cells, jnp.zeros((BLOCK - cells.shape[0], BLOCK), jnp.float32)], axis=0)
-        return cells.T[:rows]
-
-    names, marks = by_row(fetch), by_row(tissue)
-    wide[3 * planes, :, 0:BLOCK] = names
+    marks = by_row(tissue, rows)
     for z in range(planes):
-        wide[z] = moving[z].astype(jnp.float32)
-        wide[planes + z] = template[z].astype(jnp.float32)
         marked = jnp.concatenate(
             [
                 jnp.broadcast_to(marks[:, z * blocks + b : z * blocks + b + 1], (rows, BLOCK))
@@ -230,40 +261,77 @@
             ],
             axis=1,
         )
-        wide[2 * planes + z] = marked * stiffness[z] * COEFFICIENT_UNIT + 0.5
+        wide[z] = marked * stiffness[z] * COEFFICIENT_UNIT + 0.5
     for step in range(slabs):
-        part = pl.ds(pl.multiple_of(around(me + step, slabs) * share, share), share)
-        for z in range(0, 2 * planes, 2):
+        part = pl.ds(pl.multiple_of(around(place[0] + step, slabs) * share, share), share)
+        for z in range(0, planes, 2):
+            both = jnp.concatenate([wide[z, part, :], wide[z + 1, part, :]], axis=0)
+            weights[step][z * share : (z + 2) * share] = both.astype(jnp.int32).astype(jnp.int16)
+
+
+def send_images_kernel(slabs, place, moving_in, template_in, fetch_in, above, below, *refs):
+    images, (wide, names, moving, template, fetch, done) = refs[:slabs], refs[slabs:]
+    fetch_all([(moving_in, moving), (template_in, template), (fetch_in, fetch)], done)
+    planes, rows, x_length = moving.shape
+    share = rows // slabs
+    blocks = x_length // BLOCK
+    lane = lax.broadcasted_iota(jnp.int32, (planes, BLOCK), 1)
+    names[...] = by_row(fetch, rows)
+    over, under = above[...].astype(jnp.float32), below[...].astype(jnp.float32)
+    for z in range(planes):
+        wide[z, share : share + rows, :] = moving[z].astype(jnp.float32)
+        wide[z, share - 1 : share, :] = over[z : z + 1]
+        wide[z, share + rows : share + rows + 1, :] = under[z : z + 1]
+        wide[planes + z, 0:rows, :] = template[z].astype(jnp.float32)
+
+    def narrow(cells):
+        packed = jnp.zeros((planes, BLOCK), jnp.float32)
+        for b in range(blocks):
+            packed = jnp.where(lane == b, cells[:, b * BLOCK : (b + 1) * BLOCK], packed)
+        return packed
+
+    for step in range(slabs):
+        to = around(place[0] + step, slabs)
+        first = pl.multiple_of(to * share, share)
+        for z in range(0, planes, 2):
+            part = pl.ds(first + share, share)
             both = jnp.concatenate([wide[z, part, :], wide[z + 1, part, :]], axis=0)
             images[step][z * share : (z + 2) * share] = both.astype(jnp.bfloat16)
-        asked = jnp.concatenate([wide[3 * planes, part, 0:BLOCK]] * blocks, axis=1)
-        images[step][2 * planes * share : (2 * planes + 1) * share] = asked.astype(jnp.bfloat16)
-        for z in range(0, planes, 2):
-            both = jnp.concatenate([wide[2 * planes + z, part, :], wide[2 * planes + z + 1, part, :]], axis=0)
-            weights[step][z * share : (z + 2) * share] = both.astype(jnp.int32).astype(jnp.int16)
+            part = pl.ds(first, share)
+            both = jnp.concatenate([wide[planes + z, part, :], wide[planes + z + 1, part, :]], axis=0)
+            images[step][(planes + z) * share : (planes + z + 2) * share] = both.astype(jnp.bfloat16)
+        before = jnp.where(to == 0, over[planes:], names_at(fetch, first - 1))
+        after = jnp.where(to == slabs - 1, under[planes:], names_at(fetch, first + share))
+        asked = [names[pl.ds(first, share), :], narrow(before), narrow(after)]
+        asked = jnp.concatenate(asked + [asked[0]] * (blocks - 3), axis=1)
+        row_over = jnp.concatenate([wide[z, pl.ds(first + (share - 1), 1), :] for z in range(planes)], axis=0)
+        row_under = jnp.concatenate([wide[z, pl.ds(first + 2 * share, 1), :] for z in range(planes)], axis=0)
+        base = 2 * planes * share
+        images[step][base : base + 16] = jnp.concatenate([asked, row_over], axis=0).astype(jnp.bfloat16)
+        images[step][base + 16 : base + 24] = row_under.astype(jnp.bfloat16)
 
 
 def pick_kernel(slabs, planes, place, *refs):
     received, sends = refs[:slabs], refs[slabs : 2 * slabs]
-    image, residual, first, last, edges = refs[2 * slabs :]
+    image, residual, edges = refs[2 * slabs :]
     total, share, x_length = image.shape
     blocks = x_length // BLOCK
+    base = 2 * planes * share
     me = place[0]
     group = 2
+
+    def spread(cells, first):
+        return jnp.concatenate(
+            [jnp.broadcast_to(cells[:, k : k + 1], (share, BLOCK)) for k in range(first, first + blocks)], axis=1
+        )
+
+    asked = [r[base : base + 16].astype(jnp.float32) for r in received]
+    rows_of = [[a[8:16] for a in asked], [r[base + 16 : base + 24].astype(jnp.float32) for r in received]]
+    asked = [a[0:8] for a in asked]
     for step in range(slabs):
-        base = around(me - step, slabs) * planes
-        names = received[step][2 * planes * share : (2 * planes + 1) * share, 0:BLOCK].astype(jnp.float32)
+        mine = around(me - step, slabs) * planes
         for start in range(0, planes, group):
-            wanted = [
-                jnp.concatenate(
-                    [
-                        jnp.broadcast_to(names[:, z * blocks + b : z * blocks + b + 1], (share, BLOCK))
-                        for b in range(blocks)
-                    ],
-                    axis=1,
-                )
-                for z in range(start, start + group)
-            ]
+            wanted = [spread(asked[step], z * blocks) for z in range(start, start + group)]
             found = [jnp.zeros((share, x_length), jnp.float32) for _ in range(group)]
             for other in range(slabs):
                 name = (around(me - other, slabs) * planes).astype(jnp.float32)
@@ -276,28 +344,33 @@
                         ]
             both = received[step][(planes + start) * share : (planes + start + 2) * share].astype(jnp.float32)
             for k in range(group):
-                z = base + (start + k)
+                z = mine + (start + k)
                 image[z] = found[k]
                 residual[z] = found[k] - both[k * share : (k + 1) * share]
-                edges[0, pl.ds(z, 1), :] = found[k][0:1]
-                edges[1, pl.ds(z, 1), :] = found[k][share - 1 : share]
-    first[...] = edges[0].astype(jnp.bfloat16)
-    last[...] = edges[1].astype(jnp.bfloat16)
+        wanted = [spread(asked[step], (1 + side) * BLOCK) for side in range(2)]
+        found = [jnp.zeros((planes, x_length), jnp.float32) for _ in range(2)]
+        for other in range(slabs):
+            name = (around(me - other, slabs) * planes).astype(jnp.float32)
+            for plane in range(planes):
+                found = [
+                    jnp.where(w == name + float(plane), rows_of[side][other][plane : plane + 1], f)
+                    for side, (w, f) in enumerate(zip(wanted, found))
+                ]
+        for side in range(2):
+            edges[side, pl.ds(pl.multiple_of(mine, planes), planes), :] = found[side]
     for step, send in enumerate(sends):
-        base = around(me + step, slabs) * planes
+        mine = around(me + step, slabs) * planes
         for z in range(0, planes, 2):
-            both = jnp.concatenate([image[base + z], image[base + (z + 1)]], axis=0)
+            both = jnp.concatenate([image[mine + z], image[mine + (z + 1)]], axis=0)
             send[z * share : (z + 2) * share] = both.astype(jnp.bfloat16)
 
 
 def force_kernel(slabs, place, *refs):
     weights = refs[:slabs]
-    above, below, image, residual, basis_x, basis_z, spectra, edges, force = refs[slabs:]
+    image, residual, edges, basis_x, basis_z, spectra, force = refs[slabs:]
     total, share, x_length = image.shape
     planes = total // slabs
     me = place[0]
-    edges[0] = above[...].astype(jnp.float32)
-    edges[1] = below[...].astype(jnp.float32)
     row = lax.broadcasted_iota(jnp.int32, (share, x_length), 0)
     for step in range(slabs):
         base = around(me - step, slabs) * planes
@@ -405,53 +478,97 @@
         ]
 
     def exchange(values):
-        values = values.astype(jnp.float16)
         return lax.all_to_all(values, both_axes, split_axis=0, concat_axis=0, tiled=True)
 
-    images = shape(((2 * planes + 1) * share, x_length), bf16)
-    weights = shape((planes * share, x_length), jnp.int16)
-    sends = call(
-        functools.partial(send_rows_kernel, slabs),
-        [images] * slabs + [weights] * slabs,
-        (slab_id, moving, template, stiffness, fetch_plane.swapaxes(1, 2), tissue.swapaxes(1, 2)),
-        [pltpu.VMEM((3 * planes + 1, rows, x_length), f32)],
-    )
-    images, weights = scatter(sends[:slabs]), scatter(sends[slabs:])
-    *sends, image, residual, first, last = call(
+    fetch, marks = fetch_plane.swapaxes(1, 2), tissue.swapaxes(1, 2)
+    brick, field = pltpu.VMEM(moving.shape, bf16), pltpu.VMEM(stiffness.shape, f32)
+    small = pltpu.VMEM(fetch.shape, jnp.int32)
+    first, last = call(
+        edge_rows_kernel,
+        [shape((2 * planes, x_length), bf16)] * 2,
+        (moving,),
+        (fetch,),
+        scratch=[brick, small, pltpu.SemaphoreType.DMA((2,))],
+    )
+    above = lax.ppermute(last, "sub", [(i, (i + 1) % subs) for i in range(subs)])
+    below = lax.ppermute(first, "sub", [((i + 1) % subs, i) for i in range(subs)])
+    weights = call(
+        functools.partial(send_weights_kernel, slabs),
+        [shape((planes * share, x_length), jnp.int16)] * slabs,
+        slab_id,
+        (stiffness,),
+        (marks,),
+        scratch=[field, field, small, pltpu.SemaphoreType.DMA((2,))],
+    )
+    weights = scatter(weights)
+    images = call(
+        functools.partial(send_images_kernel, slabs),
+        [shape(((2 * planes + 3) * share, x_length), bf16)] * slabs,
+        slab_id,
+        (moving,),
+        (template,),
+        (fetch,),
+        above,
+        below,
+        scratch=[
+            pltpu.VMEM((2 * planes, rows + 2 * share, x_length), f32),
+            pltpu.VMEM((rows, BLOCK), f32),
+            brick,
+            brick,
+            small,
+            pltpu.SemaphoreType.DMA((3,)),
+        ],
+    )
+    images = scatter(images)
+    *sends, image, residual, edges = call(
         functools.partial(pick_kernel, slabs, planes),
         [shape((planes * share, x_length), bf16)] * slabs
         + [shape((total_z, share, x_length))] * 2
-        + [shape((total_z, x_length), bf16)] * 2,
-        (slab_id, *images),
-        [pltpu.VMEM((2, total_z, x_length), f32)],
-    )
-    ring = [s * subs + q for q in range(subs) for s in range(slabs)]
-    onward = [(ring[i], ring[(i + 1) % devices]) for i in range(devices)]
-    above = lax.ppermute(last, both_axes, onward)
-    below = lax.ppermute(first, both_axes, [(b, a) for a, b in onward])
+        + [shape((2, total_z, x_length))],
+        slab_id,
+        *images,
+        flops=1 << 30,
+    )
+    warped = scatter(sends)
     basis_z = in_two(np.kron(real_basis(total_z), np.eye(share)))
     spectra = call(
         functools.partial(force_kernel, slabs),
         shape((devices, 3 * part, area)),
-        (slab_id, *weights, above, below, image, residual, in_two(8.0 * real_basis(x_length)), basis_z),
-        [pltpu.VMEM((2, total_z, x_length), f32), pltpu.VMEM((3, total_z, share, x_length), f32)],
-    )
+        slab_id,
+        *weights,
+        image,
+        residual,
+        edges,
+        in_two(8.0 * real_basis(x_length)),
+        basis_z,
+        scratch=[pltpu.VMEM((3, total_z, share, x_length), f32)],
+        flops=3 << 30,
+    )
+    spectra = spectra.astype(jnp.float16)
+    spectra, warped = lax.optimization_barrier((spectra, warped))
     spectra = exchange(spectra)
-    spectra, sends = lax.optimization_barrier((spectra, sends))
-    warped = scatter(sends)
     spectra = call(
         functools.partial(solve_kernel, subs),
         shape((devices, 3 * part, area)),
-        (place_id, spectra.astype(f32), basis_z, in_two(real_basis(total_y))),
-        [pltpu.VMEM((total_z, total_y, 128), f32)],
-    )
-    spectra = exchange(spectra)
+        place_id,
+        spectra.astype(f32),
+        basis_z,
+        in_two(real_basis(total_y)),
+        scratch=[pltpu.VMEM((total_z, total_y, 128), f32)],
+        flops=3 << 30,
+    )
+    spectra = exchange(spectra.astype(jnp.float16))
     return tuple(
         call(
             functools.partial(update_kernel, slabs),
             [shape(velocity.shape), shape(moving.shape, bf16)],
-            (slab_id, spectra.astype(f32), velocity, in_two(real_basis(x_length)), *warped),
-            [pltpu.VMEM((planes, rows, x_length), f32)],
+            slab_id,
+            spectra.astype(f32),
+            velocity,
+            in_two(real_basis(x_length)),
+            *warped,
+            scratch=[pltpu.VMEM((planes, rows, x_length), f32)],
+            flops=3 << 30,
         )
     )
 
@@ -468,6 +585,7 @@
         and planes * slabs * 8 == 256
         and rows * subs == BLOCK
         and planes * (x_length // BLOCK) <= BLOCK
+        and 3 <= x_length // BLOCK <= BLOCK
     )
     run = local_rows if fits else local_general
     return run(velocity, template, moving, stiffness, fetch_plane, tissue)

time: 103 us -> 98.7 us (0.958)
  blocking collectives: 0 us -> 25.7 us
  waiting for transfers between devices: 48.5 us -> 25.3 us
  starting transfers between devices: 32 us -> 25.5 us
  local copies, waits for them, and re-layouts: 4.49 us -> 7.33 us
  other arithmetic: 3.71 us -> 1.44 us
  Pallas kernels: 13.2 us -> 11.7 us
    all_to_all x0 -> x1, blocking collectives: none -> 25.7 us  [exchange(): lax.all_to_all(values, both_axes, split_axis=0, concat_axis=0, tiled=True)]
    all_to_all x2 -> x1, waiting for transfers between devices: 32.1 us -> 18.7 us  [exchange(): lax.all_to_all(values, both_axes, split_axis=0, concat_axis=0, tiled=True)]
    ppermute x9, waiting for transfers between devices: 12.7 us -> 5.2 us  [scatter(): lax.ppermute(sends[d], 'slab', [(i, (i + d) % slabs) for i in range(slabs)])]
    all_to_all x2 -> x1, starting transfers between devices: 10.8 us -> 4.45 us  [exchange(): lax.all_to_all(values, both_axes, split_axis=0, concat_axis=0, tiled=True)]
    unnamed x18 -> x24, local copies, waits for them, and re-layouts: 4.49 us -> 7.33 us
    ppermute x2, starting transfers between devices: 5.31 us -> 2.49 us  [the longest x1 1.99 us: local_rows(): lax.ppermute(first, 'sub', [((i + 1) % subs, i) for i in range(subs)])]
    ppermute x9, starting transfers between devices: 15.9 us -> 18.6 us  [scatter(): lax.ppermute(sends[d], 'slab', [(i, (i + d) % slabs) for i in range(slabs)])]
    ppermute x2, waiting for transfers between devices: 3.75 us -> 1.44 us  [the longest x1 1.36 us: local_rows(): lax.ppermute(last, 'sub', [(i, (i + 1) % subs) for i in range(subs)])]
  transfers between devices with their start and end apart: 13 -> 12, of which waited for: 9 -> 6; matrix products, arithmetic and copies ran while one was open for 0% -> 1% of each run, Pallas kernels for 1% -> 5%
where the time goes in v3:
time: 98.7 us; the launch traced here: 97.8 us
  blocking collectives  25.7 us (26%)
  starting transfers between devices  25.5 us (26%)
  waiting for transfers between devices  25.3 us (26%)
  Pallas kernels  11.7 us (12%)
  local copies, waits for them, and re-layouts  7.33 us (7%)
  other arithmetic  1.44 us (1%)
    all_to_all x1, blocking collectives, exchange(): lax.all_to_all(values, both_axes, split_axis=0, concat_axis=0, tiled=True)  25.7 us
    all_to_all x1, waiting for transfers between devices, exchange(): lax.all_to_all(values, both_axes, split_axis=0, concat_axis=0, tiled=True)  18.7 us
    ppermute x9, starting transfers between devices, scatter(): lax.ppermute(sends[d], 'slab', [(i, (i + d) % slabs) for i in range(slabs)])  18.6 us
    pallas_call x7, Pallas kernels, call(): pl.pallas_call(kernel, out_shape=out_shape, in_specs=places, out_specs=ja...  11.7 us
    unnamed x24, local copies, waits for them, and re-layouts  7.33 us
    ppermute x9, waiting for transfers between devices, scatter(): lax.ppermute(sends[d], 'slab', [(i, (i + d) % slabs) for i in range(slabs)])  5.2 us
    all_to_all x1, starting transfers between devices, exchange(): lax.all_to_all(values, both_axes, split_axis=0, concat_axis=0, tiled=True)  4.45 us
    ppermute x1, starting transfers between devices, local_rows(): lax.ppermute(first, 'sub', [((i + 1) % subs, i) for i in range(subs)])  1.99 us
  transfers between devices with their start and end apart: 12, of which 6 were waited for; matrix products, arithmetic and copies ran while one was open for 1% of the time, Pallas kernels for 5%

profile of v3, /device:TPU:0, one launch (start us, length us, event | category | flops | bytes accessed | tf_op | source)
XLA Modules:
  0.0 97.8 jit_solution(2213387071136617111)
XLA Ops:
  0.6 0.0 copy-start
  0.6 0.9 copy-done
  1.6 0.0 copy-start.4
  1.6 0.7 copy-done.4
  2.3 0.2 shard_map.114
  2.5 0.5 collective-permute-start.3
  3.0 2.0 %collective-permute-start.4 = (bf16[16,512]{1,0:T(8,128)(2,1)S(1)}, bf16[16,512]{1,0:T(8,128)(2,1)S(1)}, u32[]{:S(2)}, u32[]{:S(2)}) collective-permute-start(bf16[16,512]{1,0:T(8,128)(2,1)S(1)} %get-tuple-element.29), channel_id=1, source_target_pairs={{1,0},{2,1},{3,2},{0,3},{5,4},{6,5},{7,6},{4,7},{9,8},{10,9},{11,1... | collective-permute-start | bytes 49160 | tf_op jit(solution)/shard_map/ppermute | solution.py:494
  5.0 1.4 %collective-permute-done.3.above = bf16[16,512]{1,0:T(8,128)(2,1)S(1)} collective-permute-done((bf16[16,512]{1,0:T(8,128)(2,1)S(1)}, bf16[16,512]{1,0:T(8,128)(2,1)S(1)}, u32[]{:S(2)}, u32[]{:S(2)}) %collective-permute-start.3) | collective-permute-done | bytes 16416 | tf_op jit(solution)/shard_map/ppermute | solution.py:493
  6.3 0.1 collective-permute-done.4.below
  6.4 0.0 copy-start.1
  6.4 0.9 copy-done.1
  7.4 0.0 copy-start.3
  7.4 0.9 copy-done.3
  8.3 0.0 copy-start.5
  8.3 0.7 copy-done.5
  9.0 0.4 shard_map.115
  9.4 2.4 %collective-permute-start.5 = (bf16[152,512]{1,0:T(8,128)(2,1)S(1)}, bf16[152,512]{1,0:T(8,128)(2,1)S(1)}, u32[]{:S(2)}, u32[]{:S(2)}) collective-permute-start(bf16[152,512]{1,0:T(8,128)(2,1)S(1)} %get-tuple-element.31), channel_id=1, source_target_pairs={{0,4},{4,8},{8,12},{12,0},{1,5},{5,9},{9,13},{13,1},{2,6},{6,10},{... | collective-permute-start | bytes 466952 | tf_op jit(solution)/shard_map/ppermute | solution.py:476
  11.8 2.6 %collective-permute-start.6 = (bf16[152,512]{1,0:T(8,128)(2,1)S(1)}, bf16[152,512]{1,0:T(8,128)(2,1)S(1)}, u32[]{:S(2)}, u32[]{:S(2)}) collective-permute-start(bf16[152,512]{1,0:T(8,128)(2,1)S(1)} %get-tuple-element.32), channel_id=1, source_target_pairs={{0,8},{4,12},{8,0},{12,4},{1,9},{5,13},{9,1},{13,5},{2,10},{6,14},... | collective-permute-start | bytes 466952 | tf_op jit(solution)/shard_map/ppermute | solution.py:476
  14.4 1.3 %collective-permute-start.7 = (bf16[152,512]{1,0:T(8,128)(2,1)S(1)}, bf16[152,512]{1,0:T(8,128)(2,1)S(1)}, u32[]{:S(2)}, u32[]{:S(2)}) collective-permute-start(bf16[152,512]{1,0:T(8,128)(2,1)S(1)} %get-tuple-element.33), channel_id=1, source_target_pairs={{0,12},{4,0},{8,4},{12,8},{1,13},{5,1},{9,5},{13,9},{2,14},{6,2},{... | collective-permute-start | bytes 466952 | tf_op jit(solution)/shard_map/ppermute | solution.py:476
  15.8 0.0 copy-start.2
  15.8 1.0 %copy-done.2 = f32[8,32,512]{2,1,0:T(8,128)S(1)} copy-done((f32[8,32,512]{2,1,0:T(8,128)S(1)}, f32[8,32,512]{2,1,0:T(8,128)}, u32[]{:S(2)}) %copy-start.2) | copy-done | bytes 524312
  16.8 0.0 copy-start.6
  16.8 0.7 copy-done.6
  17.5 0.5 shard_map.113
  18.0 0.7 collective-permute-start
  18.7 0.3 collective-permute-start.1
  19.1 0.0 collective-permute-done.5.refs_1_
  19.1 2.8 %collective-permute-start.2 = (s16[64,512]{1,0:T(8,128)(2,1)S(1)}, s16[64,512]{1,0:T(8,128)(2,1)S(1)}, u32[]{:S(2)}, u32[]{:S(2)}) collective-permute-start(s16[64,512]{1,0:T(8,128)(2,1)S(1)} %get-tuple-element.27), channel_id=1, source_target_pairs={{0,12},{4,0},{8,4},{12,8},{1,13},{5,1},{9,5},{13,9},{2,14},{6,2},{... | collective-permute-start | bytes 196616 | tf_op jit(solution)/shard_map/ppermute | solution.py:476
  21.9 4.4 %collective-permute-done.6.refs_2_ = bf16[152,512]{1,0:T(8,128)(2,1)S(1)} collective-permute-done((bf16[152,512]{1,0:T(8,128)(2,1)S(1)}, bf16[152,512]{1,0:T(8,128)(2,1)S(1)}, u32[]{:S(2)}, u32[]{:S(2)}) %collective-permute-start.6) | collective-permute-done | bytes 155680 | tf_op jit(solution)/shard_map/ppermute | solution.py:476
  26.3 0.0 collective-permute-done.7.refs_3_
  26.3 0.0 copy-start.9
  26.3 0.0 copy-start.10
  26.3 1.9 %shard_map.116 = (bf16[64,512]{1,0:T(8,128)(2,1)S(1)}, bf16[64,512]{1,0:T(8,128)(2,1)S(1)}, bf16[64,512]{1,0:T(8,128)(2,1)S(1)}, bf16[64,512]{1,0:T(8,128)(2,1)S...) custom-call(s32[1]{0:T(128)} %bitcast.place, ...), custom_call_target="tpu_custom_call" | custom-call | flops 1073741824 | bytes 2064388 | tf_op jit(solution)/shard_map/pallas_call | solution.py:202
  28.2 5.9 %collective-permute-start.8 = (bf16[64,512]{1,0:T(8,128)(2,1)S(1)}, bf16[64,512]{1,0:T(8,128)(2,1)S(1)}, u32[]{:S(2)}, u32[]{:S(2)}) collective-permute-start(bf16[64,512]{1,0:T(8,128)(2,1)S(1)} %get-tuple-element.38), channel_id=1, source_target_pairs={{0,4},{4,8},{8,12},{12,0},{1,5},{5,9},{9,13},{13,1},{2,6},{6,10},{... | collective-permute-start | bytes 196616 | tf_op jit(solution)/shard_map/ppermute | solution.py:476
  34.1 1.3 %collective-permute-start.9 = (bf16[64,512]{1,0:T(8,128)(2,1)S(1)}, bf16[64,512]{1,0:T(8,128)(2,1)S(1)}, u32[]{:S(2)}, u32[]{:S(2)}) collective-permute-start(bf16[64,512]{1,0:T(8,128)(2,1)S(1)} %get-tuple-element.39), channel_id=1, source_target_pairs={{0,8},{4,12},{8,0},{12,4},{1,9},{5,13},{9,1},{13,5},{2,10},{6,14},... | collective-permute-start | bytes 196616 | tf_op jit(solution)/shard_map/ppermute | solution.py:476
  35.5 0.0 collective-permute-done.refs_1_
  35.5 1.1 %collective-permute-start.10 = (bf16[64,512]{1,0:T(8,128)(2,1)S(1)}, bf16[64,512]{1,0:T(8,128)(2,1)S(1)}, u32[]{:S(2)}, u32[]{:S(2)}) collective-permute-start(bf16[64,512]{1,0:T(8,128)(2,1)S(1)} %get-tuple-element.40), channel_id=1, source_target_pairs={{0,12},{4,0},{8,4},{12,8},{1,13},{5,1},{9,5},{13,9},{2,14},{6,2},{... | collective-permute-start | bytes 196616 | tf_op jit(solution)/shard_map/ppermute | solution.py:476
  36.6 0.0 collective-permute-done.1.refs_2_
  36.6 0.0 collective-permute-done.2.refs_3_
  36.6 0.0 copy-done.9
  36.6 0.0 copy-done.10
  36.6 2.7 %shard_map.117 = f32[16,96,256]{2,1,0:T(8,128)S(1)} custom-call(s32[1]{0:T(128)} %bitcast.place, s16[64,512]{1,0:T(8,128)(2,1)S(1)} %get-tuple-element.24.refs_0_, s16[64,512]{1,0:T(8,128)(2,1)S(1)} %collective-permute-done.refs_1_, s16[64,512]{1,0:T(8,128)(2,1)S(1)} %collective-permute-done.1.refs_2_, s16[64,512]{1,0:T(8,128)(2,1)S(1)} %collective-permute-done.2.refs_3_, ...), custom_call_target="tpu_custom_call" | custom-call | flops 3221225472 | bytes 4325380 | tf_op jit(solution)/shard_map/pallas_call | solution.py:202
  39.3 1.0 %convert_element_type.12 = f16[16,96,256]{2,1,0:T(8,128)(2,1)} convert(f32[16,96,256]{2,1,0:T(8,128)S(1)} %shard_map.117) | non-fusion elementwise | flops 393216 | bytes 2359296 | tf_op jit(solution)/shard_map/convert_element_type | solution.py:547
  40.3 0.0 collective-permute-done.8.refs_1_
  40.3 0.5 collective-permute-done.9.refs_2_
  40.8 0.4 collective-permute-done.10.refs_3_
  41.1 4.4 %all-to-all-start = ((f16[16,96,256]{2,1,0:T(8,128)(2,1)}), f16[16,96,256]{2,1,0:T(8,128)(2,1)S(1)}, u32[]{:S(2)}, u32[]{:S(2)}) async-start(f16[16,96,256]{2,1,0:T(8,128)(2,1)} %convert_element_type.12), calls=%async_computation | async-start | bytes 1572864 | tf_op jit(solution)/shard_map/all_to_all | solution.py:481
  45.6 0.0 copy-start.11
  45.6 18.7 %all-to-all-done = f16[16,96,256]{2,1,0:T(8,128)(2,1)S(1)} async-done(((f16[16,96,256]{2,1,0:T(8,128)(2,1)}), f16[16,96,256]{2,1,0:T(8,128)(2,1)S(1)}, u32[]{:S(2)}, u32[]{:S(2)}) %all-to-all-start) | async-done | bytes 786464 | tf_op jit(solution)/shard_map/all_to_all | solution.py:481
  64.3 0.1 convert_element_type.13.spectra
  64.4 0.0 copy-done.11
  64.5 3.4 %shard_map.118 = f32[16,96,256]{2,1,0:T(8,128)S(1)} custom-call(s32[1]{0:T(128)} %bitcast.1.place, f32[16,96,256]{2,1,0:T(8,128)S(1)} %convert_element_type.13.spectra, bf16[2,256,256]{2,1,0:T(8,128)(2,1)S(1)} %copy-done.10, bf16[2,128,128]{2,1,0:T(8,128)(2,1)S(1)} %copy-done.11), custom_call_target="tpu_custom_call" | custom-call | flops 3221225472 | bytes 3473412 | tf_op jit(solution)/shard_map/pallas_call | solution.py:202
  67.8 0.2 convert_element_type.14
  68.0 0.0 copy-start.8
  68.0 25.7 %all_to_all.10 = f16[16,96,256]{2,1,0:T(8,128)(2,1)S(1)} all-to-all(f16[16,96,256]{2,1,0:T(8,128)(2,1)S(1)} %convert_element_type.14), channel_id=1, replica_groups=mesh['groups'=2,'slab'=4,'sub'=4] {'slab','sub'}, dimensions={0} | all-to-all | bytes 1572864 | tf_op jit(solution)/shard_map/all_to_all | solution.py:481
  93.7 0.0 copy-start.7
  93.7 0.1 convert_element_type.15.spectra
  93.8 0.0 copy-done.8
  93.8 1.3 %copy-done.7 = f32[3,8,32,512]{3,2,1,0:T(8,128)S(1)} copy-done((f32[3,8,32,512]{3,2,1,0:T(8,128)S(1)}, f32[3,8,32,512]{3,2,1,0:T(8,128)}, u32[]{:S(2)}) %copy-start.7) | copy-done | bytes 1572888
  95.1 2.7 %shard_map.119 = (f32[3,8,32,512]{3,2,1,0:T(8,128)}, bf16[8,32,512]{2,1,0:T(8,128)(2,1)}) custom-call(s32[1]{0:T(128)} %bitcast.place, f32[16,96,256]{2,1,0:T(8,128)S(1)} %convert_element_type.15.spectra, f32[3,8,32,512]{3,2,1,0:T(8,128)S(1)} %copy-done.7, bf16[2,512,512]{2,1,0:T(8,128)(2,1)S(1)} %copy-done.8, ...), custom_call_target="tpu_custom_call" | custom-call | flops 3221225472 | bytes 6291460 | tf_op jit(solution)/shard_map/pallas_call | solution.py:202
Async XLA Ops:
  0.6 1.0 copy-start
  1.6 0.7 copy-start.4
  2.5 3.9 %collective-permute-start.3 = (bf16[16,512]{1,0:T(8,128)(2,1)S(1)}, bf16[16,512]{1,0:T(8,128)(2,1)S(1)}, u32[]{:S(2)}, u32[]{:S(2)}) collective-permute-start(bf16[16,512]{1,0:T(8,128)(2,1)S(1)} %get-tuple-element.28), channel_id=1, source_target_pairs={{0,1},{1,2},{2,3},{3,0},{4,5},{5,6},{6,7},{7,4},{8,9},{9,10},{10,1... | collective-permute-start | bytes 49160 | tf_op jit(solution)/shard_map/ppermute | solution.py:493
  3.0 3.4 %collective-permute-start.4 = (bf16[16,512]{1,0:T(8,128)(2,1)S(1)}, bf16[16,512]{1,0:T(8,128)(2,1)S(1)}, u32[]{:S(2)}, u32[]{:S(2)}) collective-permute-start(bf16[16,512]{1,0:T(8,128)(2,1)S(1)} %get-tuple-element.29), channel_id=1, source_target_pairs={{1,0},{2,1},{3,2},{0,3},{5,4},{6,5},{7,6},{4,7},{9,8},{10,9},{11,1... | collective-permute-start | bytes 49160 | tf_op jit(solution)/shard_map/ppermute | solution.py:494
  6.4 0.9 copy-start.1
  7.4 0.9 copy-start.3
  8.3 0.7 copy-start.5
  9.4 9.6 %collective-permute-start.5 = (bf16[152,512]{1,0:T(8,128)(2,1)S(1)}, bf16[152,512]{1,0:T(8,128)(2,1)S(1)}, u32[]{:S(2)}, u32[]{:S(2)}) collective-permute-start(bf16[152,512]{1,0:T(8,128)(2,1)S(1)} %get-tuple-element.31), channel_id=1, source_target_pairs={{0,4},{4,8},{8,12},{12,0},{1,5},{5,9},{9,13},{13,1},{2,6},{6,10},{... | collective-permute-start | bytes 466952 | tf_op jit(solution)/shard_map/ppermute | solution.py:476
  11.8 14.4 %collective-permute-start.6 = (bf16[152,512]{1,0:T(8,128)(2,1)S(1)}, bf16[152,512]{1,0:T(8,128)(2,1)S(1)}, u32[]{:S(2)}, u32[]{:S(2)}) collective-permute-start(bf16[152,512]{1,0:T(8,128)(2,1)S(1)} %get-tuple-element.32), channel_id=1, source_target_pairs={{0,8},{4,12},{8,0},{12,4},{1,9},{5,13},{9,1},{13,5},{2,10},{6,14},... | collective-permute-start | bytes 466952 | tf_op jit(solution)/shard_map/ppermute | solution.py:476
  14.4 11.9 %collective-permute-start.7 = (bf16[152,512]{1,0:T(8,128)(2,1)S(1)}, bf16[152,512]{1,0:T(8,128)(2,1)S(1)}, u32[]{:S(2)}, u32[]{:S(2)}) collective-permute-start(bf16[152,512]{1,0:T(8,128)(2,1)S(1)} %get-tuple-element.33), channel_id=1, source_target_pairs={{0,12},{4,0},{8,4},{12,8},{1,13},{5,1},{9,5},{13,9},{2,14},{6,2},{... | collective-permute-start | bytes 466952 | tf_op jit(solution)/shard_map/ppermute | solution.py:476
  15.8 1.0 %copy-start.2 = (f32[8,32,512]{2,1,0:T(8,128)S(1)}, f32[8,32,512]{2,1,0:T(8,128)}, u32[]{:S(2)}) copy-start(f32[8,32,512]{2,1,0:T(8,128)} %stiffness_in.1) | copy-start | bytes 1572868
  16.8 0.7 copy-start.6
  18.0 17.5 %collective-permute-start = (s16[64,512]{1,0:T(8,128)(2,1)S(1)}, s16[64,512]{1,0:T(8,128)(2,1)S(1)}, u32[]{:S(2)}, u32[]{:S(2)}) collective-permute-start(s16[64,512]{1,0:T(8,128)(2,1)S(1)} %get-tuple-element.25), channel_id=1, source_target_pairs={{0,4},{4,8},{8,12},{12,0},{1,5},{5,9},{9,13},{13,1},{2,6},{6,10},{... | collective-permute-start | bytes 196616 | tf_op jit(solution)/shard_map/ppermute | solution.py:476
  18.7 17.9 %collective-permute-start.1 = (s16[64,512]{1,0:T(8,128)(2,1)S(1)}, s16[64,512]{1,0:T(8,128)(2,1)S(1)}, u32[]{:S(2)}, u32[]{:S(2)}) collective-permute-start(s16[64,512]{1,0:T(8,128)(2,1)S(1)} %get-tuple-element.26), channel_id=1, source_target_pairs={{0,8},{4,12},{8,0},{12,4},{1,9},{5,13},{9,1},{13,5},{2,10},{6,14},... | collective-permute-start | bytes 196616 | tf_op jit(solution)/shard_map/ppermute | solution.py:476
  19.1 17.5 %collective-permute-start.2 = (s16[64,512]{1,0:T(8,128)(2,1)S(1)}, s16[64,512]{1,0:T(8,128)(2,1)S(1)}, u32[]{:S(2)}, u32[]{:S(2)}) collective-permute-start(s16[64,512]{1,0:T(8,128)(2,1)S(1)} %get-tuple-element.27), channel_id=1, source_target_pairs={{0,12},{4,0},{8,4},{12,8},{1,13},{5,1},{9,5},{13,9},{2,14},{6,2},{... | collective-permute-start | bytes 196616 | tf_op jit(solution)/shard_map/ppermute | solution.py:476
  26.3 10.3 %copy-start.9 = (bf16[2,512,512]{2,1,0:T(8,128)(2,1)S(1)}, bf16[2,512,512]{2,1,0:T(8,128)(2,1)}, u32[]{:S(2)}) copy-start(bf16[2,512,512]{2,1,0:T(8,128)(2,1)} %constant.17.clone.refs_7_) | copy-start | bytes 3145732
  26.3 10.3 %copy-start.10 = (bf16[2,256,256]{2,1,0:T(8,128)(2,1)S(1)}, bf16[2,256,256]{2,1,0:T(8,128)(2,1)}, u32[]{:S(2)}) copy-start(bf16[2,256,256]{2,1,0:T(8,128)(2,1)} %constant.18.clone.refs_8_.basis_z) | copy-start | bytes 786436
  28.2 12.1 %collective-permute-start.8 = (bf16[64,512]{1,0:T(8,128)(2,1)S(1)}, bf16[64,512]{1,0:T(8,128)(2,1)S(1)}, u32[]{:S(2)}, u32[]{:S(2)}) collective-permute-start(bf16[64,512]{1,0:T(8,128)(2,1)S(1)} %get-tuple-element.38), channel_id=1, source_target_pairs={{0,4},{4,8},{8,12},{12,0},{1,5},{5,9},{9,13},{13,1},{2,6},{6,10},{... | collective-permute-start | bytes 196616 | tf_op jit(solution)/shard_map/ppermute | solution.py:476
  34.1 6.7 %collective-permute-start.9 = (bf16[64,512]{1,0:T(8,128)(2,1)S(1)}, bf16[64,512]{1,0:T(8,128)(2,1)S(1)}, u32[]{:S(2)}, u32[]{:S(2)}) collective-permute-start(bf16[64,512]{1,0:T(8,128)(2,1)S(1)} %get-tuple-element.39), channel_id=1, source_target_pairs={{0,8},{4,12},{8,0},{12,4},{1,9},{5,13},{9,1},{13,5},{2,10},{6,14},... | collective-permute-start | bytes 196616 | tf_op jit(solution)/shard_map/ppermute | solution.py:476
  35.5 5.7 %collective-permute-start.10 = (bf16[64,512]{1,0:T(8,128)(2,1)S(1)}, bf16[64,512]{1,0:T(8,128)(2,1)S(1)}, u32[]{:S(2)}, u32[]{:S(2)}) collective-permute-start(bf16[64,512]{1,0:T(8,128)(2,1)S(1)} %get-tuple-element.40), channel_id=1, source_target_pairs={{0,12},{4,0},{8,4},{12,8},{1,13},{5,1},{9,5},{13,9},{2,14},{6,2},{... | collective-permute-start | bytes 196616 | tf_op jit(solution)/shard_map/ppermute | solution.py:476
  41.1 23.2 %all-to-all-start = ((f16[16,96,256]{2,1,0:T(8,128)(2,1)}), f16[16,96,256]{2,1,0:T(8,128)(2,1)S(1)}, u32[]{:S(2)}, u32[]{:S(2)}) async-start(f16[16,96,256]{2,1,0:T(8,128)(2,1)} %convert_element_type.12), calls=%async_computation | async-start | bytes 1572864 | tf_op jit(solution)/shard_map/all_to_all | solution.py:481
  45.6 18.8 %copy-start.11 = (bf16[2,128,128]{2,1,0:T(8,128)(2,1)S(1)}, bf16[2,128,128]{2,1,0:T(8,128)(2,1)}, u32[]{:S(2)}) copy-start(bf16[2,128,128]{2,1,0:T(8,128)(2,1)} %constant.19.clone.basis_y) | copy-start | bytes 196612
  68.0 25.8 %copy-start.8 = (bf16[2,512,512]{2,1,0:T(8,128)(2,1)S(1)}, bf16[2,512,512]{2,1,0:T(8,128)(2,1)}, u32[]{:S(2)}) copy-start(bf16[2,512,512]{2,1,0:T(8,128)(2,1)} %constant.20.clone.basis) | copy-start | bytes 3145732
  93.7 1.4 %copy-start.7 = (f32[3,8,32,512]{3,2,1,0:T(8,128)S(1)}, f32[3,8,32,512]{3,2,1,0:T(8,128)}, u32[]{:S(2)}) copy-start(f32[3,8,32,512]{3,2,1,0:T(8,128)} %velocity.1) | copy-start | bytes 4718596

commit v4 on v3

--- a/solution.py
+++ b/solution.py
@@ -149,6 +149,7 @@
 
 
 VMEM_BYTES = 24 * 1024 * 1024
+WHOLE_VMEM_BYTES = 63 * 1024 * 1024
 COEFFICIENT_UNIT = 8191.0
 
 
@@ -191,21 +192,24 @@
     return lax.rem(value + 2 * count, count)
 
 
-def call(kernel, out_shape, *arguments, scratch=(), flops=0):
+def call(kernel, out_shape, *arguments, scratch=(), flops=0, stays=0, limit=VMEM_BYTES):
     places = [
-        pl.BlockSpec(memory_space=pl.ANY if isinstance(a, tuple) else pltpu.SMEM if a.ndim == 1 else pltpu.VMEM)
+        pl.BlockSpec(memory_space=pltpu.HBM if isinstance(a, tuple) else pltpu.SMEM if a.ndim == 1 else pltpu.VMEM)
         for a in arguments
     ]
     arguments = [a[0] if isinstance(a, tuple) else a for a in arguments]
-    vmem = pl.BlockSpec(memory_space=pltpu.VMEM)
+    out_places = [
+        pl.BlockSpec(memory_space=pltpu.HBM if k < stays else pltpu.VMEM)
+        for k in range(len(jax.tree.leaves(out_shape)))
+    ]
     nbytes = sum(a.size * a.dtype.itemsize for a in arguments + jax.tree.leaves(out_shape))
     return pl.pallas_call(
         kernel,
         out_shape=out_shape,
         in_specs=places,
-        out_specs=jax.tree.map(lambda _: vmem, out_shape),
+        out_specs=jax.tree.unflatten(jax.tree.structure(out_shape), out_places),
         scratch_shapes=list(scratch),
-        compiler_params=pltpu.CompilerParams(vmem_limit_bytes=VMEM_BYTES),
+        compiler_params=pltpu.CompilerParams(vmem_limit_bytes=limit),
         cost_estimate=pl.CostEstimate(flops=flops, bytes_accessed=nbytes, transcendentals=0),
     )(*arguments)
 
@@ -236,24 +240,20 @@
     return jnp.concatenate(wide, axis=1)
 
 
-def edge_rows_kernel(moving_in, fetch_in, first, last, moving, fetch, done):
-    fetch_all([(moving_in, moving), (fetch_in, fetch)], done)
-    planes, rows, _ = moving.shape
-    for row, out in ((0, first), (rows - 1, last)):
-        own = jnp.concatenate(
-            [moving[z].astype(jnp.float32)[row : row + 1] for z in range(planes)], axis=0
-        )
-        out[...] = jnp.concatenate([own, names_at(fetch, row)], axis=0).astype(jnp.bfloat16)
-
-
-def send_weights_kernel(slabs, place, stiffness_in, tissue_in, *refs):
-    weights, (wide, stiffness, tissue, done) = refs[:slabs], refs[slabs:]
-    fetch_all([(stiffness_in, stiffness), (tissue_in, tissue)], done)
-    planes, rows, x_length = stiffness.shape
+def send_rows_kernel(slabs, place, *refs):
+    arguments, refs = refs[:5], refs[5:]
+    images, weights, edges = refs[:slabs], refs[slabs : 2 * slabs], refs[2 * slabs : 3 * slabs]
+    (first, last), refs = refs[3 * slabs : -8], refs[-8:]
+    wide, names, (moving, template, fetch, stiffness, tissue), done = refs[0], refs[1], refs[2:7], refs[7]
+    fetch_all(list(zip(arguments, (moving, template, fetch, stiffness, tissue))), done)
+    planes, rows, x_length = moving.shape
     share = rows // slabs
     blocks = x_length // BLOCK
+    names[...] = by_row(fetch, rows)
     marks = by_row(tissue, rows)
     for z in range(planes):
+        wide[z] = moving[z].astype(jnp.float32)
+        wide[planes + z] = template[z].astype(jnp.float32)
         marked = jnp.concatenate(
             [
                 jnp.broadcast_to(marks[:, z * blocks + b : z * blocks + b + 1], (rows, BLOCK))
@@ -261,59 +261,49 @@
             ],
             axis=1,
         )
-        wide[z] = marked * stiffness[z] * COEFFICIENT_UNIT + 0.5
+        wide[2 * planes + z] = marked * stiffness[z] * COEFFICIENT_UNIT + 0.5
+    def edge(row):
+        own = [wide[z, pl.ds(row, 1), :] for z in range(planes)]
+        return jnp.concatenate(own, axis=0), names_at(fetch, row)
+
+    for row, out in ((0, first), (rows - 1, last)):
+        out[...] = jnp.concatenate(edge(row), axis=0).astype(jnp.bfloat16)
+    for step in range(slabs):
+        to = around(place[0] + step, slabs)
+        over, over_names = edge(jnp.maximum(to * share - 1, 0))
+        under, under_names = edge(jnp.minimum((to + 1) * share, rows - 1))
+        edges[step][0:16] = jnp.concatenate([over, under], axis=0).astype(jnp.bfloat16)
+        edges[step][16:32] = jnp.concatenate([over_names, under_names], axis=0).astype(jnp.bfloat16)
     for step in range(slabs):
         part = pl.ds(pl.multiple_of(around(place[0] + step, slabs) * share, share), share)
+        for z in range(0, 2 * planes, 2):
+            both = jnp.concatenate([wide[z, part, :], wide[z + 1, part, :]], axis=0)
+            images[step][z * share : (z + 2) * share] = both.astype(jnp.bfloat16)
+        asked = jnp.concatenate([names[part, :]] * blocks, axis=1)
+        images[step][2 * planes * share : (2 * planes + 1) * share] = asked.astype(jnp.bfloat16)
         for z in range(0, planes, 2):
-            both = jnp.concatenate([wide[z, part, :], wide[z + 1, part, :]], axis=0)
+            both = jnp.concatenate([wide[2 * planes + z, part, :], wide[2 * planes + z + 1, part, :]], axis=0)
             weights[step][z * share : (z + 2) * share] = both.astype(jnp.int32).astype(jnp.int16)
 
 
-def send_images_kernel(slabs, place, moving_in, template_in, fetch_in, above, below, *refs):
-    images, (wide, names, moving, template, fetch, done) = refs[:slabs], refs[slabs:]
-    fetch_all([(moving_in, moving), (template_in, template), (fetch_in, fetch)], done)
-    planes, rows, x_length = moving.shape
-    share = rows // slabs
-    blocks = x_length // BLOCK
-    lane = lax.broadcasted_iota(jnp.int32, (planes, BLOCK), 1)
-    names[...] = by_row(fetch, rows)
+def send_edges_kernel(slabs, place, above, below, *refs):
+    edges, sends = refs[:slabs], refs[slabs:]
+    planes = above.shape[0] // 2
     over, under = above[...].astype(jnp.float32), below[...].astype(jnp.float32)
-    for z in range(planes):
-        wide[z, share : share + rows, :] = moving[z].astype(jnp.float32)
-        wide[z, share - 1 : share, :] = over[z : z + 1]
-        wide[z, share + rows : share + rows + 1, :] = under[z : z + 1]
-        wide[planes + z, 0:rows, :] = template[z].astype(jnp.float32)
-
-    def narrow(cells):
-        packed = jnp.zeros((planes, BLOCK), jnp.float32)
-        for b in range(blocks):
-            packed = jnp.where(lane == b, cells[:, b * BLOCK : (b + 1) * BLOCK], packed)
-        return packed
-
     for step in range(slabs):
         to = around(place[0] + step, slabs)
-        first = pl.multiple_of(to * share, share)
-        for z in range(0, planes, 2):
-            part = pl.ds(first + share, share)
-            both = jnp.concatenate([wide[z, part, :], wide[z + 1, part, :]], axis=0)
-            images[step][z * share : (z + 2) * share] = both.astype(jnp.bfloat16)
-            part = pl.ds(first, share)
-            both = jnp.concatenate([wide[planes + z, part, :], wide[planes + z + 1, part, :]], axis=0)
-            images[step][(planes + z) * share : (planes + z + 2) * share] = both.astype(jnp.bfloat16)
-        before = jnp.where(to == 0, over[planes:], names_at(fetch, first - 1))
-        after = jnp.where(to == slabs - 1, under[planes:], names_at(fetch, first + share))
-        asked = [names[pl.ds(first, share), :], narrow(before), narrow(after)]
-        asked = jnp.concatenate(asked + [asked[0]] * (blocks - 3), axis=1)
-        row_over = jnp.concatenate([wide[z, pl.ds(first + (share - 1), 1), :] for z in range(planes)], axis=0)
-        row_under = jnp.concatenate([wide[z, pl.ds(first + 2 * share, 1), :] for z in range(planes)], axis=0)
-        base = 2 * planes * share
-        images[step][base : base + 16] = jnp.concatenate([asked, row_over], axis=0).astype(jnp.bfloat16)
-        images[step][base + 16 : base + 24] = row_under.astype(jnp.bfloat16)
+        for half in range(2):
+            own = edges[step][2 * planes * half : 2 * planes * (half + 1)].astype(jnp.float32)
+            part = slice(planes * half, planes * (half + 1))
+            before = jnp.where(to == 0, over[part], own[:planes])
+            after = jnp.where(to == slabs - 1, under[part], own[planes:])
+            own = jnp.concatenate([before, after], axis=0)
+            sends[step][2 * planes * half : 2 * planes * (half + 1)] = own.astype(jnp.bfloat16)
 
 
 def pick_kernel(slabs, planes, place, *refs):
-    received, sends = refs[:slabs], refs[slabs : 2 * slabs]
-    image, residual, edges = refs[2 * slabs :]
+    received, sides, sends = refs[:slabs], refs[slabs : 2 * slabs], refs[2 * slabs : 3 * slabs]
+    image, residual, edges = refs[3 * slabs :]
     total, share, x_length = image.shape
     blocks = x_length // BLOCK
     base = 2 * planes * share
@@ -325,9 +315,10 @@
             [jnp.broadcast_to(cells[:, k : k + 1], (share, BLOCK)) for k in range(first, first + blocks)], axis=1
         )
 
-    asked = [r[base : base + 16].astype(jnp.float32) for r in received]
-    rows_of = [[a[8:16] for a in asked], [r[base + 16 : base + 24].astype(jnp.float32) for r in received]]
-    asked = [a[0:8] for a in asked]
+    asked = [r[base : base + 8].astype(jnp.float32) for r in received]
+    beside = [s[0:16].astype(jnp.float32) for s in sides]
+    rows_of = [[b[0:8] for b in beside], [b[8:16] for b in beside]]
+    beside = [s[16:32].astype(jnp.float32) for s in sides]
     for step in range(slabs):
         mine = around(me - step, slabs) * planes
         for start in range(0, planes, group):
@@ -347,7 +338,7 @@
                 z = mine + (start + k)
                 image[z] = found[k]
                 residual[z] = found[k] - both[k * share : (k + 1) * share]
-        wanted = [spread(asked[step], (1 + side) * BLOCK) for side in range(2)]
+        wanted = [beside[step][side * planes : (side + 1) * planes] for side in range(2)]
         found = [jnp.zeros((planes, x_length), jnp.float32) for _ in range(2)]
         for other in range(slabs):
             name = (around(me - other, slabs) * planes).astype(jnp.float32)
@@ -435,12 +426,22 @@
         out[d] = block.reshape(area, lanes).T[:lanes_used]
 
 
-def update_kernel(slabs, place, spectra, velocity, basis, *refs):
-    received, (out, warped, wide) = refs[:slabs], refs[slabs:]
+def update_kernel(slabs, place, velocity_in, spectra, basis, *refs):
+    received, (out, warped, wide, velocity, result, done) = refs[:slabs], refs[slabs:]
     devices, part, area = spectra.shape
     part //= 3
     _, planes, rows, x_length = velocity.shape
     share = rows // slabs
+    arriving = [pltpu.make_async_copy(velocity_in.at[a], velocity.at[a], done.at[a]) for a in range(3)]
+    leaving = [pltpu.make_async_copy(result.at[a], out.at[a], done.at[3 + a]) for a in range(3)]
+    for copy in arriving:
+        copy.start()
+    for a in range(3):
+        own = spectra[:, a * part : (a + 1) * part, :].reshape(x_length, area).T
+        smoothed = times(split(own), (basis[0], basis[1]), ((1,), (0,)))
+        arriving[a].wait()
+        result[a] = 0.5 * (velocity[a] - 32.0 * smoothed.reshape(planes, rows, x_length))
+        leaving[a].start()
     for step in range(slabs):
         place_of = pl.ds(pl.multiple_of(around(place[0] - step, slabs) * share, share), share)
         for z in range(0, planes, 2):
@@ -448,10 +449,8 @@
             wide[z, place_of, :] = both[:share]
             wide[z + 1, place_of, :] = both[share:]
     warped[...] = wide[...].astype(jnp.bfloat16)
-    for a in range(3):
-        own = spectra[:, a * part : (a + 1) * part, :].reshape(x_length, area).T
-        smoothed = times(split(own), (basis[0], basis[1]), ((1,), (0,)))
-        out[a] = 0.5 * (velocity[a] - 32.0 * smoothed.reshape(planes, rows, x_length))
+    for copy in leaving:
+        copy.wait()
 
 
 def local_rows(velocity, template, moving, stiffness, fetch_plane, tissue):
@@ -483,43 +482,46 @@
     fetch, marks = fetch_plane.swapaxes(1, 2), tissue.swapaxes(1, 2)
     brick, field = pltpu.VMEM(moving.shape, bf16), pltpu.VMEM(stiffness.shape, f32)
     small = pltpu.VMEM(fetch.shape, jnp.int32)
-    first, last = call(
-        edge_rows_kernel,
-        [shape((2 * planes, x_length), bf16)] * 2,
-        (moving,),
-        (fetch,),
-        scratch=[brick, small, pltpu.SemaphoreType.DMA((2,))],
-    )
-    above = lax.ppermute(last, "sub", [(i, (i + 1) % subs) for i in range(subs)])
-    below = lax.ppermute(first, "sub", [((i + 1) % subs, i) for i in range(subs)])
-    weights = call(
-        functools.partial(send_weights_kernel, slabs),
-        [shape((planes * share, x_length), jnp.int16)] * slabs,
-        slab_id,
-        (stiffness,),
-        (marks,),
-        scratch=[field, field, small, pltpu.SemaphoreType.DMA((2,))],
-    )
-    weights = scatter(weights)
-    images = call(
-        functools.partial(send_images_kernel, slabs),
-        [shape(((2 * planes + 3) * share, x_length), bf16)] * slabs,
+    sends = call(
+        functools.partial(send_rows_kernel, slabs),
+        [shape(((2 * planes + 1) * share, x_length), bf16)] * slabs
+        + [shape((planes * share, x_length), jnp.int16)] * slabs
+        + [shape((4 * planes, x_length), bf16)] * slabs
+        + [shape((2 * planes, x_length), bf16)] * 2,
         slab_id,
         (moving,),
         (template,),
         (fetch,),
-        above,
-        below,
+        (stiffness,),
+        (marks,),
         scratch=[
-            pltpu.VMEM((2 * planes, rows + 2 * share, x_length), f32),
+            pltpu.VMEM((3 * planes, rows, x_length), f32),
             pltpu.VMEM((rows, BLOCK), f32),
             brick,
             brick,
             small,
-            pltpu.SemaphoreType.DMA((3,)),
+            field,
+            small,
+            pltpu.SemaphoreType.DMA((5,)),
         ],
-    )
+        limit=WHOLE_VMEM_BYTES,
+    )
+    images, weights, edges = sends[:slabs], sends[slabs : 2 * slabs], sends[2 * slabs : 3 * slabs]
+    first, last = sends[3 * slabs :]
     images = scatter(images)
+    above = lax.ppermute(last, "sub", [(i, (i + 1) % subs) for i in range(subs)])
+    below = lax.ppermute(first, "sub", [((i + 1) % subs, i) for i in range(subs)])
+    edges = call(
+        functools.partial(send_edges_kernel, slabs),
+        [shape((4 * planes, x_length), bf16)] * slabs,
+        slab_id,
+        above,
+        below,
+        *edges,
+    )
+    edges = scatter(edges)
+    weights = scatter(weights)
+    images, edges, weights = lax.optimization_barrier((images, edges, weights))
     *sends, image, residual, edges = call(
         functools.partial(pick_kernel, slabs, planes),
         [shape((planes * share, x_length), bf16)] * slabs
@@ -527,9 +529,9 @@
         + [shape((2, total_z, x_length))],
         slab_id,
         *images,
+        *edges,
         flops=1 << 30,
     )
-    warped = scatter(sends)
     basis_z = in_two(np.kron(real_basis(total_z), np.eye(share)))
     spectra = call(
         functools.partial(force_kernel, slabs),
@@ -544,9 +546,9 @@
         scratch=[pltpu.VMEM((3, total_z, share, x_length), f32)],
         flops=3 << 30,
     )
-    spectra = spectra.astype(jnp.float16)
-    spectra, warped = lax.optimization_barrier((spectra, warped))
-    spectra = exchange(spectra)
+    spectra = exchange(spectra.astype(jnp.float16))
+    spectra, sends = lax.optimization_barrier((spectra, sends))
+    warped = scatter(sends)
     spectra = call(
         functools.partial(solve_kernel, subs),
         shape((devices, 3 * part, area)),
@@ -557,18 +559,21 @@
         scratch=[pltpu.VMEM((total_z, total_y, 128), f32)],
         flops=3 << 30,
     )
-    spectra = exchange(spectra.astype(jnp.float16))
+    spectra, warped = lax.optimization_barrier((spectra.astype(jnp.float16), warped))
+    spectra = exchange(spectra)
     return tuple(
         call(
             functools.partial(update_kernel, slabs),
             [shape(velocity.shape), shape(moving.shape, bf16)],
             slab_id,
+            (velocity,),
             spectra.astype(f32),
-            velocity,
             in_two(real_basis(x_length)),
             *warped,
-            scratch=[pltpu.VMEM((planes, rows, x_length), f32)],
+            scratch=[field, pltpu.VMEM(velocity.shape, f32), pltpu.VMEM(velocity.shape, f32)]
+            + [pltpu.SemaphoreType.DMA((6,))],
             flops=3 << 30,
+            stays=1,
         )
     )
 

time: 98.7 us -> 113 us (1.14)
  waiting for transfers between devices: 25.3 us -> 41.7 us
  Pallas kernels: 11.7 us -> 14.2 us
  local copies, waits for them, and re-layouts: 7.33 us -> 5.23 us
  blocking collectives: 25.7 us -> 23.9 us
    ppermute x9 -> x12, waiting for transfers between devices: 5.2 us -> 21.4 us  [scatter(): lax.ppermute(sends[d], 'slab', [(i, (i + d) % slabs) for i in range(slabs)])]
    pallas_call x7 -> x6, Pallas kernels: 11.7 us -> 14.2 us  [call(): pl.pallas_call(kernel, out_shape=out_shape, in_specs=places, out_specs=ja...]
    unnamed x24 -> x22, local copies, waits for them, and re-layouts: 7.33 us -> 5.23 us
    all_to_all x1, blocking collectives: 25.7 us -> 23.9 us  [exchange(): lax.all_to_all(values, both_axes, split_axis=0, concat_axis=0, tiled=True)]
    ppermute x9 -> x12, starting transfers between devices: 18.6 us -> 17.6 us  [scatter(): lax.ppermute(sends[d], 'slab', [(i, (i + d) % slabs) for i in range(slabs)])]
  transfers between devices with their start and end apart: 12 -> 15, of which waited for: 6 -> 6; matrix products, arithmetic and copies ran while one was open for 1% -> 0% of each run, Pallas kernels for 5% -> 3%
where the time goes in v4:
time: 113 us; the launch traced here: 112 us
  waiting for transfers between devices  41.7 us (37%)
  starting transfers between devices  25 us (22%)
  blocking collectives  23.9 us (21%)
  Pallas kernels  14.2 us (13%)
  local copies, waits for them, and re-layouts  5.23 us (5%)
  other arithmetic  1.44 us (1%)
    all_to_all x1, blocking collectives, exchange(): lax.all_to_all(values, both_axes, split_axis=0, concat_axis=0, tiled=True)  23.9 us
    ppermute x12, waiting for transfers between devices, scatter(): lax.ppermute(sends[d], 'slab', [(i, (i + d) % slabs) for i in range(slabs)])  21.4 us
    all_to_all x1, waiting for transfers between devices, exchange(): lax.all_to_all(values, both_axes, split_axis=0, concat_axis=0, tiled=True)  18.7 us
    ppermute x12, starting transfers between devices, scatter(): lax.ppermute(sends[d], 'slab', [(i, (i + d) % slabs) for i in range(slabs)])  17.6 us
    pallas_call x6, Pallas kernels, call(): pl.pallas_call(kernel, out_shape=out_shape, in_specs=places, out_specs=ja...  14.2 us
    unnamed x22, local copies, waits for them, and re-layouts  5.23 us
    all_to_all x1, starting transfers between devices, exchange(): lax.all_to_all(values, both_axes, split_axis=0, concat_axis=0, tiled=True)  4.89 us
  transfers between devices with their start and end apart: 15, of which 6 were waited for; matrix products, arithmetic and copies ran while one was open for 0% of the time, Pallas kernels for 3%

profile of v4, /device:TPU:0, one launch (start us, length us, event | category | flops | bytes accessed | tf_op | source)
XLA Modules:
  0.0 112.3 jit_solution(4997024407492504486)
XLA Ops:
  0.6 2.7 %shard_map.113 = (bf16[136,512]{1,0:T(8,128)(2,1)}, bf16[136,512]{1,0:T(8,128)(2,1)}, bf16[136,512]{1,0:T(8,128)(2,1)}, bf16[136,512]{1,0:T(8,128)(2,1)}, s16[64...) custom-call(s32[1]{0:T(128)} %bitcast.place, ...), custom_call_target="tpu_custom_call" | custom-call | bytes 2039812 | tf_op jit(solution)/shard_map/pallas_call | solution.py:206
  3.3 0.5 collective-permute-start.3
  3.8 2.0 %collective-permute-start.4 = (bf16[16,512]{1,0:T(8,128)(2,1)}, bf16[16,512]{1,0:T(8,128)(2,1)S(1)}, u32[]{:S(2)}, u32[]{:S(2)}) collective-permute-start(bf16[16,512]{1,0:T(8,128)(2,1)} %get-tuple-element.54), channel_id=1, source_target_pairs={{1,0},{2,1},{3,2},{0,3},{5,4},{6,5},{7,6},{4,7},{9,8},{10,9},{11,1... | collective-permute-start | bytes 49160 | tf_op jit(solution)/shard_map/ppermute | solution.py:513
  5.8 1.6 %collective-permute-done.3.above = bf16[16,512]{1,0:T(8,128)(2,1)S(1)} collective-permute-done((bf16[16,512]{1,0:T(8,128)(2,1)}, bf16[16,512]{1,0:T(8,128)(2,1)S(1)}, u32[]{:S(2)}, u32[]{:S(2)}) %collective-permute-start.3) | collective-permute-done | bytes 16416 | tf_op jit(solution)/shard_map/ppermute | solution.py:512
  7.4 0.1 collective-permute-done.4.below
  7.5 0.0 copy-start
  7.5 0.8 copy-done
  8.2 0.0 copy-start.1
  8.2 0.8 copy-done.1
  9.0 0.0 copy-start.2
  9.0 0.8 copy-done.2
  9.7 0.0 copy-start.3
  9.7 0.8 copy-done.3
  10.5 2.4 %collective-permute-start.5 = (bf16[32,512]{1,0:T(8,128)(2,1)S(1)}, bf16[32,512]{1,0:T(8,128)(2,1)S(1)}, u32[]{:S(2)}, u32[]{:S(2)}) collective-permute-start(bf16[32,512]{1,0:T(8,128)(2,1)S(1)} %get-tuple-element.60), channel_id=1, source_target_pairs={{0,4},{4,8},{8,12},{12,0},{1,5},{5,9},{9,13},{13,1},{2,6},{6,10},{... | collective-permute-start | bytes 98312 | tf_op jit(solution)/shard_map/ppermute | solution.py:475
  12.9 1.6 %collective-permute-start = (bf16[136,512]{1,0:T(8,128)(2,1)}, bf16[136,512]{1,0:T(8,128)(2,1)S(1)}, u32[]{:S(2)}, u32[]{:S(2)}) collective-permute-start(bf16[136,512]{1,0:T(8,128)(2,1)} %get-tuple-element.50), channel_id=1, source_target_pairs={{0,4},{4,8},{8,12},{12,0},{1,5},{5,9},{9,13},{13,1},{2,6},{6,10},{... | collective-permute-start | bytes 417800 | tf_op jit(solution)/shard_map/ppermute | solution.py:475
  14.5 1.1 collective-permute-start.1
  15.6 2.9 %collective-permute-start.2 = (bf16[136,512]{1,0:T(8,128)(2,1)}, bf16[136,512]{1,0:T(8,128)(2,1)S(1)}, u32[]{:S(2)}, u32[]{:S(2)}) collective-permute-start(bf16[136,512]{1,0:T(8,128)(2,1)} %get-tuple-element.52), channel_id=1, source_target_pairs={{0,12},{4,0},{8,4},{12,8},{1,13},{5,1},{9,5},{13,9},{2,14},{6,2},{... | collective-permute-start | bytes 417800 | tf_op jit(solution)/shard_map/ppermute | solution.py:475
  18.4 0.3 collective-permute-start.6
  18.8 0.0 collective-permute-done.5.refs_5_
  18.8 0.7 collective-permute-start.8
  19.4 13.8 %collective-permute-done.6.refs_6_ = bf16[32,512]{1,0:T(8,128)(2,1)S(1)} collective-permute-done((bf16[32,512]{1,0:T(8,128)(2,1)S(1)}, bf16[32,512]{1,0:T(8,128)(2,1)S(1)}, u32[]{:S(2)}, u32[]{:S(2)}) %collective-permute-start.6) | collective-permute-done | bytes 32800 | tf_op jit(solution)/shard_map/ppermute | solution.py:475
  33.3 0.0 collective-permute-start.7
  33.3 3.9 %collective-permute-done.7.refs_7_ = bf16[32,512]{1,0:T(8,128)(2,1)S(1)} collective-permute-done((bf16[32,512]{1,0:T(8,128)(2,1)S(1)}, bf16[32,512]{1,0:T(8,128)(2,1)S(1)}, u32[]{:S(2)}, u32[]{:S(2)}) %collective-permute-start.7) | collective-permute-done | bytes 32800 | tf_op jit(solution)/shard_map/ppermute | solution.py:475
  37.2 0.0 collective-permute-start.9
  37.2 0.0 collective-permute-done.8.refs_1_
  37.2 2.1 %collective-permute-start.10 = (s16[64,512]{1,0:T(8,128)(2,1)}, s16[64,512]{1,0:T(8,128)(2,1)S(1)}, u32[]{:S(2)}, u32[]{:S(2)}) collective-permute-start(s16[64,512]{1,0:T(8,128)(2,1)} %get-tuple-element.66), channel_id=1, source_target_pairs={{0,12},{4,0},{8,4},{12,8},{1,13},{5,1},{9,5},{13,9},{2,14},{6,2},{... | collective-permute-start | bytes 196616 | tf_op jit(solution)/shard_map/ppermute | solution.py:475
  39.3 3.6 %collective-permute-done.9.refs_2_ = s16[64,512]{1,0:T(8,128)(2,1)S(1)} collective-permute-done((s16[64,512]{1,0:T(8,128)(2,1)}, s16[64,512]{1,0:T(8,128)(2,1)S(1)}, u32[]{:S(2)}, u32[]{:S(2)}) %collective-permute-start.9) | collective-permute-done | bytes 65568 | tf_op jit(solution)/shard_map/ppermute | solution.py:475
  42.9 0.0 collective-permute-done.10.refs_3_
  42.9 0.0 collective-permute-done.refs_1_
  42.9 0.0 collective-permute-done.1.refs_2_
  42.9 0.0 collective-permute-done.2.refs_3_
  42.9 0.0 copy-start.5
  42.9 0.9 copy-done.5
  43.8 0.0 copy-start.6
  43.8 0.0 copy-start.8
  43.8 0.0 copy-start.9
  43.8 1.7 %shard_map.115 = (bf16[64,512]{1,0:T(8,128)(2,1)S(1)}, bf16[64,512]{1,0:T(8,128)(2,1)S(1)}, bf16[64,512]{1,0:T(8,128)(2,1)S(1)}, bf16[64,512]{1,0:T(8,128)(2,1)S...) custom-call(s32[1]{0:T(128)} %bitcast.place, ...), custom_call_target="tpu_custom_call" | custom-call | flops 1073741824 | bytes 2129924 | tf_op jit(solution)/shard_map/pallas_call | solution.py:206
  45.5 0.0 copy-done.6
  45.6 0.0 copy-done.8
  45.6 0.0 copy-done.9
  45.6 2.7 %shard_map.116 = f32[16,96,256]{2,1,0:T(8,128)S(1)} custom-call(s32[1]{0:T(128)} %bitcast.place, s16[64,512]{1,0:T(8,128)(2,1)S(1)} %copy-done.6, s16[64,512]{1,0:T(8,128)(2,1)S(1)} %collective-permute-done.8.refs_1_, s16[64,512]{1,0:T(8,128)(2,1)S(1)} %collective-permute-done.9.refs_2_, s16[64,512]{1,0:T(8,128)(2,1)S(1)} %collective-permute-done.10.refs_3_, ...), custom_call_target="tpu_custom_call" | custom-call | flops 3221225472 | bytes 4325380 | tf_op jit(solution)/shard_map/pallas_call | solution.py:206
  48.3 1.0 convert_element_type.12
  49.3 4.9 %all-to-all-start = ((f16[16,96,256]{2,1,0:T(8,128)(2,1)}), f16[16,96,256]{2,1,0:T(8,128)(2,1)S(1)}, u32[]{:S(2)}, u32[]{:S(2)}) async-start(f16[16,96,256]{2,1,0:T(8,128)(2,1)} %convert_element_type.12), calls=%async_computation | async-start | bytes 1572864 | tf_op jit(solution)/shard_map/all_to_all | solution.py:480
  54.2 0.0 copy-start.10
  54.2 18.7 %all-to-all-done = f16[16,96,256]{2,1,0:T(8,128)(2,1)S(1)} async-done(((f16[16,96,256]{2,1,0:T(8,128)(2,1)}), f16[16,96,256]{2,1,0:T(8,128)(2,1)S(1)}, u32[]{:S(2)}, u32[]{:S(2)}) %all-to-all-start) | async-done | bytes 786464 | tf_op jit(solution)/shard_map/all_to_all | solution.py:480
  72.9 2.2 %collective-permute-start.11 = (bf16[64,512]{1,0:T(8,128)(2,1)S(1)}, bf16[64,512]{1,0:T(8,128)(2,1)S(1)}, u32[]{:S(2)}, u32[]{:S(2)}) collective-permute-start(bf16[64,512]{1,0:T(8,128)(2,1)S(1)} %get-tuple-element.88), channel_id=1, source_target_pairs={{0,4},{4,8},{8,12},{12,0},{1,5},{5,9},{9,13},{13,1},{2,6},{6,10},{... | collective-permute-start | bytes 196616 | tf_op jit(solution)/shard_map/ppermute | solution.py:475
  75.1 1.5 %collective-permute-start.12 = (bf16[64,512]{1,0:T(8,128)(2,1)S(1)}, bf16[64,512]{1,0:T(8,128)(2,1)S(1)}, u32[]{:S(2)}, u32[]{:S(2)}) collective-permute-start(bf16[64,512]{1,0:T(8,128)(2,1)S(1)} %get-tuple-element.89), channel_id=1, source_target_pairs={{0,8},{4,12},{8,0},{12,4},{1,9},{5,13},{9,1},{13,5},{2,10},{6,14},... | collective-permute-start | bytes 196616 | tf_op jit(solution)/shard_map/ppermute | solution.py:475
  76.6 2.9 %collective-permute-start.13 = (bf16[64,512]{1,0:T(8,128)(2,1)S(1)}, bf16[64,512]{1,0:T(8,128)(2,1)S(1)}, u32[]{:S(2)}, u32[]{:S(2)}) collective-permute-start(bf16[64,512]{1,0:T(8,128)(2,1)S(1)} %get-tuple-element.90), channel_id=1, source_target_pairs={{0,12},{4,0},{8,4},{12,8},{1,13},{5,1},{9,5},{13,9},{2,14},{6,2},{... | collective-permute-start | bytes 196616 | tf_op jit(solution)/shard_map/ppermute | solution.py:475
  79.5 0.1 convert_element_type.13.spectra
  79.7 0.0 copy-done.10
  79.7 3.4 %shard_map.117 = f32[16,96,256]{2,1,0:T(8,128)S(1)} custom-call(s32[1]{0:T(128)} %bitcast.1.place, f32[16,96,256]{2,1,0:T(8,128)S(1)} %convert_element_type.13.spectra, bf16[2,256,256]{2,1,0:T(8,128)(2,1)S(1)} %copy-done.9, bf16[2,128,128]{2,1,0:T(8,128)(2,1)S(1)} %copy-done.10), custom_call_target="tpu_custom_call" | custom-call | flops 3221225472 | bytes 3473412 | tf_op jit(solution)/shard_map/pallas_call | solution.py:206
  83.0 0.2 convert_element_type.14
  83.2 0.0 collective-permute-done.11.refs_1_
  83.2 0.0 collective-permute-done.12.refs_2_
  83.2 0.0 collective-permute-done.13.refs_3_
  83.2 0.0 copy-start.7
  83.2 23.9 %all_to_all.10 = f16[16,96,256]{2,1,0:T(8,128)(2,1)S(1)} all-to-all(f16[16,96,256]{2,1,0:T(8,128)(2,1)S(1)} %convert_element_type.14), channel_id=1, replica_groups=mesh['groups'=2,'slab'=4,'sub'=4] {'slab','sub'}, dimensions={0} | all-to-all | bytes 1572864 | tf_op jit(solution)/shard_map/all_to_all | solution.py:480
  107.2 0.0 copy-start.4
  107.2 0.1 convert_element_type.15.spectra
  107.3 0.0 copy-done.7
  107.3 1.3 %copy-done.4 = f32[3,8,32,512]{3,2,1,0:T(8,128)S(1)} copy-done((f32[3,8,32,512]{3,2,1,0:T(8,128)S(1)}, f32[3,8,32,512]{3,2,1,0:T(8,128)}, u32[]{:S(2)}) %copy-start.4) | copy-done | bytes 1572888
  108.6 3.8 %shard_map.118 = (f32[3,8,32,512]{3,2,1,0:T(8,128)}, bf16[8,32,512]{2,1,0:T(8,128)(2,1)}) custom-call(s32[1]{0:T(128)} %bitcast.place, f32[3,8,32,512]{3,2,1,0:T(8,128)S(1)} %copy-done.4, f32[16,96,256]{2,1,0:T(8,128)S(1)} %convert_element_type.15.spectra, bf16[2,512,512]{2,1,0:T(8,128)(2,1)S(1)} %copy-done.7, ...), custom_call_target="tpu_custom_call" | custom-call | flops 3221225472 | bytes 6291460 | tf_op jit(solution)/shard_map/pallas_call | solution.py:206
  (1 shorter events, 0.0 us)
Async XLA Ops:
  3.3 4.1 %collective-permute-start.3 = (bf16[16,512]{1,0:T(8,128)(2,1)}, bf16[16,512]{1,0:T(8,128)(2,1)S(1)}, u32[]{:S(2)}, u32[]{:S(2)}) collective-permute-start(bf16[16,512]{1,0:T(8,128)(2,1)} %get-tuple-element.53), channel_id=1, source_target_pairs={{0,1},{1,2},{2,3},{3,0},{4,5},{5,6},{6,7},{7,4},{8,9},{9,10},{10,1... | collective-permute-start | bytes 49160 | tf_op jit(solution)/shard_map/ppermute | solution.py:512
  3.8 3.6 %collective-permute-start.4 = (bf16[16,512]{1,0:T(8,128)(2,1)}, bf16[16,512]{1,0:T(8,128)(2,1)S(1)}, u32[]{:S(2)}, u32[]{:S(2)}) collective-permute-start(bf16[16,512]{1,0:T(8,128)(2,1)} %get-tuple-element.54), channel_id=1, source_target_pairs={{1,0},{2,1},{3,2},{0,3},{5,4},{6,5},{7,6},{4,7},{9,8},{10,9},{11,1... | collective-permute-start | bytes 49160 | tf_op jit(solution)/shard_map/ppermute | solution.py:513
  7.5 0.8 copy-start
  8.2 0.8 copy-start.1
  9.0 0.8 copy-start.2
  9.7 0.8 copy-start.3
  10.5 8.2 %collective-permute-start.5 = (bf16[32,512]{1,0:T(8,128)(2,1)S(1)}, bf16[32,512]{1,0:T(8,128)(2,1)S(1)}, u32[]{:S(2)}, u32[]{:S(2)}) collective-permute-start(bf16[32,512]{1,0:T(8,128)(2,1)S(1)} %get-tuple-element.60), channel_id=1, source_target_pairs={{0,4},{4,8},{8,12},{12,0},{1,5},{5,9},{9,13},{13,1},{2,6},{6,10},{... | collective-permute-start | bytes 98312 | tf_op jit(solution)/shard_map/ppermute | solution.py:475
  12.9 30.0 %collective-permute-start = (bf16[136,512]{1,0:T(8,128)(2,1)}, bf16[136,512]{1,0:T(8,128)(2,1)S(1)}, u32[]{:S(2)}, u32[]{:S(2)}) collective-permute-start(bf16[136,512]{1,0:T(8,128)(2,1)} %get-tuple-element.50), channel_id=1, source_target_pairs={{0,4},{4,8},{8,12},{12,0},{1,5},{5,9},{9,13},{13,1},{2,6},{6,10},{... | collective-permute-start | bytes 417800 | tf_op jit(solution)/shard_map/ppermute | solution.py:475
  14.5 28.4 %collective-permute-start.1 = (bf16[136,512]{1,0:T(8,128)(2,1)}, bf16[136,512]{1,0:T(8,128)(2,1)S(1)}, u32[]{:S(2)}, u32[]{:S(2)}) collective-permute-start(bf16[136,512]{1,0:T(8,128)(2,1)} %get-tuple-element.51), channel_id=1, source_target_pairs={{0,8},{4,12},{8,0},{12,4},{1,9},{5,13},{9,1},{13,5},{2,10},{6,14},... | collective-permute-start | bytes 417800 | tf_op jit(solution)/shard_map/ppermute | solution.py:475
  15.6 27.3 %collective-permute-start.2 = (bf16[136,512]{1,0:T(8,128)(2,1)}, bf16[136,512]{1,0:T(8,128)(2,1)S(1)}, u32[]{:S(2)}, u32[]{:S(2)}) collective-permute-start(bf16[136,512]{1,0:T(8,128)(2,1)} %get-tuple-element.52), channel_id=1, source_target_pairs={{0,12},{4,0},{8,4},{12,8},{1,13},{5,1},{9,5},{13,9},{2,14},{6,2},{... | collective-permute-start | bytes 417800 | tf_op jit(solution)/shard_map/ppermute | solution.py:475
  18.4 14.8 %collective-permute-start.6 = (bf16[32,512]{1,0:T(8,128)(2,1)S(1)}, bf16[32,512]{1,0:T(8,128)(2,1)S(1)}, u32[]{:S(2)}, u32[]{:S(2)}) collective-permute-start(bf16[32,512]{1,0:T(8,128)(2,1)S(1)} %get-tuple-element.61), channel_id=1, source_target_pairs={{0,8},{4,12},{8,0},{12,4},{1,9},{5,13},{9,1},{13,5},{2,10},{6,14},... | collective-permute-start | bytes 98312 | tf_op jit(solution)/shard_map/ppermute | solution.py:475
  18.8 18.4 %collective-permute-start.8 = (s16[64,512]{1,0:T(8,128)(2,1)}, s16[64,512]{1,0:T(8,128)(2,1)S(1)}, u32[]{:S(2)}, u32[]{:S(2)}) collective-permute-start(s16[64,512]{1,0:T(8,128)(2,1)} %get-tuple-element.64), channel_id=1, source_target_pairs={{0,4},{4,8},{8,12},{12,0},{1,5},{5,9},{9,13},{13,1},{2,6},{6,10},{... | collective-permute-start | bytes 196616 | tf_op jit(solution)/shard_map/ppermute | solution.py:475
  33.3 3.9 %collective-permute-start.7 = (bf16[32,512]{1,0:T(8,128)(2,1)S(1)}, bf16[32,512]{1,0:T(8,128)(2,1)S(1)}, u32[]{:S(2)}, u32[]{:S(2)}) collective-permute-start(bf16[32,512]{1,0:T(8,128)(2,1)S(1)} %get-tuple-element.62), channel_id=1, source_target_pairs={{0,12},{4,0},{8,4},{12,8},{1,13},{5,1},{9,5},{13,9},{2,14},{6,2},{... | collective-permute-start | bytes 98312 | tf_op jit(solution)/shard_map/ppermute | solution.py:475
  37.2 5.7 %collective-permute-start.9 = (s16[64,512]{1,0:T(8,128)(2,1)}, s16[64,512]{1,0:T(8,128)(2,1)S(1)}, u32[]{:S(2)}, u32[]{:S(2)}) collective-permute-start(s16[64,512]{1,0:T(8,128)(2,1)} %get-tuple-element.65), channel_id=1, source_target_pairs={{0,8},{4,12},{8,0},{12,4},{1,9},{5,13},{9,1},{13,5},{2,10},{6,14},... | collective-permute-start | bytes 196616 | tf_op jit(solution)/shard_map/ppermute | solution.py:475
  37.2 5.7 %collective-permute-start.10 = (s16[64,512]{1,0:T(8,128)(2,1)}, s16[64,512]{1,0:T(8,128)(2,1)S(1)}, u32[]{:S(2)}, u32[]{:S(2)}) collective-permute-start(s16[64,512]{1,0:T(8,128)(2,1)} %get-tuple-element.66), channel_id=1, source_target_pairs={{0,12},{4,0},{8,4},{12,8},{1,13},{5,1},{9,5},{13,9},{2,14},{6,2},{... | collective-permute-start | bytes 196616 | tf_op jit(solution)/shard_map/ppermute | solution.py:475
  42.9 0.9 copy-start.5
  43.8 1.8 %copy-start.6 = (s16[64,512]{1,0:T(8,128)(2,1)S(1)}, s16[64,512]{1,0:T(8,128)(2,1)}, u32[]{:S(2)}) copy-start(s16[64,512]{1,0:T(8,128)(2,1)} %get-tuple-element.67.refs_0_) | copy-start | bytes 196612
  43.8 1.8 %copy-start.8 = (bf16[2,512,512]{2,1,0:T(8,128)(2,1)S(1)}, bf16[2,512,512]{2,1,0:T(8,128)(2,1)}, u32[]{:S(2)}) copy-start(bf16[2,512,512]{2,1,0:T(8,128)(2,1)} %constant.17.clone.refs_7_) | copy-start | bytes 3145732
  43.8 1.8 %copy-start.9 = (bf16[2,256,256]{2,1,0:T(8,128)(2,1)S(1)}, bf16[2,256,256]{2,1,0:T(8,128)(2,1)}, u32[]{:S(2)}) copy-start(bf16[2,256,256]{2,1,0:T(8,128)(2,1)} %constant.18.clone.refs_8_.basis_z) | copy-start | bytes 786436
  49.3 23.6 %all-to-all-start = ((f16[16,96,256]{2,1,0:T(8,128)(2,1)}), f16[16,96,256]{2,1,0:T(8,128)(2,1)S(1)}, u32[]{:S(2)}, u32[]{:S(2)}) async-start(f16[16,96,256]{2,1,0:T(8,128)(2,1)} %convert_element_type.12), calls=%async_computation | async-start | bytes 1572864 | tf_op jit(solution)/shard_map/all_to_all | solution.py:480
  54.2 25.4 %copy-start.10 = (bf16[2,128,128]{2,1,0:T(8,128)(2,1)S(1)}, bf16[2,128,128]{2,1,0:T(8,128)(2,1)}, u32[]{:S(2)}) copy-start(bf16[2,128,128]{2,1,0:T(8,128)(2,1)} %constant.19.clone.basis_y) | copy-start | bytes 196612
  72.9 10.3 %collective-permute-start.11 = (bf16[64,512]{1,0:T(8,128)(2,1)S(1)}, bf16[64,512]{1,0:T(8,128)(2,1)S(1)}, u32[]{:S(2)}, u32[]{:S(2)}) collective-permute-start(bf16[64,512]{1,0:T(8,128)(2,1)S(1)} %get-tuple-element.88), channel_id=1, source_target_pairs={{0,4},{4,8},{8,12},{12,0},{1,5},{5,9},{9,13},{13,1},{2,6},{6,10},{... | collective-permute-start | bytes 196616 | tf_op jit(solution)/shard_map/ppermute | solution.py:475
  75.1 8.1 %collective-permute-start.12 = (bf16[64,512]{1,0:T(8,128)(2,1)S(1)}, bf16[64,512]{1,0:T(8,128)(2,1)S(1)}, u32[]{:S(2)}, u32[]{:S(2)}) collective-permute-start(bf16[64,512]{1,0:T(8,128)(2,1)S(1)} %get-tuple-element.89), channel_id=1, source_target_pairs={{0,8},{4,12},{8,0},{12,4},{1,9},{5,13},{9,1},{13,5},{2,10},{6,14},... | collective-permute-start | bytes 196616 | tf_op jit(solution)/shard_map/ppermute | solution.py:475
  76.6 6.6 %collective-permute-start.13 = (bf16[64,512]{1,0:T(8,128)(2,1)S(1)}, bf16[64,512]{1,0:T(8,128)(2,1)S(1)}, u32[]{:S(2)}, u32[]{:S(2)}) collective-permute-start(bf16[64,512]{1,0:T(8,128)(2,1)S(1)} %get-tuple-element.90), channel_id=1, source_target_pairs={{0,12},{4,0},{8,4},{12,8},{1,13},{5,1},{9,5},{13,9},{2,14},{6,2},{... | collective-permute-start | bytes 196616 | tf_op jit(solution)/shard_map/ppermute | solution.py:475
  83.2 24.1 %copy-start.7 = (bf16[2,512,512]{2,1,0:T(8,128)(2,1)S(1)}, bf16[2,512,512]{2,1,0:T(8,128)(2,1)}, u32[]{:S(2)}) copy-start(bf16[2,512,512]{2,1,0:T(8,128)(2,1)} %constant.20.clone.basis) | copy-start | bytes 3145732
  107.2 1.4 %copy-start.4 = (f32[3,8,32,512]{3,2,1,0:T(8,128)S(1)}, f32[3,8,32,512]{3,2,1,0:T(8,128)}, u32[]{:S(2)}) copy-start(f32[3,8,32,512]{3,2,1,0:T(8,128)} %velocity_in.1) | copy-start | bytes 4718596

commit v5 on v1

--- a/solution.py
+++ b/solution.py
@@ -148,7 +148,7 @@
     return (new_velocity, warped)
 
 
-VMEM_BYTES = 50 * 1024 * 1024
+VMEM_BYTES = 24 * 1024 * 1024
 
 
 def real_basis(length):
@@ -190,34 +190,44 @@
     return lax.rem(value + 2 * count, count)
 
 
-def call(kernel, out_shape, arguments, scratch=(), flops=0, nbytes=0):
-    smem = pl.BlockSpec(memory_space=pltpu.SMEM)
-    vmem = pl.BlockSpec(memory_space=pltpu.VMEM)
+def call(kernel, out_shape, *arguments, scratch=(), flops=0, stays=0):
+    places = [
+        pl.BlockSpec(memory_space=pltpu.HBM if isinstance(a, tuple) else pltpu.SMEM if a.ndim == 1 else pltpu.VMEM)
+        for a in arguments
+    ]
+    arguments = [a[0] if isinstance(a, tuple) else a for a in arguments]
+    out_places = [
+        pl.BlockSpec(memory_space=pltpu.HBM if k < stays else pltpu.VMEM)
+        for k in range(len(jax.tree.leaves(out_shape)))
+    ]
+    nbytes = sum(a.size * a.dtype.itemsize for a in arguments + jax.tree.leaves(out_shape))
     return pl.pallas_call(
         kernel,
         out_shape=out_shape,
-        in_specs=[smem] + [vmem] * (len(arguments) - 1),
-        out_specs=jax.tree.map(lambda _: vmem, out_shape),
+        in_specs=places,
+        out_specs=jax.tree.unflatten(jax.tree.structure(out_shape), out_places),
         scratch_shapes=list(scratch),
         compiler_params=pltpu.CompilerParams(vmem_limit_bytes=VMEM_BYTES),
         cost_estimate=pl.CostEstimate(flops=flops, bytes_accessed=nbytes, transcendentals=0),
     )(*arguments)
 
 
+def by_row(ref, rows):
+    cells = jnp.concatenate([ref[z].astype(jnp.float32) for z in range(ref.shape[0])], axis=0)
+    cells = jnp.concatenate([cells, jnp.zeros((cells.shape[0], BLOCK - rows), jnp.float32)], axis=1)
+    cells = jnp.concatenate([cells, jnp.zeros((BLOCK - cells.shape[0], BLOCK), jnp.float32)], axis=0)
+    return cells.T[:rows]
+
+
 def send_columns_kernel(slabs, place, moving, fetch, *sends):
     planes, rows, _ = moving.shape
-    me = place[0]
-    lane = lax.broadcasted_iota(jnp.int32, (rows, BLOCK), 1)
-    narrow = lax.broadcasted_iota(jnp.int32, (rows, fetch.shape[2]), 1)
     for step, send in enumerate(sends):
-        to = around(me + step, slabs)
-        columns = pl.ds(pl.multiple_of(to * BLOCK, BLOCK), BLOCK)
-        send[0:planes] = moving[:, :, columns]
-        wanted = jnp.zeros((rows, BLOCK), jnp.float32)
-        for z in range(planes):
-            one = jnp.sum(jnp.where(narrow == to, fetch[z].astype(jnp.float32), 0.0), axis=1, keepdims=True)
-            wanted = jnp.where(lane == z, one, wanted)
-        send[planes] = wanted.astype(jnp.bfloat16)
+        to = around(place[0] + step, slabs)
+        send[0:planes] = moving[:, :, pl.ds(pl.multiple_of(to * BLOCK, BLOCK), BLOCK)]
+        wanted = jnp.concatenate([fetch[z, pl.ds(to, 1), :] for z in range(planes)], axis=0).astype(jnp.float32)
+        wanted = jnp.concatenate([wanted, jnp.zeros((planes, BLOCK - rows), jnp.float32)], axis=1)
+        wanted = jnp.concatenate([wanted, jnp.zeros((BLOCK - planes, BLOCK), jnp.float32)], axis=0)
+        send[planes] = wanted.T[:rows].astype(jnp.bfloat16)
 
 
 def pick_kernel(slabs, place, *refs):
@@ -250,83 +260,176 @@
             send[k] = picked[around(first + (k - 1), total)]
 
 
-def force_kernel(slabs, place, *refs):
-    received = refs[:slabs]
-    above, below, template, stiffness, tissue, basis, warped, spectra, image, edges = refs[slabs:]
+def edge_rows_kernel(slabs, *refs):
+    received, (first, last) = refs[1 : 1 + slabs], refs[1 + slabs :]
+    planes, rows, _ = received[0].shape
+    for d in range(slabs):
+        cells = [received[d][z].astype(jnp.float32) for z in range(1, planes - 1)]
+        first[d] = jnp.concatenate([c[0:1] for c in cells], axis=0).astype(jnp.bfloat16)
+        last[d] = jnp.concatenate([c[rows - 1 : rows] for c in cells], axis=0).astype(jnp.bfloat16)
+
+
+def force_z_kernel(slabs, subs, place, *refs):
+    received, refs = refs[:slabs], refs[slabs:]
+    template, stiffness, tissue, basis, warped, image, weight, spectra, planes_of, wide = refs
     planes, rows, x_length = template.shape
-    me = place[0]
+    blocks = x_length // BLOCK
     for step in range(slabs):
-        block = pl.ds(pl.multiple_of(around(me - step, slabs) * BLOCK, BLOCK), BLOCK)
-        image[:, :, block] = received[step][...].astype(jnp.float32)
+        block = pl.ds(pl.multiple_of(around(place[0] - step, slabs) * BLOCK, BLOCK), BLOCK)
+        planes_of[:, :, block] = received[step][...].astype(jnp.float32)
         warped[:, :, block] = received[step][1:-1]
+    marks = by_row(tissue, rows)
+    force = []
+    for z in range(planes):
+        here = planes_of[z + 1]
+        marked = jnp.concatenate(
+            [
+                jnp.broadcast_to(marks[:, z * blocks + b : z * blocks + b + 1], (rows, BLOCK))
+                for b in range(blocks)
+            ],
+            axis=1,
+        )
+        own = 0.5 * (marked * stiffness[z] * (here - template[z].astype(jnp.float32)))
+        image[z] = here
+        weight[z] = own
+        force.append(own * (planes_of[z + 2] - planes_of[z]))
+    force = split(jnp.concatenate(force, axis=0))
+    wide[...] = times((basis[0], basis[1]), force, ((1,), (1,)))
+    part = x_length // (slabs * subs)
+    for d in range(slabs):
+        for e in range(subs):
+            first = (around(place[0] + d, slabs) * subs + around(place[1] + e, subs)) * part
+            spectra[d, e] = wide[pl.ds(pl.multiple_of(first, part), part), :]
+
+
+def force_xy_kernel(slabs, place, above, below, image, weight, basis, spectra, edges):
+    planes, rows, x_length = image.shape
+    for step in range(slabs):
+        block = pl.ds(pl.multiple_of(around(place[0] - step, slabs) * BLOCK, BLOCK), BLOCK)
         edges[0, :, block] = above[step].astype(jnp.float32)
         edges[1, :, block] = below[step].astype(jnp.float32)
     row = lax.broadcasted_iota(jnp.int32, (rows, x_length), 0)
-    forces = [[], [], []]
+    forces = [[], []]
     for z in range(planes):
-        here = image[z + 1]
-        marked = tissue[z].astype(jnp.float32)
-        marked = jnp.concatenate(
-            [jnp.broadcast_to(marked[:, b : b + 1], (rows, BLOCK)) for b in range(x_length // BLOCK)], axis=1
-        )
-        weight = 0.5 * (marked * stiffness[z] * (here - template[z].astype(jnp.float32)))
+        here, own = image[z], weight[z]
         before = jnp.where(row == 0, edges[0, z : z + 1, :], pltpu.roll(here, 1, 0))
         after = jnp.where(row == rows - 1, edges[1, z : z + 1, :], pltpu.roll(here, rows - 1, 0))
-        forces[0].append(weight * (image[z + 2] - image[z]))
-        forces[1].append(weight * (after - before))
-        forces[2].append(weight * (pltpu.roll(here, x_length - 1, 1) - pltpu.roll(here, 1, 1)))
+        forces[0].append(own * (after - before))
+        forces[1].append(own * (pltpu.roll(here, x_length - 1, 1) - pltpu.roll(here, 1, 1)))
     devices, part = spectra.shape[:2]
-    part //= 3
-    for a in range(3):
+    part //= 2
+    for a in range(2):
         force = split(jnp.concatenate(forces[a], axis=0))
         spectrum = times((basis[0], basis[1]), force, ((1,), (1,)))
         spectra[:, a * part : (a + 1) * part, :] = spectrum.reshape(devices, part, planes * rows)
 
 
-def solve_kernel(subs, place, spectra, basis_z, basis_y, out, cells):
-    devices, lanes_used, area = spectra.shape
-    total_z, total_y, lanes = cells.shape
+def solve(first, x_length, part, subs, spectra, basis_z, basis_y, cells):
+    devices, used, area = spectra.shape
+    total_z, _, total_y = cells.shape
     slabs = devices // subs
     planes, rows = total_z // slabs, total_y // subs
-    pad = jnp.zeros((lanes - lanes_used, area), jnp.float32)
-    for d in range(devices):
-        block = jnp.concatenate([spectra[d], pad], axis=0).T.reshape(planes, rows, lanes)
-        s, q = d // subs, d % subs
-        cells[s * planes : (s + 1) * planes, q * rows : (q + 1) * rows, :] = block
-    tables_z, tables_y = (basis_z[0], basis_z[1]), (basis_y[0], basis_y[1])
-    part = lanes_used // 3
-    lane = lax.broadcasted_iota(jnp.int32, (1, lanes), 1)
-    x_sq = wave_sq(place[0] * part + lax.rem(lane, part), part * devices)
-    y_sq = wave_sq(lax.broadcasted_iota(jnp.int32, (total_y, 1), 0), total_y)
-    xy = (x_sq + y_sq) * 256.0 + 1.0
-    tile = basis_z.shape[1] // total_z
-    for g in range(total_y // tile):
-        own = cells[:, g * tile : (g + 1) * tile, :].reshape(total_z * tile, lanes)
-        own = times(tables_z, split(own), ((1,), (0,)))
-        cells[:, g * tile : (g + 1) * tile, :] = own.reshape(total_z, tile, lanes)
-    for z in range(total_z):
-        wave = 2.0 * np.pi / total_z * (z if z <= total_z // 2 else z - total_z // 2)
-        own = times(tables_y, split(cells[z]), ((1,), (0,)))
-        own = own / (xy + 256.0 * wave * wave)
-        cells[z] = times(tables_y, split(own), ((0,), (0,)))
-    for g in range(total_y // tile):
-        own = cells[:, g * tile : (g + 1) * tile, :].reshape(total_z * tile, lanes)
-        own = times(tables_z, split(own), ((0,), (0,)))
-        cells[:, g * tile : (g + 1) * tile, :] = own.reshape(total_z, tile, lanes)
-    for d in range(devices):
-        s, q = d // subs, d % subs
-        block = cells[s * planes : (s + 1) * planes, q * rows : (q + 1) * rows, :]
-        out[d] = block.reshape(area, lanes).T[:lanes_used]
-
-
-def update_kernel(place, spectra, velocity, basis, out):
+    tile = 8
+
+    def along_y(k):
+        high, low = basis_y[2 * k], basis_y[2 * k + 1]
+        both = jnp.concatenate([high, high], axis=0)
+
+        def run(values):
+            parts = split(values)
+            sums = jnp.dot(jnp.concatenate(parts, axis=1), both, preferred_element_type=jnp.float32)
+            return sums + jnp.dot(parts[0], low, preferred_element_type=jnp.float32)
+
+        return run
+
+    run = along_y(0)
+    for s in range(slabs):
+        own = []
+        for z in range(planes):
+            lanes = slice(z * rows, (z + 1) * rows)
+            own.append(jnp.concatenate([spectra[s * subs + q][:, lanes] for q in range(subs)], axis=1))
+        own = run(jnp.concatenate(own, axis=0))
+        cells[s * planes : (s + 1) * planes] = own.reshape(planes, used, total_y)
+    index = lax.broadcasted_iota(jnp.int32, (total_z * tile, 1), 0)
+    z_sq = wave_sq(index // tile, total_z)
+    y_sq = wave_sq(lax.broadcasted_iota(jnp.int32, (1, total_y), 1), total_y)
+    table = (basis_z[0], basis_z[1])
+    for g in range(0, used, 2 * tile):
+        own, scale = [], []
+        for start in (g, g + tile):
+            own.append(cells[:, start : start + tile, :].reshape(total_z * tile, total_y))
+            x_sq = wave_sq(first + start % part + lax.rem(index, tile), x_length)
+            scale.append((z_sq + x_sq + y_sq) * 256.0 + 1.0)
+        own = times(table, split(jnp.concatenate(own, axis=1)), ((1,), (0,)))
+        own = own / jnp.concatenate(scale, axis=1)
+        own = times(table, split(own), ((0,), (0,)))
+        for k, start in enumerate((g, g + tile)):
+            half = own[:, k * total_y : (k + 1) * total_y]
+            cells[:, start : start + tile, :] = half.reshape(total_z, tile, total_y)
+    run = along_y(1)
+    for s in range(slabs):
+        own = run(cells[s * planes : (s + 1) * planes].reshape(planes * used, total_y))
+        for q in range(subs):
+            lanes = slice(q * rows, (q + 1) * rows)
+            spectra[s * subs + q] = jnp.concatenate(
+                [own[z * used : (z + 1) * used, lanes] for z in range(planes)], axis=1
+            )
+
+
+def solve_xy_kernel(subs, x_length, place, spectra, basis_z, basis_y, out, cells):
+    devices = out.shape[0]
+    part = x_length // devices
+    out[...] = spectra[...]
+    solve((place[0] * subs + place[1]) * part, x_length, part, subs, out, basis_z, basis_y, cells)
+
+
+def solve_z_kernel(slabs, subs, x_length, place, *refs):
+    received, refs = refs[:subs], refs[subs:]
+    basis_z, basis_y, sends, (spectra, cells) = refs[0], refs[1], refs[2 : 2 + slabs], refs[2 + slabs :]
+    part = x_length // (slabs * subs)
+    for e in range(subs):
+        for d in range(slabs):
+            spectra[around(place[0] - d, slabs) * subs + around(place[1] - e, subs)] = received[e][d]
+    solve((place[0] * subs + place[1]) * part, x_length, part, subs, spectra, basis_z, basis_y, cells)
+    for d in range(slabs):
+        for e in range(subs):
+            sends[d][e] = spectra[around(place[0] + d, slabs) * subs + around(place[1] + e, subs)]
+
+
+def moved(spectra, velocity, basis):
+    smoothed = times(split(spectra.T), (basis[0], basis[1]), ((1,), (0,)))
+    return 0.5 * (velocity - 32.0 * smoothed.reshape(velocity.shape))
+
+
+def update_z_kernel(slabs, subs, place, basis, velocity_in, *refs):
+    received, (out, gathered, velocity, done) = refs[:subs], refs[subs:]
+    part = received[0].shape[1]
+    arriving = pltpu.make_async_copy(velocity_in.at[0], velocity, done.at[0])
+    arriving.start()
+    for e in range(subs):
+        for d in range(slabs):
+            first = (around(place[0] - d, slabs) * subs + around(place[1] - e, subs)) * part
+            gathered[pl.ds(pl.multiple_of(first, part), part), :] = received[e][d]
+    arriving.wait()
+    out[...] = moved(gathered[...], velocity[...], basis)
+
+
+def update_kernel(place, velocity_in, spectra, basis, updated, out, velocity, result, done):
     devices, part, area = spectra.shape
-    part //= 3
-    _, planes, rows, x_length = velocity.shape
-    for a in range(3):
-        own = spectra[:, a * part : (a + 1) * part, :].reshape(x_length, area).T
-        smoothed = times(split(own), (basis[0], basis[1]), ((1,), (0,)))
-        out[a] = 0.5 * (velocity[a] - 32.0 * smoothed.reshape(planes, rows, x_length))
+    part //= 2
+    arriving = [pltpu.make_async_copy(velocity_in.at[a], velocity.at[a - 1], done.at[a]) for a in (1, 2)]
+    leaving = [pltpu.make_async_copy(result.at[a - 1], out.at[a], done.at[2 + a]) for a in (1, 2)]
+    leaving.append(pltpu.make_async_copy(updated, out.at[0], done.at[0]))
+    leaving[2].start()
+    for copy in arriving:
+        copy.start()
+    for a in range(2):
+        own = spectra[:, a * part : (a + 1) * part, :].reshape(devices * part, area)
+        arriving[a].wait()
+        result[a] = moved(own, velocity[a], basis)
+        leaving[a].start()
+    for copy in leaving:
+        copy.wait()
 
 
 def local_blocks(velocity, template, moving, stiffness, fetch_plane, tissue):
@@ -336,61 +439,136 @@
     devices = slabs * subs
     part = x_length // devices
     area = planes * rows
-    my_slab = lax.axis_index("slab")
-    my_place = my_slab * subs + lax.axis_index("sub")
-    slab_id, place_id = my_slab.reshape(1), my_place.reshape(1)
-    bf16, f32 = jnp.bfloat16, jnp.float32
+    place = jnp.stack([lax.axis_index("slab"), lax.axis_index("sub")])
+    bf16, f16, f32 = jnp.bfloat16, jnp.float16, jnp.float32
 
     def shape(dims, kind=f32):
         return jax.ShapeDtypeStruct(dims, kind)
 
-    def scatter(sends):
+    def scatter(sends, axis):
+        count = lax.axis_size(axis)
         return [sends[0]] + [
-            lax.ppermute(sends[d], "slab", [(i, (i + d) % slabs) for i in range(slabs)])
-            for d in range(1, slabs)
+            lax.ppermute(sends[d], axis, [(i, (i + d) % count) for i in range(count)]) for d in range(1, count)
         ]
 
+    def exchange(values):
+        return lax.all_to_all(values, ("slab", "sub"), split_axis=0, concat_axis=0, tiled=True)
+
+    fetch, marks = fetch_plane.swapaxes(1, 2), tissue.swapaxes(1, 2)
     sends = call(
         functools.partial(send_columns_kernel, slabs),
         [shape((planes + 1, rows, BLOCK), bf16)] * slabs,
-        (slab_id, moving, fetch_plane),
-    )
-    received = scatter(sends)
+        place,
+        moving,
+        fetch,
+    )
     sends = call(
         functools.partial(pick_kernel, slabs),
         [shape((planes + 2, rows, BLOCK), bf16)] * slabs,
-        (slab_id, *received),
-        [pltpu.VMEM((total_z, rows, BLOCK), bf16)],
-    )
-    received = scatter(sends)
-    last = jnp.stack([r[1:-1, rows - 1] for r in received])
-    first = jnp.stack([r[1:-1, 0] for r in received])
+        place,
+        *scatter(sends, "slab"),
+        scratch=[pltpu.VMEM((total_z, rows, BLOCK), bf16)],
+        flops=1 << 30,
+    )
+    received = scatter(sends, "slab")
+    first, last = call(
+        functools.partial(edge_rows_kernel, slabs),
+        [shape((slabs, planes, BLOCK), bf16)] * 2,
+        place,
+        *received,
+    )
     above = lax.ppermute(last, "sub", [(i, (i + 1) % subs) for i in range(subs)])
     below = lax.ppermute(first, "sub", [((i + 1) % subs, i) for i in range(subs)])
+    basis_x = in_two(8.0 * real_basis(x_length))
+    basis_z = in_two(np.kron(real_basis(total_z), np.eye(8)))
+    basis_y = np.concatenate([in_two(real_basis(total_y).T), in_two(real_basis(total_y))])
+    warped, image, weight, spectra_z = call(
+        functools.partial(force_z_kernel, slabs, subs),
+        [
+            shape(moving.shape, bf16),
+            shape(moving.shape),
+            shape(moving.shape),
+            shape((slabs, subs, part, area)),
+        ],
+        place,
+        *received,
+        template,
+        stiffness,
+        marks,
+        basis_x,
+        scratch=[pltpu.VMEM((planes + 2, rows, x_length), f32), pltpu.VMEM((x_length, area), f32)],
+        flops=2 << 30,
+    )
+    spectra_z = spectra_z.astype(f16)
+    spectra_z = scatter([spectra_z[d] for d in range(slabs)], "slab")
+    spectra_z = scatter([jnp.stack([r[e] for r in spectra_z]) for e in range(subs)], "sub")
+    spectra_xy = call(
+        functools.partial(force_xy_kernel, slabs),
+        shape((devices, 2 * part, area)),
+        place,
+        above,
+        below,
+        image,
+        weight,
+        basis_x,
+        scratch=[pltpu.VMEM((2, planes, x_length), f32)],
+        flops=3 << 30,
+    )
+    spectra_xy = exchange(spectra_xy.astype(f16))
+    spectra_z = call(
+        functools.partial(solve_z_kernel, slabs, subs, x_length),
+        [shape((subs, part, area))] * slabs,
+        place,
+        *[r.astype(f32) for r in spectra_z],
+        basis_z,
+        basis_y,
+        scratch=[pltpu.VMEM((devices, part, area), f32), pltpu.VMEM((total_z, part, total_y), f32)],
+        flops=2 << 30,
+    )
+    _, spectra_xy = lax.optimization_barrier((spectra_z, spectra_xy))
+    spectra_z = scatter([r.astype(f16) for r in spectra_z], "slab")
+    spectra_z = scatter([jnp.stack([r[e] for r in spectra_z]) for e in range(subs)], "sub")
+    spectra_xy = call(
+        functools.partial(solve_xy_kernel, subs, x_length),
+        shape((devices, 2 * part, area)),
+        place,
+        spectra_xy.astype(f32),
+        basis_z,
+        basis_y,
+        scratch=[pltpu.VMEM((total_z, 2 * part, total_y), f32)],
+        flops=3 << 30,
+    )
+    spectra_xy = exchange(spectra_xy.astype(f16))
     basis_x = in_two(real_basis(x_length))
-    tile = 8
-    basis_z = in_two(np.kron(real_basis(total_z), np.eye(tile)))
-    basis_y = in_two(real_basis(total_y))
-    warped, spectra = call(
-        functools.partial(force_kernel, slabs),
-        [shape((planes, rows, x_length), bf16), shape((devices, 3 * part, area))],
-        (slab_id, *received, above, below, template, stiffness, tissue, in_two(8.0 * real_basis(x_length))),
-        [pltpu.VMEM((planes + 2, rows, x_length), f32), pltpu.VMEM((2, planes, x_length), f32)],
-    )
-    spectra = spectra.astype(jnp.float16)
-    spectra = lax.all_to_all(spectra, ("slab", "sub"), split_axis=0, concat_axis=0, tiled=True)
-    spectra = call(
-        functools.partial(solve_kernel, subs),
-        shape((devices, 3 * part, area)),
-        (place_id, spectra.astype(f32), basis_z, basis_y),
-        [pltpu.VMEM((total_z, total_y, 128), f32)],
-    )
-    spectra = spectra.astype(jnp.float16)
-    spectra = lax.all_to_all(spectra, ("slab", "sub"), split_axis=0, concat_axis=0, tiled=True)
+    updated = call(
+        functools.partial(update_z_kernel, slabs, subs),
+        shape(moving.shape),
+        place,
+        basis_x,
+        (velocity,),
+        *[r.astype(f32) for r in spectra_z],
+        scratch=[
+            pltpu.VMEM((x_length, area), f32),
+            pltpu.VMEM(moving.shape, f32),
+            pltpu.SemaphoreType.DMA((1,)),
+        ],
+        flops=1 << 30,
+    )
     new_velocity = call(
         update_kernel,
         shape(velocity.shape),
-        (place_id, spectra.astype(f32), velocity, basis_x),
+        place,
+        (velocity,),
+        spectra_xy.astype(f32),
+        basis_x,
+        updated,
+        scratch=[
+            pltpu.VMEM((2,) + moving.shape, f32),
+            pltpu.VMEM((2,) + moving.shape, f32),
+            pltpu.SemaphoreType.DMA((5,)),
+        ],
+        flops=2 << 30,
+        stays=1,
     )
     return (new_velocity, warped)
 
@@ -398,15 +576,13 @@
 def local(velocity, template, moving, stiffness, fetch_plane, tissue):
     planes, rows, x_length = moving.shape
     slabs, subs = lax.axis_size("slab"), lax.axis_size("sub")
-    part = x_length // (slabs * subs)
     fits = (
         x_length == slabs * BLOCK
         and planes == 8
+        and planes * slabs * 8 == 256
         and rows % 16 == 0
-        and part % 16 == 0
-        and 3 * part <= 128
-        and planes * slabs * 8 == 256
-        and rows * subs == 128
+        and rows * subs == BLOCK
+        and x_length % (16 * slabs * subs) == 0
     )
     run = local_blocks if fits else local_general
     return run(velocity, template, moving, stiffness, fetch_plane, tissue)

time: 97.1 us -> 90.2 us (0.929)
  blocking collectives: 25.5 us -> 0 us
  starting transfers between devices: 16.6 us -> 41 us
  waiting for transfers between devices: 34.1 us -> 24.4 us
  Pallas kernels: 13.7 us -> 18 us
  local copies, waits for them, and re-layouts: 4.14 us -> 1.86 us
  other arithmetic: 1.46 us -> 3.42 us
    all_to_all x1 -> x0, blocking collectives: 25.5 us -> none  [local_blocks(): lax.all_to_all(spectra, ('slab', 'sub'), split_axis=0, concat_axis=0, til...]
    ppermute x6 -> x18, starting transfers between devices: 10.9 us -> 27.1 us  [scatter(): lax.ppermute(sends[d], axis, [(i, (i + d) % count) for i in range(count)])]
    all_to_all x1 -> x2, waiting for transfers between devices: 18.7 us -> 4.69 us  [exchange(): lax.all_to_all(values, ('slab', 'sub'), split_axis=0, concat_axis=0, tile...]
    all_to_all x1 -> x2, starting transfers between devices: 3.89 us -> 12.2 us  [exchange(): lax.all_to_all(values, ('slab', 'sub'), split_axis=0, concat_axis=0, tile...]
    ppermute x6 -> x18, waiting for transfers between devices: 15 us -> 19.7 us  [scatter(): lax.ppermute(sends[d], axis, [(i, (i + d) % count) for i in range(count)])]
    pallas_call x5 -> x9, Pallas kernels: 13.7 us -> 18 us  [call(): pl.pallas_call(kernel, out_shape=out_shape, in_specs=places, out_specs=ja...]
    unnamed x16 -> x20, local copies, waits for them, and re-layouts: 3.89 us -> 1.7 us
    convert_element_type x4 -> x17, other arithmetic: 1.45 us -> 3.19 us  [the longest x2 1.8 us: local_blocks(): spectra_xy = exchange(spectra_xy.astype(f16))]
  transfers between devices with their start and end apart: 9 -> 22, of which waited for: 8 -> 11; matrix products, arithmetic and copies ran while one was open for 1% -> 3% of each run, Pallas kernels for 0% -> 14%
where the time goes in v5:
time: 90.2 us; the launch traced here: 89.7 us
  starting transfers between devices  41 us (45%)
  waiting for transfers between devices  24.4 us (27%)
  Pallas kernels  18 us (20%)
  other arithmetic  3.42 us (4%)
  local copies, waits for them, and re-layouts  1.86 us (2%)
  between operations  1.02 us (1%)
    ppermute x18, starting transfers between devices, scatter(): lax.ppermute(sends[d], axis, [(i, (i + d) % count) for i in range(count)])  27.1 us
    ppermute x18, waiting for transfers between devices, scatter(): lax.ppermute(sends[d], axis, [(i, (i + d) % count) for i in range(count)])  19.7 us
    pallas_call x9, Pallas kernels, call(): pl.pallas_call(kernel, out_shape=out_shape, in_specs=places, out_specs=ja...  18 us
    all_to_all x2, starting transfers between devices, exchange(): lax.all_to_all(values, ('slab', 'sub'), split_axis=0, concat_axis=0, tile...  12.2 us
    all_to_all x2, waiting for transfers between devices, exchange(): lax.all_to_all(values, ('slab', 'sub'), split_axis=0, concat_axis=0, tile...  4.69 us
  transfers between devices with their start and end apart: 22, of which 11 were waited for; matrix products, arithmetic and copies ran while one was open for 3% of the time, Pallas kernels for 14%

profile of v5, /device:TPU:0, one launch (start us, length us, event | category | flops | bytes accessed | tf_op | source)
XLA Modules:
  0.0 89.7 jit_solution(16829715277916880658)
XLA Ops:
  0.6 0.1 pad_add_fusion.place.refs_0_
  0.7 0.9 %copy-done = bf16[8,32,512]{2,1,0:T(8,128)(2,1)S(1)} copy-done((bf16[8,32,512]{2,1,0:T(8,128)(2,1)S(1)}, bf16[8,32,512]{2,1,0:T(8,128)(2,1)}, u32[]{:S(2)}) %copy-start) | copy-done | bytes 262168
  1.7 0.7 copy-done.1
  2.4 0.7 shard_map.113
  3.1 3.0 %collective-permute-start = (bf16[9,32,128]{2,1,0:T(8,128)(2,1)S(1)}, bf16[9,32,128]{2,1,0:T(8,128)(2,1)S(1)}, u32[]{:S(2)}, u32[]{:S(2)}) collective-permute-start(bf16[9,32,128]{2,1,0:T(8,128)(2,1)S(1)} %get-tuple-element.22), channel_id=1, source_target_pairs={{0,4},{4,8},{8,12},{12,0},{1,5},{5,9},{9,13},{13,1},{2,6},{6,10},{... | collective-permute-start | bytes 221192 | tf_op jit(solution)/shard_map/ppermute | solution.py:451
  6.1 2.6 %collective-permute-start.1 = (bf16[9,32,128]{2,1,0:T(8,128)(2,1)S(1)}, bf16[9,32,128]{2,1,0:T(8,128)(2,1)S(1)}, u32[]{:S(2)}, u32[]{:S(2)}) collective-permute-start(bf16[9,32,128]{2,1,0:T(8,128)(2,1)S(1)} %get-tuple-element.23), channel_id=1, source_target_pairs={{0,8},{4,12},{8,0},{12,4},{1,9},{5,13},{9,1},{13,5},{2,10},{6,14},... | collective-permute-start | bytes 221192 | tf_op jit(solution)/shard_map/ppermute | solution.py:451
  8.7 1.3 %collective-permute-start.2 = (bf16[9,32,128]{2,1,0:T(8,128)(2,1)S(1)}, bf16[9,32,128]{2,1,0:T(8,128)(2,1)S(1)}, u32[]{:S(2)}, u32[]{:S(2)}) collective-permute-start(bf16[9,32,128]{2,1,0:T(8,128)(2,1)S(1)} %get-tuple-element.24), channel_id=1, source_target_pairs={{0,12},{4,0},{8,4},{12,8},{1,13},{5,1},{9,5},{13,9},{2,14},{6,2},{... | collective-permute-start | bytes 221192 | tf_op jit(solution)/shard_map/ppermute | solution.py:451
  10.0 0.8 collective-permute-done.refs_1_
  10.9 2.8 %collective-permute-done.1.refs_2_ = bf16[9,32,128]{2,1,0:T(8,128)(2,1)S(1)} collective-permute-done((bf16[9,32,128]{2,1,0:T(8,128)(2,1)S(1)}, bf16[9,32,128]{2,1,0:T(8,128)(2,1)S(1)}, u32[]{:S(2)}, u32[]{:S(2)}) %collective-permute-start.1) | collective-permute-done | bytes 73760 | tf_op jit(solution)/shard_map/ppermute | solution.py:451
  13.7 0.2 collective-permute-done.2.refs_3_
  13.9 1.8 %shard_map.114 = (bf16[10,32,128]{2,1,0:T(8,128)(2,1)S(1)}, bf16[10,32,128]{2,1,0:T(8,128)(2,1)S(1)}, bf16[10,32,128]{2,1,0:T(8,128)(2,1)S(1)}, bf16[10,32,128]{2,1,0:T(8,128)(2,1)S(1)}) custom-call(s32[2]{0:T(128)S(1)} %pad_add_fusion.place.refs_0_, bf16[9,32,128]{2,1,0:T(8,128)(2,1)S(1)} %get-tuple-element.21.refs_0_, ...), custom_call_target="tpu_custom_call" | custom-call | flops 1073741824 | bytes 622600 | tf_op jit(solution)/shard_map/pallas_call | solution.py:204
  15.7 1.9 %collective-permute-start.3 = (bf16[10,32,128]{2,1,0:T(8,128)(2,1)S(1)}, bf16[10,32,128]{2,1,0:T(8,128)(2,1)S(1)}, u32[]{:S(2)}, u32[]{:S(2)}) collective-permute-start(bf16[10,32,128]{2,1,0:T(8,128)(2,1)S(1)} %get-tuple-element.26), channel_id=1, source_target_pairs={{0,4},{4,8},{8,12},{12,0},{1,5},{5,9},{9,13},{13,1},{2,6},{6,10},{... | collective-permute-start | bytes 245768 | tf_op jit(solution)/shard_map/ppermute | solution.py:451
  17.6 1.9 %collective-permute-start.4 = (bf16[10,32,128]{2,1,0:T(8,128)(2,1)S(1)}, bf16[10,32,128]{2,1,0:T(8,128)(2,1)S(1)}, u32[]{:S(2)}, u32[]{:S(2)}) collective-permute-start(bf16[10,32,128]{2,1,0:T(8,128)(2,1)S(1)} %get-tuple-element.27), channel_id=1, source_target_pairs={{0,8},{4,12},{8,0},{12,4},{1,9},{5,13},{9,1},{13,5},{2,10},{6,14},... | collective-permute-start | bytes 245768 | tf_op jit(solution)/shard_map/ppermute | solution.py:451
  19.5 0.7 collective-permute-start.5
  20.2 2.7 %collective-permute-done.3.refs_1_.refs_2_ = bf16[10,32,128]{2,1,0:T(8,128)(2,1)S(1)} collective-permute-done((bf16[10,32,128]{2,1,0:T(8,128)(2,1)S(1)}, bf16[10,32,128]{2,1,0:T(8,128)(2,1)S(1)}, u32[]{:S(2)}, u32[]{:S(2)}) %collective-permute-start.3) | collective-permute-done | bytes 81952 | tf_op jit(solution)/shard_map/ppermute | solution.py:451
  22.9 2.3 %collective-permute-done.4.refs_2_.refs_3_ = bf16[10,32,128]{2,1,0:T(8,128)(2,1)S(1)} collective-permute-done((bf16[10,32,128]{2,1,0:T(8,128)(2,1)S(1)}, bf16[10,32,128]{2,1,0:T(8,128)(2,1)S(1)}, u32[]{:S(2)}, u32[]{:S(2)}) %collective-permute-start.4) | collective-permute-done | bytes 81952 | tf_op jit(solution)/shard_map/ppermute | solution.py:451
  25.2 0.0 collective-permute-done.5.refs_3_.refs_4_
  25.2 0.6 shard_map.117
  25.8 0.1 collective-permute-start.12
  25.9 1.7 %collective-permute-start.13 = (bf16[4,8,128]{2,1,0:T(8,128)(2,1)S(1)}, bf16[4,8,128]{2,1,0:T(8,128)(2,1)S(1)}, u32[]{:S(2)}, u32[]{:S(2)}) collective-permute-start(bf16[4,8,128]{2,1,0:T(8,128)(2,1)S(1)} %get-tuple-element.35), channel_id=1, source_target_pairs={{1,0},{2,1},{3,2},{0,3},{5,4},{6,5},{7,6},{4,7},{9,8},{10,9},{11,1... | collective-permute-start | bytes 24584 | tf_op jit(solution)/shard_map/ppermute | solution.py:481
  27.6 0.0 copy-done.4
  27.6 0.0 copy-done.7
  27.6 2.2 %shard_map.115 = (bf16[8,32,512]{2,1,0:T(8,128)(2,1)}, f32[8,32,512]{2,1,0:T(8,128)S(1)}, f32[8,32,512]{2,1,0:T(8,128)S(1)}, f32[4,4,32,256]{3,2,1,0:T(8,128)S(1)}) custom-call(s32[2]{0:T(128)S(1)} %pad_add_fusion.place.refs_0_, bf16[10,32,128]{2,1,0:T(8,128)(2,1)S(1)} %get-tuple-element.25.refs_0_.refs_1_, ...), custom_call_target="tpu_custom_call" | custom-call | flops 2147483648 | bytes 4001800 | tf_op jit(solution)/shard_map/pallas_call | solution.py:204
  30.0 2.3 %collective-permute-start.6 = (f16[4,32,256]{2,1,0:T(8,128)(2,1)S(1)}, f16[4,32,256]{2,1,0:T(8,128)(2,1)S(1)}, u32[]{:S(2)}, u32[]{:S(2)}) collective-permute-start(f16[4,32,256]{2,1,0:T(8,128)(2,1)S(1)} %get-tuple-element.44), channel_id=1, source_target_pairs={{0,4},{4,8},{8,12},{12,0},{1,5},{5,9},{9,13},{13,1},{2,6},{6,10},{... | collective-permute-start | bytes 196616 | tf_op jit(solution)/shard_map/ppermute | solution.py:451
  32.2 1.6 %collective-permute-start.8 = (f16[4,32,256]{2,1,0:T(8,128)(2,1)S(1)}, f16[4,32,256]{2,1,0:T(8,128)(2,1)S(1)}, u32[]{:S(2)}, u32[]{:S(2)}) collective-permute-start(f16[4,32,256]{2,1,0:T(8,128)(2,1)S(1)} %get-tuple-element.45), channel_id=1, source_target_pairs={{0,12},{4,0},{8,4},{12,8},{1,13},{5,1},{9,5},{13,9},{2,14},{6,2},{... | collective-permute-start | bytes 196616 | tf_op jit(solution)/shard_map/ppermute | solution.py:451
  33.8 0.0 collective-permute-start.7
  33.8 0.0 collective-permute-done.12.above
  33.9 0.0 collective-permute-done.13.below
  33.9 1.8 %shard_map.118 = f32[16,64,256]{2,1,0:T(8,128)S(1)} custom-call(s32[2]{0:T(128)S(1)} %pad_add_fusion.place.refs_0_, bf16[4,8,128]{2,1,0:T(8,128)(2,1)S(1)} %collective-permute-done.12.above, bf16[4,8,128]{2,1,0:T(8,128)(2,1)S(1)} %collective-permute-done.13.below, f32[8,32,512]{2,1,0:T(8,128)S(1)} %get-tuple-element.36.image, ...), custom_call_target="tpu_custom_call" | custom-call | flops 3221225472 | bytes 3162120 | tf_op jit(solution)/shard_map/pallas_call | solution.py:204
  35.7 0.9 %convert_element_type.56 = f16[16,64,256]{2,1,0:T(8,128)(2,1)} convert(f32[16,64,256]{2,1,0:T(8,128)S(1)} %shard_map.118) | non-fusion elementwise | flops 262144 | bytes 1572864 | tf_op jit(solution)/shard_map/convert_element_type | solution.py:517
  36.6 5.3 %all-to-all-start = ((f16[16,64,256]{2,1,0:T(8,128)(2,1)}), f16[16,64,256]{2,1,0:T(8,128)(2,1)S(1)}, u32[]{:S(2)}, u32[]{:S(2)}) async-start(f16[16,64,256]{2,1,0:T(8,128)(2,1)} %convert_element_type.56), calls=%async_computation | async-start | bytes 1048576 | tf_op jit(solution)/shard_map/all_to_all | solution.py:455
  41.9 0.0 collective-permute-done.6
  41.9 0.0 collective-permute-done.8
  42.0 0.0 collective-permute-done.7
  42.0 0.5 collective-permute-start.9
  42.5 1.7 %collective-permute-start.10 = (f16[4,32,256]{2,1,0:T(8,128)(2,1)S(1)}, f16[4,32,256]{2,1,0:T(8,128)(2,1)S(1)}, u32[]{:S(2)}, u32[]{:S(2)}) collective-permute-start(f16[4,32,256]{2,1,0:T(8,128)(2,1)S(1)} %pad_maximum_fusion.1), channel_id=1, source_target_pairs={{0,2},{1,3},{2,0},{3,1},{4,6},{5,7},{6,4},{7,5},{8,10},{9,11},{10,... | collective-permute-start | bytes 196616 | tf_op jit(solution)/shard_map/ppermute | solution.py:451
  44.3 1.4 %collective-permute-start.11 = (f16[4,32,256]{2,1,0:T(8,128)(2,1)S(1)}, f16[4,32,256]{2,1,0:T(8,128)(2,1)S(1)}, u32[]{:S(2)}, u32[]{:S(2)}) collective-permute-start(f16[4,32,256]{2,1,0:T(8,128)(2,1)S(1)} %pad_maximum_fusion.2), channel_id=1, source_target_pairs={{0,3},{1,0},{2,1},{3,2},{4,7},{5,4},{6,5},{7,6},{8,11},{9,8},{10,9... | collective-permute-start | bytes 196616 | tf_op jit(solution)/shard_map/ppermute | solution.py:451
  45.7 3.2 %collective-permute-done.9 = f16[4,32,256]{2,1,0:T(8,128)(2,1)S(1)} collective-permute-done((f16[4,32,256]{2,1,0:T(8,128)(2,1)S(1)}, f16[4,32,256]{2,1,0:T(8,128)(2,1)S(1)}, u32[]{:S(2)}, u32[]{:S(2)}) %collective-permute-start.9) | collective-permute-done | bytes 65568 | tf_op jit(solution)/shard_map/ppermute | solution.py:451
  48.9 1.5 %collective-permute-done.10 = f16[4,32,256]{2,1,0:T(8,128)(2,1)S(1)} collective-permute-done((f16[4,32,256]{2,1,0:T(8,128)(2,1)S(1)}, f16[4,32,256]{2,1,0:T(8,128)(2,1)S(1)}, u32[]{:S(2)}, u32[]{:S(2)}) %collective-permute-start.10) | collective-permute-done | bytes 65568 | tf_op jit(solution)/shard_map/ppermute | solution.py:451
  50.4 0.0 collective-permute-done.11
  50.5 0.0 copy-done.8
  50.5 2.8 %shard_map.116 = (f32[4,32,256]{2,1,0:T(8,128)S(1)}, f32[4,32,256]{2,1,0:T(8,128)S(1)}, f32[4,32,256]{2,1,0:T(8,128)S(1)}, f32[4,32,256]{2,1,0:T(8,128)S(1)}) custom-call(s32[2]{0:T(128)S(1)} %pad_add_fusion.place.refs_0_, f32[4,32,256]{2,1,0:T(8,128)S(1)} %maximum_convert_fusion.refs_0_, f32[4,32,256]{2,1,0:T(8,128)S(1)} %convert_element_type.53.refs_1_, ...), custom_call_target="tpu_custom_call" | custom-call | flops 2147483648 | bytes 1441800 | tf_op jit(solution)/shard_map/pallas_call | solution.py:204
  53.3 4.0 %collective-permute-start.16 = (f16[4,32,256]{2,1,0:T(8,128)(2,1)S(1)}, f16[4,32,256]{2,1,0:T(8,128)(2,1)S(1)}, u32[]{:S(2)}, u32[]{:S(2)}) collective-permute-start(f16[4,32,256]{2,1,0:T(8,128)(2,1)S(1)} %convert_element_type.63), channel_id=1, source_target_pairs={{0,12},{4,0},{8,4},{12,8},{1,13},{5,1},{9,5},{13,9},{2,14},{6,2},{... | collective-permute-start | bytes 196616 | tf_op jit(solution)/shard_map/ppermute | solution.py:451
  57.3 0.1 collective-permute-start.15
  57.4 0.6 collective-permute-start.14
  58.0 1.4 %collective-permute-done.16 = f16[4,32,256]{2,1,0:T(8,128)(2,1)S(1)} collective-permute-done((f16[4,32,256]{2,1,0:T(8,128)(2,1)S(1)}, f16[4,32,256]{2,1,0:T(8,128)(2,1)S(1)}, u32[]{:S(2)}, u32[]{:S(2)}) %collective-permute-start.16) | collective-permute-done | bytes 65568 | tf_op jit(solution)/shard_map/ppermute | solution.py:451
  59.4 0.0 all-to-all-done
  59.4 0.1 convert_element_type.57.spectra
  59.5 4.0 %shard_map.119 = f32[16,64,256]{2,1,0:T(8,128)S(1)} custom-call(s32[2]{0:T(128)S(1)} %pad_add_fusion.place.refs_0_, f32[16,64,256]{2,1,0:T(8,128)S(1)} %convert_element_type.57.spectra, bf16[2,256,256]{2,1,0:T(8,128)(2,1)S(1)} %copy-done.8, bf16[4,128,128]{2,1,0:T(8,128)(2,1)S(1)} %copy-done.9), custom_call_target="tpu_custom_call" | custom-call | flops 3221225472 | bytes 2490376 | tf_op jit(solution)/shard_map/pallas_call | solution.py:204
  63.5 0.0 copy-start.6
  63.5 0.9 %convert_element_type.58 = f16[16,64,256]{2,1,0:T(8,128)(2,1)} convert(f32[16,64,256]{2,1,0:T(8,128)S(1)} %shard_map.119) | non-fusion elementwise | flops 262144 | bytes 1572864 | tf_op jit(solution)/shard_map/convert_element_type | solution.py:541
  64.4 6.9 %all-to-all-start.1 = ((f16[16,64,256]{2,1,0:T(8,128)(2,1)}), f16[16,64,256]{2,1,0:T(8,128)(2,1)}, u32[]{:S(2)}, u32[]{:S(2)}) async-start(f16[16,64,256]{2,1,0:T(8,128)(2,1)} %convert_element_type.58), calls=%async_computation.1 | async-start | bytes 1048576 | tf_op jit(solution)/shard_map/all_to_all | solution.py:455
  71.3 0.0 collective-permute-done.15
  71.3 0.0 collective-permute-done.14
  71.4 0.4 collective-permute-start.17
  71.8 1.7 %collective-permute-start.18 = (f16[4,32,256]{2,1,0:T(8,128)(2,1)S(1)}, f16[4,32,256]{2,1,0:T(8,128)(2,1)S(1)}, u32[]{:S(2)}, u32[]{:S(2)}) collective-permute-start(f16[4,32,256]{2,1,0:T(8,128)(2,1)S(1)} %pad_maximum_fusion.4), channel_id=1, source_target_pairs={{0,2},{1,3},{2,0},{3,1},{4,6},{5,7},{6,4},{7,5},{8,10},{9,11},{10,... | collective-permute-start | bytes 196616 | tf_op jit(solution)/shard_map/ppermute | solution.py:451
  73.6 1.4 %collective-permute-start.19 = (f16[4,32,256]{2,1,0:T(8,128)(2,1)S(1)}, f16[4,32,256]{2,1,0:T(8,128)(2,1)S(1)}, u32[]{:S(2)}, u32[]{:S(2)}) collective-permute-start(f16[4,32,256]{2,1,0:T(8,128)(2,1)S(1)} %pad_maximum_fusion.5), channel_id=1, source_target_pairs={{0,3},{1,0},{2,1},{3,2},{4,7},{5,4},{6,5},{7,6},{8,11},{9,8},{10,9... | collective-permute-start | bytes 196616 | tf_op jit(solution)/shard_map/ppermute | solution.py:451
  75.0 3.2 %collective-permute-done.17 = f16[4,32,256]{2,1,0:T(8,128)(2,1)S(1)} collective-permute-done((f16[4,32,256]{2,1,0:T(8,128)(2,1)S(1)}, f16[4,32,256]{2,1,0:T(8,128)(2,1)S(1)}, u32[]{:S(2)}, u32[]{:S(2)}) %collective-permute-start.17) | collective-permute-done | bytes 65568 | tf_op jit(solution)/shard_map/ppermute | solution.py:451
  78.2 1.5 %collective-permute-done.18 = f16[4,32,256]{2,1,0:T(8,128)(2,1)S(1)} collective-permute-done((f16[4,32,256]{2,1,0:T(8,128)(2,1)S(1)}, f16[4,32,256]{2,1,0:T(8,128)(2,1)S(1)}, u32[]{:S(2)}, u32[]{:S(2)}) %collective-permute-start.18) | collective-permute-done | bytes 65568 | tf_op jit(solution)/shard_map/ppermute | solution.py:451
  79.8 0.0 collective-permute-done.19
  79.8 1.3 %shard_map.120.updated = f32[8,32,512]{2,1,0:T(8,128)S(1)} custom-call(s32[2]{0:T(128)S(1)} %pad_add_fusion.place.refs_0_, bf16[2,512,512]{2,1,0:T(8,128)(2,1)S(1)} %copy-done.6, f32[3,8,32,512]{3,2,1,0:T(8,128)S(1)} %copy-done.2, f32[4,32,256]{2,1,0:T(8,128)S(1)} %maximum_convert_fusion.1.refs_0_, f32[4,32,256]{2,1,0:T(8,128)S(1)} %convert_element_type.65.refs_1_, ...), custom_call_target="tpu_custom_call" | custom-call | flops 1073741824 | bytes 3670024 | tf_op jit(solution)/shard_map/pallas_call | solution.py:204
  81.1 4.7 %all-to-all-done.1 = f16[16,64,256]{2,1,0:T(8,128)(2,1)} async-done(((f16[16,64,256]{2,1,0:T(8,128)(2,1)}), f16[16,64,256]{2,1,0:T(8,128)(2,1)}, u32[]{:S(2)}, u32[]{:S(2)}) %all-to-all-start.1) | async-done | bytes 524320 | tf_op jit(solution)/shard_map/all_to_all | solution.py:455
  85.8 1.1 %convert_element_type.59.spectra = f32[16,64,256]{2,1,0:T(8,128)S(1)} convert(f16[16,64,256]{2,1,0:T(8,128)(2,1)} %all-to-all-done.1) | non-fusion elementwise | flops 262144 | bytes 1572864 | tf_op jit(solution)/shard_map/convert_element_type | solution.py:562
  86.9 2.8 %shard_map.121 = f32[3,8,32,512]{3,2,1,0:T(8,128)} custom-call(s32[2]{0:T(128)S(1)} %pad_add_fusion.place.refs_0_, f32[3,8,32,512]{3,2,1,0:T(8,128)S(1)} %copy-done.2, f32[16,64,256]{2,1,0:T(8,128)S(1)} %convert_element_type.59.spectra, bf16[2,512,512]{2,1,0:T(8,128)(2,1)S(1)} %copy-done.6, f32[8,32,512]{2,1,0:T(8,128)S(1)} %shard_map.120.updated), custom_call_target="tpu_custom_call" | custom-call | flops 2147483648 | bytes 5767176 | tf_op jit(solution)/shard_map/pallas_call | solution.py:204
  (42 shorter events, 0.5 us)
Async XLA Ops:
  0.7 1.0 %copy-start = (bf16[8,32,512]{2,1,0:T(8,128)(2,1)S(1)}, bf16[8,32,512]{2,1,0:T(8,128)(2,1)}, u32[]{:S(2)}) copy-start(bf16[8,32,512]{2,1,0:T(8,128)(2,1)} %moving.1) | copy-start | bytes 786436
  1.7 0.7 copy-start.1
  3.1 7.8 %collective-permute-start = (bf16[9,32,128]{2,1,0:T(8,128)(2,1)S(1)}, bf16[9,32,128]{2,1,0:T(8,128)(2,1)S(1)}, u32[]{:S(2)}, u32[]{:S(2)}) collective-permute-start(bf16[9,32,128]{2,1,0:T(8,128)(2,1)S(1)} %get-tuple-element.22), channel_id=1, source_target_pairs={{0,4},{4,8},{8,12},{12,0},{1,5},{5,9},{9,13},{13,1},{2,6},{6,10},{... | collective-permute-start | bytes 221192 | tf_op jit(solution)/shard_map/ppermute | solution.py:451
  6.1 7.5 %collective-permute-start.1 = (bf16[9,32,128]{2,1,0:T(8,128)(2,1)S(1)}, bf16[9,32,128]{2,1,0:T(8,128)(2,1)S(1)}, u32[]{:S(2)}, u32[]{:S(2)}) collective-permute-start(bf16[9,32,128]{2,1,0:T(8,128)(2,1)S(1)} %get-tuple-element.23), channel_id=1, source_target_pairs={{0,8},{4,12},{8,0},{12,4},{1,9},{5,13},{9,1},{13,5},{2,10},{6,14},... | collective-permute-start | bytes 221192 | tf_op jit(solution)/shard_map/ppermute | solution.py:451
  8.7 5.2 %collective-permute-start.2 = (bf16[9,32,128]{2,1,0:T(8,128)(2,1)S(1)}, bf16[9,32,128]{2,1,0:T(8,128)(2,1)S(1)}, u32[]{:S(2)}, u32[]{:S(2)}) collective-permute-start(bf16[9,32,128]{2,1,0:T(8,128)(2,1)S(1)} %get-tuple-element.24), channel_id=1, source_target_pairs={{0,12},{4,0},{8,4},{12,8},{1,13},{5,1},{9,5},{13,9},{2,14},{6,2},{... | collective-permute-start | bytes 221192 | tf_op jit(solution)/shard_map/ppermute | solution.py:451
  13.9 13.7 %copy-start.3 = (f32[8,32,512]{2,1,0:T(8,128)S(1)}, f32[8,32,512]{2,1,0:T(8,128)}, u32[]{:S(2)}) copy-start(f32[8,32,512]{2,1,0:T(8,128)} %refs_5_.2) | copy-start | bytes 1572868
  13.9 13.7 %copy-start.4 = (bf16[8,32,512]{2,1,0:T(8,128)(2,1)S(1)}, bf16[8,32,512]{2,1,0:T(8,128)(2,1)}, u32[]{:S(2)}) copy-start(bf16[8,32,512]{2,1,0:T(8,128)(2,1)} %refs_4_.2) | copy-start | bytes 786436
  13.9 13.7 %copy-start.5 = (s32[8,32,4]{1,2,0:T(4,128)S(1)}, s32[8,32,4]{1,2,0:T(4,128)}, u32[]{:S(2)}) copy-start(s32[8,32,4]{1,2,0:T(4,128)} %param.15) | copy-start | bytes 12292
  13.9 13.7 %copy-start.7 = (bf16[2,512,512]{2,1,0:T(8,128)(2,1)S(1)}, bf16[2,512,512]{2,1,0:T(8,128)(2,1)}, u32[]{:S(2)}) copy-start(bf16[2,512,512]{2,1,0:T(8,128)(2,1)} %constant.15.clone.refs_7_.basis) | copy-start | bytes 3145732
  15.7 7.3 %collective-permute-start.3 = (bf16[10,32,128]{2,1,0:T(8,128)(2,1)S(1)}, bf16[10,32,128]{2,1,0:T(8,128)(2,1)S(1)}, u32[]{:S(2)}, u32[]{:S(2)}) collective-permute-start(bf16[10,32,128]{2,1,0:T(8,128)(2,1)S(1)} %get-tuple-element.26), channel_id=1, source_target_pairs={{0,4},{4,8},{8,12},{12,0},{1,5},{5,9},{9,13},{13,1},{2,6},{6,10},{... | collective-permute-start | bytes 245768 | tf_op jit(solution)/shard_map/ppermute | solution.py:451
  17.6 7.6 %collective-permute-start.4 = (bf16[10,32,128]{2,1,0:T(8,128)(2,1)S(1)}, bf16[10,32,128]{2,1,0:T(8,128)(2,1)S(1)}, u32[]{:S(2)}, u32[]{:S(2)}) collective-permute-start(bf16[10,32,128]{2,1,0:T(8,128)(2,1)S(1)} %get-tuple-element.27), channel_id=1, source_target_pairs={{0,8},{4,12},{8,0},{12,4},{1,9},{5,13},{9,1},{13,5},{2,10},{6,14},... | collective-permute-start | bytes 245768 | tf_op jit(solution)/shard_map/ppermute | solution.py:451
  19.5 5.7 %collective-permute-start.5 = (bf16[10,32,128]{2,1,0:T(8,128)(2,1)S(1)}, bf16[10,32,128]{2,1,0:T(8,128)(2,1)S(1)}, u32[]{:S(2)}, u32[]{:S(2)}) collective-permute-start(bf16[10,32,128]{2,1,0:T(8,128)(2,1)S(1)} %get-tuple-element.28), channel_id=1, source_target_pairs={{0,12},{4,0},{8,4},{12,8},{1,13},{5,1},{9,5},{13,9},{2,14},{6,2},{... | collective-permute-start | bytes 245768 | tf_op jit(solution)/shard_map/ppermute | solution.py:451
  25.8 8.0 %collective-permute-start.12 = (bf16[4,8,128]{2,1,0:T(8,128)(2,1)S(1)}, bf16[4,8,128]{2,1,0:T(8,128)(2,1)S(1)}, u32[]{:S(2)}, u32[]{:S(2)}) collective-permute-start(bf16[4,8,128]{2,1,0:T(8,128)(2,1)S(1)} %get-tuple-element.34), channel_id=1, source_target_pairs={{0,1},{1,2},{2,3},{3,0},{4,5},{5,6},{6,7},{7,4},{8,9},{9,10},{10,1... | collective-permute-start | bytes 24584 | tf_op jit(solution)/shard_map/ppermute | solution.py:480
  25.9 8.0 %collective-permute-start.13 = (bf16[4,8,128]{2,1,0:T(8,128)(2,1)S(1)}, bf16[4,8,128]{2,1,0:T(8,128)(2,1)S(1)}, u32[]{:S(2)}, u32[]{:S(2)}) collective-permute-start(bf16[4,8,128]{2,1,0:T(8,128)(2,1)S(1)} %get-tuple-element.35), channel_id=1, source_target_pairs={{1,0},{2,1},{3,2},{0,3},{5,4},{6,5},{7,6},{4,7},{9,8},{10,9},{11,1... | collective-permute-start | bytes 24584 | tf_op jit(solution)/shard_map/ppermute | solution.py:481
  30.0 11.9 %collective-permute-start.6 = (f16[4,32,256]{2,1,0:T(8,128)(2,1)S(1)}, f16[4,32,256]{2,1,0:T(8,128)(2,1)S(1)}, u32[]{:S(2)}, u32[]{:S(2)}) collective-permute-start(f16[4,32,256]{2,1,0:T(8,128)(2,1)S(1)} %get-tuple-element.44), channel_id=1, source_target_pairs={{0,4},{4,8},{8,12},{12,0},{1,5},{5,9},{9,13},{13,1},{2,6},{6,10},{... | collective-permute-start | bytes 196616 | tf_op jit(solution)/shard_map/ppermute | solution.py:451
  32.2 9.7 %collective-permute-start.8 = (f16[4,32,256]{2,1,0:T(8,128)(2,1)S(1)}, f16[4,32,256]{2,1,0:T(8,128)(2,1)S(1)}, u32[]{:S(2)}, u32[]{:S(2)}) collective-permute-start(f16[4,32,256]{2,1,0:T(8,128)(2,1)S(1)} %get-tuple-element.45), channel_id=1, source_target_pairs={{0,12},{4,0},{8,4},{12,8},{1,13},{5,1},{9,5},{13,9},{2,14},{6,2},{... | collective-permute-start | bytes 196616 | tf_op jit(solution)/shard_map/ppermute | solution.py:451
  33.8 8.1 %collective-permute-start.7 = (f16[4,32,256]{2,1,0:T(8,128)(2,1)S(1)}, f16[4,32,256]{2,1,0:T(8,128)(2,1)S(1)}, u32[]{:S(2)}, u32[]{:S(2)}) collective-permute-start(f16[4,32,256]{2,1,0:T(8,128)(2,1)S(1)} %get-tuple-element.46), channel_id=1, source_target_pairs={{0,8},{4,12},{8,0},{12,4},{1,9},{5,13},{9,1},{13,5},{2,10},{6,14},... | collective-permute-start | bytes 196616 | tf_op jit(solution)/shard_map/ppermute | solution.py:451
  36.6 13.9 %copy-start.8 = (bf16[2,256,256]{2,1,0:T(8,128)(2,1)S(1)}, bf16[2,256,256]{2,1,0:T(8,128)(2,1)}, u32[]{:S(2)}) copy-start(bf16[2,256,256]{2,1,0:T(8,128)(2,1)} %constant.16.clone.refs_4_.basis_z) | copy-start | bytes 786436
  36.6 13.9 %copy-start.9 = (bf16[4,128,128]{2,1,0:T(8,128)(2,1)S(1)}, bf16[4,128,128]{2,1,0:T(8,128)(2,1)}, u32[]{:S(2)}) copy-start(bf16[4,128,128]{2,1,0:T(8,128)(2,1)} %constant.17.clone.refs_5_.basis_y) | copy-start | bytes 393220
  36.6 22.8 %all-to-all-start = ((f16[16,64,256]{2,1,0:T(8,128)(2,1)}), f16[16,64,256]{2,1,0:T(8,128)(2,1)S(1)}, u32[]{:S(2)}, u32[]{:S(2)}) async-start(f16[16,64,256]{2,1,0:T(8,128)(2,1)} %convert_element_type.56), calls=%async_computation | async-start | bytes 1048576 | tf_op jit(solution)/shard_map/all_to_all | solution.py:455
  42.0 6.9 %collective-permute-start.9 = (f16[4,32,256]{2,1,0:T(8,128)(2,1)S(1)}, f16[4,32,256]{2,1,0:T(8,128)(2,1)S(1)}, u32[]{:S(2)}, u32[]{:S(2)}) collective-permute-start(f16[4,32,256]{2,1,0:T(8,128)(2,1)S(1)} %pad_maximum_fusion), channel_id=1, source_target_pairs={{0,1},{1,2},{2,3},{3,0},{4,5},{5,6},{6,7},{7,4},{8,9},{9,10},{10,1... | collective-permute-start | bytes 196616 | tf_op jit(solution)/shard_map/ppermute | solution.py:451
  42.5 7.9 %collective-permute-start.10 = (f16[4,32,256]{2,1,0:T(8,128)(2,1)S(1)}, f16[4,32,256]{2,1,0:T(8,128)(2,1)S(1)}, u32[]{:S(2)}, u32[]{:S(2)}) collective-permute-start(f16[4,32,256]{2,1,0:T(8,128)(2,1)S(1)} %pad_maximum_fusion.1), channel_id=1, source_target_pairs={{0,2},{1,3},{2,0},{3,1},{4,6},{5,7},{6,4},{7,5},{8,10},{9,11},{10,... | collective-permute-start | bytes 196616 | tf_op jit(solution)/shard_map/ppermute | solution.py:451
  44.3 6.2 %collective-permute-start.11 = (f16[4,32,256]{2,1,0:T(8,128)(2,1)S(1)}, f16[4,32,256]{2,1,0:T(8,128)(2,1)S(1)}, u32[]{:S(2)}, u32[]{:S(2)}) collective-permute-start(f16[4,32,256]{2,1,0:T(8,128)(2,1)S(1)} %pad_maximum_fusion.2), channel_id=1, source_target_pairs={{0,3},{1,0},{2,1},{3,2},{4,7},{5,4},{6,5},{7,6},{8,11},{9,8},{10,9... | collective-permute-start | bytes 196616 | tf_op jit(solution)/shard_map/ppermute | solution.py:451
  53.3 6.0 %collective-permute-start.16 = (f16[4,32,256]{2,1,0:T(8,128)(2,1)S(1)}, f16[4,32,256]{2,1,0:T(8,128)(2,1)S(1)}, u32[]{:S(2)}, u32[]{:S(2)}) collective-permute-start(f16[4,32,256]{2,1,0:T(8,128)(2,1)S(1)} %convert_element_type.63), channel_id=1, source_target_pairs={{0,12},{4,0},{8,4},{12,8},{1,13},{5,1},{9,5},{13,9},{2,14},{6,2},{... | collective-permute-start | bytes 196616 | tf_op jit(solution)/shard_map/ppermute | solution.py:451
  57.3 14.0 %collective-permute-start.15 = (f16[4,32,256]{2,1,0:T(8,128)(2,1)S(1)}, f16[4,32,256]{2,1,0:T(8,128)(2,1)S(1)}, u32[]{:S(2)}, u32[]{:S(2)}) collective-permute-start(f16[4,32,256]{2,1,0:T(8,128)(2,1)S(1)} %convert_element_type.62), channel_id=1, source_target_pairs={{0,8},{4,12},{8,0},{12,4},{1,9},{5,13},{9,1},{13,5},{2,10},{6,14},... | collective-permute-start | bytes 196616 | tf_op jit(solution)/shard_map/ppermute | solution.py:451
  57.4 13.9 %collective-permute-start.14 = (f16[4,32,256]{2,1,0:T(8,128)(2,1)S(1)}, f16[4,32,256]{2,1,0:T(8,128)(2,1)S(1)}, u32[]{:S(2)}, u32[]{:S(2)}) collective-permute-start(f16[4,32,256]{2,1,0:T(8,128)(2,1)S(1)} %convert_element_type.61), channel_id=1, source_target_pairs={{0,4},{4,8},{8,12},{12,0},{1,5},{5,9},{9,13},{13,1},{2,6},{6,10},{... | collective-permute-start | bytes 196616 | tf_op jit(solution)/shard_map/ppermute | solution.py:451
  63.5 16.3 %copy-start.6 = (bf16[2,512,512]{2,1,0:T(8,128)(2,1)S(1)}, bf16[2,512,512]{2,1,0:T(8,128)(2,1)}, u32[]{:S(2)}) copy-start(bf16[2,512,512]{2,1,0:T(8,128)(2,1)} %constant.18.clone.basis) | copy-start | bytes 3145732
  64.4 15.4 %copy-start.2 = (f32[3,8,32,512]{3,2,1,0:T(8,128)S(1)}, f32[3,8,32,512]{3,2,1,0:T(8,128)}, u32[]{:S(2)}) copy-start(f32[3,8,32,512]{3,2,1,0:T(8,128)} %velocity_in.3) | copy-start | bytes 4718596
  64.4 21.4 %all-to-all-start.1 = ((f16[16,64,256]{2,1,0:T(8,128)(2,1)}), f16[16,64,256]{2,1,0:T(8,128)(2,1)}, u32[]{:S(2)}, u32[]{:S(2)}) async-start(f16[16,64,256]{2,1,0:T(8,128)(2,1)} %convert_element_type.58), calls=%async_computation.1 | async-start | bytes 1048576 | tf_op jit(solution)/shard_map/all_to_all | solution.py:455
  71.4 6.8 %collective-permute-start.17 = (f16[4,32,256]{2,1,0:T(8,128)(2,1)S(1)}, f16[4,32,256]{2,1,0:T(8,128)(2,1)S(1)}, u32[]{:S(2)}, u32[]{:S(2)}) collective-permute-start(f16[4,32,256]{2,1,0:T(8,128)(2,1)S(1)} %pad_maximum_fusion.3), channel_id=1, source_target_pairs={{0,1},{1,2},{2,3},{3,0},{4,5},{5,6},{6,7},{7,4},{8,9},{9,10},{10,1... | collective-permute-start | bytes 196616 | tf_op jit(solution)/shard_map/ppermute | solution.py:451
  71.8 7.9 %collective-permute-start.18 = (f16[4,32,256]{2,1,0:T(8,128)(2,1)S(1)}, f16[4,32,256]{2,1,0:T(8,128)(2,1)S(1)}, u32[]{:S(2)}, u32[]{:S(2)}) collective-permute-start(f16[4,32,256]{2,1,0:T(8,128)(2,1)S(1)} %pad_maximum_fusion.4), channel_id=1, source_target_pairs={{0,2},{1,3},{2,0},{3,1},{4,6},{5,7},{6,4},{7,5},{8,10},{9,11},{10,... | collective-permute-start | bytes 196616 | tf_op jit(solution)/shard_map/ppermute | solution.py:451
  73.6 6.2 %collective-permute-start.19 = (f16[4,32,256]{2,1,0:T(8,128)(2,1)S(1)}, f16[4,32,256]{2,1,0:T(8,128)(2,1)S(1)}, u32[]{:S(2)}, u32[]{:S(2)}) collective-permute-start(f16[4,32,256]{2,1,0:T(8,128)(2,1)S(1)} %pad_maximum_fusion.5), channel_id=1, source_target_pairs={{0,3},{1,0},{2,1},{3,2},{4,7},{5,4},{6,5},{7,6},{8,11},{9,8},{10,9... | collective-permute-start | bytes 196616 | tf_op jit(solution)/shard_map/ppermute | solution.py:451

commit v6 on v5

--- a/solution.py
+++ b/solution.py
@@ -269,9 +269,9 @@
         last[d] = jnp.concatenate([c[rows - 1 : rows] for c in cells], axis=0).astype(jnp.bfloat16)
 
 
-def force_z_kernel(slabs, subs, place, *refs):
+def force_zx_kernel(slabs, subs, place, *refs):
     received, refs = refs[:slabs], refs[slabs:]
-    template, stiffness, tissue, basis, warped, image, weight, spectra, planes_of, wide = refs
+    template, stiffness, tissue, basis, warped, image, weight, spectra, kept, planes_of, wide = refs
     planes, rows, x_length = template.shape
     blocks = x_length // BLOCK
     for step in range(slabs):
@@ -279,7 +279,7 @@
         planes_of[:, :, block] = received[step][...].astype(jnp.float32)
         warped[:, :, block] = received[step][1:-1]
     marks = by_row(tissue, rows)
-    force = []
+    forces = [[], []]
     for z in range(planes):
         here = planes_of[z + 1]
         marked = jnp.concatenate(
@@ -292,39 +292,43 @@
         own = 0.5 * (marked * stiffness[z] * (here - template[z].astype(jnp.float32)))
         image[z] = here
         weight[z] = own
-        force.append(own * (planes_of[z + 2] - planes_of[z]))
-    force = split(jnp.concatenate(force, axis=0))
-    wide[...] = times((basis[0], basis[1]), force, ((1,), (1,)))
+        forces[0].append(own * (planes_of[z + 2] - planes_of[z]))
+        forces[1].append(own * (pltpu.roll(here, x_length - 1, 1) - pltpu.roll(here, 1, 1)))
+    for a in range(2):
+        force = split(jnp.concatenate(forces[a], axis=0))
+        wide[a] = times((basis[0], basis[1]), force, ((1,), (1,)))
     part = x_length // (slabs * subs)
+    half = part // 2
     for d in range(slabs):
         for e in range(subs):
             first = (around(place[0] + d, slabs) * subs + around(place[1] + e, subs)) * part
-            spectra[d, e] = wide[pl.ds(pl.multiple_of(first, part), part), :]
-
-
-def force_xy_kernel(slabs, place, above, below, image, weight, basis, spectra, edges):
+            spectra[d, e, :part] = wide[0, pl.ds(pl.multiple_of(first, part), part), :]
+            spectra[d, e, part:] = wide[1, pl.ds(pl.multiple_of(first + half, half), half), :]
+    for k in range(slabs * subs):
+        kept[k] = wide[1, k * part : k * part + half, :]
+
+
+def force_y_kernel(slabs, place, above, below, image, weight, basis, kept, spectra, edges):
     planes, rows, x_length = image.shape
     for step in range(slabs):
         block = pl.ds(pl.multiple_of(around(place[0] - step, slabs) * BLOCK, BLOCK), BLOCK)
         edges[0, :, block] = above[step].astype(jnp.float32)
         edges[1, :, block] = below[step].astype(jnp.float32)
     row = lax.broadcasted_iota(jnp.int32, (rows, x_length), 0)
-    forces = [[], []]
+    force = []
     for z in range(planes):
-        here, own = image[z], weight[z]
+        here = image[z]
         before = jnp.where(row == 0, edges[0, z : z + 1, :], pltpu.roll(here, 1, 0))
         after = jnp.where(row == rows - 1, edges[1, z : z + 1, :], pltpu.roll(here, rows - 1, 0))
-        forces[0].append(own * (after - before))
-        forces[1].append(own * (pltpu.roll(here, x_length - 1, 1) - pltpu.roll(here, 1, 1)))
-    devices, part = spectra.shape[:2]
-    part //= 2
-    for a in range(2):
-        force = split(jnp.concatenate(forces[a], axis=0))
-        spectrum = times((basis[0], basis[1]), force, ((1,), (1,)))
-        spectra[:, a * part : (a + 1) * part, :] = spectrum.reshape(devices, part, planes * rows)
-
-
-def solve(first, x_length, part, subs, spectra, basis_z, basis_y, cells):
+        force.append(weight[z] * (after - before))
+    devices = spectra.shape[0]
+    part = x_length // devices
+    spectrum = times((basis[0], basis[1]), split(jnp.concatenate(force, axis=0)), ((1,), (1,)))
+    spectra[:, :part, :] = spectrum.reshape(devices, part, planes * rows)
+    spectra[:, part:, :] = kept[...]
+
+
+def solve(first, x_length, offsets, subs, spectra, basis_z, basis_y, cells):
     devices, used, area = spectra.shape
     total_z, _, total_y = cells.shape
     slabs = devices // subs
@@ -358,7 +362,7 @@
         own, scale = [], []
         for start in (g, g + tile):
             own.append(cells[:, start : start + tile, :].reshape(total_z * tile, total_y))
-            x_sq = wave_sq(first + start % part + lax.rem(index, tile), x_length)
+            x_sq = wave_sq(first + offsets[start // tile] + lax.rem(index, tile), x_length)
             scale.append((z_sq + x_sq + y_sq) * 256.0 + 1.0)
         own = times(table, split(jnp.concatenate(own, axis=1)), ((1,), (0,)))
         own = own / jnp.concatenate(scale, axis=1)
@@ -376,21 +380,23 @@
             )
 
 
-def solve_xy_kernel(subs, x_length, place, spectra, basis_z, basis_y, out, cells):
+def solve_yx_kernel(subs, x_length, place, spectra, basis_z, basis_y, out, cells):
     devices = out.shape[0]
     part = x_length // devices
+    offsets = list(range(0, part, 8)) + list(range(0, part // 2, 8))
     out[...] = spectra[...]
-    solve((place[0] * subs + place[1]) * part, x_length, part, subs, out, basis_z, basis_y, cells)
-
-
-def solve_z_kernel(slabs, subs, x_length, place, *refs):
+    solve((place[0] * subs + place[1]) * part, x_length, offsets, subs, out, basis_z, basis_y, cells)
+
+
+def solve_zx_kernel(slabs, subs, x_length, place, *refs):
     received, refs = refs[:subs], refs[subs:]
     basis_z, basis_y, sends, (spectra, cells) = refs[0], refs[1], refs[2 : 2 + slabs], refs[2 + slabs :]
     part = x_length // (slabs * subs)
+    offsets = list(range(0, part, 8)) + list(range(part // 2, part, 8))
     for e in range(subs):
         for d in range(slabs):
             spectra[around(place[0] - d, slabs) * subs + around(place[1] - e, subs)] = received[e][d]
-    solve((place[0] * subs + place[1]) * part, x_length, part, subs, spectra, basis_z, basis_y, cells)
+    solve((place[0] * subs + place[1]) * part, x_length, offsets, subs, spectra, basis_z, basis_y, cells)
     for d in range(slabs):
         for e in range(subs):
             sends[d][e] = spectra[around(place[0] + d, slabs) * subs + around(place[1] + e, subs)]
@@ -402,21 +408,23 @@
 
 
 def update_z_kernel(slabs, subs, place, basis, velocity_in, *refs):
-    received, (out, gathered, velocity, done) = refs[:subs], refs[subs:]
-    part = received[0].shape[1]
+    received, (out, kept, gathered, velocity, done) = refs[:subs], refs[subs:]
+    half = kept.shape[1]
+    part = 2 * half
     arriving = pltpu.make_async_copy(velocity_in.at[0], velocity, done.at[0])
     arriving.start()
     for e in range(subs):
         for d in range(slabs):
-            first = (around(place[0] - d, slabs) * subs + around(place[1] - e, subs)) * part
-            gathered[pl.ds(pl.multiple_of(first, part), part), :] = received[e][d]
+            index = around(place[0] - d, slabs) * subs + around(place[1] - e, subs)
+            gathered[pl.ds(pl.multiple_of(index * part, part), part), :] = received[e][d, :part]
+            kept[index] = received[e][d, part:]
     arriving.wait()
     out[...] = moved(gathered[...], velocity[...], basis)
 
 
-def update_kernel(place, velocity_in, spectra, basis, updated, out, velocity, result, done):
-    devices, part, area = spectra.shape
-    part //= 2
+def update_kernel(place, velocity_in, spectra, basis, updated, kept, out, velocity, result, done):
+    devices, half, area = kept.shape
+    part = 2 * half
     arriving = [pltpu.make_async_copy(velocity_in.at[a], velocity.at[a - 1], done.at[a]) for a in (1, 2)]
     leaving = [pltpu.make_async_copy(result.at[a - 1], out.at[a], done.at[2 + a]) for a in (1, 2)]
     leaving.append(pltpu.make_async_copy(updated, out.at[0], done.at[0]))
@@ -424,7 +432,11 @@
     for copy in arriving:
         copy.start()
     for a in range(2):
-        own = spectra[:, a * part : (a + 1) * part, :].reshape(devices * part, area)
+        if a:
+            own = jnp.concatenate([spectra[:, part:, :], kept[...]], axis=1)
+        else:
+            own = spectra[:, :part, :]
+        own = own.reshape(devices * part, area)
         arriving[a].wait()
         result[a] = moved(own, velocity[a], basis)
         leaving[a].start()
@@ -482,13 +494,15 @@
     basis_x = in_two(8.0 * real_basis(x_length))
     basis_z = in_two(np.kron(real_basis(total_z), np.eye(8)))
     basis_y = np.concatenate([in_two(real_basis(total_y).T), in_two(real_basis(total_y))])
-    warped, image, weight, spectra_z = call(
-        functools.partial(force_z_kernel, slabs, subs),
+    each = part + part // 2
+    warped, image, weight, chain, kept = call(
+        functools.partial(force_zx_kernel, slabs, subs),
         [
             shape(moving.shape, bf16),
             shape(moving.shape),
             shape(moving.shape),
-            shape((slabs, subs, part, area)),
+            shape((slabs, subs, each, area)),
+            shape((devices, part // 2, area)),
         ],
         place,
         *received,
@@ -496,57 +510,58 @@
         stiffness,
         marks,
         basis_x,
-        scratch=[pltpu.VMEM((planes + 2, rows, x_length), f32), pltpu.VMEM((x_length, area), f32)],
-        flops=2 << 30,
-    )
-    spectra_z = spectra_z.astype(f16)
-    spectra_z = scatter([spectra_z[d] for d in range(slabs)], "slab")
-    spectra_z = scatter([jnp.stack([r[e] for r in spectra_z]) for e in range(subs)], "sub")
-    spectra_xy = call(
-        functools.partial(force_xy_kernel, slabs),
-        shape((devices, 2 * part, area)),
+        scratch=[pltpu.VMEM((planes + 2, rows, x_length), f32), pltpu.VMEM((2, x_length, area), f32)],
+        flops=3 << 30,
+    )
+    chain = chain.astype(f16)
+    chain = scatter([chain[d] for d in range(slabs)], "slab")
+    chain = scatter([jnp.stack([r[e] for r in chain]) for e in range(subs)], "sub")
+    spectra = call(
+        functools.partial(force_y_kernel, slabs),
+        shape((devices, each, area)),
         place,
         above,
         below,
         image,
         weight,
         basis_x,
+        kept,
         scratch=[pltpu.VMEM((2, planes, x_length), f32)],
-        flops=3 << 30,
-    )
-    spectra_xy = exchange(spectra_xy.astype(f16))
-    spectra_z = call(
-        functools.partial(solve_z_kernel, slabs, subs, x_length),
-        [shape((subs, part, area))] * slabs,
-        place,
-        *[r.astype(f32) for r in spectra_z],
+        flops=2 << 30,
+    )
+    spectra = exchange(spectra.astype(f16))
+    chain = call(
+        functools.partial(solve_zx_kernel, slabs, subs, x_length),
+        [shape((subs, each, area))] * slabs,
+        place,
+        *[r.astype(f32) for r in chain],
         basis_z,
         basis_y,
-        scratch=[pltpu.VMEM((devices, part, area), f32), pltpu.VMEM((total_z, part, total_y), f32)],
+        scratch=[pltpu.VMEM((devices, each, area), f32), pltpu.VMEM((total_z, each, total_y), f32)],
         flops=2 << 30,
     )
-    _, spectra_xy = lax.optimization_barrier((spectra_z, spectra_xy))
-    spectra_z = scatter([r.astype(f16) for r in spectra_z], "slab")
-    spectra_z = scatter([jnp.stack([r[e] for r in spectra_z]) for e in range(subs)], "sub")
-    spectra_xy = call(
-        functools.partial(solve_xy_kernel, subs, x_length),
-        shape((devices, 2 * part, area)),
-        place,
-        spectra_xy.astype(f32),
+    chain, spectra = lax.optimization_barrier((chain, spectra))
+    chain = scatter([r.astype(f16) for r in chain], "slab")
+    chain = scatter([jnp.stack([r[e] for r in chain]) for e in range(subs)], "sub")
+    spectra = call(
+        functools.partial(solve_yx_kernel, subs, x_length),
+        shape((devices, each, area)),
+        place,
+        spectra.astype(f32),
         basis_z,
         basis_y,
-        scratch=[pltpu.VMEM((total_z, 2 * part, total_y), f32)],
-        flops=3 << 30,
-    )
-    spectra_xy = exchange(spectra_xy.astype(f16))
+        scratch=[pltpu.VMEM((total_z, each, total_y), f32)],
+        flops=2 << 30,
+    )
+    spectra = exchange(spectra.astype(f16))
     basis_x = in_two(real_basis(x_length))
-    updated = call(
+    updated, kept = call(
         functools.partial(update_z_kernel, slabs, subs),
-        shape(moving.shape),
+        [shape(moving.shape), shape((devices, part // 2, area))],
         place,
         basis_x,
         (velocity,),
-        *[r.astype(f32) for r in spectra_z],
+        *[r.astype(f32) for r in chain],
         scratch=[
             pltpu.VMEM((x_length, area), f32),
             pltpu.VMEM(moving.shape, f32),
@@ -559,9 +574,10 @@
         shape(velocity.shape),
         place,
         (velocity,),
-        spectra_xy.astype(f32),
+        spectra.astype(f32),
         basis_x,
         updated,
+        kept,
         scratch=[
             pltpu.VMEM((2,) + moving.shape, f32),
             pltpu.VMEM((2,) + moving.shape, f32),
@@ -582,7 +598,7 @@
         and planes * slabs * 8 == 256
         and rows % 16 == 0
         and rows * subs == BLOCK
-        and x_length % (16 * slabs * subs) == 0
+        and x_length % (32 * slabs * subs) == 0
     )
     run = local_blocks if fits else local_general
     return run(velocity, template, moving, stiffness, fetch_plane, tissue)

time: 90.2 us -> 85.8 us (0.951)
  starting transfers between devices: 41 us -> 38.6 us
  waiting for transfers between devices: 24.4 us -> 22.4 us
    all_to_all x2, waiting for transfers between devices: 4.69 us -> 1.47 us  [exchange(): lax.all_to_all(values, ('slab', 'sub'), split_axis=0, concat_axis=0, tile...]
    all_to_all x2, starting transfers between devices: 12.2 us -> 10.6 us  [exchange(): lax.all_to_all(values, ('slab', 'sub'), split_axis=0, concat_axis=0, tile...]
    ppermute x18, waiting for transfers between devices: 19.7 us -> 21 us  [scatter(): lax.ppermute(sends[d], axis, [(i, (i + d) % count) for i in range(count)])]
  transfers between devices with their start and end apart: 22 -> 22, of which waited for: 11 -> 13; matrix products, arithmetic and copies ran while one was open for 3% -> 3% of each run, Pallas kernels for 14% -> 14%
where the time goes in v6:
time: 85.8 us; the launch traced here: 85.3 us
  starting transfers between devices  38.6 us (45%)
  waiting for transfers between devices  22.4 us (26%)
  Pallas kernels  18.1 us (21%)
  other arithmetic  3.33 us (4%)
  local copies, waits for them, and re-layouts  1.92 us (2%)
  between operations  1 us (1%)
    ppermute x18, starting transfers between devices, scatter(): lax.ppermute(sends[d], axis, [(i, (i + d) % count) for i in range(count)])  26.2 us
    ppermute x18, waiting for transfers between devices, scatter(): lax.ppermute(sends[d], axis, [(i, (i + d) % count) for i in range(count)])  21 us
    pallas_call x9, Pallas kernels, call(): pl.pallas_call(kernel, out_shape=out_shape, in_specs=places, out_specs=ja...  18.1 us
    all_to_all x2, starting transfers between devices, exchange(): lax.all_to_all(values, ('slab', 'sub'), split_axis=0, concat_axis=0, tile...  10.6 us
    ppermute x1, starting transfers between devices, local_blocks(): lax.ppermute(first, 'sub', [((i + 1) % subs, i) for i in range(subs)])  1.73 us
  transfers between devices with their start and end apart: 22, of which 13 were waited for; matrix products, arithmetic and copies ran while one was open for 3% of the time, Pallas kernels for 14%

profile of v6, /device:TPU:0, one launch (start us, length us, event | category | flops | bytes accessed | tf_op | source)
XLA Modules:
  0.0 85.3 jit_solution(12926790170561573955)
XLA Ops:
  0.6 0.1 pad_add_fusion.place.refs_0_
  0.7 0.9 %copy-done = bf16[8,32,512]{2,1,0:T(8,128)(2,1)S(1)} copy-done((bf16[8,32,512]{2,1,0:T(8,128)(2,1)S(1)}, bf16[8,32,512]{2,1,0:T(8,128)(2,1)}, u32[]{:S(2)}) %copy-start) | copy-done | bytes 262168
  1.7 0.7 copy-done.1
  2.4 0.7 shard_map.113
  3.1 3.0 %collective-permute-start = (bf16[9,32,128]{2,1,0:T(8,128)(2,1)S(1)}, bf16[9,32,128]{2,1,0:T(8,128)(2,1)S(1)}, u32[]{:S(2)}, u32[]{:S(2)}) collective-permute-start(bf16[9,32,128]{2,1,0:T(8,128)(2,1)S(1)} %get-tuple-element.29), channel_id=1, source_target_pairs={{0,4},{4,8},{8,12},{12,0},{1,5},{5,9},{9,13},{13,1},{2,6},{6,10},{... | collective-permute-start | bytes 221192 | tf_op jit(solution)/shard_map/ppermute | solution.py:463
  6.1 2.6 %collective-permute-start.1 = (bf16[9,32,128]{2,1,0:T(8,128)(2,1)S(1)}, bf16[9,32,128]{2,1,0:T(8,128)(2,1)S(1)}, u32[]{:S(2)}, u32[]{:S(2)}) collective-permute-start(bf16[9,32,128]{2,1,0:T(8,128)(2,1)S(1)} %get-tuple-element.30), channel_id=1, source_target_pairs={{0,8},{4,12},{8,0},{12,4},{1,9},{5,13},{9,1},{13,5},{2,10},{6,14},... | collective-permute-start | bytes 221192 | tf_op jit(solution)/shard_map/ppermute | solution.py:463
  8.7 1.3 %collective-permute-start.2 = (bf16[9,32,128]{2,1,0:T(8,128)(2,1)S(1)}, bf16[9,32,128]{2,1,0:T(8,128)(2,1)S(1)}, u32[]{:S(2)}, u32[]{:S(2)}) collective-permute-start(bf16[9,32,128]{2,1,0:T(8,128)(2,1)S(1)} %get-tuple-element.31), channel_id=1, source_target_pairs={{0,12},{4,0},{8,4},{12,8},{1,13},{5,1},{9,5},{13,9},{2,14},{6,2},{... | collective-permute-start | bytes 221192 | tf_op jit(solution)/shard_map/ppermute | solution.py:463
  10.0 0.8 collective-permute-done.refs_1_
  10.9 2.8 %collective-permute-done.1.refs_2_ = bf16[9,32,128]{2,1,0:T(8,128)(2,1)S(1)} collective-permute-done((bf16[9,32,128]{2,1,0:T(8,128)(2,1)S(1)}, bf16[9,32,128]{2,1,0:T(8,128)(2,1)S(1)}, u32[]{:S(2)}, u32[]{:S(2)}) %collective-permute-start.1) | collective-permute-done | bytes 73760 | tf_op jit(solution)/shard_map/ppermute | solution.py:463
  13.7 0.2 collective-permute-done.2.refs_3_
  13.9 1.8 %shard_map.114 = (bf16[10,32,128]{2,1,0:T(8,128)(2,1)S(1)}, bf16[10,32,128]{2,1,0:T(8,128)(2,1)S(1)}, bf16[10,32,128]{2,1,0:T(8,128)(2,1)S(1)}, bf16[10,32,128]{2,1,0:T(8,128)(2,1)S(1)}) custom-call(s32[2]{0:T(128)S(1)} %pad_add_fusion.place.refs_0_, bf16[9,32,128]{2,1,0:T(8,128)(2,1)S(1)} %get-tuple-element.28.refs_0_, ...), custom_call_target="tpu_custom_call" | custom-call | flops 1073741824 | bytes 622600 | tf_op jit(solution)/shard_map/pallas_call | solution.py:204
  15.7 1.9 %collective-permute-start.3 = (bf16[10,32,128]{2,1,0:T(8,128)(2,1)S(1)}, bf16[10,32,128]{2,1,0:T(8,128)(2,1)S(1)}, u32[]{:S(2)}, u32[]{:S(2)}) collective-permute-start(bf16[10,32,128]{2,1,0:T(8,128)(2,1)S(1)} %get-tuple-element.33), channel_id=1, source_target_pairs={{0,4},{4,8},{8,12},{12,0},{1,5},{5,9},{9,13},{13,1},{2,6},{6,10},{... | collective-permute-start | bytes 245768 | tf_op jit(solution)/shard_map/ppermute | solution.py:463
  17.6 1.9 %collective-permute-start.4 = (bf16[10,32,128]{2,1,0:T(8,128)(2,1)S(1)}, bf16[10,32,128]{2,1,0:T(8,128)(2,1)S(1)}, u32[]{:S(2)}, u32[]{:S(2)}) collective-permute-start(bf16[10,32,128]{2,1,0:T(8,128)(2,1)S(1)} %get-tuple-element.34), channel_id=1, source_target_pairs={{0,8},{4,12},{8,0},{12,4},{1,9},{5,13},{9,1},{13,5},{2,10},{6,14},... | collective-permute-start | bytes 245768 | tf_op jit(solution)/shard_map/ppermute | solution.py:463
  19.5 0.7 collective-permute-start.5
  20.2 2.7 %collective-permute-done.3.refs_1_.refs_2_ = bf16[10,32,128]{2,1,0:T(8,128)(2,1)S(1)} collective-permute-done((bf16[10,32,128]{2,1,0:T(8,128)(2,1)S(1)}, bf16[10,32,128]{2,1,0:T(8,128)(2,1)S(1)}, u32[]{:S(2)}, u32[]{:S(2)}) %collective-permute-start.3) | collective-permute-done | bytes 81952 | tf_op jit(solution)/shard_map/ppermute | solution.py:463
  22.9 2.3 %collective-permute-done.4.refs_2_.refs_3_ = bf16[10,32,128]{2,1,0:T(8,128)(2,1)S(1)} collective-permute-done((bf16[10,32,128]{2,1,0:T(8,128)(2,1)S(1)}, bf16[10,32,128]{2,1,0:T(8,128)(2,1)S(1)}, u32[]{:S(2)}, u32[]{:S(2)}) %collective-permute-start.4) | collective-permute-done | bytes 81952 | tf_op jit(solution)/shard_map/ppermute | solution.py:463
  25.2 0.0 collective-permute-done.5.refs_3_.refs_4_
  25.2 0.6 shard_map.117
  25.8 0.1 collective-permute-start.12
  25.9 1.7 %collective-permute-start.13 = (bf16[4,8,128]{2,1,0:T(8,128)(2,1)S(1)}, bf16[4,8,128]{2,1,0:T(8,128)(2,1)S(1)}, u32[]{:S(2)}, u32[]{:S(2)}) collective-permute-start(bf16[4,8,128]{2,1,0:T(8,128)(2,1)S(1)} %get-tuple-element.42), channel_id=1, source_target_pairs={{1,0},{2,1},{3,2},{0,3},{5,4},{6,5},{7,6},{4,7},{9,8},{10,9},{11,1... | collective-permute-start | bytes 24584 | tf_op jit(solution)/shard_map/ppermute | solution.py:493
  27.6 0.0 copy-done.3
  27.6 2.9 %shard_map.115 = (bf16[8,32,512]{2,1,0:T(8,128)(2,1)}, f32[8,32,512]{2,1,0:T(8,128)S(1)}, f32[8,32,512]{2,1,0:T(8,128)S(1)}, f32[4,4,48,256]{3,2,1,0:T(8,128)S(1)}, f32[16,16,256]{2,1,0:T(8,128)S(1)}) custom-call(s32[2]{0:T(128)S(1)} %pad_add_fusion.place.refs_0_, bf16[10,32,128]{2,1,0:T(8,128)(2,1)S(1)} %get-tuple-element.32.refs_0_.refs_1_, ...), custom_call_target="tpu_custom_call" | custom-call | flops 3221225472 | bytes 4526088 | tf_op jit(solution)/shard_map/pallas_call | solution.py:204
  30.5 0.1 convert_element_type.51
  30.6 0.1 slice_bitcast_fusion.2
  30.7 2.3 %collective-permute-start.6 = (f16[4,48,256]{2,1,0:T(8,128)(2,1)S(1)}, f16[4,48,256]{2,1,0:T(8,128)(2,1)S(1)}, u32[]{:S(2)}, u32[]{:S(2)}) collective-permute-start(f16[4,48,256]{2,1,0:T(8,128)(2,1)S(1)} %get-tuple-element.58), channel_id=1, source_target_pairs={{0,4},{4,8},{8,12},{12,0},{1,5},{5,9},{9,13},{13,1},{2,6},{6,10},{... | collective-permute-start | bytes 294920 | tf_op jit(solution)/shard_map/ppermute | solution.py:463
  32.9 1.6 %collective-permute-start.8 = (f16[4,48,256]{2,1,0:T(8,128)(2,1)S(1)}, f16[4,48,256]{2,1,0:T(8,128)(2,1)S(1)}, u32[]{:S(2)}, u32[]{:S(2)}) collective-permute-start(f16[4,48,256]{2,1,0:T(8,128)(2,1)S(1)} %get-tuple-element.59), channel_id=1, source_target_pairs={{0,12},{4,0},{8,4},{12,8},{1,13},{5,1},{9,5},{13,9},{2,14},{6,2},{... | collective-permute-start | bytes 294920 | tf_op jit(solution)/shard_map/ppermute | solution.py:463
  34.5 0.0 collective-permute-start.7
  34.5 0.0 collective-permute-done.12.above
  34.5 0.0 collective-permute-done.13.below
  34.6 1.3 %shard_map.118 = f32[16,48,256]{2,1,0:T(8,128)S(1)} custom-call(s32[2]{0:T(128)S(1)} %pad_add_fusion.place.refs_0_, bf16[4,8,128]{2,1,0:T(8,128)(2,1)S(1)} %collective-permute-done.12.above, bf16[4,8,128]{2,1,0:T(8,128)(2,1)S(1)} %collective-permute-done.13.below, f32[8,32,512]{2,1,0:T(8,128)S(1)} %get-tuple-element.43.image, ...), custom_call_target="tpu_custom_call" | custom-call | flops 2147483648 | bytes 3162120 | tf_op jit(solution)/shard_map/pallas_call | solution.py:204
  35.8 0.8 convert_element_type.56
  36.6 5.3 %all-to-all-start = ((f16[16,48,256]{2,1,0:T(8,128)(2,1)}), f16[16,48,256]{2,1,0:T(8,128)(2,1)S(1)}, u32[]{:S(2)}, u32[]{:S(2)}) async-start(f16[16,48,256]{2,1,0:T(8,128)(2,1)} %convert_element_type.56), calls=%async_computation | async-start | bytes 786432 | tf_op jit(solution)/shard_map/all_to_all | solution.py:467
  42.0 0.0 collective-permute-done.6
  42.0 0.0 collective-permute-done.8
  42.0 1.1 %collective-permute-done.7 = f16[4,48,256]{2,1,0:T(8,128)(2,1)S(1)} collective-permute-done((f16[4,48,256]{2,1,0:T(8,128)(2,1)S(1)}, f16[4,48,256]{2,1,0:T(8,128)(2,1)S(1)}, u32[]{:S(2)}, u32[]{:S(2)}) %collective-permute-start.7) | collective-permute-done | bytes 98336 | tf_op jit(solution)/shard_map/ppermute | solution.py:463
  43.2 0.1 collective-permute-start.9
  43.3 1.0 %collective-permute-start.10 = (f16[4,48,256]{2,1,0:T(8,128)(2,1)S(1)}, f16[4,48,256]{2,1,0:T(8,128)(2,1)S(1)}, u32[]{:S(2)}, u32[]{:S(2)}) collective-permute-start(f16[4,48,256]{2,1,0:T(8,128)(2,1)S(1)} %pad_maximum_fusion.1), channel_id=1, source_target_pairs={{0,2},{1,3},{2,0},{3,1},{4,6},{5,7},{6,4},{7,5},{8,10},{9,11},{10,... | collective-permute-start | bytes 294920 | tf_op jit(solution)/shard_map/ppermute | solution.py:463
  44.4 1.4 %collective-permute-start.11 = (f16[4,48,256]{2,1,0:T(8,128)(2,1)S(1)}, f16[4,48,256]{2,1,0:T(8,128)(2,1)S(1)}, u32[]{:S(2)}, u32[]{:S(2)}) collective-permute-start(f16[4,48,256]{2,1,0:T(8,128)(2,1)S(1)} %pad_maximum_fusion.2), channel_id=1, source_target_pairs={{0,3},{1,0},{2,1},{3,2},{4,7},{5,4},{6,5},{7,6},{8,11},{9,8},{10,9... | collective-permute-start | bytes 294920 | tf_op jit(solution)/shard_map/ppermute | solution.py:463
  45.8 3.9 %collective-permute-done.9 = f16[4,48,256]{2,1,0:T(8,128)(2,1)S(1)} collective-permute-done((f16[4,48,256]{2,1,0:T(8,128)(2,1)S(1)}, f16[4,48,256]{2,1,0:T(8,128)(2,1)S(1)}, u32[]{:S(2)}, u32[]{:S(2)}) %collective-permute-start.9) | collective-permute-done | bytes 98336 | tf_op jit(solution)/shard_map/ppermute | solution.py:463
  49.7 0.3 collective-permute-done.10
  50.0 1.2 %collective-permute-done.11 = f16[4,48,256]{2,1,0:T(8,128)(2,1)S(1)} collective-permute-done((f16[4,48,256]{2,1,0:T(8,128)(2,1)S(1)}, f16[4,48,256]{2,1,0:T(8,128)(2,1)S(1)}, u32[]{:S(2)}, u32[]{:S(2)}) %collective-permute-start.11) | collective-permute-done | bytes 98336 | tf_op jit(solution)/shard_map/ppermute | solution.py:463
  51.2 0.0 copy-done.8
  51.3 3.5 %shard_map.116 = (f32[4,48,256]{2,1,0:T(8,128)S(1)}, f32[4,48,256]{2,1,0:T(8,128)S(1)}, f32[4,48,256]{2,1,0:T(8,128)S(1)}, f32[4,48,256]{2,1,0:T(8,128)S(1)}) custom-call(s32[2]{0:T(128)S(1)} %pad_add_fusion.place.refs_0_, f32[4,48,256]{2,1,0:T(8,128)S(1)} %maximum_convert_fusion.refs_0_, f32[4,48,256]{2,1,0:T(8,128)S(1)} %convert_element_type.53.refs_1_, ...), custom_call_target="tpu_custom_call" | custom-call | flops 2147483648 | bytes 1966088 | tf_op jit(solution)/shard_map/pallas_call | solution.py:204
  54.7 0.0 all-to-all-done
  54.8 3.5 %collective-permute-start.16 = (f16[4,48,256]{2,1,0:T(8,128)(2,1)S(1)}, f16[4,48,256]{2,1,0:T(8,128)(2,1)S(1)}, u32[]{:S(2)}, u32[]{:S(2)}) collective-permute-start(f16[4,48,256]{2,1,0:T(8,128)(2,1)S(1)} %convert_element_type.63), channel_id=1, source_target_pairs={{0,12},{4,0},{8,4},{12,8},{1,13},{5,1},{9,5},{13,9},{2,14},{6,2},{... | collective-permute-start | bytes 294920 | tf_op jit(solution)/shard_map/ppermute | solution.py:463
  58.3 0.0 collective-permute-start.15
  58.3 1.4 %collective-permute-start.14 = (f16[4,48,256]{2,1,0:T(8,128)(2,1)S(1)}, f16[4,48,256]{2,1,0:T(8,128)(2,1)S(1)}, u32[]{:S(2)}, u32[]{:S(2)}) collective-permute-start(f16[4,48,256]{2,1,0:T(8,128)(2,1)S(1)} %convert_element_type.61), channel_id=1, source_target_pairs={{0,4},{4,8},{8,12},{12,0},{1,5},{5,9},{9,13},{13,1},{2,6},{6,10},{... | collective-permute-start | bytes 294920 | tf_op jit(solution)/shard_map/ppermute | solution.py:463
  59.7 0.1 convert_element_type.57.spectra
  59.8 3.3 %shard_map.119 = f32[16,48,256]{2,1,0:T(8,128)S(1)} custom-call(s32[2]{0:T(128)S(1)} %pad_add_fusion.place.refs_0_, f32[16,48,256]{2,1,0:T(8,128)S(1)} %convert_element_type.57.spectra, bf16[2,256,256]{2,1,0:T(8,128)(2,1)S(1)} %copy-done.8, bf16[4,128,128]{2,1,0:T(8,128)(2,1)S(1)} %copy-done.9), custom_call_target="tpu_custom_call" | custom-call | flops 2147483648 | bytes 1966088 | tf_op jit(solution)/shard_map/pallas_call | solution.py:204
  63.1 0.8 convert_element_type.58
  63.9 5.3 %all-to-all-start.1 = ((f16[16,48,256]{2,1,0:T(8,128)(2,1)}), f16[16,48,256]{2,1,0:T(8,128)(2,1)}, u32[]{:S(2)}, u32[]{:S(2)}) async-start(f16[16,48,256]{2,1,0:T(8,128)(2,1)} %convert_element_type.58), calls=%async_computation.1 | async-start | bytes 786432 | tf_op jit(solution)/shard_map/all_to_all | solution.py:467
  69.2 0.0 collective-permute-done.16
  69.3 0.0 collective-permute-done.15
  69.3 0.0 collective-permute-done.14
  69.4 0.4 collective-permute-start.17
  69.8 1.7 %collective-permute-start.18 = (f16[4,48,256]{2,1,0:T(8,128)(2,1)S(1)}, f16[4,48,256]{2,1,0:T(8,128)(2,1)S(1)}, u32[]{:S(2)}, u32[]{:S(2)}) collective-permute-start(f16[4,48,256]{2,1,0:T(8,128)(2,1)S(1)} %pad_maximum_fusion.4), channel_id=1, source_target_pairs={{0,2},{1,3},{2,0},{3,1},{4,6},{5,7},{6,4},{7,5},{8,10},{9,11},{10,... | collective-permute-start | bytes 294920 | tf_op jit(solution)/shard_map/ppermute | solution.py:463
  71.6 1.4 %collective-permute-start.19 = (f16[4,48,256]{2,1,0:T(8,128)(2,1)S(1)}, f16[4,48,256]{2,1,0:T(8,128)(2,1)S(1)}, u32[]{:S(2)}, u32[]{:S(2)}) collective-permute-start(f16[4,48,256]{2,1,0:T(8,128)(2,1)S(1)} %pad_maximum_fusion.5), channel_id=1, source_target_pairs={{0,3},{1,0},{2,1},{3,2},{4,7},{5,4},{6,5},{7,6},{8,11},{9,8},{10,9... | collective-permute-start | bytes 294920 | tf_op jit(solution)/shard_map/ppermute | solution.py:463
  73.0 3.6 %collective-permute-done.17 = f16[4,48,256]{2,1,0:T(8,128)(2,1)S(1)} collective-permute-done((f16[4,48,256]{2,1,0:T(8,128)(2,1)S(1)}, f16[4,48,256]{2,1,0:T(8,128)(2,1)S(1)}, u32[]{:S(2)}, u32[]{:S(2)}) %collective-permute-start.17) | collective-permute-done | bytes 98336 | tf_op jit(solution)/shard_map/ppermute | solution.py:463
  76.6 1.3 %collective-permute-done.18 = f16[4,48,256]{2,1,0:T(8,128)(2,1)S(1)} collective-permute-done((f16[4,48,256]{2,1,0:T(8,128)(2,1)S(1)}, f16[4,48,256]{2,1,0:T(8,128)(2,1)S(1)}, u32[]{:S(2)}, u32[]{:S(2)}) %collective-permute-start.18) | collective-permute-done | bytes 98336 | tf_op jit(solution)/shard_map/ppermute | solution.py:463
  77.9 0.7 collective-permute-done.19
  78.7 1.3 %shard_map.120 = (f32[8,32,512]{2,1,0:T(8,128)S(1)}, f32[16,16,256]{2,1,0:T(8,128)S(1)}) custom-call(s32[2]{0:T(128)S(1)} %pad_add_fusion.place.refs_0_, bf16[2,512,512]{2,1,0:T(8,128)(2,1)S(1)} %copy-done.6, f32[3,8,32,512]{3,2,1,0:T(8,128)S(1)} %copy-done.2, f32[4,48,256]{2,1,0:T(8,128)S(1)} %maximum_convert_fusion.1.refs_0_, ...), custom_call_target="tpu_custom_call" | custom-call | flops 1073741824 | bytes 4194312 | tf_op jit(solution)/shard_map/pallas_call | solution.py:204
  80.0 1.5 %all-to-all-done.1 = f16[16,48,256]{2,1,0:T(8,128)(2,1)} async-done(((f16[16,48,256]{2,1,0:T(8,128)(2,1)}), f16[16,48,256]{2,1,0:T(8,128)(2,1)}, u32[]{:S(2)}, u32[]{:S(2)}) %all-to-all-start.1) | async-done | bytes 393248 | tf_op jit(solution)/shard_map/all_to_all | solution.py:467
  81.5 1.1 %convert_element_type.59.spectra = f32[16,48,256]{2,1,0:T(8,128)S(1)} convert(f16[16,48,256]{2,1,0:T(8,128)(2,1)} %all-to-all-done.1) | non-fusion elementwise | flops 196608 | bytes 1179648 | tf_op jit(solution)/shard_map/convert_element_type | solution.py:577
  82.6 2.8 %shard_map.121 = f32[3,8,32,512]{3,2,1,0:T(8,128)} custom-call(s32[2]{0:T(128)S(1)} %pad_add_fusion.place.refs_0_, f32[3,8,32,512]{3,2,1,0:T(8,128)S(1)} %copy-done.2, f32[16,48,256]{2,1,0:T(8,128)S(1)} %convert_element_type.59.spectra, bf16[2,512,512]{2,1,0:T(8,128)(2,1)S(1)} %copy-done.6, f32[8,32,512]{2,1,0:T(8,128)S(1)} %get-tuple-element.51.updated, ...), custom_call_target="tpu_custom_call" | custom-call | flops 2147483648 | bytes 5767176 | tf_op jit(solution)/shard_map/pallas_call | solution.py:204
  (42 shorter events, 0.6 us)
Async XLA Ops:
  0.7 1.0 %copy-start = (bf16[8,32,512]{2,1,0:T(8,128)(2,1)S(1)}, bf16[8,32,512]{2,1,0:T(8,128)(2,1)}, u32[]{:S(2)}) copy-start(bf16[8,32,512]{2,1,0:T(8,128)(2,1)} %moving.1) | copy-start | bytes 786436
  1.7 0.7 copy-start.1
  3.1 7.8 %collective-permute-start = (bf16[9,32,128]{2,1,0:T(8,128)(2,1)S(1)}, bf16[9,32,128]{2,1,0:T(8,128)(2,1)S(1)}, u32[]{:S(2)}, u32[]{:S(2)}) collective-permute-start(bf16[9,32,128]{2,1,0:T(8,128)(2,1)S(1)} %get-tuple-element.29), channel_id=1, source_target_pairs={{0,4},{4,8},{8,12},{12,0},{1,5},{5,9},{9,13},{13,1},{2,6},{6,10},{... | collective-permute-start | bytes 221192 | tf_op jit(solution)/shard_map/ppermute | solution.py:463
  6.1 7.5 %collective-permute-start.1 = (bf16[9,32,128]{2,1,0:T(8,128)(2,1)S(1)}, bf16[9,32,128]{2,1,0:T(8,128)(2,1)S(1)}, u32[]{:S(2)}, u32[]{:S(2)}) collective-permute-start(bf16[9,32,128]{2,1,0:T(8,128)(2,1)S(1)} %get-tuple-element.30), channel_id=1, source_target_pairs={{0,8},{4,12},{8,0},{12,4},{1,9},{5,13},{9,1},{13,5},{2,10},{6,14},... | collective-permute-start | bytes 221192 | tf_op jit(solution)/shard_map/ppermute | solution.py:463
  8.7 5.2 %collective-permute-start.2 = (bf16[9,32,128]{2,1,0:T(8,128)(2,1)S(1)}, bf16[9,32,128]{2,1,0:T(8,128)(2,1)S(1)}, u32[]{:S(2)}, u32[]{:S(2)}) collective-permute-start(bf16[9,32,128]{2,1,0:T(8,128)(2,1)S(1)} %get-tuple-element.31), channel_id=1, source_target_pairs={{0,12},{4,0},{8,4},{12,8},{1,13},{5,1},{9,5},{13,9},{2,14},{6,2},{... | collective-permute-start | bytes 221192 | tf_op jit(solution)/shard_map/ppermute | solution.py:463
  13.9 13.7 %copy-start.3 = (f32[8,32,512]{2,1,0:T(8,128)S(1)}, f32[8,32,512]{2,1,0:T(8,128)}, u32[]{:S(2)}) copy-start(f32[8,32,512]{2,1,0:T(8,128)} %refs_5_.2) | copy-start | bytes 1572868
  13.9 13.7 %copy-start.4 = (bf16[8,32,512]{2,1,0:T(8,128)(2,1)S(1)}, bf16[8,32,512]{2,1,0:T(8,128)(2,1)}, u32[]{:S(2)}) copy-start(bf16[8,32,512]{2,1,0:T(8,128)(2,1)} %refs_4_.2) | copy-start | bytes 786436
  13.9 13.7 %copy-start.5 = (s32[8,32,4]{1,2,0:T(4,128)S(1)}, s32[8,32,4]{1,2,0:T(4,128)}, u32[]{:S(2)}) copy-start(s32[8,32,4]{1,2,0:T(4,128)} %param.15) | copy-start | bytes 12292
  13.9 13.7 %copy-start.7 = (bf16[2,512,512]{2,1,0:T(8,128)(2,1)S(1)}, bf16[2,512,512]{2,1,0:T(8,128)(2,1)}, u32[]{:S(2)}) copy-start(bf16[2,512,512]{2,1,0:T(8,128)(2,1)} %constant.15.clone.refs_7_.basis) | copy-start | bytes 3145732
  15.7 7.3 %collective-permute-start.3 = (bf16[10,32,128]{2,1,0:T(8,128)(2,1)S(1)}, bf16[10,32,128]{2,1,0:T(8,128)(2,1)S(1)}, u32[]{:S(2)}, u32[]{:S(2)}) collective-permute-start(bf16[10,32,128]{2,1,0:T(8,128)(2,1)S(1)} %get-tuple-element.33), channel_id=1, source_target_pairs={{0,4},{4,8},{8,12},{12,0},{1,5},{5,9},{9,13},{13,1},{2,6},{6,10},{... | collective-permute-start | bytes 245768 | tf_op jit(solution)/shard_map/ppermute | solution.py:463
  17.6 7.6 %collective-permute-start.4 = (bf16[10,32,128]{2,1,0:T(8,128)(2,1)S(1)}, bf16[10,32,128]{2,1,0:T(8,128)(2,1)S(1)}, u32[]{:S(2)}, u32[]{:S(2)}) collective-permute-start(bf16[10,32,128]{2,1,0:T(8,128)(2,1)S(1)} %get-tuple-element.34), channel_id=1, source_target_pairs={{0,8},{4,12},{8,0},{12,4},{1,9},{5,13},{9,1},{13,5},{2,10},{6,14},... | collective-permute-start | bytes 245768 | tf_op jit(solution)/shard_map/ppermute | solution.py:463
  19.5 5.7 %collective-permute-start.5 = (bf16[10,32,128]{2,1,0:T(8,128)(2,1)S(1)}, bf16[10,32,128]{2,1,0:T(8,128)(2,1)S(1)}, u32[]{:S(2)}, u32[]{:S(2)}) collective-permute-start(bf16[10,32,128]{2,1,0:T(8,128)(2,1)S(1)} %get-tuple-element.35), channel_id=1, source_target_pairs={{0,12},{4,0},{8,4},{12,8},{1,13},{5,1},{9,5},{13,9},{2,14},{6,2},{... | collective-permute-start | bytes 245768 | tf_op jit(solution)/shard_map/ppermute | solution.py:463
  25.8 8.7 %collective-permute-start.12 = (bf16[4,8,128]{2,1,0:T(8,128)(2,1)S(1)}, bf16[4,8,128]{2,1,0:T(8,128)(2,1)S(1)}, u32[]{:S(2)}, u32[]{:S(2)}) collective-permute-start(bf16[4,8,128]{2,1,0:T(8,128)(2,1)S(1)} %get-tuple-element.41), channel_id=1, source_target_pairs={{0,1},{1,2},{2,3},{3,0},{4,5},{5,6},{6,7},{7,4},{8,9},{9,10},{10,1... | collective-permute-start | bytes 24584 | tf_op jit(solution)/shard_map/ppermute | solution.py:492
  25.9 8.7 %collective-permute-start.13 = (bf16[4,8,128]{2,1,0:T(8,128)(2,1)S(1)}, bf16[4,8,128]{2,1,0:T(8,128)(2,1)S(1)}, u32[]{:S(2)}, u32[]{:S(2)}) collective-permute-start(bf16[4,8,128]{2,1,0:T(8,128)(2,1)S(1)} %get-tuple-element.42), channel_id=1, source_target_pairs={{1,0},{2,1},{3,2},{0,3},{5,4},{6,5},{7,6},{4,7},{9,8},{10,9},{11,1... | collective-permute-start | bytes 24584 | tf_op jit(solution)/shard_map/ppermute | solution.py:493
  30.7 11.3 %collective-permute-start.6 = (f16[4,48,256]{2,1,0:T(8,128)(2,1)S(1)}, f16[4,48,256]{2,1,0:T(8,128)(2,1)S(1)}, u32[]{:S(2)}, u32[]{:S(2)}) collective-permute-start(f16[4,48,256]{2,1,0:T(8,128)(2,1)S(1)} %get-tuple-element.58), channel_id=1, source_target_pairs={{0,4},{4,8},{8,12},{12,0},{1,5},{5,9},{9,13},{13,1},{2,6},{6,10},{... | collective-permute-start | bytes 294920 | tf_op jit(solution)/shard_map/ppermute | solution.py:463
  32.9 9.1 %collective-permute-start.8 = (f16[4,48,256]{2,1,0:T(8,128)(2,1)S(1)}, f16[4,48,256]{2,1,0:T(8,128)(2,1)S(1)}, u32[]{:S(2)}, u32[]{:S(2)}) collective-permute-start(f16[4,48,256]{2,1,0:T(8,128)(2,1)S(1)} %get-tuple-element.59), channel_id=1, source_target_pairs={{0,12},{4,0},{8,4},{12,8},{1,13},{5,1},{9,5},{13,9},{2,14},{6,2},{... | collective-permute-start | bytes 294920 | tf_op jit(solution)/shard_map/ppermute | solution.py:463
  34.5 8.6 %collective-permute-start.7 = (f16[4,48,256]{2,1,0:T(8,128)(2,1)S(1)}, f16[4,48,256]{2,1,0:T(8,128)(2,1)S(1)}, u32[]{:S(2)}, u32[]{:S(2)}) collective-permute-start(f16[4,48,256]{2,1,0:T(8,128)(2,1)S(1)} %get-tuple-element.60), channel_id=1, source_target_pairs={{0,8},{4,12},{8,0},{12,4},{1,9},{5,13},{9,1},{13,5},{2,10},{6,14},... | collective-permute-start | bytes 294920 | tf_op jit(solution)/shard_map/ppermute | solution.py:463
  36.6 14.6 %copy-start.8 = (bf16[2,256,256]{2,1,0:T(8,128)(2,1)S(1)}, bf16[2,256,256]{2,1,0:T(8,128)(2,1)}, u32[]{:S(2)}) copy-start(bf16[2,256,256]{2,1,0:T(8,128)(2,1)} %constant.16.clone.refs_4_.basis_z) | copy-start | bytes 786436
  36.6 14.6 %copy-start.9 = (bf16[4,128,128]{2,1,0:T(8,128)(2,1)S(1)}, bf16[4,128,128]{2,1,0:T(8,128)(2,1)}, u32[]{:S(2)}) copy-start(bf16[4,128,128]{2,1,0:T(8,128)(2,1)} %constant.17.clone.refs_5_.basis_y) | copy-start | bytes 393220
  36.6 18.1 %all-to-all-start = ((f16[16,48,256]{2,1,0:T(8,128)(2,1)}), f16[16,48,256]{2,1,0:T(8,128)(2,1)S(1)}, u32[]{:S(2)}, u32[]{:S(2)}) async-start(f16[16,48,256]{2,1,0:T(8,128)(2,1)} %convert_element_type.56), calls=%async_computation | async-start | bytes 786432 | tf_op jit(solution)/shard_map/all_to_all | solution.py:467
  43.2 6.5 %collective-permute-start.9 = (f16[4,48,256]{2,1,0:T(8,128)(2,1)S(1)}, f16[4,48,256]{2,1,0:T(8,128)(2,1)S(1)}, u32[]{:S(2)}, u32[]{:S(2)}) collective-permute-start(f16[4,48,256]{2,1,0:T(8,128)(2,1)S(1)} %pad_maximum_fusion), channel_id=1, source_target_pairs={{0,1},{1,2},{2,3},{3,0},{4,5},{5,6},{6,7},{7,4},{8,9},{9,10},{10,1... | collective-permute-start | bytes 294920 | tf_op jit(solution)/shard_map/ppermute | solution.py:463
  43.3 6.6 %collective-permute-start.10 = (f16[4,48,256]{2,1,0:T(8,128)(2,1)S(1)}, f16[4,48,256]{2,1,0:T(8,128)(2,1)S(1)}, u32[]{:S(2)}, u32[]{:S(2)}) collective-permute-start(f16[4,48,256]{2,1,0:T(8,128)(2,1)S(1)} %pad_maximum_fusion.1), channel_id=1, source_target_pairs={{0,2},{1,3},{2,0},{3,1},{4,6},{5,7},{6,4},{7,5},{8,10},{9,11},{10,... | collective-permute-start | bytes 294920 | tf_op jit(solution)/shard_map/ppermute | solution.py:463
  44.4 6.8 %collective-permute-start.11 = (f16[4,48,256]{2,1,0:T(8,128)(2,1)S(1)}, f16[4,48,256]{2,1,0:T(8,128)(2,1)S(1)}, u32[]{:S(2)}, u32[]{:S(2)}) collective-permute-start(f16[4,48,256]{2,1,0:T(8,128)(2,1)S(1)} %pad_maximum_fusion.2), channel_id=1, source_target_pairs={{0,3},{1,0},{2,1},{3,2},{4,7},{5,4},{6,5},{7,6},{8,11},{9,8},{10,9... | collective-permute-start | bytes 294920 | tf_op jit(solution)/shard_map/ppermute | solution.py:463
  54.8 14.4 %collective-permute-start.16 = (f16[4,48,256]{2,1,0:T(8,128)(2,1)S(1)}, f16[4,48,256]{2,1,0:T(8,128)(2,1)S(1)}, u32[]{:S(2)}, u32[]{:S(2)}) collective-permute-start(f16[4,48,256]{2,1,0:T(8,128)(2,1)S(1)} %convert_element_type.63), channel_id=1, source_target_pairs={{0,12},{4,0},{8,4},{12,8},{1,13},{5,1},{9,5},{13,9},{2,14},{6,2},{... | collective-permute-start | bytes 294920 | tf_op jit(solution)/shard_map/ppermute | solution.py:463
  58.3 10.9 %collective-permute-start.15 = (f16[4,48,256]{2,1,0:T(8,128)(2,1)S(1)}, f16[4,48,256]{2,1,0:T(8,128)(2,1)S(1)}, u32[]{:S(2)}, u32[]{:S(2)}) collective-permute-start(f16[4,48,256]{2,1,0:T(8,128)(2,1)S(1)} %convert_element_type.62), channel_id=1, source_target_pairs={{0,8},{4,12},{8,0},{12,4},{1,9},{5,13},{9,1},{13,5},{2,10},{6,14},... | collective-permute-start | bytes 294920 | tf_op jit(solution)/shard_map/ppermute | solution.py:463
  58.3 11.0 %collective-permute-start.14 = (f16[4,48,256]{2,1,0:T(8,128)(2,1)S(1)}, f16[4,48,256]{2,1,0:T(8,128)(2,1)S(1)}, u32[]{:S(2)}, u32[]{:S(2)}) collective-permute-start(f16[4,48,256]{2,1,0:T(8,128)(2,1)S(1)} %convert_element_type.61), channel_id=1, source_target_pairs={{0,4},{4,8},{8,12},{12,0},{1,5},{5,9},{9,13},{13,1},{2,6},{6,10},{... | collective-permute-start | bytes 294920 | tf_op jit(solution)/shard_map/ppermute | solution.py:463
  63.9 14.7 %copy-start.2 = (f32[3,8,32,512]{3,2,1,0:T(8,128)S(1)}, f32[3,8,32,512]{3,2,1,0:T(8,128)}, u32[]{:S(2)}) copy-start(f32[3,8,32,512]{3,2,1,0:T(8,128)} %velocity_in.3) | copy-start | bytes 4718596
  63.9 14.7 %copy-start.6 = (bf16[2,512,512]{2,1,0:T(8,128)(2,1)S(1)}, bf16[2,512,512]{2,1,0:T(8,128)(2,1)}, u32[]{:S(2)}) copy-start(bf16[2,512,512]{2,1,0:T(8,128)(2,1)} %constant.18.clone.basis) | copy-start | bytes 3145732
  63.9 17.5 %all-to-all-start.1 = ((f16[16,48,256]{2,1,0:T(8,128)(2,1)}), f16[16,48,256]{2,1,0:T(8,128)(2,1)}, u32[]{:S(2)}, u32[]{:S(2)}) async-start(f16[16,48,256]{2,1,0:T(8,128)(2,1)} %convert_element_type.58), calls=%async_computation.1 | async-start | bytes 786432 | tf_op jit(solution)/shard_map/all_to_all | solution.py:467
  69.4 7.2 %collective-permute-start.17 = (f16[4,48,256]{2,1,0:T(8,128)(2,1)S(1)}, f16[4,48,256]{2,1,0:T(8,128)(2,1)S(1)}, u32[]{:S(2)}, u32[]{:S(2)}) collective-permute-start(f16[4,48,256]{2,1,0:T(8,128)(2,1)S(1)} %pad_maximum_fusion.3), channel_id=1, source_target_pairs={{0,1},{1,2},{2,3},{3,0},{4,5},{5,6},{6,7},{7,4},{8,9},{9,10},{10,1... | collective-permute-start | bytes 294920 | tf_op jit(solution)/shard_map/ppermute | solution.py:463
  69.8 8.1 %collective-permute-start.18 = (f16[4,48,256]{2,1,0:T(8,128)(2,1)S(1)}, f16[4,48,256]{2,1,0:T(8,128)(2,1)S(1)}, u32[]{:S(2)}, u32[]{:S(2)}) collective-permute-start(f16[4,48,256]{2,1,0:T(8,128)(2,1)S(1)} %pad_maximum_fusion.4), channel_id=1, source_target_pairs={{0,2},{1,3},{2,0},{3,1},{4,6},{5,7},{6,4},{7,5},{8,10},{9,11},{10,... | collective-permute-start | bytes 294920 | tf_op jit(solution)/shard_map/ppermute | solution.py:463
  71.6 7.1 %collective-permute-start.19 = (f16[4,48,256]{2,1,0:T(8,128)(2,1)S(1)}, f16[4,48,256]{2,1,0:T(8,128)(2,1)S(1)}, u32[]{:S(2)}, u32[]{:S(2)}) collective-permute-start(f16[4,48,256]{2,1,0:T(8,128)(2,1)S(1)} %pad_maximum_fusion.5), channel_id=1, source_target_pairs={{0,3},{1,0},{2,1},{3,2},{4,7},{5,4},{6,5},{7,6},{8,11},{9,8},{10,9... | collective-permute-start | bytes 294920 | tf_op jit(solution)/shard_map/ppermute | solution.py:463

commit v7 on v6

--- a/solution.py
+++ b/solution.py
@@ -237,47 +237,44 @@
     me = place[0]
     total = slabs * planes
     group = 4
+
+    def name(other, plane):
+        number = (around(me - other, slabs) * planes).astype(jnp.float32) + float(plane)
+        return jnp.full((rows, BLOCK), number, jnp.float32).astype(jnp.bfloat16)
+
     for step in range(slabs):
         first = around(me - step, slabs) * planes
         names = received[step][planes].astype(jnp.float32)
         for start in range(0, planes, group):
             wanted = [
-                jnp.broadcast_to(names[:, z : z + 1], (rows, BLOCK)) for z in range(start, start + group)
+                jnp.broadcast_to(names[:, z : z + 1], (rows, BLOCK)).astype(jnp.bfloat16)
+                for z in range(start, start + group)
             ]
-            found = [jnp.zeros((rows, BLOCK), jnp.float32) for _ in range(group)]
+            found = [jnp.zeros((rows, BLOCK), jnp.bfloat16) for _ in range(group)]
             for other in range(slabs):
-                base = (around(me - other, slabs) * planes).astype(jnp.float32)
                 for plane in range(planes):
-                    values = received[other][plane].astype(jnp.float32)
-                    found = [
-                        jnp.where(w == base + float(plane), values, f) for w, f in zip(wanted, found)
-                    ]
+                    values = received[other][plane]
+                    own = name(other, plane)
+                    found = [jnp.where(w == own, values, f) for w, f in zip(wanted, found)]
             for z in range(group):
-                picked[first + start + z] = found[z].astype(jnp.bfloat16)
+                picked[first + start + z] = found[z]
     for step, send in enumerate(sends):
         first = around(me + step, slabs) * planes
         for k in range(planes + 2):
             send[k] = picked[around(first + (k - 1), total)]
 
 
-def edge_rows_kernel(slabs, *refs):
-    received, (first, last) = refs[1 : 1 + slabs], refs[1 + slabs :]
-    planes, rows, _ = received[0].shape
-    for d in range(slabs):
-        cells = [received[d][z].astype(jnp.float32) for z in range(1, planes - 1)]
-        first[d] = jnp.concatenate([c[0:1] for c in cells], axis=0).astype(jnp.bfloat16)
-        last[d] = jnp.concatenate([c[rows - 1 : rows] for c in cells], axis=0).astype(jnp.bfloat16)
-
-
 def force_zx_kernel(slabs, subs, place, *refs):
     received, refs = refs[:slabs], refs[slabs:]
-    template, stiffness, tissue, basis, warped, image, weight, spectra, kept, planes_of, wide = refs
+    template, stiffness, tissue, basis, first, last, image, weight, spectra, kept, planes_of, wide = refs
     planes, rows, x_length = template.shape
     blocks = x_length // BLOCK
     for step in range(slabs):
         block = pl.ds(pl.multiple_of(around(place[0] - step, slabs) * BLOCK, BLOCK), BLOCK)
         planes_of[:, :, block] = received[step][...].astype(jnp.float32)
-        warped[:, :, block] = received[step][1:-1]
+    for edge, row in ((first, 0), (last, rows - 1)):
+        own = [planes_of[z + 1, row : row + 1, :] for z in range(planes)]
+        edge[...] = jnp.concatenate(own * 2, axis=0).astype(jnp.bfloat16)
     marks = by_row(tissue, rows)
     forces = [[], []]
     for z in range(planes):
@@ -301,25 +298,22 @@
     half = part // 2
     for d in range(slabs):
         for e in range(subs):
-            first = (around(place[0] + d, slabs) * subs + around(place[1] + e, subs)) * part
-            spectra[d, e, :part] = wide[0, pl.ds(pl.multiple_of(first, part), part), :]
-            spectra[d, e, part:] = wide[1, pl.ds(pl.multiple_of(first + half, half), half), :]
+            start = (around(place[0] + d, slabs) * subs + around(place[1] + e, subs)) * part
+            spectra[d, e, :part] = wide[0, pl.ds(pl.multiple_of(start, part), part), :]
+            spectra[d, e, part:] = wide[1, pl.ds(pl.multiple_of(start + half, half), half), :]
     for k in range(slabs * subs):
         kept[k] = wide[1, k * part : k * part + half, :]
 
 
-def force_y_kernel(slabs, place, above, below, image, weight, basis, kept, spectra, edges):
+def force_y_kernel(above, below, image, weight, basis, kept, spectra):
     planes, rows, x_length = image.shape
-    for step in range(slabs):
-        block = pl.ds(pl.multiple_of(around(place[0] - step, slabs) * BLOCK, BLOCK), BLOCK)
-        edges[0, :, block] = above[step].astype(jnp.float32)
-        edges[1, :, block] = below[step].astype(jnp.float32)
+    edges = above[...].astype(jnp.float32), below[...].astype(jnp.float32)
     row = lax.broadcasted_iota(jnp.int32, (rows, x_length), 0)
     force = []
     for z in range(planes):
         here = image[z]
-        before = jnp.where(row == 0, edges[0, z : z + 1, :], pltpu.roll(here, 1, 0))
-        after = jnp.where(row == rows - 1, edges[1, z : z + 1, :], pltpu.roll(here, rows - 1, 0))
+        before = jnp.where(row == 0, edges[0][z : z + 1], pltpu.roll(here, 1, 0))
+        after = jnp.where(row == rows - 1, edges[1][z : z + 1], pltpu.roll(here, rows - 1, 0))
         force.append(weight[z] * (after - before))
     devices = spectra.shape[0]
     part = x_length // devices
@@ -328,64 +322,83 @@
     spectra[:, part:, :] = kept[...]
 
 
-def solve(first, x_length, offsets, subs, spectra, basis_z, basis_y, cells):
+def swap_blocks(values):
+    width = values[0].shape[1]
+    lane = lax.broadcasted_iota(jnp.int32, values[0].shape, 1)
+    lower, even = lane < width // 2, lax.rem(lane // (width // 4), 2) == 0
+
+    def turn(own, count):
+        return pltpu.roll(own, count * (width // 4), 1)
+
+    a, b, c, d = values
+    a, c = jnp.where(lower, a, turn(c, 2)), jnp.where(lower, turn(a, 2), c)
+    b, d = jnp.where(lower, b, turn(d, 2)), jnp.where(lower, turn(b, 2), d)
+    return [
+        jnp.where(even, a, turn(b, 1)),
+        jnp.where(even, turn(a, 3), b),
+        jnp.where(even, c, turn(d, 1)),
+        jnp.where(even, turn(c, 3), d),
+    ]
+
+
+def solve(first, x_length, offsets, subs, spectra, basis_z, basis_y, out, cells):
     devices, used, area = spectra.shape
     total_z, _, total_y = cells.shape
     slabs = devices // subs
     planes, rows = total_z // slabs, total_y // subs
+    fold = total_y // rows
     tile = 8
 
-    def along_y(k):
+    def along_y(k, values):
         high, low = basis_y[2 * k], basis_y[2 * k + 1]
-        both = jnp.concatenate([high, high], axis=0)
-
-        def run(values):
-            parts = split(values)
-            sums = jnp.dot(jnp.concatenate(parts, axis=1), both, preferred_element_type=jnp.float32)
-            return sums + jnp.dot(parts[0], low, preferred_element_type=jnp.float32)
-
-        return run
-
-    run = along_y(0)
+        four = jnp.concatenate(
+            [jnp.concatenate([high, low], axis=1), jnp.concatenate([high, jnp.zeros_like(low)], axis=1)], axis=0
+        )
+        sums = jnp.dot(jnp.concatenate(split(values), axis=1), four, preferred_element_type=jnp.float32)
+        return sums[:, :total_y] + sums[:, total_y:]
+
+    def along_z(k, values):
+        high, low = basis_z[2 * k], basis_z[2 * k + 1]
+        parts = split(values)
+        return jnp.dot(
+            jnp.concatenate([high, high, low], axis=1),
+            jnp.concatenate([parts[0], parts[1], parts[0]], axis=0),
+            preferred_element_type=jnp.float32,
+        )
+
     for s in range(slabs):
         own = []
-        for z in range(planes):
-            lanes = slice(z * rows, (z + 1) * rows)
-            own.append(jnp.concatenate([spectra[s * subs + q][:, lanes] for q in range(subs)], axis=1))
-        own = run(jnp.concatenate(own, axis=0))
+        for f in range(0, planes // fold):
+            lanes = slice(f * total_y, (f + 1) * total_y)
+            own += swap_blocks([spectra[s * subs + q][:, lanes] for q in range(subs)])
+        own = along_y(0, jnp.concatenate(own, axis=0))
         cells[s * planes : (s + 1) * planes] = own.reshape(planes, used, total_y)
     index = lax.broadcasted_iota(jnp.int32, (total_z * tile, 1), 0)
     z_sq = wave_sq(index // tile, total_z)
     y_sq = wave_sq(lax.broadcasted_iota(jnp.int32, (1, total_y), 1), total_y)
-    table = (basis_z[0], basis_z[1])
-    for g in range(0, used, 2 * tile):
-        own, scale = [], []
-        for start in (g, g + tile):
-            own.append(cells[:, start : start + tile, :].reshape(total_z * tile, total_y))
-            x_sq = wave_sq(first + offsets[start // tile] + lax.rem(index, tile), x_length)
-            scale.append((z_sq + x_sq + y_sq) * 256.0 + 1.0)
-        own = times(table, split(jnp.concatenate(own, axis=1)), ((1,), (0,)))
-        own = own / jnp.concatenate(scale, axis=1)
-        own = times(table, split(own), ((0,), (0,)))
-        for k, start in enumerate((g, g + tile)):
-            half = own[:, k * total_y : (k + 1) * total_y]
-            cells[:, start : start + tile, :] = half.reshape(total_z, tile, total_y)
-    run = along_y(1)
+    own, scale = [], []
+    for start in range(0, used, tile):
+        own.append(cells[:, start : start + tile, :].reshape(total_z * tile, total_y))
+        x_sq = wave_sq(first + offsets[start // tile] + lax.rem(index, tile), x_length)
+        scale.append((z_sq + x_sq + y_sq) * 256.0 + 1.0)
+    own = along_z(0, jnp.concatenate(own, axis=1))
+    own = along_z(1, own / jnp.concatenate(scale, axis=1))
+    for k, start in enumerate(range(0, used, tile)):
+        part = own[:, k * total_y : (k + 1) * total_y]
+        cells[:, start : start + tile, :] = part.reshape(total_z, tile, total_y)
     for s in range(slabs):
-        own = run(cells[s * planes : (s + 1) * planes].reshape(planes * used, total_y))
-        for q in range(subs):
-            lanes = slice(q * rows, (q + 1) * rows)
-            spectra[s * subs + q] = jnp.concatenate(
-                [own[z * used : (z + 1) * used, lanes] for z in range(planes)], axis=1
-            )
+        own = along_y(1, cells[s * planes : (s + 1) * planes].reshape(planes * used, total_y))
+        for f in range(0, planes // fold):
+            blocks = swap_blocks([own[z * used : (z + 1) * used] for z in range(f * fold, (f + 1) * fold)])
+            for q in range(subs):
+                out[s * subs + q, :, f * total_y : (f + 1) * total_y] = blocks[q]
 
 
 def solve_yx_kernel(subs, x_length, place, spectra, basis_z, basis_y, out, cells):
     devices = out.shape[0]
     part = x_length // devices
     offsets = list(range(0, part, 8)) + list(range(0, part // 2, 8))
-    out[...] = spectra[...]
-    solve((place[0] * subs + place[1]) * part, x_length, offsets, subs, out, basis_z, basis_y, cells)
+    solve((place[0] * subs + place[1]) * part, x_length, offsets, subs, spectra, basis_z, basis_y, out, cells)
 
 
 def solve_zx_kernel(slabs, subs, x_length, place, *refs):
@@ -396,7 +409,7 @@
     for e in range(subs):
         for d in range(slabs):
             spectra[around(place[0] - d, slabs) * subs + around(place[1] - e, subs)] = received[e][d]
-    solve((place[0] * subs + place[1]) * part, x_length, offsets, subs, spectra, basis_z, basis_y, cells)
+    solve((place[0] * subs + place[1]) * part, x_length, offsets, subs, spectra, basis_z, basis_y, spectra, cells)
     for d in range(slabs):
         for e in range(subs):
             sends[d][e] = spectra[around(place[0] + d, slabs) * subs + around(place[1] + e, subs)]
@@ -407,41 +420,40 @@
     return 0.5 * (velocity - 32.0 * smoothed.reshape(velocity.shape))
 
 
-def update_z_kernel(slabs, subs, place, basis, velocity_in, *refs):
-    received, (out, kept, gathered, velocity, done) = refs[:subs], refs[subs:]
+def update_z_kernel(slabs, subs, place, basis, velocity, *refs):
+    received, (out, kept, gathered) = refs[:subs], refs[subs:]
     half = kept.shape[1]
     part = 2 * half
-    arriving = pltpu.make_async_copy(velocity_in.at[0], velocity, done.at[0])
-    arriving.start()
     for e in range(subs):
         for d in range(slabs):
             index = around(place[0] - d, slabs) * subs + around(place[1] - e, subs)
             gathered[pl.ds(pl.multiple_of(index * part, part), part), :] = received[e][d, :part]
             kept[index] = received[e][d, part:]
-    arriving.wait()
-    out[...] = moved(gathered[...], velocity[...], basis)
-
-
-def update_kernel(place, velocity_in, spectra, basis, updated, kept, out, velocity, result, done):
+    out[...] = moved(gathered[...], velocity[0], basis)
+
+
+def update_kernel(spectra, basis, velocity, updated, kept, out, result, done):
     devices, half, area = kept.shape
     part = 2 * half
-    arriving = [pltpu.make_async_copy(velocity_in.at[a], velocity.at[a - 1], done.at[a]) for a in (1, 2)]
-    leaving = [pltpu.make_async_copy(result.at[a - 1], out.at[a], done.at[2 + a]) for a in (1, 2)]
-    leaving.append(pltpu.make_async_copy(updated, out.at[0], done.at[0]))
-    leaving[2].start()
-    for copy in arriving:
-        copy.start()
+    leaving = [pltpu.make_async_copy(updated, out.at[0], done.at[0])]
+    leaving[0].start()
     for a in range(2):
         if a:
             own = jnp.concatenate([spectra[:, part:, :], kept[...]], axis=1)
         else:
             own = spectra[:, :part, :]
-        own = own.reshape(devices * part, area)
-        arriving[a].wait()
-        result[a] = moved(own, velocity[a], basis)
-        leaving[a].start()
+        result[a] = moved(own.reshape(devices * part, area), velocity[a + 1], basis)
+        leaving.append(pltpu.make_async_copy(result.at[a], out.at[a + 1], done.at[a + 1]))
+        leaving[-1].start()
     for copy in leaving:
         copy.wait()
+
+
+def place_kernel(slabs, place, *refs):
+    received, warped = refs[:slabs], refs[slabs]
+    for step in range(slabs):
+        block = pl.ds(pl.multiple_of(around(place[0] - step, slabs) * BLOCK, BLOCK), BLOCK)
+        warped[:, :, block] = received[step][1:-1]
 
 
 def local_blocks(velocity, template, moving, stiffness, fetch_plane, tissue):
@@ -483,22 +495,16 @@
         flops=1 << 30,
     )
     received = scatter(sends, "slab")
-    first, last = call(
-        functools.partial(edge_rows_kernel, slabs),
-        [shape((slabs, planes, BLOCK), bf16)] * 2,
-        place,
-        *received,
-    )
-    above = lax.ppermute(last, "sub", [(i, (i + 1) % subs) for i in range(subs)])
-    below = lax.ppermute(first, "sub", [((i + 1) % subs, i) for i in range(subs)])
     basis_x = in_two(8.0 * real_basis(x_length))
-    basis_z = in_two(np.kron(real_basis(total_z), np.eye(8)))
+    basis_z = np.kron(real_basis(total_z), np.eye(8))
+    basis_z = np.concatenate([in_two(basis_z), in_two(basis_z.T)])
     basis_y = np.concatenate([in_two(real_basis(total_y).T), in_two(real_basis(total_y))])
     each = part + part // 2
-    warped, image, weight, chain, kept = call(
+    first, last, image, weight, chain, kept = call(
         functools.partial(force_zx_kernel, slabs, subs),
         [
-            shape(moving.shape, bf16),
+            shape((2 * planes, x_length), bf16),
+            shape((2 * planes, x_length), bf16),
             shape(moving.shape),
             shape(moving.shape),
             shape((slabs, subs, each, area)),
@@ -513,20 +519,22 @@
         scratch=[pltpu.VMEM((planes + 2, rows, x_length), f32), pltpu.VMEM((2, x_length, area), f32)],
         flops=3 << 30,
     )
+    above = lax.ppermute(last, "sub", [(i, (i + 1) % subs) for i in range(subs)])
+    below = lax.ppermute(first, "sub", [((i + 1) % subs, i) for i in range(subs)])
     chain = chain.astype(f16)
     chain = scatter([chain[d] for d in range(slabs)], "slab")
+    later, *chain = lax.optimization_barrier((place, *chain))
+    warped = call(functools.partial(place_kernel, slabs), shape(moving.shape, bf16), later, *received)
     chain = scatter([jnp.stack([r[e] for r in chain]) for e in range(subs)], "sub")
     spectra = call(
-        functools.partial(force_y_kernel, slabs),
+        force_y_kernel,
         shape((devices, each, area)),
-        place,
         above,
         below,
         image,
         weight,
         basis_x,
         kept,
-        scratch=[pltpu.VMEM((2, planes, x_length), f32)],
         flops=2 << 30,
     )
     spectra = exchange(spectra.astype(f16))
@@ -540,7 +548,7 @@
         scratch=[pltpu.VMEM((devices, each, area), f32), pltpu.VMEM((total_z, each, total_y), f32)],
         flops=2 << 30,
     )
-    chain, spectra = lax.optimization_barrier((chain, spectra))
+    chain, spectra, warped = lax.optimization_barrier((chain, spectra, warped))
     chain = scatter([r.astype(f16) for r in chain], "slab")
     chain = scatter([jnp.stack([r[e] for r in chain]) for e in range(subs)], "sub")
     spectra = call(
@@ -560,29 +568,20 @@
         [shape(moving.shape), shape((devices, part // 2, area))],
         place,
         basis_x,
-        (velocity,),
+        velocity,
         *[r.astype(f32) for r in chain],
-        scratch=[
-            pltpu.VMEM((x_length, area), f32),
-            pltpu.VMEM(moving.shape, f32),
-            pltpu.SemaphoreType.DMA((1,)),
-        ],
+        scratch=[pltpu.VMEM((x_length, area), f32)],
         flops=1 << 30,
     )
     new_velocity = call(
         update_kernel,
         shape(velocity.shape),
-        place,
-        (velocity,),
         spectra.astype(f32),
         basis_x,
+        velocity,
         updated,
         kept,
-        scratch=[
-            pltpu.VMEM((2,) + moving.shape, f32),
-            pltpu.VMEM((2,) + moving.shape, f32),
-            pltpu.SemaphoreType.DMA((5,)),
-        ],
+        scratch=[pltpu.VMEM((2,) + moving.shape, f32), pltpu.SemaphoreType.DMA((3,))],
         flops=2 << 30,
         stays=1,
     )
@@ -598,6 +597,7 @@
         and planes * slabs * 8 == 256
         and rows % 16 == 0
         and rows * subs == BLOCK
+        and subs == 4
         and x_length % (32 * slabs * subs) == 0
     )
     run = local_blocks if fits else local_general

time: 85.8 us -> 81.6 us (0.951)
  Pallas kernels: 18.1 us -> 14.7 us
  waiting for transfers between devices: 22.4 us -> 21.3 us
    pallas_call x9, Pallas kernels: 18.1 us -> 14.7 us  [call(): pl.pallas_call(kernel, out_shape=out_shape, in_specs=places, out_specs=ja...]
    ppermute x18, waiting for transfers between devices: 21 us -> 19.8 us  [scatter(): lax.ppermute(sends[d], axis, [(i, (i + d) % count) for i in range(count)])]
  transfers between devices with their start and end apart: 22 -> 22, of which waited for: 13 -> 13; matrix products, arithmetic and copies ran while one was open for 3% -> 3% of each run, Pallas kernels for 14% -> 11%
where the time goes in v7:
time: 81.6 us; the launch traced here: 81.2 us
  starting transfers between devices  38.9 us (48%)
  waiting for transfers between devices  21.3 us (26%)
  Pallas kernels  14.7 us (18%)
  other arithmetic  3.33 us (4%)
  local copies, waits for them, and re-layouts  1.94 us (2%)
  between operations  0.98 us (1%)
    ppermute x18, starting transfers between devices, scatter(): lax.ppermute(sends[d], axis, [(i, (i + d) % count) for i in range(count)])  25.9 us
    ppermute x18, waiting for transfers between devices, scatter(): lax.ppermute(sends[d], axis, [(i, (i + d) % count) for i in range(count)])  19.8 us
    pallas_call x9, Pallas kernels, call(): pl.pallas_call(kernel, out_shape=out_shape, in_specs=places, out_specs=ja...  14.7 us
    all_to_all x2, starting transfers between devices, exchange(): lax.all_to_all(values, ('slab', 'sub'), split_axis=0, concat_axis=0, tile...  11.2 us
    ppermute x1, starting transfers between devices, local_blocks(): lax.ppermute(first, 'sub', [((i + 1) % subs, i) for i in range(subs)])  1.73 us
    unnamed x20, local copies, waits for them, and re-layouts  1.7 us
  transfers between devices with their start and end apart: 22, of which 13 were waited for; matrix products, arithmetic and copies ran while one was open for 3% of the time, Pallas kernels for 11%

profile of v7, /device:TPU:0, one launch (start us, length us, event | category | flops | bytes accessed | tf_op | source)
XLA Modules:
  0.0 81.2 jit_solution(4169757303726918304)
XLA Ops:
  0.6 0.1 pad_add_fusion.place
  0.7 0.9 %copy-done = bf16[8,32,512]{2,1,0:T(8,128)(2,1)S(1)} copy-done((bf16[8,32,512]{2,1,0:T(8,128)(2,1)S(1)}, bf16[8,32,512]{2,1,0:T(8,128)(2,1)}, u32[]{:S(2)}) %copy-start) | copy-done | bytes 262168
  1.7 0.7 copy-done.1
  2.4 0.7 shard_map.113
  3.1 3.0 %collective-permute-start = (bf16[9,32,128]{2,1,0:T(8,128)(2,1)S(1)}, bf16[9,32,128]{2,1,0:T(8,128)(2,1)S(1)}, u32[]{:S(2)}, u32[]{:S(2)}) collective-permute-start(bf16[9,32,128]{2,1,0:T(8,128)(2,1)S(1)} %get-tuple-element.34), channel_id=1, source_target_pairs={{0,4},{4,8},{8,12},{12,0},{1,5},{5,9},{9,13},{13,1},{2,6},{6,10},{... | collective-permute-start | bytes 221192 | tf_op jit(solution)/shard_map/ppermute | solution.py:475
  6.1 2.6 %collective-permute-start.1 = (bf16[9,32,128]{2,1,0:T(8,128)(2,1)S(1)}, bf16[9,32,128]{2,1,0:T(8,128)(2,1)S(1)}, u32[]{:S(2)}, u32[]{:S(2)}) collective-permute-start(bf16[9,32,128]{2,1,0:T(8,128)(2,1)S(1)} %get-tuple-element.35), channel_id=1, source_target_pairs={{0,8},{4,12},{8,0},{12,4},{1,9},{5,13},{9,1},{13,5},{2,10},{6,14},... | collective-permute-start | bytes 221192 | tf_op jit(solution)/shard_map/ppermute | solution.py:475
  8.7 1.3 %collective-permute-start.2 = (bf16[9,32,128]{2,1,0:T(8,128)(2,1)S(1)}, bf16[9,32,128]{2,1,0:T(8,128)(2,1)S(1)}, u32[]{:S(2)}, u32[]{:S(2)}) collective-permute-start(bf16[9,32,128]{2,1,0:T(8,128)(2,1)S(1)} %get-tuple-element.36), channel_id=1, source_target_pairs={{0,12},{4,0},{8,4},{12,8},{1,13},{5,1},{9,5},{13,9},{2,14},{6,2},{... | collective-permute-start | bytes 221192 | tf_op jit(solution)/shard_map/ppermute | solution.py:475
  10.0 0.8 %collective-permute-done.refs_1_ = bf16[9,32,128]{2,1,0:T(8,128)(2,1)S(1)} collective-permute-done((bf16[9,32,128]{2,1,0:T(8,128)(2,1)S(1)}, bf16[9,32,128]{2,1,0:T(8,128)(2,1)S(1)}, u32[]{:S(2)}, u32[]{:S(2)}) %collective-permute-start) | collective-permute-done | bytes 73760 | tf_op jit(solution)/shard_map/ppermute | solution.py:475
  10.9 2.8 %collective-permute-done.1.refs_2_ = bf16[9,32,128]{2,1,0:T(8,128)(2,1)S(1)} collective-permute-done((bf16[9,32,128]{2,1,0:T(8,128)(2,1)S(1)}, bf16[9,32,128]{2,1,0:T(8,128)(2,1)S(1)}, u32[]{:S(2)}, u32[]{:S(2)}) %collective-permute-start.1) | collective-permute-done | bytes 73760 | tf_op jit(solution)/shard_map/ppermute | solution.py:475
  13.7 0.2 collective-permute-done.2.refs_3_
  13.9 1.3 %shard_map.114 = (bf16[10,32,128]{2,1,0:T(8,128)(2,1)S(1)}, bf16[10,32,128]{2,1,0:T(8,128)(2,1)S(1)}, bf16[10,32,128]{2,1,0:T(8,128)(2,1)S(1)}, bf16[10,32,128]{2,1,0:T(8,128)(2,1)S(1)}) custom-call(s32[2]{0:T(128)S(1)} %pad_add_fusion.place, bf16[9,32,128]{2,1,0:T(8,128)(2,1)S(1)} %get-tuple-element.33.refs_0_, ...), custom_call_target="tpu_custom_call" | custom-call | flops 1073741824 | bytes 622600 | tf_op jit(solution)/shard_map/pallas_call | solution.py:204
  15.2 1.9 %collective-permute-start.3 = (bf16[10,32,128]{2,1,0:T(8,128)(2,1)S(1)}, bf16[10,32,128]{2,1,0:T(8,128)(2,1)S(1)}, u32[]{:S(2)}, u32[]{:S(2)}) collective-permute-start(bf16[10,32,128]{2,1,0:T(8,128)(2,1)S(1)} %get-tuple-element.38), channel_id=1, source_target_pairs={{0,4},{4,8},{8,12},{12,0},{1,5},{5,9},{9,13},{13,1},{2,6},{6,10},{... | collective-permute-start | bytes 245768 | tf_op jit(solution)/shard_map/ppermute | solution.py:475
  17.1 1.9 %collective-permute-start.4 = (bf16[10,32,128]{2,1,0:T(8,128)(2,1)S(1)}, bf16[10,32,128]{2,1,0:T(8,128)(2,1)S(1)}, u32[]{:S(2)}, u32[]{:S(2)}) collective-permute-start(bf16[10,32,128]{2,1,0:T(8,128)(2,1)S(1)} %get-tuple-element.39), channel_id=1, source_target_pairs={{0,8},{4,12},{8,0},{12,4},{1,9},{5,13},{9,1},{13,5},{2,10},{6,14},... | collective-permute-start | bytes 245768 | tf_op jit(solution)/shard_map/ppermute | solution.py:475
  19.0 0.7 collective-permute-start.5
  19.7 2.7 %collective-permute-done.3.refs_1_ = bf16[10,32,128]{2,1,0:T(8,128)(2,1)S(1)} collective-permute-done((bf16[10,32,128]{2,1,0:T(8,128)(2,1)S(1)}, bf16[10,32,128]{2,1,0:T(8,128)(2,1)S(1)}, u32[]{:S(2)}, u32[]{:S(2)}) %collective-permute-start.3) | collective-permute-done | bytes 81952 | tf_op jit(solution)/shard_map/ppermute | solution.py:475
  22.4 2.3 %collective-permute-done.4.refs_2_ = bf16[10,32,128]{2,1,0:T(8,128)(2,1)S(1)} collective-permute-done((bf16[10,32,128]{2,1,0:T(8,128)(2,1)S(1)}, bf16[10,32,128]{2,1,0:T(8,128)(2,1)S(1)}, u32[]{:S(2)}, u32[]{:S(2)}) %collective-permute-start.4) | collective-permute-done | bytes 81952 | tf_op jit(solution)/shard_map/ppermute | solution.py:475
  24.7 0.0 collective-permute-done.5.refs_3_
  24.7 0.0 copy-done.3
  24.7 0.0 copy-done.4
  24.7 2.2 %shard_map.115 = (bf16[16,512]{1,0:T(8,128)(2,1)S(1)}, bf16[16,512]{1,0:T(8,128)(2,1)S(1)}, f32[8,32,512]{2,1,0:T(8,128)S(1)}, f32[8,32,512]{2,1,0:T(8,128)S(1)}...) custom-call(s32[2]{0:T(128)S(1)} %pad_add_fusion.place, bf16[10,32,128]{2,1,0:T(8,128)(2,1)S(1)} %get-tuple-element.37.refs_0_, ...), custom_call_target="tpu_custom_call" | custom-call | flops 3221225472 | bytes 4296712 | tf_op jit(solution)/shard_map/pallas_call | solution.py:204
  26.9 0.1 convert_element_type.51
  27.0 0.1 collective-permute-start.12
  27.0 1.7 %collective-permute-start.13 = (bf16[16,512]{1,0:T(8,128)(2,1)S(1)}, bf16[16,512]{1,0:T(8,128)(2,1)S(1)}, u32[]{:S(2)}, u32[]{:S(2)}) collective-permute-start(bf16[16,512]{1,0:T(8,128)(2,1)S(1)} %get-tuple-element.51), channel_id=1, source_target_pairs={{1,0},{2,1},{3,2},{0,3},{5,4},{6,5},{7,6},{4,7},{9,8},{10,9},{11,1... | collective-permute-start | bytes 49160 | tf_op jit(solution)/shard_map/ppermute | solution.py:523
  28.8 0.1 slice_bitcast_fusion
  28.8 2.7 %collective-permute-start.8 = (f16[4,48,256]{2,1,0:T(8,128)(2,1)S(1)}, f16[4,48,256]{2,1,0:T(8,128)(2,1)S(1)}, u32[]{:S(2)}, u32[]{:S(2)}) collective-permute-start(f16[4,48,256]{2,1,0:T(8,128)(2,1)S(1)} %get-tuple-element.64), channel_id=1, source_target_pairs={{0,12},{4,0},{8,4},{12,8},{1,13},{5,1},{9,5},{13,9},{2,14},{6,2},{... | collective-permute-start | bytes 294920 | tf_op jit(solution)/shard_map/ppermute | solution.py:475
  31.6 1.0 %collective-permute-start.7 = (f16[4,48,256]{2,1,0:T(8,128)(2,1)S(1)}, f16[4,48,256]{2,1,0:T(8,128)(2,1)S(1)}, u32[]{:S(2)}, u32[]{:S(2)}) collective-permute-start(f16[4,48,256]{2,1,0:T(8,128)(2,1)S(1)} %get-tuple-element.65), channel_id=1, source_target_pairs={{0,8},{4,12},{8,0},{12,4},{1,9},{5,13},{9,1},{13,5},{2,10},{6,14},... | collective-permute-start | bytes 294920 | tf_op jit(solution)/shard_map/ppermute | solution.py:475
  32.6 0.0 collective-permute-start.6
  32.6 0.0 collective-permute-done.12.above
  32.6 0.0 collective-permute-done.13.below
  32.6 0.7 shard_map.117
  33.3 0.8 convert_element_type.56
  34.1 5.9 %all-to-all-start = ((f16[16,48,256]{2,1,0:T(8,128)(2,1)}), f16[16,48,256]{2,1,0:T(8,128)(2,1)S(1)}, u32[]{:S(2)}, u32[]{:S(2)}) async-start(f16[16,48,256]{2,1,0:T(8,128)(2,1)} %convert_element_type.56), calls=%async_computation | async-start | bytes 786432 | tf_op jit(solution)/shard_map/all_to_all | solution.py:479
  40.1 0.0 collective-permute-done.8
  40.1 1.2 %collective-permute-done.7 = f16[4,48,256]{2,1,0:T(8,128)(2,1)S(1)} collective-permute-done((f16[4,48,256]{2,1,0:T(8,128)(2,1)S(1)}, f16[4,48,256]{2,1,0:T(8,128)(2,1)S(1)}, u32[]{:S(2)}, u32[]{:S(2)}) %collective-permute-start.7) | collective-permute-done | bytes 98336 | tf_op jit(solution)/shard_map/ppermute | solution.py:475
  41.3 0.0 collective-permute-done.6
  41.4 0.1 collective-permute-start.9
  41.6 0.9 %collective-permute-start.10 = (f16[4,48,256]{2,1,0:T(8,128)(2,1)S(1)}, f16[4,48,256]{2,1,0:T(8,128)(2,1)S(1)}, u32[]{:S(2)}, u32[]{:S(2)}) collective-permute-start(f16[4,48,256]{2,1,0:T(8,128)(2,1)S(1)} %pad_maximum_fusion.1), channel_id=1, source_target_pairs={{0,2},{1,3},{2,0},{3,1},{4,6},{5,7},{6,4},{7,5},{8,10},{9,11},{10,... | collective-permute-start | bytes 294920 | tf_op jit(solution)/shard_map/ppermute | solution.py:475
  42.5 1.5 %collective-permute-start.11 = (f16[4,48,256]{2,1,0:T(8,128)(2,1)S(1)}, f16[4,48,256]{2,1,0:T(8,128)(2,1)S(1)}, u32[]{:S(2)}, u32[]{:S(2)}) collective-permute-start(f16[4,48,256]{2,1,0:T(8,128)(2,1)S(1)} %pad_maximum_fusion.2), channel_id=1, source_target_pairs={{0,3},{1,0},{2,1},{3,2},{4,7},{5,4},{6,5},{7,6},{8,11},{9,8},{10,9... | collective-permute-start | bytes 294920 | tf_op jit(solution)/shard_map/ppermute | solution.py:475
  44.0 1.3 %shard_map.118 = bf16[8,32,512]{2,1,0:T(8,128)(2,1)} custom-call(s32[2]{0:T(128)S(1)} %pad_add_fusion.place, bf16[10,32,128]{2,1,0:T(8,128)(2,1)S(1)} %get-tuple-element.37.refs_0_, bf16[10,32,128]{2,1,0:T(8,128)(2,1)S(1)} %collective-permute-done.3.refs_1_, bf16[10,32,128]{2,1,0:T(8,128)(2,1)S(1)} %collective-permute-done.4.refs_2_, ...), custom_call_target="tpu_custom_call" | custom-call | bytes 589832 | tf_op jit(solution)/shard_map/pallas_call | solution.py:204
  45.4 2.4 %collective-permute-done.9 = f16[4,48,256]{2,1,0:T(8,128)(2,1)S(1)} collective-permute-done((f16[4,48,256]{2,1,0:T(8,128)(2,1)S(1)}, f16[4,48,256]{2,1,0:T(8,128)(2,1)S(1)}, u32[]{:S(2)}, u32[]{:S(2)}) %collective-permute-start.9) | collective-permute-done | bytes 98336 | tf_op jit(solution)/shard_map/ppermute | solution.py:475
  47.8 0.3 collective-permute-done.10
  48.1 1.4 %collective-permute-done.11 = f16[4,48,256]{2,1,0:T(8,128)(2,1)S(1)} collective-permute-done((f16[4,48,256]{2,1,0:T(8,128)(2,1)S(1)}, f16[4,48,256]{2,1,0:T(8,128)(2,1)S(1)}, u32[]{:S(2)}, u32[]{:S(2)}) %collective-permute-start.11) | collective-permute-done | bytes 98336 | tf_op jit(solution)/shard_map/ppermute | solution.py:475
  49.6 2.8 %shard_map.116 = (f32[4,48,256]{2,1,0:T(8,128)S(1)}, f32[4,48,256]{2,1,0:T(8,128)S(1)}, f32[4,48,256]{2,1,0:T(8,128)S(1)}, f32[4,48,256]{2,1,0:T(8,128)S(1)}) custom-call(s32[2]{0:T(128)S(1)} %pad_add_fusion.place, f32[4,48,256]{2,1,0:T(8,128)S(1)} %maximum_convert_fusion.refs_0_, f32[4,48,256]{2,1,0:T(8,128)S(1)} %convert_element_type.53.refs_1_, ...), custom_call_target="tpu_custom_call" | custom-call | flops 2147483648 | bytes 2228232 | tf_op jit(solution)/shard_map/pallas_call | solution.py:204
  52.4 0.0 all-to-all-done
  52.5 3.2 %collective-permute-start.16 = (f16[4,48,256]{2,1,0:T(8,128)(2,1)S(1)}, f16[4,48,256]{2,1,0:T(8,128)(2,1)S(1)}, u32[]{:S(2)}, u32[]{:S(2)}) collective-permute-start(f16[4,48,256]{2,1,0:T(8,128)(2,1)S(1)} %convert_element_type.63), channel_id=1, source_target_pairs={{0,12},{4,0},{8,4},{12,8},{1,13},{5,1},{9,5},{13,9},{2,14},{6,2},{... | collective-permute-start | bytes 294920 | tf_op jit(solution)/shard_map/ppermute | solution.py:475
  55.7 0.0 collective-permute-start.15
  55.7 1.4 %collective-permute-start.14 = (f16[4,48,256]{2,1,0:T(8,128)(2,1)S(1)}, f16[4,48,256]{2,1,0:T(8,128)(2,1)S(1)}, u32[]{:S(2)}, u32[]{:S(2)}) collective-permute-start(f16[4,48,256]{2,1,0:T(8,128)(2,1)S(1)} %convert_element_type.61), channel_id=1, source_target_pairs={{0,4},{4,8},{8,12},{12,0},{1,5},{5,9},{9,13},{13,1},{2,6},{6,10},{... | collective-permute-start | bytes 294920 | tf_op jit(solution)/shard_map/ppermute | solution.py:475
  57.2 0.1 convert_element_type.57.spectra
  57.2 2.7 %shard_map.119 = f32[16,48,256]{2,1,0:T(8,128)S(1)} custom-call(s32[2]{0:T(128)S(1)} %pad_add_fusion.place, f32[16,48,256]{2,1,0:T(8,128)S(1)} %convert_element_type.57.spectra, bf16[4,256,256]{2,1,0:T(8,128)(2,1)S(1)} %copy-done.8, bf16[4,128,128]{2,1,0:T(8,128)(2,1)S(1)} %copy-done.9), custom_call_target="tpu_custom_call" | custom-call | flops 2147483648 | bytes 2228232 | tf_op jit(solution)/shard_map/pallas_call | solution.py:204
  59.9 0.8 %convert_element_type.58 = f16[16,48,256]{2,1,0:T(8,128)(2,1)} convert(f32[16,48,256]{2,1,0:T(8,128)S(1)} %shard_map.119) | non-fusion elementwise | flops 196608 | bytes 1179648 | tf_op jit(solution)/shard_map/convert_element_type | solution.py:564
  60.7 5.2 %all-to-all-start.1 = ((f16[16,48,256]{2,1,0:T(8,128)(2,1)}), f16[16,48,256]{2,1,0:T(8,128)(2,1)}, u32[]{:S(2)}, u32[]{:S(2)}) async-start(f16[16,48,256]{2,1,0:T(8,128)(2,1)} %convert_element_type.58), calls=%async_computation.1 | async-start | bytes 786432 | tf_op jit(solution)/shard_map/all_to_all | solution.py:479
  66.0 0.0 collective-permute-done.16
  66.0 0.0 collective-permute-done.15
  66.0 0.0 collective-permute-done.14
  66.1 0.4 collective-permute-start.17
  66.6 1.7 %collective-permute-start.18 = (f16[4,48,256]{2,1,0:T(8,128)(2,1)S(1)}, f16[4,48,256]{2,1,0:T(8,128)(2,1)S(1)}, u32[]{:S(2)}, u32[]{:S(2)}) collective-permute-start(f16[4,48,256]{2,1,0:T(8,128)(2,1)S(1)} %pad_maximum_fusion.4), channel_id=1, source_target_pairs={{0,2},{1,3},{2,0},{3,1},{4,6},{5,7},{6,4},{7,5},{8,10},{9,11},{10,... | collective-permute-start | bytes 294920 | tf_op jit(solution)/shard_map/ppermute | solution.py:475
  68.3 1.4 %collective-permute-start.19 = (f16[4,48,256]{2,1,0:T(8,128)(2,1)S(1)}, f16[4,48,256]{2,1,0:T(8,128)(2,1)S(1)}, u32[]{:S(2)}, u32[]{:S(2)}) collective-permute-start(f16[4,48,256]{2,1,0:T(8,128)(2,1)S(1)} %pad_maximum_fusion.5), channel_id=1, source_target_pairs={{0,3},{1,0},{2,1},{3,2},{4,7},{5,4},{6,5},{7,6},{8,11},{9,8},{10,9... | collective-permute-start | bytes 294920 | tf_op jit(solution)/shard_map/ppermute | solution.py:475
  69.8 3.6 %collective-permute-done.17 = f16[4,48,256]{2,1,0:T(8,128)(2,1)S(1)} collective-permute-done((f16[4,48,256]{2,1,0:T(8,128)(2,1)S(1)}, f16[4,48,256]{2,1,0:T(8,128)(2,1)S(1)}, u32[]{:S(2)}, u32[]{:S(2)}) %collective-permute-start.17) | collective-permute-done | bytes 98336 | tf_op jit(solution)/shard_map/ppermute | solution.py:475
  73.3 1.3 %collective-permute-done.18 = f16[4,48,256]{2,1,0:T(8,128)(2,1)S(1)} collective-permute-done((f16[4,48,256]{2,1,0:T(8,128)(2,1)S(1)}, f16[4,48,256]{2,1,0:T(8,128)(2,1)S(1)}, u32[]{:S(2)}, u32[]{:S(2)}) %collective-permute-start.18) | collective-permute-done | bytes 98336 | tf_op jit(solution)/shard_map/ppermute | solution.py:475
  74.7 0.7 collective-permute-done.19
  75.4 1.2 %shard_map.120 = (f32[8,32,512]{2,1,0:T(8,128)S(1)}, f32[16,16,256]{2,1,0:T(8,128)S(1)}) custom-call(s32[2]{0:T(128)S(1)} %pad_add_fusion.place, bf16[2,512,512]{2,1,0:T(8,128)(2,1)S(1)} %copy-done.6, f32[3,8,32,512]{3,2,1,0:T(8,128)S(1)} %copy-done.2, f32[4,48,256]{2,1,0:T(8,128)S(1)} %maximum_convert_fusion.1.refs_0_, ...), custom_call_target="tpu_custom_call" | custom-call | flops 1073741824 | bytes 4194312 | tf_op jit(solution)/shard_map/pallas_call | solution.py:204
  76.7 1.5 %all-to-all-done.1 = f16[16,48,256]{2,1,0:T(8,128)(2,1)} async-done(((f16[16,48,256]{2,1,0:T(8,128)(2,1)}), f16[16,48,256]{2,1,0:T(8,128)(2,1)}, u32[]{:S(2)}, u32[]{:S(2)}) %all-to-all-start.1) | async-done | bytes 393248 | tf_op jit(solution)/shard_map/all_to_all | solution.py:479
  78.2 1.1 %convert_element_type.59.spectra = f32[16,48,256]{2,1,0:T(8,128)S(1)} convert(f16[16,48,256]{2,1,0:T(8,128)(2,1)} %all-to-all-done.1) | non-fusion elementwise | flops 196608 | bytes 1179648 | tf_op jit(solution)/shard_map/convert_element_type | solution.py:579
  79.3 1.9 %shard_map.121 = f32[3,8,32,512]{3,2,1,0:T(8,128)} custom-call(f32[16,48,256]{2,1,0:T(8,128)S(1)} %convert_element_type.59.spectra, bf16[2,512,512]{2,1,0:T(8,128)(2,1)S(1)} %copy-done.6, f32[3,8,32,512]{3,2,1,0:T(8,128)S(1)} %copy-done.2, f32[8,32,512]{2,1,0:T(8,128)S(1)} %get-tuple-element.61.updated, f32[16,16,256]{2,1,0:T(8,128)S(1)} %get-tuple-element.62.kept), custom_call_target="tpu_custom_call" | custom-call | flops 2147483648 | bytes 5767168 | tf_op jit(solution)/shard_map/pallas_call | solution.py:204
  (40 shorter events, 0.6 us)
Async XLA Ops:
  0.7 1.0 %copy-start = (bf16[8,32,512]{2,1,0:T(8,128)(2,1)S(1)}, bf16[8,32,512]{2,1,0:T(8,128)(2,1)}, u32[]{:S(2)}) copy-start(bf16[8,32,512]{2,1,0:T(8,128)(2,1)} %moving.1) | copy-start | bytes 786436
  1.7 0.7 copy-start.1
  3.1 7.8 %collective-permute-start = (bf16[9,32,128]{2,1,0:T(8,128)(2,1)S(1)}, bf16[9,32,128]{2,1,0:T(8,128)(2,1)S(1)}, u32[]{:S(2)}, u32[]{:S(2)}) collective-permute-start(bf16[9,32,128]{2,1,0:T(8,128)(2,1)S(1)} %get-tuple-element.34), channel_id=1, source_target_pairs={{0,4},{4,8},{8,12},{12,0},{1,5},{5,9},{9,13},{13,1},{2,6},{6,10},{... | collective-permute-start | bytes 221192 | tf_op jit(solution)/shard_map/ppermute | solution.py:475
  6.1 7.5 %collective-permute-start.1 = (bf16[9,32,128]{2,1,0:T(8,128)(2,1)S(1)}, bf16[9,32,128]{2,1,0:T(8,128)(2,1)S(1)}, u32[]{:S(2)}, u32[]{:S(2)}) collective-permute-start(bf16[9,32,128]{2,1,0:T(8,128)(2,1)S(1)} %get-tuple-element.35), channel_id=1, source_target_pairs={{0,8},{4,12},{8,0},{12,4},{1,9},{5,13},{9,1},{13,5},{2,10},{6,14},... | collective-permute-start | bytes 221192 | tf_op jit(solution)/shard_map/ppermute | solution.py:475
  8.7 5.2 %collective-permute-start.2 = (bf16[9,32,128]{2,1,0:T(8,128)(2,1)S(1)}, bf16[9,32,128]{2,1,0:T(8,128)(2,1)S(1)}, u32[]{:S(2)}, u32[]{:S(2)}) collective-permute-start(bf16[9,32,128]{2,1,0:T(8,128)(2,1)S(1)} %get-tuple-element.36), channel_id=1, source_target_pairs={{0,12},{4,0},{8,4},{12,8},{1,13},{5,1},{9,5},{13,9},{2,14},{6,2},{... | collective-permute-start | bytes 221192 | tf_op jit(solution)/shard_map/ppermute | solution.py:475
  13.9 10.8 %copy-start.3 = (f32[8,32,512]{2,1,0:T(8,128)S(1)}, f32[8,32,512]{2,1,0:T(8,128)}, u32[]{:S(2)}) copy-start(f32[8,32,512]{2,1,0:T(8,128)} %refs_5_.2) | copy-start | bytes 1572868
  13.9 10.8 %copy-start.4 = (bf16[8,32,512]{2,1,0:T(8,128)(2,1)S(1)}, bf16[8,32,512]{2,1,0:T(8,128)(2,1)}, u32[]{:S(2)}) copy-start(bf16[8,32,512]{2,1,0:T(8,128)(2,1)} %refs_4_.2) | copy-start | bytes 786436
  13.9 10.8 %copy-start.5 = (s32[8,32,4]{1,2,0:T(4,128)S(1)}, s32[8,32,4]{1,2,0:T(4,128)}, u32[]{:S(2)}) copy-start(s32[8,32,4]{1,2,0:T(4,128)} %param.15) | copy-start | bytes 12292
  13.9 10.8 %copy-start.7 = (bf16[2,512,512]{2,1,0:T(8,128)(2,1)S(1)}, bf16[2,512,512]{2,1,0:T(8,128)(2,1)}, u32[]{:S(2)}) copy-start(bf16[2,512,512]{2,1,0:T(8,128)(2,1)} %constant.15.clone.refs_7_.basis) | copy-start | bytes 3145732
  15.2 7.3 %collective-permute-start.3 = (bf16[10,32,128]{2,1,0:T(8,128)(2,1)S(1)}, bf16[10,32,128]{2,1,0:T(8,128)(2,1)S(1)}, u32[]{:S(2)}, u32[]{:S(2)}) collective-permute-start(bf16[10,32,128]{2,1,0:T(8,128)(2,1)S(1)} %get-tuple-element.38), channel_id=1, source_target_pairs={{0,4},{4,8},{8,12},{12,0},{1,5},{5,9},{9,13},{13,1},{2,6},{6,10},{... | collective-permute-start | bytes 245768 | tf_op jit(solution)/shard_map/ppermute | solution.py:475
  17.1 7.6 %collective-permute-start.4 = (bf16[10,32,128]{2,1,0:T(8,128)(2,1)S(1)}, bf16[10,32,128]{2,1,0:T(8,128)(2,1)S(1)}, u32[]{:S(2)}, u32[]{:S(2)}) collective-permute-start(bf16[10,32,128]{2,1,0:T(8,128)(2,1)S(1)} %get-tuple-element.39), channel_id=1, source_target_pairs={{0,8},{4,12},{8,0},{12,4},{1,9},{5,13},{9,1},{13,5},{2,10},{6,14},... | collective-permute-start | bytes 245768 | tf_op jit(solution)/shard_map/ppermute | solution.py:475
  19.0 5.7 %collective-permute-start.5 = (bf16[10,32,128]{2,1,0:T(8,128)(2,1)S(1)}, bf16[10,32,128]{2,1,0:T(8,128)(2,1)S(1)}, u32[]{:S(2)}, u32[]{:S(2)}) collective-permute-start(bf16[10,32,128]{2,1,0:T(8,128)(2,1)S(1)} %get-tuple-element.40), channel_id=1, source_target_pairs={{0,12},{4,0},{8,4},{12,8},{1,13},{5,1},{9,5},{13,9},{2,14},{6,2},{... | collective-permute-start | bytes 245768 | tf_op jit(solution)/shard_map/ppermute | solution.py:475
  27.0 5.6 %collective-permute-start.12 = (bf16[16,512]{1,0:T(8,128)(2,1)S(1)}, bf16[16,512]{1,0:T(8,128)(2,1)S(1)}, u32[]{:S(2)}, u32[]{:S(2)}) collective-permute-start(bf16[16,512]{1,0:T(8,128)(2,1)S(1)} %get-tuple-element.50), channel_id=1, source_target_pairs={{0,1},{1,2},{2,3},{3,0},{4,5},{5,6},{6,7},{7,4},{8,9},{9,10},{10,1... | collective-permute-start | bytes 49160 | tf_op jit(solution)/shard_map/ppermute | solution.py:522
  27.0 5.6 %collective-permute-start.13 = (bf16[16,512]{1,0:T(8,128)(2,1)S(1)}, bf16[16,512]{1,0:T(8,128)(2,1)S(1)}, u32[]{:S(2)}, u32[]{:S(2)}) collective-permute-start(bf16[16,512]{1,0:T(8,128)(2,1)S(1)} %get-tuple-element.51), channel_id=1, source_target_pairs={{1,0},{2,1},{3,2},{0,3},{5,4},{6,5},{7,6},{4,7},{9,8},{10,9},{11,1... | collective-permute-start | bytes 49160 | tf_op jit(solution)/shard_map/ppermute | solution.py:523
  28.8 11.2 %collective-permute-start.8 = (f16[4,48,256]{2,1,0:T(8,128)(2,1)S(1)}, f16[4,48,256]{2,1,0:T(8,128)(2,1)S(1)}, u32[]{:S(2)}, u32[]{:S(2)}) collective-permute-start(f16[4,48,256]{2,1,0:T(8,128)(2,1)S(1)} %get-tuple-element.64), channel_id=1, source_target_pairs={{0,12},{4,0},{8,4},{12,8},{1,13},{5,1},{9,5},{13,9},{2,14},{6,2},{... | collective-permute-start | bytes 294920 | tf_op jit(solution)/shard_map/ppermute | solution.py:475
  31.6 9.7 %collective-permute-start.7 = (f16[4,48,256]{2,1,0:T(8,128)(2,1)S(1)}, f16[4,48,256]{2,1,0:T(8,128)(2,1)S(1)}, u32[]{:S(2)}, u32[]{:S(2)}) collective-permute-start(f16[4,48,256]{2,1,0:T(8,128)(2,1)S(1)} %get-tuple-element.65), channel_id=1, source_target_pairs={{0,8},{4,12},{8,0},{12,4},{1,9},{5,13},{9,1},{13,5},{2,10},{6,14},... | collective-permute-start | bytes 294920 | tf_op jit(solution)/shard_map/ppermute | solution.py:475
  32.6 8.7 %collective-permute-start.6 = (f16[4,48,256]{2,1,0:T(8,128)(2,1)S(1)}, f16[4,48,256]{2,1,0:T(8,128)(2,1)S(1)}, u32[]{:S(2)}, u32[]{:S(2)}) collective-permute-start(f16[4,48,256]{2,1,0:T(8,128)(2,1)S(1)} %get-tuple-element.66), channel_id=1, source_target_pairs={{0,4},{4,8},{8,12},{12,0},{1,5},{5,9},{9,13},{13,1},{2,6},{6,10},{... | collective-permute-start | bytes 294920 | tf_op jit(solution)/shard_map/ppermute | solution.py:475
  34.1 18.2 %all-to-all-start = ((f16[16,48,256]{2,1,0:T(8,128)(2,1)}), f16[16,48,256]{2,1,0:T(8,128)(2,1)S(1)}, u32[]{:S(2)}, u32[]{:S(2)}) async-start(f16[16,48,256]{2,1,0:T(8,128)(2,1)} %convert_element_type.56), calls=%async_computation | async-start | bytes 786432 | tf_op jit(solution)/shard_map/all_to_all | solution.py:479
  41.3 8.3 %copy-start.8 = (bf16[4,256,256]{2,1,0:T(8,128)(2,1)S(1)}, bf16[4,256,256]{2,1,0:T(8,128)(2,1)}, u32[]{:S(2)}) copy-start(bf16[4,256,256]{2,1,0:T(8,128)(2,1)} %constant.16.clone.refs_4_.basis_z) | copy-start | bytes 1572868
  41.3 8.3 %copy-start.9 = (bf16[4,128,128]{2,1,0:T(8,128)(2,1)S(1)}, bf16[4,128,128]{2,1,0:T(8,128)(2,1)}, u32[]{:S(2)}) copy-start(bf16[4,128,128]{2,1,0:T(8,128)(2,1)} %constant.17.clone.refs_5_.basis_y) | copy-start | bytes 393220
  41.4 6.4 %collective-permute-start.9 = (f16[4,48,256]{2,1,0:T(8,128)(2,1)S(1)}, f16[4,48,256]{2,1,0:T(8,128)(2,1)S(1)}, u32[]{:S(2)}, u32[]{:S(2)}) collective-permute-start(f16[4,48,256]{2,1,0:T(8,128)(2,1)S(1)} %pad_maximum_fusion), channel_id=1, source_target_pairs={{0,1},{1,2},{2,3},{3,0},{4,5},{5,6},{6,7},{7,4},{8,9},{9,10},{10,1... | collective-permute-start | bytes 294920 | tf_op jit(solution)/shard_map/ppermute | solution.py:475
  41.6 6.5 %collective-permute-start.10 = (f16[4,48,256]{2,1,0:T(8,128)(2,1)S(1)}, f16[4,48,256]{2,1,0:T(8,128)(2,1)S(1)}, u32[]{:S(2)}, u32[]{:S(2)}) collective-permute-start(f16[4,48,256]{2,1,0:T(8,128)(2,1)S(1)} %pad_maximum_fusion.1), channel_id=1, source_target_pairs={{0,2},{1,3},{2,0},{3,1},{4,6},{5,7},{6,4},{7,5},{8,10},{9,11},{10,... | collective-permute-start | bytes 294920 | tf_op jit(solution)/shard_map/ppermute | solution.py:475
  42.5 7.0 %collective-permute-start.11 = (f16[4,48,256]{2,1,0:T(8,128)(2,1)S(1)}, f16[4,48,256]{2,1,0:T(8,128)(2,1)S(1)}, u32[]{:S(2)}, u32[]{:S(2)}) collective-permute-start(f16[4,48,256]{2,1,0:T(8,128)(2,1)S(1)} %pad_maximum_fusion.2), channel_id=1, source_target_pairs={{0,3},{1,0},{2,1},{3,2},{4,7},{5,4},{6,5},{7,6},{8,11},{9,8},{10,9... | collective-permute-start | bytes 294920 | tf_op jit(solution)/shard_map/ppermute | solution.py:475
  52.5 13.5 %collective-permute-start.16 = (f16[4,48,256]{2,1,0:T(8,128)(2,1)S(1)}, f16[4,48,256]{2,1,0:T(8,128)(2,1)S(1)}, u32[]{:S(2)}, u32[]{:S(2)}) collective-permute-start(f16[4,48,256]{2,1,0:T(8,128)(2,1)S(1)} %convert_element_type.63), channel_id=1, source_target_pairs={{0,12},{4,0},{8,4},{12,8},{1,13},{5,1},{9,5},{13,9},{2,14},{6,2},{... | collective-permute-start | bytes 294920 | tf_op jit(solution)/shard_map/ppermute | solution.py:475
  55.7 10.3 %collective-permute-start.15 = (f16[4,48,256]{2,1,0:T(8,128)(2,1)S(1)}, f16[4,48,256]{2,1,0:T(8,128)(2,1)S(1)}, u32[]{:S(2)}, u32[]{:S(2)}) collective-permute-start(f16[4,48,256]{2,1,0:T(8,128)(2,1)S(1)} %convert_element_type.62), channel_id=1, source_target_pairs={{0,8},{4,12},{8,0},{12,4},{1,9},{5,13},{9,1},{13,5},{2,10},{6,14},... | collective-permute-start | bytes 294920 | tf_op jit(solution)/shard_map/ppermute | solution.py:475
  55.7 10.3 %collective-permute-start.14 = (f16[4,48,256]{2,1,0:T(8,128)(2,1)S(1)}, f16[4,48,256]{2,1,0:T(8,128)(2,1)S(1)}, u32[]{:S(2)}, u32[]{:S(2)}) collective-permute-start(f16[4,48,256]{2,1,0:T(8,128)(2,1)S(1)} %convert_element_type.61), channel_id=1, source_target_pairs={{0,4},{4,8},{8,12},{12,0},{1,5},{5,9},{9,13},{13,1},{2,6},{6,10},{... | collective-permute-start | bytes 294920 | tf_op jit(solution)/shard_map/ppermute | solution.py:475
  60.7 14.7 %copy-start.2 = (f32[3,8,32,512]{3,2,1,0:T(8,128)S(1)}, f32[3,8,32,512]{3,2,1,0:T(8,128)}, u32[]{:S(2)}) copy-start(f32[3,8,32,512]{3,2,1,0:T(8,128)} %velocity.3) | copy-start | bytes 4718596
  60.7 14.7 %copy-start.6 = (bf16[2,512,512]{2,1,0:T(8,128)(2,1)S(1)}, bf16[2,512,512]{2,1,0:T(8,128)(2,1)}, u32[]{:S(2)}) copy-start(bf16[2,512,512]{2,1,0:T(8,128)(2,1)} %constant.18.clone.basis) | copy-start | bytes 3145732
  60.7 17.5 %all-to-all-start.1 = ((f16[16,48,256]{2,1,0:T(8,128)(2,1)}), f16[16,48,256]{2,1,0:T(8,128)(2,1)}, u32[]{:S(2)}, u32[]{:S(2)}) async-start(f16[16,48,256]{2,1,0:T(8,128)(2,1)} %convert_element_type.58), calls=%async_computation.1 | async-start | bytes 786432 | tf_op jit(solution)/shard_map/all_to_all | solution.py:479
  66.1 7.2 %collective-permute-start.17 = (f16[4,48,256]{2,1,0:T(8,128)(2,1)S(1)}, f16[4,48,256]{2,1,0:T(8,128)(2,1)S(1)}, u32[]{:S(2)}, u32[]{:S(2)}) collective-permute-start(f16[4,48,256]{2,1,0:T(8,128)(2,1)S(1)} %pad_maximum_fusion.3), channel_id=1, source_target_pairs={{0,1},{1,2},{2,3},{3,0},{4,5},{5,6},{6,7},{7,4},{8,9},{9,10},{10,1... | collective-permute-start | bytes 294920 | tf_op jit(solution)/shard_map/ppermute | solution.py:475
  66.6 8.1 %collective-permute-start.18 = (f16[4,48,256]{2,1,0:T(8,128)(2,1)S(1)}, f16[4,48,256]{2,1,0:T(8,128)(2,1)S(1)}, u32[]{:S(2)}, u32[]{:S(2)}) collective-permute-start(f16[4,48,256]{2,1,0:T(8,128)(2,1)S(1)} %pad_maximum_fusion.4), channel_id=1, source_target_pairs={{0,2},{1,3},{2,0},{3,1},{4,6},{5,7},{6,4},{7,5},{8,10},{9,11},{10,... | collective-permute-start | bytes 294920 | tf_op jit(solution)/shard_map/ppermute | solution.py:475
  68.3 7.1 %collective-permute-start.19 = (f16[4,48,256]{2,1,0:T(8,128)(2,1)S(1)}, f16[4,48,256]{2,1,0:T(8,128)(2,1)S(1)}, u32[]{:S(2)}, u32[]{:S(2)}) collective-permute-start(f16[4,48,256]{2,1,0:T(8,128)(2,1)S(1)} %pad_maximum_fusion.5), channel_id=1, source_target_pairs={{0,3},{1,0},{2,1},{3,2},{4,7},{5,4},{6,5},{7,6},{8,11},{9,8},{10,9... | collective-permute-start | bytes 294920 | tf_op jit(solution)/shard_map/ppermute | solution.py:475

commit v8 on v7

--- a/solution.py
+++ b/solution.py
@@ -223,19 +223,18 @@
     planes, rows, _ = moving.shape
     for step, send in enumerate(sends):
         to = around(place[0] + step, slabs)
-        send[0:planes] = moving[:, :, pl.ds(pl.multiple_of(to * BLOCK, BLOCK), BLOCK)]
-        wanted = jnp.concatenate([fetch[z, pl.ds(to, 1), :] for z in range(planes)], axis=0).astype(jnp.float32)
-        wanted = jnp.concatenate([wanted, jnp.zeros((planes, BLOCK - rows), jnp.float32)], axis=1)
-        wanted = jnp.concatenate([wanted, jnp.zeros((BLOCK - planes, BLOCK), jnp.float32)], axis=0)
-        send[planes] = wanted.T[:rows].astype(jnp.bfloat16)
+        block = pl.ds(pl.multiple_of(to * BLOCK, BLOCK), BLOCK)
+        for z in range(planes):
+            send[z * rows : (z + 1) * rows] = moving[z, :, block]
+        asked = jnp.concatenate([fetch[z, pl.ds(to, 1), :] for z in range(planes)] * 2, axis=0).astype(jnp.float32)
+        asked = jnp.concatenate([asked, jnp.zeros((2 * planes, BLOCK - rows), jnp.float32)], axis=1)
+        send[planes * rows :] = asked.astype(jnp.bfloat16)
 
 
 def pick_kernel(slabs, place, *refs):
-    received, sends, picked = refs[:slabs], refs[slabs:-1], refs[-1]
-    planes = received[0].shape[0] - 1
-    rows = received[0].shape[1]
+    received, sends = refs[:slabs], refs[slabs:]
+    planes, rows = sends[0].shape[0] - 2, sends[0].shape[1]
     me = place[0]
-    total = slabs * planes
     group = 4
 
     def name(other, plane):
@@ -243,8 +242,8 @@
         return jnp.full((rows, BLOCK), number, jnp.float32).astype(jnp.bfloat16)
 
     for step in range(slabs):
-        first = around(me - step, slabs) * planes
-        names = received[step][planes].astype(jnp.float32)
+        names = received[step][planes * rows :].astype(jnp.float32)[:planes]
+        names = jnp.concatenate([names, jnp.zeros((BLOCK - planes, BLOCK), jnp.float32)], axis=0).T[:rows]
         for start in range(0, planes, group):
             wanted = [
                 jnp.broadcast_to(names[:, z : z + 1], (rows, BLOCK)).astype(jnp.bfloat16)
@@ -253,32 +252,24 @@
             found = [jnp.zeros((rows, BLOCK), jnp.bfloat16) for _ in range(group)]
             for other in range(slabs):
                 for plane in range(planes):
-                    values = received[other][plane]
+                    values = received[other][plane * rows : (plane + 1) * rows]
                     own = name(other, plane)
                     found = [jnp.where(w == own, values, f) for w, f in zip(wanted, found)]
+            back = (slabs - step) % slabs
             for z in range(group):
-                picked[first + start + z] = found[z]
-    for step, send in enumerate(sends):
-        first = around(me + step, slabs) * planes
-        for k in range(planes + 2):
-            send[k] = picked[around(first + (k - 1), total)]
-
-
-def force_zx_kernel(slabs, subs, place, *refs):
-    received, refs = refs[:slabs], refs[slabs:]
-    template, stiffness, tissue, basis, first, last, image, weight, spectra, kept, planes_of, wide = refs
-    planes, rows, x_length = template.shape
+                own = start + z
+                sends[back][own + 1] = found[z]
+                if own == 0:
+                    sends[(back - 1) % slabs][planes + 1] = found[z]
+                if own == planes - 1:
+                    sends[(back + 1) % slabs][0] = found[z]
+
+
+def coefficient_kernel(stiffness, tissue, out):
+    planes, rows, x_length = stiffness.shape
     blocks = x_length // BLOCK
-    for step in range(slabs):
-        block = pl.ds(pl.multiple_of(around(place[0] - step, slabs) * BLOCK, BLOCK), BLOCK)
-        planes_of[:, :, block] = received[step][...].astype(jnp.float32)
-    for edge, row in ((first, 0), (last, rows - 1)):
-        own = [planes_of[z + 1, row : row + 1, :] for z in range(planes)]
-        edge[...] = jnp.concatenate(own * 2, axis=0).astype(jnp.bfloat16)
     marks = by_row(tissue, rows)
-    forces = [[], []]
     for z in range(planes):
-        here = planes_of[z + 1]
         marked = jnp.concatenate(
             [
                 jnp.broadcast_to(marks[:, z * blocks + b : z * blocks + b + 1], (rows, BLOCK))
@@ -286,35 +277,52 @@
             ],
             axis=1,
         )
-        own = 0.5 * (marked * stiffness[z] * (here - template[z].astype(jnp.float32)))
+        out[z] = 0.5 * marked * stiffness[z]
+
+
+def force_zx_kernel(slabs, subs, place, *refs):
+    received, refs = refs[:slabs], refs[slabs:]
+    template, coefficient, basis, first, image, weight, spectra, kept, planes_of, wide = refs
+    planes, rows, x_length = template.shape
+    for step in range(slabs):
+        block = pl.ds(pl.multiple_of(around(place[0] - step, slabs) * BLOCK, BLOCK), BLOCK)
+        planes_of[:, :, block] = received[step][...].astype(jnp.float32)
+    forces = [[], []]
+    for z in range(planes):
+        here = planes_of[z + 1]
+        own = coefficient[z] * (here - template[z].astype(jnp.float32))
         image[z] = here
         weight[z] = own
+        first[z : z + 1] = here[0:1]
+        first[planes + z : planes + z + 1] = here[1:2]
+        first[2 * planes + z : 2 * planes + z + 1] = own[0:1]
         forces[0].append(own * (planes_of[z + 2] - planes_of[z]))
         forces[1].append(own * (pltpu.roll(here, x_length - 1, 1) - pltpu.roll(here, 1, 1)))
     for a in range(2):
         force = split(jnp.concatenate(forces[a], axis=0))
         wide[a] = times((basis[0], basis[1]), force, ((1,), (1,)))
     part = x_length // (slabs * subs)
-    half = part // 2
+    cut = kept.shape[1]
     for d in range(slabs):
         for e in range(subs):
             start = (around(place[0] + d, slabs) * subs + around(place[1] + e, subs)) * part
             spectra[d, e, :part] = wide[0, pl.ds(pl.multiple_of(start, part), part), :]
-            spectra[d, e, part:] = wide[1, pl.ds(pl.multiple_of(start + half, half), half), :]
+            spectra[d, e, part:] = wide[1, pl.ds(pl.multiple_of(start + cut, 8), part - cut), :]
     for k in range(slabs * subs):
-        kept[k] = wide[1, k * part : k * part + half, :]
-
-
-def force_y_kernel(above, below, image, weight, basis, kept, spectra):
+        kept[k] = wide[1, k * part : k * part + cut, :]
+
+
+def force_y_kernel(beyond, image, weight, basis, kept, spectra):
     planes, rows, x_length = image.shape
-    edges = above[...].astype(jnp.float32), below[...].astype(jnp.float32)
     row = lax.broadcasted_iota(jnp.int32, (rows, x_length), 0)
     force = []
     for z in range(planes):
         here = image[z]
-        before = jnp.where(row == 0, edges[0][z : z + 1], pltpu.roll(here, 1, 0))
-        after = jnp.where(row == rows - 1, edges[1][z : z + 1], pltpu.roll(here, rows - 1, 0))
-        force.append(weight[z] * (after - before))
+        after = jnp.where(row == rows - 2, beyond[z : z + 1, :], pltpu.roll(here, rows - 2, 0))
+        after = jnp.where(row == rows - 1, beyond[planes + z : planes + z + 1, :], after)
+        own = pltpu.roll(weight[z], rows - 1, 0)
+        own = jnp.where(row == rows - 1, beyond[2 * planes + z : 2 * planes + z + 1, :], own)
+        force.append(own * (after - here))
     devices = spectra.shape[0]
     part = x_length // devices
     spectrum = times((basis[0], basis[1]), split(jnp.concatenate(force, axis=0)), ((1,), (1,)))
@@ -341,7 +349,7 @@
     ]
 
 
-def solve(first, x_length, offsets, subs, spectra, basis_z, basis_y, out, cells):
+def solve(first, x_length, offsets, shifted, subs, spectra, basis_z, basis_y, out, cells):
     devices, used, area = spectra.shape
     total_z, _, total_y = cells.shape
     slabs = devices // subs
@@ -371,8 +379,10 @@
         for f in range(0, planes // fold):
             lanes = slice(f * total_y, (f + 1) * total_y)
             own += swap_blocks([spectra[s * subs + q][:, lanes] for q in range(subs)])
-        own = along_y(0, jnp.concatenate(own, axis=0))
-        cells[s * planes : (s + 1) * planes] = own.reshape(planes, used, total_y)
+        for low, high, table in ((0, shifted, 2), (shifted, used, 0)):
+            if low < high:
+                some = along_y(table, jnp.concatenate([o[low:high] for o in own], axis=0))
+                cells[s * planes : (s + 1) * planes, low:high] = some.reshape(planes, high - low, total_y)
     index = lax.broadcasted_iota(jnp.int32, (total_z * tile, 1), 0)
     z_sq = wave_sq(index // tile, total_z)
     y_sq = wave_sq(lax.broadcasted_iota(jnp.int32, (1, total_y), 1), total_y)
@@ -397,19 +407,19 @@
 def solve_yx_kernel(subs, x_length, place, spectra, basis_z, basis_y, out, cells):
     devices = out.shape[0]
     part = x_length // devices
-    offsets = list(range(0, part, 8)) + list(range(0, part // 2, 8))
-    solve((place[0] * subs + place[1]) * part, x_length, offsets, subs, spectra, basis_z, basis_y, out, cells)
+    offsets = list(range(0, part, 8)) + list(range(0, out.shape[1] - part, 8))
+    solve((place[0] * subs + place[1]) * part, x_length, offsets, part, subs, spectra, basis_z, basis_y, out, cells)
 
 
 def solve_zx_kernel(slabs, subs, x_length, place, *refs):
     received, refs = refs[:subs], refs[subs:]
     basis_z, basis_y, sends, (spectra, cells) = refs[0], refs[1], refs[2 : 2 + slabs], refs[2 + slabs :]
     part = x_length // (slabs * subs)
-    offsets = list(range(0, part, 8)) + list(range(part // 2, part, 8))
+    offsets = list(range(0, part, 8)) + list(range(2 * part - received[0].shape[1], part, 8))
     for e in range(subs):
         for d in range(slabs):
             spectra[around(place[0] - d, slabs) * subs + around(place[1] - e, subs)] = received[e][d]
-    solve((place[0] * subs + place[1]) * part, x_length, offsets, subs, spectra, basis_z, basis_y, spectra, cells)
+    solve((place[0] * subs + place[1]) * part, x_length, offsets, 0, subs, spectra, basis_z, basis_y, spectra, cells)
     for d in range(slabs):
         for e in range(subs):
             sends[d][e] = spectra[around(place[0] + d, slabs) * subs + around(place[1] + e, subs)]
@@ -422,8 +432,7 @@
 
 def update_z_kernel(slabs, subs, place, basis, velocity, *refs):
     received, (out, kept, gathered) = refs[:subs], refs[subs:]
-    half = kept.shape[1]
-    part = 2 * half
+    part = received[0].shape[1] - kept.shape[1]
     for e in range(subs):
         for d in range(slabs):
             index = around(place[0] - d, slabs) * subs + around(place[1] - e, subs)
@@ -433,8 +442,8 @@
 
 
 def update_kernel(spectra, basis, velocity, updated, kept, out, result, done):
-    devices, half, area = kept.shape
-    part = 2 * half
+    devices, _, area = kept.shape
+    part = (spectra.shape[1] + kept.shape[1]) // 2
     leaving = [pltpu.make_async_copy(updated, out.at[0], done.at[0])]
     leaving[0].start()
     for a in range(2):
@@ -479,9 +488,10 @@
         return lax.all_to_all(values, ("slab", "sub"), split_axis=0, concat_axis=0, tiled=True)
 
     fetch, marks = fetch_plane.swapaxes(1, 2), tissue.swapaxes(1, 2)
+    coefficient = call(coefficient_kernel, shape(moving.shape), stiffness, marks, flops=1 << 30)
     sends = call(
         functools.partial(send_columns_kernel, slabs),
-        [shape((planes + 1, rows, BLOCK), bf16)] * slabs,
+        [shape(((rows + 2) * planes, BLOCK), bf16)] * slabs,
         place,
         moving,
         fetch,
@@ -491,36 +501,34 @@
         [shape((planes + 2, rows, BLOCK), bf16)] * slabs,
         place,
         *scatter(sends, "slab"),
-        scratch=[pltpu.VMEM((total_z, rows, BLOCK), bf16)],
         flops=1 << 30,
     )
     received = scatter(sends, "slab")
     basis_x = in_two(8.0 * real_basis(x_length))
     basis_z = np.kron(real_basis(total_z), np.eye(8))
     basis_z = np.concatenate([in_two(basis_z), in_two(basis_z.T)])
-    basis_y = np.concatenate([in_two(real_basis(total_y).T), in_two(real_basis(total_y))])
-    each = part + part // 2
-    first, last, image, weight, chain, kept = call(
+    basis_y = real_basis(total_y)
+    basis_y = np.concatenate([in_two(b) for b in (basis_y.T, basis_y, np.roll(basis_y.T, -1, 0))])
+    cut = part // 2
+    with_z, with_y = 2 * part - cut, part + cut
+    first, image, weight, chain, kept = call(
         functools.partial(force_zx_kernel, slabs, subs),
         [
-            shape((2 * planes, x_length), bf16),
-            shape((2 * planes, x_length), bf16),
+            shape((3 * planes, x_length)),
             shape(moving.shape),
             shape(moving.shape),
-            shape((slabs, subs, each, area)),
-            shape((devices, part // 2, area)),
+            shape((slabs, subs, with_z, area)),
+            shape((devices, cut, area)),
         ],
         place,
         *received,
         template,
-        stiffness,
-        marks,
+        coefficient,
         basis_x,
         scratch=[pltpu.VMEM((planes + 2, rows, x_length), f32), pltpu.VMEM((2, x_length, area), f32)],
         flops=3 << 30,
     )
-    above = lax.ppermute(last, "sub", [(i, (i + 1) % subs) for i in range(subs)])
-    below = lax.ppermute(first, "sub", [((i + 1) % subs, i) for i in range(subs)])
+    beyond = lax.ppermute(first, "sub", [((i + 1) % subs, i) for i in range(subs)])
     chain = chain.astype(f16)
     chain = scatter([chain[d] for d in range(slabs)], "slab")
     later, *chain = lax.optimization_barrier((place, *chain))
@@ -528,9 +536,8 @@
     chain = scatter([jnp.stack([r[e] for r in chain]) for e in range(subs)], "sub")
     spectra = call(
         force_y_kernel,
-        shape((devices, each, area)),
-        above,
-        below,
+        shape((devices, with_y, area)),
+        beyond,
         image,
         weight,
         basis_x,
@@ -540,12 +547,12 @@
     spectra = exchange(spectra.astype(f16))
     chain = call(
         functools.partial(solve_zx_kernel, slabs, subs, x_length),
-        [shape((subs, each, area))] * slabs,
+        [shape((subs, with_z, area))] * slabs,
         place,
         *[r.astype(f32) for r in chain],
         basis_z,
         basis_y,
-        scratch=[pltpu.VMEM((devices, each, area), f32), pltpu.VMEM((total_z, each, total_y), f32)],
+        scratch=[pltpu.VMEM((devices, with_z, area), f32), pltpu.VMEM((total_z, with_z, total_y), f32)],
         flops=2 << 30,
     )
     chain, spectra, warped = lax.optimization_barrier((chain, spectra, warped))
@@ -553,19 +560,19 @@
     chain = scatter([jnp.stack([r[e] for r in chain]) for e in range(subs)], "sub")
     spectra = call(
         functools.partial(solve_yx_kernel, subs, x_length),
-        shape((devices, each, area)),
+        shape((devices, with_y, area)),
         place,
         spectra.astype(f32),
         basis_z,
         basis_y,
-        scratch=[pltpu.VMEM((total_z, each, total_y), f32)],
+        scratch=[pltpu.VMEM((total_z, with_y, total_y), f32)],
         flops=2 << 30,
     )
     spectra = exchange(spectra.astype(f16))
     basis_x = in_two(real_basis(x_length))
     updated, kept = call(
         functools.partial(update_z_kernel, slabs, subs),
-        [shape(moving.shape), shape((devices, part // 2, area))],
+        [shape(moving.shape), shape((devices, part - cut, area))],
         place,
         basis_x,
         velocity,

time: 81.6 us -> 79.7 us (0.977)
  starting transfers between devices: 38.9 us -> 36.8 us
    ppermute x1, starting transfers between devices: 1.73 us -> 0.81 us  [local_blocks(): lax.ppermute(first, 'sub', [((i + 1) % subs, i) for i in range(subs)])]
    pallas_call x9 -> x10, Pallas kernels: 14.7 us -> 14.8 us  [call(): pl.pallas_call(kernel, out_shape=out_shape, in_specs=places, out_specs=ja...]
  transfers between devices with their start and end apart: 22 -> 21, of which waited for: 13 -> 13; matrix products, arithmetic and copies ran while one was open for 3% -> 3% of each run, Pallas kernels for 11% -> 11%
where the time goes in v8:
time: 79.7 us; the launch traced here: 79.3 us
  starting transfers between devices  36.8 us (46%)
  waiting for transfers between devices  21.4 us (27%)
  Pallas kernels  14.8 us (19%)
  other arithmetic  3.33 us (4%)
  local copies, waits for them, and re-layouts  1.94 us (2%)
  between operations  0.97 us (1%)
    ppermute x18, starting transfers between devices, scatter(): lax.ppermute(sends[d], axis, [(i, (i + d) % count) for i in range(count)])  25.3 us
    ppermute x18, waiting for transfers between devices, scatter(): lax.ppermute(sends[d], axis, [(i, (i + d) % count) for i in range(count)])  19.9 us
    pallas_call x10, Pallas kernels, call(): pl.pallas_call(kernel, out_shape=out_shape, in_specs=places, out_specs=ja...  14.8 us
    all_to_all x2, starting transfers between devices, exchange(): lax.all_to_all(values, ('slab', 'sub'), split_axis=0, concat_axis=0, tile...  10.7 us
    unnamed x20, local copies, waits for them, and re-layouts  1.7 us
    convert_element_type x2, other arithmetic, local_blocks(): spectra = exchange(spectra.astype(f16))  1.63 us
  transfers between devices with their start and end apart: 21, of which 13 were waited for; matrix products, arithmetic and copies ran while one was open for 3% of the time, Pallas kernels for 11%

profile of v8, /device:TPU:0, one launch (start us, length us, event | category | flops | bytes accessed | tf_op | source)
XLA Modules:
  0.0 79.3 jit_solution(15382513632357187776)
XLA Ops:
  0.6 0.1 pad_add_fusion.place
  0.7 0.9 %copy-done = bf16[8,32,512]{2,1,0:T(8,128)(2,1)S(1)} copy-done((bf16[8,32,512]{2,1,0:T(8,128)(2,1)S(1)}, bf16[8,32,512]{2,1,0:T(8,128)(2,1)}, u32[]{:S(2)}) %copy-start) | copy-done | bytes 262168
  1.7 0.7 copy-done.1
  2.4 0.6 shard_map.113
  3.0 3.1 %collective-permute-start = (bf16[272,128]{1,0:T(8,128)(2,1)S(1)}, bf16[272,128]{1,0:T(8,128)(2,1)S(1)}, u32[]{:S(2)}, u32[]{:S(2)}) collective-permute-start(bf16[272,128]{1,0:T(8,128)(2,1)S(1)} %get-tuple-element.33), channel_id=1, source_target_pairs={{0,4},{4,8},{8,12},{12,0},{1,5},{5,9},{9,13},{13,1},{2,6},{6,10},{... | collective-permute-start | bytes 208904 | tf_op jit(solution)/shard_map/ppermute | solution.py:484
  6.1 2.6 %collective-permute-start.1 = (bf16[272,128]{1,0:T(8,128)(2,1)S(1)}, bf16[272,128]{1,0:T(8,128)(2,1)S(1)}, u32[]{:S(2)}, u32[]{:S(2)}) collective-permute-start(bf16[272,128]{1,0:T(8,128)(2,1)S(1)} %get-tuple-element.34), channel_id=1, source_target_pairs={{0,8},{4,12},{8,0},{12,4},{1,9},{5,13},{9,1},{13,5},{2,10},{6,14},... | collective-permute-start | bytes 208904 | tf_op jit(solution)/shard_map/ppermute | solution.py:484
  8.7 1.3 %collective-permute-start.2 = (bf16[272,128]{1,0:T(8,128)(2,1)S(1)}, bf16[272,128]{1,0:T(8,128)(2,1)S(1)}, u32[]{:S(2)}, u32[]{:S(2)}) collective-permute-start(bf16[272,128]{1,0:T(8,128)(2,1)S(1)} %get-tuple-element.35), channel_id=1, source_target_pairs={{0,12},{4,0},{8,4},{12,8},{1,13},{5,1},{9,5},{13,9},{2,14},{6,2},{... | collective-permute-start | bytes 208904 | tf_op jit(solution)/shard_map/ppermute | solution.py:484
  10.0 0.7 collective-permute-done.refs_1_
  10.7 2.7 %collective-permute-done.1.refs_2_ = bf16[272,128]{1,0:T(8,128)(2,1)S(1)} collective-permute-done((bf16[272,128]{1,0:T(8,128)(2,1)S(1)}, bf16[272,128]{1,0:T(8,128)(2,1)S(1)}, u32[]{:S(2)}, u32[]{:S(2)}) %collective-permute-start.1) | collective-permute-done | bytes 69664 | tf_op jit(solution)/shard_map/ppermute | solution.py:484
  13.4 0.2 collective-permute-done.2.refs_3_
  13.6 1.3 %shard_map.114 = (bf16[10,32,128]{2,1,0:T(8,128)(2,1)S(1)}, bf16[10,32,128]{2,1,0:T(8,128)(2,1)S(1)}, bf16[10,32,128]{2,1,0:T(8,128)(2,1)S(1)}, bf16[10,32,128]{2,1,0:T(8,128)(2,1)S(1)}) custom-call(s32[2]{0:T(128)S(1)} %pad_add_fusion.place, bf16[272,128]{1,0:T(8,128)(2,1)S(1)} %get-tuple-element.32.refs_0_, ...), custom_call_target="tpu_custom_call" | custom-call | flops 1073741824 | bytes 606216 | tf_op jit(solution)/shard_map/pallas_call | solution.py:204
  14.9 1.8 %collective-permute-start.3 = (bf16[10,32,128]{2,1,0:T(8,128)(2,1)S(1)}, bf16[10,32,128]{2,1,0:T(8,128)(2,1)S(1)}, u32[]{:S(2)}, u32[]{:S(2)}) collective-permute-start(bf16[10,32,128]{2,1,0:T(8,128)(2,1)S(1)} %get-tuple-element.37), channel_id=1, source_target_pairs={{0,4},{4,8},{8,12},{12,0},{1,5},{5,9},{9,13},{13,1},{2,6},{6,10},{... | collective-permute-start | bytes 245768 | tf_op jit(solution)/shard_map/ppermute | solution.py:484
  16.7 2.0 %collective-permute-start.4 = (bf16[10,32,128]{2,1,0:T(8,128)(2,1)S(1)}, bf16[10,32,128]{2,1,0:T(8,128)(2,1)S(1)}, u32[]{:S(2)}, u32[]{:S(2)}) collective-permute-start(bf16[10,32,128]{2,1,0:T(8,128)(2,1)S(1)} %get-tuple-element.38), channel_id=1, source_target_pairs={{0,8},{4,12},{8,0},{12,4},{1,9},{5,13},{9,1},{13,5},{2,10},{6,14},... | collective-permute-start | bytes 245768 | tf_op jit(solution)/shard_map/ppermute | solution.py:484
  18.7 0.5 collective-permute-start.5
  19.2 0.0 copy-done.3
  19.2 0.0 copy-done.5
  19.2 0.3 shard_map.115.refs_5_
  19.5 2.6 %collective-permute-done.3.refs_1_ = bf16[10,32,128]{2,1,0:T(8,128)(2,1)S(1)} collective-permute-done((bf16[10,32,128]{2,1,0:T(8,128)(2,1)S(1)}, bf16[10,32,128]{2,1,0:T(8,128)(2,1)S(1)}, u32[]{:S(2)}, u32[]{:S(2)}) %collective-permute-start.3) | collective-permute-done | bytes 81952 | tf_op jit(solution)/shard_map/ppermute | solution.py:484
  22.1 2.3 %collective-permute-done.4.refs_2_ = bf16[10,32,128]{2,1,0:T(8,128)(2,1)S(1)} collective-permute-done((bf16[10,32,128]{2,1,0:T(8,128)(2,1)S(1)}, bf16[10,32,128]{2,1,0:T(8,128)(2,1)S(1)}, u32[]{:S(2)}, u32[]{:S(2)}) %collective-permute-start.4) | collective-permute-done | bytes 81952 | tf_op jit(solution)/shard_map/ppermute | solution.py:484
  24.4 0.0 collective-permute-done.5.refs_3_
  24.4 0.0 copy-done.4
  24.4 2.0 %shard_map.116 = (f32[24,512]{1,0:T(8,128)S(1)}, f32[8,32,512]{2,1,0:T(8,128)S(1)}, f32[8,32,512]{2,1,0:T(8,128)S(1)}, f32[4,4,48,256]{3,2,1,0:T(8,128)S(1)}, f32[16,16,256]{2,1,0:T(8,128)S(1)}) custom-call(s32[2]{0:T(128)S(1)} %pad_add_fusion.place, bf16[10,32,128]{2,1,0:T(8,128)(2,1)S(1)} %get-tuple-element.36.refs_0_, ...), custom_call_target="tpu_custom_call" | custom-call | flops 3221225472 | bytes 4309000 | tf_op jit(solution)/shard_map/pallas_call | solution.py:204
  26.4 0.1 convert_element_type.51
  26.5 0.8 %collective-permute-start.12 = (f32[24,512]{1,0:T(8,128)S(1)}, f32[24,512]{1,0:T(8,128)S(1)}, u32[]{:S(2)}, u32[]{:S(2)}) collective-permute-start(f32[24,512]{1,0:T(8,128)S(1)} %get-tuple-element.49), channel_id=1, source_target_pairs={{1,0},{2,1},{3,2},{0,3},{5,4},{6,5},{7,6},{4,7},{9,8},{10,9},{11,1... | collective-permute-start | bytes 147464 | tf_op jit(solution)/shard_map/ppermute | solution.py:531
  27.3 0.1 slice_bitcast_fusion
  27.4 1.9 %collective-permute-start.8 = (f16[4,48,256]{2,1,0:T(8,128)(2,1)S(1)}, f16[4,48,256]{2,1,0:T(8,128)(2,1)S(1)}, u32[]{:S(2)}, u32[]{:S(2)}) collective-permute-start(f16[4,48,256]{2,1,0:T(8,128)(2,1)S(1)} %get-tuple-element.62), channel_id=1, source_target_pairs={{0,12},{4,0},{8,4},{12,8},{1,13},{5,1},{9,5},{13,9},{2,14},{6,2},{... | collective-permute-start | bytes 294920 | tf_op jit(solution)/shard_map/ppermute | solution.py:484
  29.3 2.0 %collective-permute-start.7 = (f16[4,48,256]{2,1,0:T(8,128)(2,1)S(1)}, f16[4,48,256]{2,1,0:T(8,128)(2,1)S(1)}, u32[]{:S(2)}, u32[]{:S(2)}) collective-permute-start(f16[4,48,256]{2,1,0:T(8,128)(2,1)S(1)} %get-tuple-element.63), channel_id=1, source_target_pairs={{0,8},{4,12},{8,0},{12,4},{1,9},{5,13},{9,1},{13,5},{2,10},{6,14},... | collective-permute-start | bytes 294920 | tf_op jit(solution)/shard_map/ppermute | solution.py:484
  31.2 0.0 collective-permute-start.6
  31.2 0.0 collective-permute-done.12.beyond
  31.2 0.7 shard_map.118
  32.0 0.8 %convert_element_type.56 = f16[16,48,256]{2,1,0:T(8,128)(2,1)} convert(f32[16,48,256]{2,1,0:T(8,128)S(1)} %shard_map.118) | non-fusion elementwise | flops 196608 | bytes 1179648 | tf_op jit(solution)/shard_map/convert_element_type | solution.py:547
  32.8 5.4 %all-to-all-start = ((f16[16,48,256]{2,1,0:T(8,128)(2,1)}), f16[16,48,256]{2,1,0:T(8,128)(2,1)S(1)}, u32[]{:S(2)}, u32[]{:S(2)}) async-start(f16[16,48,256]{2,1,0:T(8,128)(2,1)} %convert_element_type.56), calls=%async_computation | async-start | bytes 786432 | tf_op jit(solution)/shard_map/all_to_all | solution.py:488
  38.2 0.0 collective-permute-done.8
  38.2 1.7 %collective-permute-done.7 = f16[4,48,256]{2,1,0:T(8,128)(2,1)S(1)} collective-permute-done((f16[4,48,256]{2,1,0:T(8,128)(2,1)S(1)}, f16[4,48,256]{2,1,0:T(8,128)(2,1)S(1)}, u32[]{:S(2)}, u32[]{:S(2)}) %collective-permute-start.7) | collective-permute-done | bytes 98336 | tf_op jit(solution)/shard_map/ppermute | solution.py:484
  40.0 0.0 collective-permute-done.6
  40.1 0.1 collective-permute-start.9
  40.2 1.3 %collective-permute-start.10 = (f16[4,48,256]{2,1,0:T(8,128)(2,1)S(1)}, f16[4,48,256]{2,1,0:T(8,128)(2,1)S(1)}, u32[]{:S(2)}, u32[]{:S(2)}) collective-permute-start(f16[4,48,256]{2,1,0:T(8,128)(2,1)S(1)} %pad_maximum_fusion.1), channel_id=1, source_target_pairs={{0,2},{1,3},{2,0},{3,1},{4,6},{5,7},{6,4},{7,5},{8,10},{9,11},{10,... | collective-permute-start | bytes 294920 | tf_op jit(solution)/shard_map/ppermute | solution.py:484
  41.5 1.5 %collective-permute-start.11 = (f16[4,48,256]{2,1,0:T(8,128)(2,1)S(1)}, f16[4,48,256]{2,1,0:T(8,128)(2,1)S(1)}, u32[]{:S(2)}, u32[]{:S(2)}) collective-permute-start(f16[4,48,256]{2,1,0:T(8,128)(2,1)S(1)} %pad_maximum_fusion.2), channel_id=1, source_target_pairs={{0,3},{1,0},{2,1},{3,2},{4,7},{5,4},{6,5},{7,6},{8,11},{9,8},{10,9... | collective-permute-start | bytes 294920 | tf_op jit(solution)/shard_map/ppermute | solution.py:484
  43.0 1.3 %shard_map.119 = bf16[8,32,512]{2,1,0:T(8,128)(2,1)} custom-call(s32[2]{0:T(128)S(1)} %pad_add_fusion.place, bf16[10,32,128]{2,1,0:T(8,128)(2,1)S(1)} %get-tuple-element.36.refs_0_, bf16[10,32,128]{2,1,0:T(8,128)(2,1)S(1)} %collective-permute-done.3.refs_1_, bf16[10,32,128]{2,1,0:T(8,128)(2,1)S(1)} %collective-permute-done.4.refs_2_, ...), custom_call_target="tpu_custom_call" | custom-call | bytes 589832 | tf_op jit(solution)/shard_map/pallas_call | solution.py:204
  44.4 1.6 %collective-permute-done.9 = f16[4,48,256]{2,1,0:T(8,128)(2,1)S(1)} collective-permute-done((f16[4,48,256]{2,1,0:T(8,128)(2,1)S(1)}, f16[4,48,256]{2,1,0:T(8,128)(2,1)S(1)}, u32[]{:S(2)}, u32[]{:S(2)}) %collective-permute-start.9) | collective-permute-done | bytes 98336 | tf_op jit(solution)/shard_map/ppermute | solution.py:484
  45.9 0.6 collective-permute-done.10
  46.6 1.9 %collective-permute-done.11 = f16[4,48,256]{2,1,0:T(8,128)(2,1)S(1)} collective-permute-done((f16[4,48,256]{2,1,0:T(8,128)(2,1)S(1)}, f16[4,48,256]{2,1,0:T(8,128)(2,1)S(1)}, u32[]{:S(2)}, u32[]{:S(2)}) %collective-permute-start.11) | collective-permute-done | bytes 98336 | tf_op jit(solution)/shard_map/ppermute | solution.py:484
  48.5 2.8 %shard_map.117 = (f32[4,48,256]{2,1,0:T(8,128)S(1)}, f32[4,48,256]{2,1,0:T(8,128)S(1)}, f32[4,48,256]{2,1,0:T(8,128)S(1)}, f32[4,48,256]{2,1,0:T(8,128)S(1)}) custom-call(s32[2]{0:T(128)S(1)} %pad_add_fusion.place, f32[4,48,256]{2,1,0:T(8,128)S(1)} %maximum_convert_fusion.refs_0_, f32[4,48,256]{2,1,0:T(8,128)S(1)} %convert_element_type.53.refs_1_, ...), custom_call_target="tpu_custom_call" | custom-call | flops 2147483648 | bytes 2293768 | tf_op jit(solution)/shard_map/pallas_call | solution.py:204
  51.3 0.0 all-to-all-done
  51.4 2.5 %collective-permute-start.15 = (f16[4,48,256]{2,1,0:T(8,128)(2,1)S(1)}, f16[4,48,256]{2,1,0:T(8,128)(2,1)S(1)}, u32[]{:S(2)}, u32[]{:S(2)}) collective-permute-start(f16[4,48,256]{2,1,0:T(8,128)(2,1)S(1)} %convert_element_type.63), channel_id=1, source_target_pairs={{0,12},{4,0},{8,4},{12,8},{1,13},{5,1},{9,5},{13,9},{2,14},{6,2},{... | collective-permute-start | bytes 294920 | tf_op jit(solution)/shard_map/ppermute | solution.py:484
  53.9 0.0 collective-permute-start.14
  53.9 1.4 %collective-permute-start.13 = (f16[4,48,256]{2,1,0:T(8,128)(2,1)S(1)}, f16[4,48,256]{2,1,0:T(8,128)(2,1)S(1)}, u32[]{:S(2)}, u32[]{:S(2)}) collective-permute-start(f16[4,48,256]{2,1,0:T(8,128)(2,1)S(1)} %convert_element_type.61), channel_id=1, source_target_pairs={{0,4},{4,8},{8,12},{12,0},{1,5},{5,9},{9,13},{13,1},{2,6},{6,10},{... | collective-permute-start | bytes 294920 | tf_op jit(solution)/shard_map/ppermute | solution.py:484
  55.3 0.1 convert_element_type.57.spectra
  55.4 2.6 %shard_map.120 = f32[16,48,256]{2,1,0:T(8,128)S(1)} custom-call(s32[2]{0:T(128)S(1)} %pad_add_fusion.place, f32[16,48,256]{2,1,0:T(8,128)S(1)} %convert_element_type.57.spectra, bf16[4,256,256]{2,1,0:T(8,128)(2,1)S(1)} %copy-done.8, bf16[6,128,128]{2,1,0:T(8,128)(2,1)S(1)} %copy-done.9), custom_call_target="tpu_custom_call" | custom-call | flops 2147483648 | bytes 2293768 | tf_op jit(solution)/shard_map/pallas_call | solution.py:204
  58.0 0.8 %convert_element_type.58 = f16[16,48,256]{2,1,0:T(8,128)(2,1)} convert(f32[16,48,256]{2,1,0:T(8,128)S(1)} %shard_map.120) | non-fusion elementwise | flops 196608 | bytes 1179648 | tf_op jit(solution)/shard_map/convert_element_type | solution.py:571
  58.8 5.3 %all-to-all-start.1 = ((f16[16,48,256]{2,1,0:T(8,128)(2,1)}), f16[16,48,256]{2,1,0:T(8,128)(2,1)}, u32[]{:S(2)}, u32[]{:S(2)}) async-start(f16[16,48,256]{2,1,0:T(8,128)(2,1)} %convert_element_type.58), calls=%async_computation.1 | async-start | bytes 786432 | tf_op jit(solution)/shard_map/all_to_all | solution.py:488
  64.1 0.0 collective-permute-done.15
  64.1 0.0 collective-permute-done.14
  64.1 0.0 collective-permute-done.13
  64.2 0.4 collective-permute-start.16
  64.7 1.7 %collective-permute-start.17 = (f16[4,48,256]{2,1,0:T(8,128)(2,1)S(1)}, f16[4,48,256]{2,1,0:T(8,128)(2,1)S(1)}, u32[]{:S(2)}, u32[]{:S(2)}) collective-permute-start(f16[4,48,256]{2,1,0:T(8,128)(2,1)S(1)} %pad_maximum_fusion.4), channel_id=1, source_target_pairs={{0,2},{1,3},{2,0},{3,1},{4,6},{5,7},{6,4},{7,5},{8,10},{9,11},{10,... | collective-permute-start | bytes 294920 | tf_op jit(solution)/shard_map/ppermute | solution.py:484
  66.4 1.4 %collective-permute-start.18 = (f16[4,48,256]{2,1,0:T(8,128)(2,1)S(1)}, f16[4,48,256]{2,1,0:T(8,128)(2,1)S(1)}, u32[]{:S(2)}, u32[]{:S(2)}) collective-permute-start(f16[4,48,256]{2,1,0:T(8,128)(2,1)S(1)} %pad_maximum_fusion.5), channel_id=1, source_target_pairs={{0,3},{1,0},{2,1},{3,2},{4,7},{5,4},{6,5},{7,6},{8,11},{9,8},{10,9... | collective-permute-start | bytes 294920 | tf_op jit(solution)/shard_map/ppermute | solution.py:484
  67.9 3.6 %collective-permute-done.16 = f16[4,48,256]{2,1,0:T(8,128)(2,1)S(1)} collective-permute-done((f16[4,48,256]{2,1,0:T(8,128)(2,1)S(1)}, f16[4,48,256]{2,1,0:T(8,128)(2,1)S(1)}, u32[]{:S(2)}, u32[]{:S(2)}) %collective-permute-start.16) | collective-permute-done | bytes 98336 | tf_op jit(solution)/shard_map/ppermute | solution.py:484
  71.4 1.3 %collective-permute-done.17 = f16[4,48,256]{2,1,0:T(8,128)(2,1)S(1)} collective-permute-done((f16[4,48,256]{2,1,0:T(8,128)(2,1)S(1)}, f16[4,48,256]{2,1,0:T(8,128)(2,1)S(1)}, u32[]{:S(2)}, u32[]{:S(2)}) %collective-permute-start.17) | collective-permute-done | bytes 98336 | tf_op jit(solution)/shard_map/ppermute | solution.py:484
  72.8 0.7 collective-permute-done.18
  73.5 1.2 %shard_map.121 = (f32[8,32,512]{2,1,0:T(8,128)S(1)}, f32[16,16,256]{2,1,0:T(8,128)S(1)}) custom-call(s32[2]{0:T(128)S(1)} %pad_add_fusion.place, bf16[2,512,512]{2,1,0:T(8,128)(2,1)S(1)} %copy-done.6, f32[3,8,32,512]{3,2,1,0:T(8,128)S(1)} %copy-done.2, f32[4,48,256]{2,1,0:T(8,128)S(1)} %maximum_convert_fusion.1.refs_0_, ...), custom_call_target="tpu_custom_call" | custom-call | flops 1073741824 | bytes 4194312 | tf_op jit(solution)/shard_map/pallas_call | solution.py:204
  74.8 1.5 %all-to-all-done.1 = f16[16,48,256]{2,1,0:T(8,128)(2,1)} async-done(((f16[16,48,256]{2,1,0:T(8,128)(2,1)}), f16[16,48,256]{2,1,0:T(8,128)(2,1)}, u32[]{:S(2)}, u32[]{:S(2)}) %all-to-all-start.1) | async-done | bytes 393248 | tf_op jit(solution)/shard_map/all_to_all | solution.py:488
  76.3 1.1 %convert_element_type.59.spectra = f32[16,48,256]{2,1,0:T(8,128)S(1)} convert(f16[16,48,256]{2,1,0:T(8,128)(2,1)} %all-to-all-done.1) | non-fusion elementwise | flops 196608 | bytes 1179648 | tf_op jit(solution)/shard_map/convert_element_type | solution.py:586
  77.4 1.9 %shard_map.122 = f32[3,8,32,512]{3,2,1,0:T(8,128)} custom-call(f32[16,48,256]{2,1,0:T(8,128)S(1)} %convert_element_type.59.spectra, bf16[2,512,512]{2,1,0:T(8,128)(2,1)S(1)} %copy-done.6, f32[3,8,32,512]{3,2,1,0:T(8,128)S(1)} %copy-done.2, f32[8,32,512]{2,1,0:T(8,128)S(1)} %get-tuple-element.59.updated, f32[16,16,256]{2,1,0:T(8,128)S(1)} %get-tuple-element.60.kept), custom_call_target="tpu_custom_call" | custom-call | flops 2147483648 | bytes 5767168 | tf_op jit(solution)/shard_map/pallas_call | solution.py:204
  (39 shorter events, 0.6 us)
Async XLA Ops:
  0.7 1.0 %copy-start = (bf16[8,32,512]{2,1,0:T(8,128)(2,1)S(1)}, bf16[8,32,512]{2,1,0:T(8,128)(2,1)}, u32[]{:S(2)}) copy-start(bf16[8,32,512]{2,1,0:T(8,128)(2,1)} %moving.1) | copy-start | bytes 786436
  1.7 0.7 copy-start.1
  3.0 7.7 %collective-permute-start = (bf16[272,128]{1,0:T(8,128)(2,1)S(1)}, bf16[272,128]{1,0:T(8,128)(2,1)S(1)}, u32[]{:S(2)}, u32[]{:S(2)}) collective-permute-start(bf16[272,128]{1,0:T(8,128)(2,1)S(1)} %get-tuple-element.33), channel_id=1, source_target_pairs={{0,4},{4,8},{8,12},{12,0},{1,5},{5,9},{9,13},{13,1},{2,6},{6,10},{... | collective-permute-start | bytes 208904 | tf_op jit(solution)/shard_map/ppermute | solution.py:484
  6.1 7.3 %collective-permute-start.1 = (bf16[272,128]{1,0:T(8,128)(2,1)S(1)}, bf16[272,128]{1,0:T(8,128)(2,1)S(1)}, u32[]{:S(2)}, u32[]{:S(2)}) collective-permute-start(bf16[272,128]{1,0:T(8,128)(2,1)S(1)} %get-tuple-element.34), channel_id=1, source_target_pairs={{0,8},{4,12},{8,0},{12,4},{1,9},{5,13},{9,1},{13,5},{2,10},{6,14},... | collective-permute-start | bytes 208904 | tf_op jit(solution)/shard_map/ppermute | solution.py:484
  8.7 4.9 %collective-permute-start.2 = (bf16[272,128]{1,0:T(8,128)(2,1)S(1)}, bf16[272,128]{1,0:T(8,128)(2,1)S(1)}, u32[]{:S(2)}, u32[]{:S(2)}) collective-permute-start(bf16[272,128]{1,0:T(8,128)(2,1)S(1)} %get-tuple-element.35), channel_id=1, source_target_pairs={{0,12},{4,0},{8,4},{12,8},{1,13},{5,1},{9,5},{13,9},{2,14},{6,2},{... | collective-permute-start | bytes 208904 | tf_op jit(solution)/shard_map/ppermute | solution.py:484
  13.5 5.6 %copy-start.3 = (f32[8,32,512]{2,1,0:T(8,128)S(1)}, f32[8,32,512]{2,1,0:T(8,128)}, u32[]{:S(2)}) copy-start(f32[8,32,512]{2,1,0:T(8,128)} %stiffness.1) | copy-start | bytes 1572868
  13.5 5.6 %copy-start.5 = (s32[8,32,4]{1,2,0:T(4,128)S(1)}, s32[8,32,4]{1,2,0:T(4,128)}, u32[]{:S(2)}) copy-start(s32[8,32,4]{1,2,0:T(4,128)} %param.15) | copy-start | bytes 12292
  14.9 7.2 %collective-permute-start.3 = (bf16[10,32,128]{2,1,0:T(8,128)(2,1)S(1)}, bf16[10,32,128]{2,1,0:T(8,128)(2,1)S(1)}, u32[]{:S(2)}, u32[]{:S(2)}) collective-permute-start(bf16[10,32,128]{2,1,0:T(8,128)(2,1)S(1)} %get-tuple-element.37), channel_id=1, source_target_pairs={{0,4},{4,8},{8,12},{12,0},{1,5},{5,9},{9,13},{13,1},{2,6},{6,10},{... | collective-permute-start | bytes 245768 | tf_op jit(solution)/shard_map/ppermute | solution.py:484
  16.7 7.7 %collective-permute-start.4 = (bf16[10,32,128]{2,1,0:T(8,128)(2,1)S(1)}, bf16[10,32,128]{2,1,0:T(8,128)(2,1)S(1)}, u32[]{:S(2)}, u32[]{:S(2)}) collective-permute-start(bf16[10,32,128]{2,1,0:T(8,128)(2,1)S(1)} %get-tuple-element.38), channel_id=1, source_target_pairs={{0,8},{4,12},{8,0},{12,4},{1,9},{5,13},{9,1},{13,5},{2,10},{6,14},... | collective-permute-start | bytes 245768 | tf_op jit(solution)/shard_map/ppermute | solution.py:484
  18.7 5.7 %collective-permute-start.5 = (bf16[10,32,128]{2,1,0:T(8,128)(2,1)S(1)}, bf16[10,32,128]{2,1,0:T(8,128)(2,1)S(1)}, u32[]{:S(2)}, u32[]{:S(2)}) collective-permute-start(bf16[10,32,128]{2,1,0:T(8,128)(2,1)S(1)} %get-tuple-element.39), channel_id=1, source_target_pairs={{0,12},{4,0},{8,4},{12,8},{1,13},{5,1},{9,5},{13,9},{2,14},{6,2},{... | collective-permute-start | bytes 245768 | tf_op jit(solution)/shard_map/ppermute | solution.py:484
  19.2 5.3 %copy-start.4 = (bf16[8,32,512]{2,1,0:T(8,128)(2,1)S(1)}, bf16[8,32,512]{2,1,0:T(8,128)(2,1)}, u32[]{:S(2)}) copy-start(bf16[8,32,512]{2,1,0:T(8,128)(2,1)} %refs_4_.2) | copy-start | bytes 786436
  19.2 5.3 %copy-start.7 = (bf16[2,512,512]{2,1,0:T(8,128)(2,1)S(1)}, bf16[2,512,512]{2,1,0:T(8,128)(2,1)}, u32[]{:S(2)}) copy-start(bf16[2,512,512]{2,1,0:T(8,128)(2,1)} %constant.15.clone.refs_6_.basis) | copy-start | bytes 3145732
  26.5 4.7 %collective-permute-start.12 = (f32[24,512]{1,0:T(8,128)S(1)}, f32[24,512]{1,0:T(8,128)S(1)}, u32[]{:S(2)}, u32[]{:S(2)}) collective-permute-start(f32[24,512]{1,0:T(8,128)S(1)} %get-tuple-element.49), channel_id=1, source_target_pairs={{1,0},{2,1},{3,2},{0,3},{5,4},{6,5},{7,6},{4,7},{9,8},{10,9},{11,1... | collective-permute-start | bytes 147464 | tf_op jit(solution)/shard_map/ppermute | solution.py:531
  27.4 10.8 %collective-permute-start.8 = (f16[4,48,256]{2,1,0:T(8,128)(2,1)S(1)}, f16[4,48,256]{2,1,0:T(8,128)(2,1)S(1)}, u32[]{:S(2)}, u32[]{:S(2)}) collective-permute-start(f16[4,48,256]{2,1,0:T(8,128)(2,1)S(1)} %get-tuple-element.62), channel_id=1, source_target_pairs={{0,12},{4,0},{8,4},{12,8},{1,13},{5,1},{9,5},{13,9},{2,14},{6,2},{... | collective-permute-start | bytes 294920 | tf_op jit(solution)/shard_map/ppermute | solution.py:484
  29.3 10.7 %collective-permute-start.7 = (f16[4,48,256]{2,1,0:T(8,128)(2,1)S(1)}, f16[4,48,256]{2,1,0:T(8,128)(2,1)S(1)}, u32[]{:S(2)}, u32[]{:S(2)}) collective-permute-start(f16[4,48,256]{2,1,0:T(8,128)(2,1)S(1)} %get-tuple-element.63), channel_id=1, source_target_pairs={{0,8},{4,12},{8,0},{12,4},{1,9},{5,13},{9,1},{13,5},{2,10},{6,14},... | collective-permute-start | bytes 294920 | tf_op jit(solution)/shard_map/ppermute | solution.py:484
  31.2 8.7 %collective-permute-start.6 = (f16[4,48,256]{2,1,0:T(8,128)(2,1)S(1)}, f16[4,48,256]{2,1,0:T(8,128)(2,1)S(1)}, u32[]{:S(2)}, u32[]{:S(2)}) collective-permute-start(f16[4,48,256]{2,1,0:T(8,128)(2,1)S(1)} %get-tuple-element.64), channel_id=1, source_target_pairs={{0,4},{4,8},{8,12},{12,0},{1,5},{5,9},{9,13},{13,1},{2,6},{6,10},{... | collective-permute-start | bytes 294920 | tf_op jit(solution)/shard_map/ppermute | solution.py:484
  32.8 18.5 %all-to-all-start = ((f16[16,48,256]{2,1,0:T(8,128)(2,1)}), f16[16,48,256]{2,1,0:T(8,128)(2,1)S(1)}, u32[]{:S(2)}, u32[]{:S(2)}) async-start(f16[16,48,256]{2,1,0:T(8,128)(2,1)} %convert_element_type.56), calls=%async_computation | async-start | bytes 786432 | tf_op jit(solution)/shard_map/all_to_all | solution.py:488
  40.0 8.5 %copy-start.8 = (bf16[4,256,256]{2,1,0:T(8,128)(2,1)S(1)}, bf16[4,256,256]{2,1,0:T(8,128)(2,1)}, u32[]{:S(2)}) copy-start(bf16[4,256,256]{2,1,0:T(8,128)(2,1)} %constant.16.clone.refs_4_.basis_z) | copy-start | bytes 1572868
  40.0 8.5 %copy-start.9 = (bf16[6,128,128]{2,1,0:T(8,128)(2,1)S(1)}, bf16[6,128,128]{2,1,0:T(8,128)(2,1)}, u32[]{:S(2)}) copy-start(bf16[6,128,128]{2,1,0:T(8,128)(2,1)} %constant.17.clone.refs_5_.basis_y) | copy-start | bytes 589828
  40.1 5.8 %collective-permute-start.9 = (f16[4,48,256]{2,1,0:T(8,128)(2,1)S(1)}, f16[4,48,256]{2,1,0:T(8,128)(2,1)S(1)}, u32[]{:S(2)}, u32[]{:S(2)}) collective-permute-start(f16[4,48,256]{2,1,0:T(8,128)(2,1)S(1)} %pad_maximum_fusion), channel_id=1, source_target_pairs={{0,1},{1,2},{2,3},{3,0},{4,5},{5,6},{6,7},{7,4},{8,9},{9,10},{10,1... | collective-permute-start | bytes 294920 | tf_op jit(solution)/shard_map/ppermute | solution.py:484
  40.2 6.4 %collective-permute-start.10 = (f16[4,48,256]{2,1,0:T(8,128)(2,1)S(1)}, f16[4,48,256]{2,1,0:T(8,128)(2,1)S(1)}, u32[]{:S(2)}, u32[]{:S(2)}) collective-permute-start(f16[4,48,256]{2,1,0:T(8,128)(2,1)S(1)} %pad_maximum_fusion.1), channel_id=1, source_target_pairs={{0,2},{1,3},{2,0},{3,1},{4,6},{5,7},{6,4},{7,5},{8,10},{9,11},{10,... | collective-permute-start | bytes 294920 | tf_op jit(solution)/shard_map/ppermute | solution.py:484
  41.5 7.0 %collective-permute-start.11 = (f16[4,48,256]{2,1,0:T(8,128)(2,1)S(1)}, f16[4,48,256]{2,1,0:T(8,128)(2,1)S(1)}, u32[]{:S(2)}, u32[]{:S(2)}) collective-permute-start(f16[4,48,256]{2,1,0:T(8,128)(2,1)S(1)} %pad_maximum_fusion.2), channel_id=1, source_target_pairs={{0,3},{1,0},{2,1},{3,2},{4,7},{5,4},{6,5},{7,6},{8,11},{9,8},{10,9... | collective-permute-start | bytes 294920 | tf_op jit(solution)/shard_map/ppermute | solution.py:484
  51.4 12.6 %collective-permute-start.15 = (f16[4,48,256]{2,1,0:T(8,128)(2,1)S(1)}, f16[4,48,256]{2,1,0:T(8,128)(2,1)S(1)}, u32[]{:S(2)}, u32[]{:S(2)}) collective-permute-start(f16[4,48,256]{2,1,0:T(8,128)(2,1)S(1)} %convert_element_type.63), channel_id=1, source_target_pairs={{0,12},{4,0},{8,4},{12,8},{1,13},{5,1},{9,5},{13,9},{2,14},{6,2},{... | collective-permute-start | bytes 294920 | tf_op jit(solution)/shard_map/ppermute | solution.py:484
  53.9 10.2 %collective-permute-start.14 = (f16[4,48,256]{2,1,0:T(8,128)(2,1)S(1)}, f16[4,48,256]{2,1,0:T(8,128)(2,1)S(1)}, u32[]{:S(2)}, u32[]{:S(2)}) collective-permute-start(f16[4,48,256]{2,1,0:T(8,128)(2,1)S(1)} %convert_element_type.62), channel_id=1, source_target_pairs={{0,8},{4,12},{8,0},{12,4},{1,9},{5,13},{9,1},{13,5},{2,10},{6,14},... | collective-permute-start | bytes 294920 | tf_op jit(solution)/shard_map/ppermute | solution.py:484
  53.9 10.3 %collective-permute-start.13 = (f16[4,48,256]{2,1,0:T(8,128)(2,1)S(1)}, f16[4,48,256]{2,1,0:T(8,128)(2,1)S(1)}, u32[]{:S(2)}, u32[]{:S(2)}) collective-permute-start(f16[4,48,256]{2,1,0:T(8,128)(2,1)S(1)} %convert_element_type.61), channel_id=1, source_target_pairs={{0,4},{4,8},{8,12},{12,0},{1,5},{5,9},{9,13},{13,1},{2,6},{6,10},{... | collective-permute-start | bytes 294920 | tf_op jit(solution)/shard_map/ppermute | solution.py:484
  58.8 14.7 %copy-start.2 = (f32[3,8,32,512]{3,2,1,0:T(8,128)S(1)}, f32[3,8,32,512]{3,2,1,0:T(8,128)}, u32[]{:S(2)}) copy-start(f32[3,8,32,512]{3,2,1,0:T(8,128)} %velocity.3) | copy-start | bytes 4718596
  58.8 14.7 %copy-start.6 = (bf16[2,512,512]{2,1,0:T(8,128)(2,1)S(1)}, bf16[2,512,512]{2,1,0:T(8,128)(2,1)}, u32[]{:S(2)}) copy-start(bf16[2,512,512]{2,1,0:T(8,128)(2,1)} %constant.18.clone.basis) | copy-start | bytes 3145732
  58.8 17.5 %all-to-all-start.1 = ((f16[16,48,256]{2,1,0:T(8,128)(2,1)}), f16[16,48,256]{2,1,0:T(8,128)(2,1)}, u32[]{:S(2)}, u32[]{:S(2)}) async-start(f16[16,48,256]{2,1,0:T(8,128)(2,1)} %convert_element_type.58), calls=%async_computation.1 | async-start | bytes 786432 | tf_op jit(solution)/shard_map/all_to_all | solution.py:488
  64.2 7.2 %collective-permute-start.16 = (f16[4,48,256]{2,1,0:T(8,128)(2,1)S(1)}, f16[4,48,256]{2,1,0:T(8,128)(2,1)S(1)}, u32[]{:S(2)}, u32[]{:S(2)}) collective-permute-start(f16[4,48,256]{2,1,0:T(8,128)(2,1)S(1)} %pad_maximum_fusion.3), channel_id=1, source_target_pairs={{0,1},{1,2},{2,3},{3,0},{4,5},{5,6},{6,7},{7,4},{8,9},{9,10},{10,1... | collective-permute-start | bytes 294920 | tf_op jit(solution)/shard_map/ppermute | solution.py:484
  64.7 8.1 %collective-permute-start.17 = (f16[4,48,256]{2,1,0:T(8,128)(2,1)S(1)}, f16[4,48,256]{2,1,0:T(8,128)(2,1)S(1)}, u32[]{:S(2)}, u32[]{:S(2)}) collective-permute-start(f16[4,48,256]{2,1,0:T(8,128)(2,1)S(1)} %pad_maximum_fusion.4), channel_id=1, source_target_pairs={{0,2},{1,3},{2,0},{3,1},{4,6},{5,7},{6,4},{7,5},{8,10},{9,11},{10,... | collective-permute-start | bytes 294920 | tf_op jit(solution)/shard_map/ppermute | solution.py:484
  66.4 7.0 %collective-permute-start.18 = (f16[4,48,256]{2,1,0:T(8,128)(2,1)S(1)}, f16[4,48,256]{2,1,0:T(8,128)(2,1)S(1)}, u32[]{:S(2)}, u32[]{:S(2)}) collective-permute-start(f16[4,48,256]{2,1,0:T(8,128)(2,1)S(1)} %pad_maximum_fusion.5), channel_id=1, source_target_pairs={{0,3},{1,0},{2,1},{3,2},{4,7},{5,4},{6,5},{7,6},{8,11},{9,8},{10,9... | collective-permute-start | bytes 294920 | tf_op jit(solution)/shard_map/ppermute | solution.py:484

commit v9 on v8

--- a/solution.py
+++ b/solution.py
@@ -277,7 +277,7 @@
             ],
             axis=1,
         )
-        out[z] = 0.5 * marked * stiffness[z]
+        out[z] = 4.0 * marked * stiffness[z]
 
 
 def force_zx_kernel(slabs, subs, place, *refs):
@@ -504,7 +504,7 @@
         flops=1 << 30,
     )
     received = scatter(sends, "slab")
-    basis_x = in_two(8.0 * real_basis(x_length))
+    basis_x = in_two(real_basis(x_length))
     basis_z = np.kron(real_basis(total_z), np.eye(8))
     basis_z = np.concatenate([in_two(basis_z), in_two(basis_z.T)])
     basis_y = real_basis(total_y)
@@ -569,7 +569,6 @@
         flops=2 << 30,
     )
     spectra = exchange(spectra.astype(f16))
-    basis_x = in_two(real_basis(x_length))
     updated, kept = call(
         functools.partial(update_z_kernel, slabs, subs),
         [shape(moving.shape), shape((devices, part - cut, area))],

time: 79.7 us -> 79.6 us (level)
    unnamed x20 -> x18, local copies, waits for them, and re-layouts: 1.7 us -> 1.69 us
where the time goes in v9:
time: 79.6 us; the launch traced here: 79.1 us
  starting transfers between devices  36.7 us (46%)
  waiting for transfers between devices  21.4 us (27%)
  Pallas kernels  14.8 us (19%)
  other arithmetic  3.33 us (4%)
  local copies, waits for them, and re-layouts  1.93 us (2%)
  between operations  0.95 us (1%)
    ppermute x18, starting transfers between devices, scatter(): lax.ppermute(sends[d], axis, [(i, (i + d) % count) for i in range(count)])  25.3 us
    ppermute x18, waiting for transfers between devices, scatter(): lax.ppermute(sends[d], axis, [(i, (i + d) % count) for i in range(count)])  19.9 us
    pallas_call x10, Pallas kernels, call(): pl.pallas_call(kernel, out_shape=out_shape, in_specs=places, out_specs=ja...  14.8 us
    all_to_all x2, starting transfers between devices, exchange(): lax.all_to_all(values, ('slab', 'sub'), split_axis=0, concat_axis=0, tile...  10.6 us
    unnamed x18, local copies, waits for them, and re-layouts  1.69 us
    convert_element_type x2, other arithmetic, local_blocks(): spectra = exchange(spectra.astype(f16))  1.63 us
  transfers between devices with their start and end apart: 21, of which 13 were waited for; matrix products, arithmetic and copies ran while one was open for 3% of the time, Pallas kernels for 11%

profile of v9, /device:TPU:0, one launch (start us, length us, event | category | flops | bytes accessed | tf_op | source)
XLA Modules:
  0.0 79.1 jit_solution(11207486267928745786)
XLA Ops:
  0.6 0.1 pad_add_fusion.place
  0.7 0.9 %copy-done = bf16[8,32,512]{2,1,0:T(8,128)(2,1)S(1)} copy-done((bf16[8,32,512]{2,1,0:T(8,128)(2,1)S(1)}, bf16[8,32,512]{2,1,0:T(8,128)(2,1)}, u32[]{:S(2)}) %copy-start) | copy-done | bytes 262168
  1.7 0.7 copy-done.1
  2.4 0.6 shard_map.104
  3.0 3.1 %collective-permute-start = (bf16[272,128]{1,0:T(8,128)(2,1)S(1)}, bf16[272,128]{1,0:T(8,128)(2,1)S(1)}, u32[]{:S(2)}, u32[]{:S(2)}) collective-permute-start(bf16[272,128]{1,0:T(8,128)(2,1)S(1)} %get-tuple-element.33), channel_id=1, source_target_pairs={{0,4},{4,8},{8,12},{12,0},{1,5},{5,9},{9,13},{13,1},{2,6},{6,10},{... | collective-permute-start | bytes 208904 | tf_op jit(solution)/shard_map/ppermute | solution.py:484
  6.1 2.6 %collective-permute-start.1 = (bf16[272,128]{1,0:T(8,128)(2,1)S(1)}, bf16[272,128]{1,0:T(8,128)(2,1)S(1)}, u32[]{:S(2)}, u32[]{:S(2)}) collective-permute-start(bf16[272,128]{1,0:T(8,128)(2,1)S(1)} %get-tuple-element.34), channel_id=1, source_target_pairs={{0,8},{4,12},{8,0},{12,4},{1,9},{5,13},{9,1},{13,5},{2,10},{6,14},... | collective-permute-start | bytes 208904 | tf_op jit(solution)/shard_map/ppermute | solution.py:484
  8.7 1.3 %collective-permute-start.2 = (bf16[272,128]{1,0:T(8,128)(2,1)S(1)}, bf16[272,128]{1,0:T(8,128)(2,1)S(1)}, u32[]{:S(2)}, u32[]{:S(2)}) collective-permute-start(bf16[272,128]{1,0:T(8,128)(2,1)S(1)} %get-tuple-element.35), channel_id=1, source_target_pairs={{0,12},{4,0},{8,4},{12,8},{1,13},{5,1},{9,5},{13,9},{2,14},{6,2},{... | collective-permute-start | bytes 208904 | tf_op jit(solution)/shard_map/ppermute | solution.py:484
  10.0 0.7 collective-permute-done.refs_1_
  10.7 2.7 %collective-permute-done.1.refs_2_ = bf16[272,128]{1,0:T(8,128)(2,1)S(1)} collective-permute-done((bf16[272,128]{1,0:T(8,128)(2,1)S(1)}, bf16[272,128]{1,0:T(8,128)(2,1)S(1)}, u32[]{:S(2)}, u32[]{:S(2)}) %collective-permute-start.1) | collective-permute-done | bytes 69664 | tf_op jit(solution)/shard_map/ppermute | solution.py:484
  13.4 0.2 collective-permute-done.2.refs_3_
  13.6 1.3 %shard_map.105 = (bf16[10,32,128]{2,1,0:T(8,128)(2,1)S(1)}, bf16[10,32,128]{2,1,0:T(8,128)(2,1)S(1)}, bf16[10,32,128]{2,1,0:T(8,128)(2,1)S(1)}, bf16[10,32,128]{2,1,0:T(8,128)(2,1)S(1)}) custom-call(s32[2]{0:T(128)S(1)} %pad_add_fusion.place, bf16[272,128]{1,0:T(8,128)(2,1)S(1)} %get-tuple-element.32.refs_0_, ...), custom_call_target="tpu_custom_call" | custom-call | flops 1073741824 | bytes 606216 | tf_op jit(solution)/shard_map/pallas_call | solution.py:204
  14.9 1.8 %collective-permute-start.3 = (bf16[10,32,128]{2,1,0:T(8,128)(2,1)S(1)}, bf16[10,32,128]{2,1,0:T(8,128)(2,1)S(1)}, u32[]{:S(2)}, u32[]{:S(2)}) collective-permute-start(bf16[10,32,128]{2,1,0:T(8,128)(2,1)S(1)} %get-tuple-element.37), channel_id=1, source_target_pairs={{0,4},{4,8},{8,12},{12,0},{1,5},{5,9},{9,13},{13,1},{2,6},{6,10},{... | collective-permute-start | bytes 245768 | tf_op jit(solution)/shard_map/ppermute | solution.py:484
  16.7 2.0 %collective-permute-start.4 = (bf16[10,32,128]{2,1,0:T(8,128)(2,1)S(1)}, bf16[10,32,128]{2,1,0:T(8,128)(2,1)S(1)}, u32[]{:S(2)}, u32[]{:S(2)}) collective-permute-start(bf16[10,32,128]{2,1,0:T(8,128)(2,1)S(1)} %get-tuple-element.38), channel_id=1, source_target_pairs={{0,8},{4,12},{8,0},{12,4},{1,9},{5,13},{9,1},{13,5},{2,10},{6,14},... | collective-permute-start | bytes 245768 | tf_op jit(solution)/shard_map/ppermute | solution.py:484
  18.7 0.5 collective-permute-start.5
  19.2 0.0 copy-done.3
  19.2 0.0 copy-done.5
  19.2 0.3 shard_map.106.refs_5_
  19.5 2.6 %collective-permute-done.3.refs_1_ = bf16[10,32,128]{2,1,0:T(8,128)(2,1)S(1)} collective-permute-done((bf16[10,32,128]{2,1,0:T(8,128)(2,1)S(1)}, bf16[10,32,128]{2,1,0:T(8,128)(2,1)S(1)}, u32[]{:S(2)}, u32[]{:S(2)}) %collective-permute-start.3) | collective-permute-done | bytes 81952 | tf_op jit(solution)/shard_map/ppermute | solution.py:484
  22.1 2.3 %collective-permute-done.4.refs_2_ = bf16[10,32,128]{2,1,0:T(8,128)(2,1)S(1)} collective-permute-done((bf16[10,32,128]{2,1,0:T(8,128)(2,1)S(1)}, bf16[10,32,128]{2,1,0:T(8,128)(2,1)S(1)}, u32[]{:S(2)}, u32[]{:S(2)}) %collective-permute-start.4) | collective-permute-done | bytes 81952 | tf_op jit(solution)/shard_map/ppermute | solution.py:484
  24.4 0.0 collective-permute-done.5.refs_3_
  24.4 0.0 copy-done.6
  24.4 2.0 %shard_map.107 = (f32[24,512]{1,0:T(8,128)S(1)}, f32[8,32,512]{2,1,0:T(8,128)S(1)}, f32[8,32,512]{2,1,0:T(8,128)S(1)}, f32[4,4,48,256]{3,2,1,0:T(8,128)S(1)}, f32[16,16,256]{2,1,0:T(8,128)S(1)}) custom-call(s32[2]{0:T(128)S(1)} %pad_add_fusion.place, bf16[10,32,128]{2,1,0:T(8,128)(2,1)S(1)} %get-tuple-element.36.refs_0_, ...), custom_call_target="tpu_custom_call" | custom-call | flops 3221225472 | bytes 4309000 | tf_op jit(solution)/shard_map/pallas_call | solution.py:204
  26.4 0.1 convert_element_type.51
  26.5 0.8 %collective-permute-start.12 = (f32[24,512]{1,0:T(8,128)S(1)}, f32[24,512]{1,0:T(8,128)S(1)}, u32[]{:S(2)}, u32[]{:S(2)}) collective-permute-start(f32[24,512]{1,0:T(8,128)S(1)} %get-tuple-element.49), channel_id=1, source_target_pairs={{1,0},{2,1},{3,2},{0,3},{5,4},{6,5},{7,6},{4,7},{9,8},{10,9},{11,1... | collective-permute-start | bytes 147464 | tf_op jit(solution)/shard_map/ppermute | solution.py:531
  27.3 0.1 slice_bitcast_fusion
  27.4 1.9 %collective-permute-start.8 = (f16[4,48,256]{2,1,0:T(8,128)(2,1)S(1)}, f16[4,48,256]{2,1,0:T(8,128)(2,1)S(1)}, u32[]{:S(2)}, u32[]{:S(2)}) collective-permute-start(f16[4,48,256]{2,1,0:T(8,128)(2,1)S(1)} %get-tuple-element.62), channel_id=1, source_target_pairs={{0,12},{4,0},{8,4},{12,8},{1,13},{5,1},{9,5},{13,9},{2,14},{6,2},{... | collective-permute-start | bytes 294920 | tf_op jit(solution)/shard_map/ppermute | solution.py:484
  29.3 2.0 %collective-permute-start.7 = (f16[4,48,256]{2,1,0:T(8,128)(2,1)S(1)}, f16[4,48,256]{2,1,0:T(8,128)(2,1)S(1)}, u32[]{:S(2)}, u32[]{:S(2)}) collective-permute-start(f16[4,48,256]{2,1,0:T(8,128)(2,1)S(1)} %get-tuple-element.63), channel_id=1, source_target_pairs={{0,8},{4,12},{8,0},{12,4},{1,9},{5,13},{9,1},{13,5},{2,10},{6,14},... | collective-permute-start | bytes 294920 | tf_op jit(solution)/shard_map/ppermute | solution.py:484
  31.2 0.0 collective-permute-start.6
  31.2 0.0 collective-permute-done.12.beyond
  31.2 0.7 shard_map.109
  32.0 0.8 %convert_element_type.56 = f16[16,48,256]{2,1,0:T(8,128)(2,1)} convert(f32[16,48,256]{2,1,0:T(8,128)S(1)} %shard_map.109) | non-fusion elementwise | flops 196608 | bytes 1179648 | tf_op jit(solution)/shard_map/convert_element_type | solution.py:547
  32.8 5.4 %all-to-all-start = ((f16[16,48,256]{2,1,0:T(8,128)(2,1)}), f16[16,48,256]{2,1,0:T(8,128)(2,1)S(1)}, u32[]{:S(2)}, u32[]{:S(2)}) async-start(f16[16,48,256]{2,1,0:T(8,128)(2,1)} %convert_element_type.56), calls=%async_computation | async-start | bytes 786432 | tf_op jit(solution)/shard_map/all_to_all | solution.py:488
  38.2 0.0 collective-permute-done.8
  38.2 1.7 %collective-permute-done.7 = f16[4,48,256]{2,1,0:T(8,128)(2,1)S(1)} collective-permute-done((f16[4,48,256]{2,1,0:T(8,128)(2,1)S(1)}, f16[4,48,256]{2,1,0:T(8,128)(2,1)S(1)}, u32[]{:S(2)}, u32[]{:S(2)}) %collective-permute-start.7) | collective-permute-done | bytes 98336 | tf_op jit(solution)/shard_map/ppermute | solution.py:484
  40.0 0.0 collective-permute-done.6
  40.1 0.1 collective-permute-start.9
  40.2 1.3 %collective-permute-start.10 = (f16[4,48,256]{2,1,0:T(8,128)(2,1)S(1)}, f16[4,48,256]{2,1,0:T(8,128)(2,1)S(1)}, u32[]{:S(2)}, u32[]{:S(2)}) collective-permute-start(f16[4,48,256]{2,1,0:T(8,128)(2,1)S(1)} %pad_maximum_fusion.1), channel_id=1, source_target_pairs={{0,2},{1,3},{2,0},{3,1},{4,6},{5,7},{6,4},{7,5},{8,10},{9,11},{10,... | collective-permute-start | bytes 294920 | tf_op jit(solution)/shard_map/ppermute | solution.py:484
  41.5 1.5 %collective-permute-start.11 = (f16[4,48,256]{2,1,0:T(8,128)(2,1)S(1)}, f16[4,48,256]{2,1,0:T(8,128)(2,1)S(1)}, u32[]{:S(2)}, u32[]{:S(2)}) collective-permute-start(f16[4,48,256]{2,1,0:T(8,128)(2,1)S(1)} %pad_maximum_fusion.2), channel_id=1, source_target_pairs={{0,3},{1,0},{2,1},{3,2},{4,7},{5,4},{6,5},{7,6},{8,11},{9,8},{10,9... | collective-permute-start | bytes 294920 | tf_op jit(solution)/shard_map/ppermute | solution.py:484
  43.0 1.3 %shard_map.110 = bf16[8,32,512]{2,1,0:T(8,128)(2,1)} custom-call(s32[2]{0:T(128)S(1)} %pad_add_fusion.place, bf16[10,32,128]{2,1,0:T(8,128)(2,1)S(1)} %get-tuple-element.36.refs_0_, bf16[10,32,128]{2,1,0:T(8,128)(2,1)S(1)} %collective-permute-done.3.refs_1_, bf16[10,32,128]{2,1,0:T(8,128)(2,1)S(1)} %collective-permute-done.4.refs_2_, ...), custom_call_target="tpu_custom_call" | custom-call | bytes 589832 | tf_op jit(solution)/shard_map/pallas_call | solution.py:204
  44.4 1.6 %collective-permute-done.9 = f16[4,48,256]{2,1,0:T(8,128)(2,1)S(1)} collective-permute-done((f16[4,48,256]{2,1,0:T(8,128)(2,1)S(1)}, f16[4,48,256]{2,1,0:T(8,128)(2,1)S(1)}, u32[]{:S(2)}, u32[]{:S(2)}) %collective-permute-start.9) | collective-permute-done | bytes 98336 | tf_op jit(solution)/shard_map/ppermute | solution.py:484
  45.9 0.6 collective-permute-done.10
  46.6 1.9 %collective-permute-done.11 = f16[4,48,256]{2,1,0:T(8,128)(2,1)S(1)} collective-permute-done((f16[4,48,256]{2,1,0:T(8,128)(2,1)S(1)}, f16[4,48,256]{2,1,0:T(8,128)(2,1)S(1)}, u32[]{:S(2)}, u32[]{:S(2)}) %collective-permute-start.11) | collective-permute-done | bytes 98336 | tf_op jit(solution)/shard_map/ppermute | solution.py:484
  48.5 2.8 %shard_map.108 = (f32[4,48,256]{2,1,0:T(8,128)S(1)}, f32[4,48,256]{2,1,0:T(8,128)S(1)}, f32[4,48,256]{2,1,0:T(8,128)S(1)}, f32[4,48,256]{2,1,0:T(8,128)S(1)}) custom-call(s32[2]{0:T(128)S(1)} %pad_add_fusion.place, f32[4,48,256]{2,1,0:T(8,128)S(1)} %maximum_convert_fusion.refs_0_, f32[4,48,256]{2,1,0:T(8,128)S(1)} %convert_element_type.53.refs_1_, ...), custom_call_target="tpu_custom_call" | custom-call | flops 2147483648 | bytes 2293768 | tf_op jit(solution)/shard_map/pallas_call | solution.py:204
  51.3 0.0 all-to-all-done
  51.4 2.5 %collective-permute-start.15 = (f16[4,48,256]{2,1,0:T(8,128)(2,1)S(1)}, f16[4,48,256]{2,1,0:T(8,128)(2,1)S(1)}, u32[]{:S(2)}, u32[]{:S(2)}) collective-permute-start(f16[4,48,256]{2,1,0:T(8,128)(2,1)S(1)} %convert_element_type.63), channel_id=1, source_target_pairs={{0,12},{4,0},{8,4},{12,8},{1,13},{5,1},{9,5},{13,9},{2,14},{6,2},{... | collective-permute-start | bytes 294920 | tf_op jit(solution)/shard_map/ppermute | solution.py:484
  53.9 0.0 collective-permute-start.14
  53.9 1.4 %collective-permute-start.13 = (f16[4,48,256]{2,1,0:T(8,128)(2,1)S(1)}, f16[4,48,256]{2,1,0:T(8,128)(2,1)S(1)}, u32[]{:S(2)}, u32[]{:S(2)}) collective-permute-start(f16[4,48,256]{2,1,0:T(8,128)(2,1)S(1)} %convert_element_type.61), channel_id=1, source_target_pairs={{0,4},{4,8},{8,12},{12,0},{1,5},{5,9},{9,13},{13,1},{2,6},{6,10},{... | collective-permute-start | bytes 294920 | tf_op jit(solution)/shard_map/ppermute | solution.py:484
  55.3 0.1 convert_element_type.57.spectra
  55.4 2.6 %shard_map.111 = f32[16,48,256]{2,1,0:T(8,128)S(1)} custom-call(s32[2]{0:T(128)S(1)} %pad_add_fusion.place, f32[16,48,256]{2,1,0:T(8,128)S(1)} %convert_element_type.57.spectra, bf16[4,256,256]{2,1,0:T(8,128)(2,1)S(1)} %copy-done.7, bf16[6,128,128]{2,1,0:T(8,128)(2,1)S(1)} %copy-done.8), custom_call_target="tpu_custom_call" | custom-call | flops 2147483648 | bytes 2293768 | tf_op jit(solution)/shard_map/pallas_call | solution.py:204
  58.0 0.8 %convert_element_type.58 = f16[16,48,256]{2,1,0:T(8,128)(2,1)} convert(f32[16,48,256]{2,1,0:T(8,128)S(1)} %shard_map.111) | non-fusion elementwise | flops 196608 | bytes 1179648 | tf_op jit(solution)/shard_map/convert_element_type | solution.py:571
  58.8 5.1 %all-to-all-start.1 = ((f16[16,48,256]{2,1,0:T(8,128)(2,1)}), f16[16,48,256]{2,1,0:T(8,128)(2,1)}, u32[]{:S(2)}, u32[]{:S(2)}) async-start(f16[16,48,256]{2,1,0:T(8,128)(2,1)} %convert_element_type.58), calls=%async_computation.1 | async-start | bytes 786432 | tf_op jit(solution)/shard_map/all_to_all | solution.py:488
  63.9 0.0 collective-permute-done.15
  64.0 0.0 collective-permute-done.14
  64.0 0.0 collective-permute-done.13
  64.1 0.4 collective-permute-start.16
  64.5 1.7 %collective-permute-start.17 = (f16[4,48,256]{2,1,0:T(8,128)(2,1)S(1)}, f16[4,48,256]{2,1,0:T(8,128)(2,1)S(1)}, u32[]{:S(2)}, u32[]{:S(2)}) collective-permute-start(f16[4,48,256]{2,1,0:T(8,128)(2,1)S(1)} %pad_maximum_fusion.4), channel_id=1, source_target_pairs={{0,2},{1,3},{2,0},{3,1},{4,6},{5,7},{6,4},{7,5},{8,10},{9,11},{10,... | collective-permute-start | bytes 294920 | tf_op jit(solution)/shard_map/ppermute | solution.py:484
  66.3 1.4 %collective-permute-start.18 = (f16[4,48,256]{2,1,0:T(8,128)(2,1)S(1)}, f16[4,48,256]{2,1,0:T(8,128)(2,1)S(1)}, u32[]{:S(2)}, u32[]{:S(2)}) collective-permute-start(f16[4,48,256]{2,1,0:T(8,128)(2,1)S(1)} %pad_maximum_fusion.5), channel_id=1, source_target_pairs={{0,3},{1,0},{2,1},{3,2},{4,7},{5,4},{6,5},{7,6},{8,11},{9,8},{10,9... | collective-permute-start | bytes 294920 | tf_op jit(solution)/shard_map/ppermute | solution.py:484
  67.7 3.5 %collective-permute-done.16 = f16[4,48,256]{2,1,0:T(8,128)(2,1)S(1)} collective-permute-done((f16[4,48,256]{2,1,0:T(8,128)(2,1)S(1)}, f16[4,48,256]{2,1,0:T(8,128)(2,1)S(1)}, u32[]{:S(2)}, u32[]{:S(2)}) %collective-permute-start.16) | collective-permute-done | bytes 98336 | tf_op jit(solution)/shard_map/ppermute | solution.py:484
  71.3 1.3 %collective-permute-done.17 = f16[4,48,256]{2,1,0:T(8,128)(2,1)S(1)} collective-permute-done((f16[4,48,256]{2,1,0:T(8,128)(2,1)S(1)}, f16[4,48,256]{2,1,0:T(8,128)(2,1)S(1)}, u32[]{:S(2)}, u32[]{:S(2)}) %collective-permute-start.17) | collective-permute-done | bytes 98336 | tf_op jit(solution)/shard_map/ppermute | solution.py:484
  72.6 0.8 collective-permute-done.18
  73.4 1.2 %shard_map.112 = (f32[8,32,512]{2,1,0:T(8,128)S(1)}, f32[16,16,256]{2,1,0:T(8,128)S(1)}) custom-call(s32[2]{0:T(128)S(1)} %pad_add_fusion.place, bf16[2,512,512]{2,1,0:T(8,128)(2,1)S(1)} %copy-done.6, f32[3,8,32,512]{3,2,1,0:T(8,128)S(1)} %copy-done.2, f32[4,48,256]{2,1,0:T(8,128)S(1)} %maximum_convert_fusion.1.refs_0_, ...), custom_call_target="tpu_custom_call" | custom-call | flops 1073741824 | bytes 4194312 | tf_op jit(solution)/shard_map/pallas_call | solution.py:204
  74.7 1.5 %all-to-all-done.1 = f16[16,48,256]{2,1,0:T(8,128)(2,1)} async-done(((f16[16,48,256]{2,1,0:T(8,128)(2,1)}), f16[16,48,256]{2,1,0:T(8,128)(2,1)}, u32[]{:S(2)}, u32[]{:S(2)}) %all-to-all-start.1) | async-done | bytes 393248 | tf_op jit(solution)/shard_map/all_to_all | solution.py:488
  76.2 1.1 %convert_element_type.59.spectra = f32[16,48,256]{2,1,0:T(8,128)S(1)} convert(f16[16,48,256]{2,1,0:T(8,128)(2,1)} %all-to-all-done.1) | non-fusion elementwise | flops 196608 | bytes 1179648 | tf_op jit(solution)/shard_map/convert_element_type | solution.py:585
  77.3 1.9 %shard_map.113 = f32[3,8,32,512]{3,2,1,0:T(8,128)} custom-call(f32[16,48,256]{2,1,0:T(8,128)S(1)} %convert_element_type.59.spectra, bf16[2,512,512]{2,1,0:T(8,128)(2,1)S(1)} %copy-done.6, f32[3,8,32,512]{3,2,1,0:T(8,128)S(1)} %copy-done.2, f32[8,32,512]{2,1,0:T(8,128)S(1)} %get-tuple-element.59.updated, f32[16,16,256]{2,1,0:T(8,128)S(1)} %get-tuple-element.60.kept), custom_call_target="tpu_custom_call" | custom-call | flops 2147483648 | bytes 5767168 | tf_op jit(solution)/shard_map/pallas_call | solution.py:204
  (37 shorter events, 0.6 us)
Async XLA Ops:
  0.7 1.0 %copy-start = (bf16[8,32,512]{2,1,0:T(8,128)(2,1)S(1)}, bf16[8,32,512]{2,1,0:T(8,128)(2,1)}, u32[]{:S(2)}) copy-start(bf16[8,32,512]{2,1,0:T(8,128)(2,1)} %moving.1) | copy-start | bytes 786436
  1.7 0.7 copy-start.1
  3.0 7.7 %collective-permute-start = (bf16[272,128]{1,0:T(8,128)(2,1)S(1)}, bf16[272,128]{1,0:T(8,128)(2,1)S(1)}, u32[]{:S(2)}, u32[]{:S(2)}) collective-permute-start(bf16[272,128]{1,0:T(8,128)(2,1)S(1)} %get-tuple-element.33), channel_id=1, source_target_pairs={{0,4},{4,8},{8,12},{12,0},{1,5},{5,9},{9,13},{13,1},{2,6},{6,10},{... | collective-permute-start | bytes 208904 | tf_op jit(solution)/shard_map/ppermute | solution.py:484
  6.1 7.3 %collective-permute-start.1 = (bf16[272,128]{1,0:T(8,128)(2,1)S(1)}, bf16[272,128]{1,0:T(8,128)(2,1)S(1)}, u32[]{:S(2)}, u32[]{:S(2)}) collective-permute-start(bf16[272,128]{1,0:T(8,128)(2,1)S(1)} %get-tuple-element.34), channel_id=1, source_target_pairs={{0,8},{4,12},{8,0},{12,4},{1,9},{5,13},{9,1},{13,5},{2,10},{6,14},... | collective-permute-start | bytes 208904 | tf_op jit(solution)/shard_map/ppermute | solution.py:484
  8.7 4.9 %collective-permute-start.2 = (bf16[272,128]{1,0:T(8,128)(2,1)S(1)}, bf16[272,128]{1,0:T(8,128)(2,1)S(1)}, u32[]{:S(2)}, u32[]{:S(2)}) collective-permute-start(bf16[272,128]{1,0:T(8,128)(2,1)S(1)} %get-tuple-element.35), channel_id=1, source_target_pairs={{0,12},{4,0},{8,4},{12,8},{1,13},{5,1},{9,5},{13,9},{2,14},{6,2},{... | collective-permute-start | bytes 208904 | tf_op jit(solution)/shard_map/ppermute | solution.py:484
  13.5 5.6 %copy-start.3 = (f32[8,32,512]{2,1,0:T(8,128)S(1)}, f32[8,32,512]{2,1,0:T(8,128)}, u32[]{:S(2)}) copy-start(f32[8,32,512]{2,1,0:T(8,128)} %stiffness.1) | copy-start | bytes 1572868
  13.5 5.6 %copy-start.5 = (s32[8,32,4]{1,2,0:T(4,128)S(1)}, s32[8,32,4]{1,2,0:T(4,128)}, u32[]{:S(2)}) copy-start(s32[8,32,4]{1,2,0:T(4,128)} %param.14) | copy-start | bytes 12292
  14.9 7.2 %collective-permute-start.3 = (bf16[10,32,128]{2,1,0:T(8,128)(2,1)S(1)}, bf16[10,32,128]{2,1,0:T(8,128)(2,1)S(1)}, u32[]{:S(2)}, u32[]{:S(2)}) collective-permute-start(bf16[10,32,128]{2,1,0:T(8,128)(2,1)S(1)} %get-tuple-element.37), channel_id=1, source_target_pairs={{0,4},{4,8},{8,12},{12,0},{1,5},{5,9},{9,13},{13,1},{2,6},{6,10},{... | collective-permute-start | bytes 245768 | tf_op jit(solution)/shard_map/ppermute | solution.py:484
  16.7 7.7 %collective-permute-start.4 = (bf16[10,32,128]{2,1,0:T(8,128)(2,1)S(1)}, bf16[10,32,128]{2,1,0:T(8,128)(2,1)S(1)}, u32[]{:S(2)}, u32[]{:S(2)}) collective-permute-start(bf16[10,32,128]{2,1,0:T(8,128)(2,1)S(1)} %get-tuple-element.38), channel_id=1, source_target_pairs={{0,8},{4,12},{8,0},{12,4},{1,9},{5,13},{9,1},{13,5},{2,10},{6,14},... | collective-permute-start | bytes 245768 | tf_op jit(solution)/shard_map/ppermute | solution.py:484
  18.7 5.7 %collective-permute-start.5 = (bf16[10,32,128]{2,1,0:T(8,128)(2,1)S(1)}, bf16[10,32,128]{2,1,0:T(8,128)(2,1)S(1)}, u32[]{:S(2)}, u32[]{:S(2)}) collective-permute-start(bf16[10,32,128]{2,1,0:T(8,128)(2,1)S(1)} %get-tuple-element.39), channel_id=1, source_target_pairs={{0,12},{4,0},{8,4},{12,8},{1,13},{5,1},{9,5},{13,9},{2,14},{6,2},{... | collective-permute-start | bytes 245768 | tf_op jit(solution)/shard_map/ppermute | solution.py:484
  19.2 5.3 %copy-start.4 = (bf16[8,32,512]{2,1,0:T(8,128)(2,1)S(1)}, bf16[8,32,512]{2,1,0:T(8,128)(2,1)}, u32[]{:S(2)}) copy-start(bf16[8,32,512]{2,1,0:T(8,128)(2,1)} %refs_4_.2) | copy-start | bytes 786436
  19.2 5.3 %copy-start.6 = (bf16[2,512,512]{2,1,0:T(8,128)(2,1)S(1)}, bf16[2,512,512]{2,1,0:T(8,128)(2,1)}, u32[]{:S(2)}) copy-start(bf16[2,512,512]{2,1,0:T(8,128)(2,1)} %constant.13.clone.refs_6_.basis) | copy-start | bytes 3145732
  26.5 4.7 %collective-permute-start.12 = (f32[24,512]{1,0:T(8,128)S(1)}, f32[24,512]{1,0:T(8,128)S(1)}, u32[]{:S(2)}, u32[]{:S(2)}) collective-permute-start(f32[24,512]{1,0:T(8,128)S(1)} %get-tuple-element.49), channel_id=1, source_target_pairs={{1,0},{2,1},{3,2},{0,3},{5,4},{6,5},{7,6},{4,7},{9,8},{10,9},{11,1... | collective-permute-start | bytes 147464 | tf_op jit(solution)/shard_map/ppermute | solution.py:531
  27.4 10.8 %collective-permute-start.8 = (f16[4,48,256]{2,1,0:T(8,128)(2,1)S(1)}, f16[4,48,256]{2,1,0:T(8,128)(2,1)S(1)}, u32[]{:S(2)}, u32[]{:S(2)}) collective-permute-start(f16[4,48,256]{2,1,0:T(8,128)(2,1)S(1)} %get-tuple-element.62), channel_id=1, source_target_pairs={{0,12},{4,0},{8,4},{12,8},{1,13},{5,1},{9,5},{13,9},{2,14},{6,2},{... | collective-permute-start | bytes 294920 | tf_op jit(solution)/shard_map/ppermute | solution.py:484
  29.3 10.7 %collective-permute-start.7 = (f16[4,48,256]{2,1,0:T(8,128)(2,1)S(1)}, f16[4,48,256]{2,1,0:T(8,128)(2,1)S(1)}, u32[]{:S(2)}, u32[]{:S(2)}) collective-permute-start(f16[4,48,256]{2,1,0:T(8,128)(2,1)S(1)} %get-tuple-element.63), channel_id=1, source_target_pairs={{0,8},{4,12},{8,0},{12,4},{1,9},{5,13},{9,1},{13,5},{2,10},{6,14},... | collective-permute-start | bytes 294920 | tf_op jit(solution)/shard_map/ppermute | solution.py:484
  31.2 8.7 %collective-permute-start.6 = (f16[4,48,256]{2,1,0:T(8,128)(2,1)S(1)}, f16[4,48,256]{2,1,0:T(8,128)(2,1)S(1)}, u32[]{:S(2)}, u32[]{:S(2)}) collective-permute-start(f16[4,48,256]{2,1,0:T(8,128)(2,1)S(1)} %get-tuple-element.64), channel_id=1, source_target_pairs={{0,4},{4,8},{8,12},{12,0},{1,5},{5,9},{9,13},{13,1},{2,6},{6,10},{... | collective-permute-start | bytes 294920 | tf_op jit(solution)/shard_map/ppermute | solution.py:484
  32.8 18.5 %all-to-all-start = ((f16[16,48,256]{2,1,0:T(8,128)(2,1)}), f16[16,48,256]{2,1,0:T(8,128)(2,1)S(1)}, u32[]{:S(2)}, u32[]{:S(2)}) async-start(f16[16,48,256]{2,1,0:T(8,128)(2,1)} %convert_element_type.56), calls=%async_computation | async-start | bytes 786432 | tf_op jit(solution)/shard_map/all_to_all | solution.py:488
  40.0 8.5 %copy-start.7 = (bf16[4,256,256]{2,1,0:T(8,128)(2,1)S(1)}, bf16[4,256,256]{2,1,0:T(8,128)(2,1)}, u32[]{:S(2)}) copy-start(bf16[4,256,256]{2,1,0:T(8,128)(2,1)} %constant.14.clone.refs_4_.basis_z) | copy-start | bytes 1572868
  40.0 8.5 %copy-start.8 = (bf16[6,128,128]{2,1,0:T(8,128)(2,1)S(1)}, bf16[6,128,128]{2,1,0:T(8,128)(2,1)}, u32[]{:S(2)}) copy-start(bf16[6,128,128]{2,1,0:T(8,128)(2,1)} %constant.15.clone.refs_5_.basis_y) | copy-start | bytes 589828
  40.1 5.8 %collective-permute-start.9 = (f16[4,48,256]{2,1,0:T(8,128)(2,1)S(1)}, f16[4,48,256]{2,1,0:T(8,128)(2,1)S(1)}, u32[]{:S(2)}, u32[]{:S(2)}) collective-permute-start(f16[4,48,256]{2,1,0:T(8,128)(2,1)S(1)} %pad_maximum_fusion), channel_id=1, source_target_pairs={{0,1},{1,2},{2,3},{3,0},{4,5},{5,6},{6,7},{7,4},{8,9},{9,10},{10,1... | collective-permute-start | bytes 294920 | tf_op jit(solution)/shard_map/ppermute | solution.py:484
  40.2 6.4 %collective-permute-start.10 = (f16[4,48,256]{2,1,0:T(8,128)(2,1)S(1)}, f16[4,48,256]{2,1,0:T(8,128)(2,1)S(1)}, u32[]{:S(2)}, u32[]{:S(2)}) collective-permute-start(f16[4,48,256]{2,1,0:T(8,128)(2,1)S(1)} %pad_maximum_fusion.1), channel_id=1, source_target_pairs={{0,2},{1,3},{2,0},{3,1},{4,6},{5,7},{6,4},{7,5},{8,10},{9,11},{10,... | collective-permute-start | bytes 294920 | tf_op jit(solution)/shard_map/ppermute | solution.py:484
  41.5 7.0 %collective-permute-start.11 = (f16[4,48,256]{2,1,0:T(8,128)(2,1)S(1)}, f16[4,48,256]{2,1,0:T(8,128)(2,1)S(1)}, u32[]{:S(2)}, u32[]{:S(2)}) collective-permute-start(f16[4,48,256]{2,1,0:T(8,128)(2,1)S(1)} %pad_maximum_fusion.2), channel_id=1, source_target_pairs={{0,3},{1,0},{2,1},{3,2},{4,7},{5,4},{6,5},{7,6},{8,11},{9,8},{10,9... | collective-permute-start | bytes 294920 | tf_op jit(solution)/shard_map/ppermute | solution.py:484
  51.4 12.5 %collective-permute-start.15 = (f16[4,48,256]{2,1,0:T(8,128)(2,1)S(1)}, f16[4,48,256]{2,1,0:T(8,128)(2,1)S(1)}, u32[]{:S(2)}, u32[]{:S(2)}) collective-permute-start(f16[4,48,256]{2,1,0:T(8,128)(2,1)S(1)} %convert_element_type.63), channel_id=1, source_target_pairs={{0,12},{4,0},{8,4},{12,8},{1,13},{5,1},{9,5},{13,9},{2,14},{6,2},{... | collective-permute-start | bytes 294920 | tf_op jit(solution)/shard_map/ppermute | solution.py:484
  53.9 10.1 %collective-permute-start.14 = (f16[4,48,256]{2,1,0:T(8,128)(2,1)S(1)}, f16[4,48,256]{2,1,0:T(8,128)(2,1)S(1)}, u32[]{:S(2)}, u32[]{:S(2)}) collective-permute-start(f16[4,48,256]{2,1,0:T(8,128)(2,1)S(1)} %convert_element_type.62), channel_id=1, source_target_pairs={{0,8},{4,12},{8,0},{12,4},{1,9},{5,13},{9,1},{13,5},{2,10},{6,14},... | collective-permute-start | bytes 294920 | tf_op jit(solution)/shard_map/ppermute | solution.py:484
  53.9 10.1 %collective-permute-start.13 = (f16[4,48,256]{2,1,0:T(8,128)(2,1)S(1)}, f16[4,48,256]{2,1,0:T(8,128)(2,1)S(1)}, u32[]{:S(2)}, u32[]{:S(2)}) collective-permute-start(f16[4,48,256]{2,1,0:T(8,128)(2,1)S(1)} %convert_element_type.61), channel_id=1, source_target_pairs={{0,4},{4,8},{8,12},{12,0},{1,5},{5,9},{9,13},{13,1},{2,6},{6,10},{... | collective-permute-start | bytes 294920 | tf_op jit(solution)/shard_map/ppermute | solution.py:484
  58.8 14.6 %copy-start.2 = (f32[3,8,32,512]{3,2,1,0:T(8,128)S(1)}, f32[3,8,32,512]{3,2,1,0:T(8,128)}, u32[]{:S(2)}) copy-start(f32[3,8,32,512]{3,2,1,0:T(8,128)} %velocity.3) | copy-start | bytes 4718596
  58.8 17.4 %all-to-all-start.1 = ((f16[16,48,256]{2,1,0:T(8,128)(2,1)}), f16[16,48,256]{2,1,0:T(8,128)(2,1)}, u32[]{:S(2)}, u32[]{:S(2)}) async-start(f16[16,48,256]{2,1,0:T(8,128)(2,1)} %convert_element_type.58), calls=%async_computation.1 | async-start | bytes 786432 | tf_op jit(solution)/shard_map/all_to_all | solution.py:488
  64.1 7.2 %collective-permute-start.16 = (f16[4,48,256]{2,1,0:T(8,128)(2,1)S(1)}, f16[4,48,256]{2,1,0:T(8,128)(2,1)S(1)}, u32[]{:S(2)}, u32[]{:S(2)}) collective-permute-start(f16[4,48,256]{2,1,0:T(8,128)(2,1)S(1)} %pad_maximum_fusion.3), channel_id=1, source_target_pairs={{0,1},{1,2},{2,3},{3,0},{4,5},{5,6},{6,7},{7,4},{8,9},{9,10},{10,1... | collective-permute-start | bytes 294920 | tf_op jit(solution)/shard_map/ppermute | solution.py:484
  64.5 8.1 %collective-permute-start.17 = (f16[4,48,256]{2,1,0:T(8,128)(2,1)S(1)}, f16[4,48,256]{2,1,0:T(8,128)(2,1)S(1)}, u32[]{:S(2)}, u32[]{:S(2)}) collective-permute-start(f16[4,48,256]{2,1,0:T(8,128)(2,1)S(1)} %pad_maximum_fusion.4), channel_id=1, source_target_pairs={{0,2},{1,3},{2,0},{3,1},{4,6},{5,7},{6,4},{7,5},{8,10},{9,11},{10,... | collective-permute-start | bytes 294920 | tf_op jit(solution)/shard_map/ppermute | solution.py:484
  66.3 7.1 %collective-permute-start.18 = (f16[4,48,256]{2,1,0:T(8,128)(2,1)S(1)}, f16[4,48,256]{2,1,0:T(8,128)(2,1)S(1)}, u32[]{:S(2)}, u32[]{:S(2)}) collective-permute-start(f16[4,48,256]{2,1,0:T(8,128)(2,1)S(1)} %pad_maximum_fusion.5), channel_id=1, source_target_pairs={{0,3},{1,0},{2,1},{3,2},{4,7},{5,4},{6,5},{7,6},{8,11},{9,8},{10,9... | collective-permute-start | bytes 294920 | tf_op jit(solution)/shard_map/ppermute | solution.py:484

commit v10 on v9

--- a/solution.py
+++ b/solution.py
@@ -390,7 +390,7 @@
     for start in range(0, used, tile):
         own.append(cells[:, start : start + tile, :].reshape(total_z * tile, total_y))
         x_sq = wave_sq(first + offsets[start // tile] + lax.rem(index, tile), x_length)
-        scale.append((z_sq + x_sq + y_sq) * 256.0 + 1.0)
+        scale.append((z_sq + y_sq) * (256.0 / (x_sq * 256.0 + 1.0)) + 1.0)
     own = along_z(0, jnp.concatenate(own, axis=1))
     own = along_z(1, own / jnp.concatenate(scale, axis=1))
     for k, start in enumerate(range(0, used, tile)):
@@ -569,11 +569,14 @@
         flops=2 << 30,
     )
     spectra = exchange(spectra.astype(f16))
+    x_wave = np.arange(x_length)
+    x_wave = 2.0 * np.pi / x_length * np.where(x_wave <= x_length // 2, x_wave, x_wave - x_length // 2)
+    basis_back = in_two(real_basis(x_length) / (256.0 * x_wave**2 + 1.0)[:, None])
     updated, kept = call(
         functools.partial(update_z_kernel, slabs, subs),
         [shape(moving.shape), shape((devices, part - cut, area))],
         place,
-        basis_x,
+        basis_back,
         velocity,
         *[r.astype(f32) for r in chain],
         scratch=[pltpu.VMEM((x_length, area), f32)],
@@ -583,7 +586,7 @@
         update_kernel,
         shape(velocity.shape),
         spectra.astype(f32),
-        basis_x,
+        basis_back,
         velocity,
         updated,
         kept,

time: 79.6 us -> 79.8 us (level)
    unnamed x18 -> x20, local copies, waits for them, and re-layouts: 1.69 us -> 1.7 us
where the time goes in v10:
time: 79.8 us; the launch traced here: 79.3 us
  starting transfers between devices  36.8 us (46%)
  waiting for transfers between devices  21.4 us (27%)
  Pallas kernels  14.9 us (19%)
  other arithmetic  3.32 us (4%)
  local copies, waits for them, and re-layouts  1.94 us (2%)
  between operations  0.97 us (1%)
    ppermute x18, starting transfers between devices, scatter(): lax.ppermute(sends[d], axis, [(i, (i + d) % count) for i in range(count)])  25.3 us
    ppermute x18, waiting for transfers between devices, scatter(): lax.ppermute(sends[d], axis, [(i, (i + d) % count) for i in range(count)])  19.9 us
    pallas_call x10, Pallas kernels, call(): pl.pallas_call(kernel, out_shape=out_shape, in_specs=places, out_specs=ja...  14.9 us
    all_to_all x2, starting transfers between devices, exchange(): lax.all_to_all(values, ('slab', 'sub'), split_axis=0, concat_axis=0, tile...  10.7 us
    unnamed x20, local copies, waits for them, and re-layouts  1.7 us
    convert_element_type x2, other arithmetic, local_blocks(): spectra = exchange(spectra.astype(f16))  1.62 us
  transfers between devices with their start and end apart: 21, of which 13 were waited for; matrix products, arithmetic and copies ran while one was open for 3% of the time, Pallas kernels for 11%

profile of v10, /device:TPU:0, one launch (start us, length us, event | category | flops | bytes accessed | tf_op | source)
XLA Modules:
  0.0 79.3 jit_solution(14138283486727540058)
XLA Ops:
  0.6 0.1 pad_add_fusion.place
  0.7 0.9 %copy-done = bf16[8,32,512]{2,1,0:T(8,128)(2,1)S(1)} copy-done((bf16[8,32,512]{2,1,0:T(8,128)(2,1)S(1)}, bf16[8,32,512]{2,1,0:T(8,128)(2,1)}, u32[]{:S(2)}) %copy-start) | copy-done | bytes 262168
  1.7 0.7 copy-done.1
  2.4 0.6 shard_map.113
  3.0 3.1 %collective-permute-start = (bf16[272,128]{1,0:T(8,128)(2,1)S(1)}, bf16[272,128]{1,0:T(8,128)(2,1)S(1)}, u32[]{:S(2)}, u32[]{:S(2)}) collective-permute-start(bf16[272,128]{1,0:T(8,128)(2,1)S(1)} %get-tuple-element.33), channel_id=1, source_target_pairs={{0,4},{4,8},{8,12},{12,0},{1,5},{5,9},{9,13},{13,1},{2,6},{6,10},{... | collective-permute-start | bytes 208904 | tf_op jit(solution)/shard_map/ppermute | solution.py:484
  6.1 2.6 %collective-permute-start.1 = (bf16[272,128]{1,0:T(8,128)(2,1)S(1)}, bf16[272,128]{1,0:T(8,128)(2,1)S(1)}, u32[]{:S(2)}, u32[]{:S(2)}) collective-permute-start(bf16[272,128]{1,0:T(8,128)(2,1)S(1)} %get-tuple-element.34), channel_id=1, source_target_pairs={{0,8},{4,12},{8,0},{12,4},{1,9},{5,13},{9,1},{13,5},{2,10},{6,14},... | collective-permute-start | bytes 208904 | tf_op jit(solution)/shard_map/ppermute | solution.py:484
  8.7 1.3 %collective-permute-start.2 = (bf16[272,128]{1,0:T(8,128)(2,1)S(1)}, bf16[272,128]{1,0:T(8,128)(2,1)S(1)}, u32[]{:S(2)}, u32[]{:S(2)}) collective-permute-start(bf16[272,128]{1,0:T(8,128)(2,1)S(1)} %get-tuple-element.35), channel_id=1, source_target_pairs={{0,12},{4,0},{8,4},{12,8},{1,13},{5,1},{9,5},{13,9},{2,14},{6,2},{... | collective-permute-start | bytes 208904 | tf_op jit(solution)/shard_map/ppermute | solution.py:484
  10.0 0.7 collective-permute-done.refs_1_
  10.7 2.7 %collective-permute-done.1.refs_2_ = bf16[272,128]{1,0:T(8,128)(2,1)S(1)} collective-permute-done((bf16[272,128]{1,0:T(8,128)(2,1)S(1)}, bf16[272,128]{1,0:T(8,128)(2,1)S(1)}, u32[]{:S(2)}, u32[]{:S(2)}) %collective-permute-start.1) | collective-permute-done | bytes 69664 | tf_op jit(solution)/shard_map/ppermute | solution.py:484
  13.4 0.2 collective-permute-done.2.refs_3_
  13.6 1.3 %shard_map.114 = (bf16[10,32,128]{2,1,0:T(8,128)(2,1)S(1)}, bf16[10,32,128]{2,1,0:T(8,128)(2,1)S(1)}, bf16[10,32,128]{2,1,0:T(8,128)(2,1)S(1)}, bf16[10,32,128]{2,1,0:T(8,128)(2,1)S(1)}) custom-call(s32[2]{0:T(128)S(1)} %pad_add_fusion.place, bf16[272,128]{1,0:T(8,128)(2,1)S(1)} %get-tuple-element.32.refs_0_, ...), custom_call_target="tpu_custom_call" | custom-call | flops 1073741824 | bytes 606216 | tf_op jit(solution)/shard_map/pallas_call | solution.py:204
  14.9 1.8 %collective-permute-start.3 = (bf16[10,32,128]{2,1,0:T(8,128)(2,1)S(1)}, bf16[10,32,128]{2,1,0:T(8,128)(2,1)S(1)}, u32[]{:S(2)}, u32[]{:S(2)}) collective-permute-start(bf16[10,32,128]{2,1,0:T(8,128)(2,1)S(1)} %get-tuple-element.37), channel_id=1, source_target_pairs={{0,4},{4,8},{8,12},{12,0},{1,5},{5,9},{9,13},{13,1},{2,6},{6,10},{... | collective-permute-start | bytes 245768 | tf_op jit(solution)/shard_map/ppermute | solution.py:484
  16.7 2.0 %collective-permute-start.4 = (bf16[10,32,128]{2,1,0:T(8,128)(2,1)S(1)}, bf16[10,32,128]{2,1,0:T(8,128)(2,1)S(1)}, u32[]{:S(2)}, u32[]{:S(2)}) collective-permute-start(bf16[10,32,128]{2,1,0:T(8,128)(2,1)S(1)} %get-tuple-element.38), channel_id=1, source_target_pairs={{0,8},{4,12},{8,0},{12,4},{1,9},{5,13},{9,1},{13,5},{2,10},{6,14},... | collective-permute-start | bytes 245768 | tf_op jit(solution)/shard_map/ppermute | solution.py:484
  18.7 0.5 collective-permute-start.5
  19.2 0.0 copy-done.5
  19.2 0.3 shard_map.115.refs_5_
  19.5 2.6 %collective-permute-done.3.refs_1_ = bf16[10,32,128]{2,1,0:T(8,128)(2,1)S(1)} collective-permute-done((bf16[10,32,128]{2,1,0:T(8,128)(2,1)S(1)}, bf16[10,32,128]{2,1,0:T(8,128)(2,1)S(1)}, u32[]{:S(2)}, u32[]{:S(2)}) %collective-permute-start.3) | collective-permute-done | bytes 81952 | tf_op jit(solution)/shard_map/ppermute | solution.py:484
  22.1 2.3 %collective-permute-done.4.refs_2_ = bf16[10,32,128]{2,1,0:T(8,128)(2,1)S(1)} collective-permute-done((bf16[10,32,128]{2,1,0:T(8,128)(2,1)S(1)}, bf16[10,32,128]{2,1,0:T(8,128)(2,1)S(1)}, u32[]{:S(2)}, u32[]{:S(2)}) %collective-permute-start.4) | collective-permute-done | bytes 81952 | tf_op jit(solution)/shard_map/ppermute | solution.py:484
  24.4 0.0 collective-permute-done.5.refs_3_
  24.4 2.0 %shard_map.116 = (f32[24,512]{1,0:T(8,128)S(1)}, f32[8,32,512]{2,1,0:T(8,128)S(1)}, f32[8,32,512]{2,1,0:T(8,128)S(1)}, f32[4,4,48,256]{3,2,1,0:T(8,128)S(1)}, f32[16,16,256]{2,1,0:T(8,128)S(1)}) custom-call(s32[2]{0:T(128)S(1)} %pad_add_fusion.place, bf16[10,32,128]{2,1,0:T(8,128)(2,1)S(1)} %get-tuple-element.36.refs_0_, ...), custom_call_target="tpu_custom_call" | custom-call | flops 3221225472 | bytes 4309000 | tf_op jit(solution)/shard_map/pallas_call | solution.py:204
  26.4 0.1 convert_element_type.51
  26.5 0.8 %collective-permute-start.12 = (f32[24,512]{1,0:T(8,128)S(1)}, f32[24,512]{1,0:T(8,128)S(1)}, u32[]{:S(2)}, u32[]{:S(2)}) collective-permute-start(f32[24,512]{1,0:T(8,128)S(1)} %get-tuple-element.49), channel_id=1, source_target_pairs={{1,0},{2,1},{3,2},{0,3},{5,4},{6,5},{7,6},{4,7},{9,8},{10,9},{11,1... | collective-permute-start | bytes 147464 | tf_op jit(solution)/shard_map/ppermute | solution.py:531
  27.3 0.1 slice_bitcast_fusion
  27.4 1.9 %collective-permute-start.8 = (f16[4,48,256]{2,1,0:T(8,128)(2,1)S(1)}, f16[4,48,256]{2,1,0:T(8,128)(2,1)S(1)}, u32[]{:S(2)}, u32[]{:S(2)}) collective-permute-start(f16[4,48,256]{2,1,0:T(8,128)(2,1)S(1)} %get-tuple-element.62), channel_id=1, source_target_pairs={{0,12},{4,0},{8,4},{12,8},{1,13},{5,1},{9,5},{13,9},{2,14},{6,2},{... | collective-permute-start | bytes 294920 | tf_op jit(solution)/shard_map/ppermute | solution.py:484
  29.3 2.0 %collective-permute-start.7 = (f16[4,48,256]{2,1,0:T(8,128)(2,1)S(1)}, f16[4,48,256]{2,1,0:T(8,128)(2,1)S(1)}, u32[]{:S(2)}, u32[]{:S(2)}) collective-permute-start(f16[4,48,256]{2,1,0:T(8,128)(2,1)S(1)} %get-tuple-element.63), channel_id=1, source_target_pairs={{0,8},{4,12},{8,0},{12,4},{1,9},{5,13},{9,1},{13,5},{2,10},{6,14},... | collective-permute-start | bytes 294920 | tf_op jit(solution)/shard_map/ppermute | solution.py:484
  31.2 0.0 collective-permute-start.6
  31.2 0.0 collective-permute-done.12.beyond
  31.2 0.7 shard_map.118
  32.0 0.8 %convert_element_type.56 = f16[16,48,256]{2,1,0:T(8,128)(2,1)} convert(f32[16,48,256]{2,1,0:T(8,128)S(1)} %shard_map.118) | non-fusion elementwise | flops 196608 | bytes 1179648 | tf_op jit(solution)/shard_map/convert_element_type | solution.py:547
  32.8 5.4 %all-to-all-start = ((f16[16,48,256]{2,1,0:T(8,128)(2,1)}), f16[16,48,256]{2,1,0:T(8,128)(2,1)S(1)}, u32[]{:S(2)}, u32[]{:S(2)}) async-start(f16[16,48,256]{2,1,0:T(8,128)(2,1)} %convert_element_type.56), calls=%async_computation | async-start | bytes 786432 | tf_op jit(solution)/shard_map/all_to_all | solution.py:488
  38.2 0.0 collective-permute-done.8
  38.2 1.7 %collective-permute-done.7 = f16[4,48,256]{2,1,0:T(8,128)(2,1)S(1)} collective-permute-done((f16[4,48,256]{2,1,0:T(8,128)(2,1)S(1)}, f16[4,48,256]{2,1,0:T(8,128)(2,1)S(1)}, u32[]{:S(2)}, u32[]{:S(2)}) %collective-permute-start.7) | collective-permute-done | bytes 98336 | tf_op jit(solution)/shard_map/ppermute | solution.py:484
  40.0 0.0 collective-permute-done.6
  40.1 0.1 collective-permute-start.9
  40.2 1.3 %collective-permute-start.10 = (f16[4,48,256]{2,1,0:T(8,128)(2,1)S(1)}, f16[4,48,256]{2,1,0:T(8,128)(2,1)S(1)}, u32[]{:S(2)}, u32[]{:S(2)}) collective-permute-start(f16[4,48,256]{2,1,0:T(8,128)(2,1)S(1)} %pad_maximum_fusion.1), channel_id=1, source_target_pairs={{0,2},{1,3},{2,0},{3,1},{4,6},{5,7},{6,4},{7,5},{8,10},{9,11},{10,... | collective-permute-start | bytes 294920 | tf_op jit(solution)/shard_map/ppermute | solution.py:484
  41.5 1.5 %collective-permute-start.11 = (f16[4,48,256]{2,1,0:T(8,128)(2,1)S(1)}, f16[4,48,256]{2,1,0:T(8,128)(2,1)S(1)}, u32[]{:S(2)}, u32[]{:S(2)}) collective-permute-start(f16[4,48,256]{2,1,0:T(8,128)(2,1)S(1)} %pad_maximum_fusion.2), channel_id=1, source_target_pairs={{0,3},{1,0},{2,1},{3,2},{4,7},{5,4},{6,5},{7,6},{8,11},{9,8},{10,9... | collective-permute-start | bytes 294920 | tf_op jit(solution)/shard_map/ppermute | solution.py:484
  43.0 1.3 %shard_map.119 = bf16[8,32,512]{2,1,0:T(8,128)(2,1)} custom-call(s32[2]{0:T(128)S(1)} %pad_add_fusion.place, bf16[10,32,128]{2,1,0:T(8,128)(2,1)S(1)} %get-tuple-element.36.refs_0_, bf16[10,32,128]{2,1,0:T(8,128)(2,1)S(1)} %collective-permute-done.3.refs_1_, bf16[10,32,128]{2,1,0:T(8,128)(2,1)S(1)} %collective-permute-done.4.refs_2_, ...), custom_call_target="tpu_custom_call" | custom-call | bytes 589832 | tf_op jit(solution)/shard_map/pallas_call | solution.py:204
  44.4 1.6 %collective-permute-done.9 = f16[4,48,256]{2,1,0:T(8,128)(2,1)S(1)} collective-permute-done((f16[4,48,256]{2,1,0:T(8,128)(2,1)S(1)}, f16[4,48,256]{2,1,0:T(8,128)(2,1)S(1)}, u32[]{:S(2)}, u32[]{:S(2)}) %collective-permute-start.9) | collective-permute-done | bytes 98336 | tf_op jit(solution)/shard_map/ppermute | solution.py:484
  45.9 0.6 collective-permute-done.10
  46.6 1.9 %collective-permute-done.11 = f16[4,48,256]{2,1,0:T(8,128)(2,1)S(1)} collective-permute-done((f16[4,48,256]{2,1,0:T(8,128)(2,1)S(1)}, f16[4,48,256]{2,1,0:T(8,128)(2,1)S(1)}, u32[]{:S(2)}, u32[]{:S(2)}) %collective-permute-start.11) | collective-permute-done | bytes 98336 | tf_op jit(solution)/shard_map/ppermute | solution.py:484
  48.5 0.0 copy-done.8
  48.5 0.0 copy-done.9
  48.5 2.8 %shard_map.117 = (f32[4,48,256]{2,1,0:T(8,128)S(1)}, f32[4,48,256]{2,1,0:T(8,128)S(1)}, f32[4,48,256]{2,1,0:T(8,128)S(1)}, f32[4,48,256]{2,1,0:T(8,128)S(1)}) custom-call(s32[2]{0:T(128)S(1)} %pad_add_fusion.place, f32[4,48,256]{2,1,0:T(8,128)S(1)} %maximum_convert_fusion.refs_0_, f32[4,48,256]{2,1,0:T(8,128)S(1)} %convert_element_type.53.refs_1_, ...), custom_call_target="tpu_custom_call" | custom-call | flops 2147483648 | bytes 2293768 | tf_op jit(solution)/shard_map/pallas_call | solution.py:204
  51.3 0.0 all-to-all-done
  51.5 2.5 %collective-permute-start.15 = (f16[4,48,256]{2,1,0:T(8,128)(2,1)S(1)}, f16[4,48,256]{2,1,0:T(8,128)(2,1)S(1)}, u32[]{:S(2)}, u32[]{:S(2)}) collective-permute-start(f16[4,48,256]{2,1,0:T(8,128)(2,1)S(1)} %convert_element_type.63), channel_id=1, source_target_pairs={{0,12},{4,0},{8,4},{12,8},{1,13},{5,1},{9,5},{13,9},{2,14},{6,2},{... | collective-permute-start | bytes 294920 | tf_op jit(solution)/shard_map/ppermute | solution.py:484
  53.9 0.0 collective-permute-start.14
  53.9 1.4 %collective-permute-start.13 = (f16[4,48,256]{2,1,0:T(8,128)(2,1)S(1)}, f16[4,48,256]{2,1,0:T(8,128)(2,1)S(1)}, u32[]{:S(2)}, u32[]{:S(2)}) collective-permute-start(f16[4,48,256]{2,1,0:T(8,128)(2,1)S(1)} %convert_element_type.61), channel_id=1, source_target_pairs={{0,4},{4,8},{8,12},{12,0},{1,5},{5,9},{9,13},{13,1},{2,6},{6,10},{... | collective-permute-start | bytes 294920 | tf_op jit(solution)/shard_map/ppermute | solution.py:484
  55.3 0.1 convert_element_type.57.spectra
  55.4 2.6 %shard_map.120 = f32[16,48,256]{2,1,0:T(8,128)S(1)} custom-call(s32[2]{0:T(128)S(1)} %pad_add_fusion.place, f32[16,48,256]{2,1,0:T(8,128)S(1)} %convert_element_type.57.spectra, bf16[4,256,256]{2,1,0:T(8,128)(2,1)S(1)} %copy-done.8, bf16[6,128,128]{2,1,0:T(8,128)(2,1)S(1)} %copy-done.9), custom_call_target="tpu_custom_call" | custom-call | flops 2147483648 | bytes 2293768 | tf_op jit(solution)/shard_map/pallas_call | solution.py:204
  58.1 0.8 %convert_element_type.58 = f16[16,48,256]{2,1,0:T(8,128)(2,1)} convert(f32[16,48,256]{2,1,0:T(8,128)S(1)} %shard_map.120) | non-fusion elementwise | flops 196608 | bytes 1179648 | tf_op jit(solution)/shard_map/convert_element_type | solution.py:571
  58.9 5.2 %all-to-all-start.1 = ((f16[16,48,256]{2,1,0:T(8,128)(2,1)}), f16[16,48,256]{2,1,0:T(8,128)(2,1)}, u32[]{:S(2)}, u32[]{:S(2)}) async-start(f16[16,48,256]{2,1,0:T(8,128)(2,1)} %convert_element_type.58), calls=%async_computation.1 | async-start | bytes 786432 | tf_op jit(solution)/shard_map/all_to_all | solution.py:488
  64.1 0.0 collective-permute-done.15
  64.2 0.0 collective-permute-done.14
  64.2 0.0 collective-permute-done.13
  64.3 0.4 collective-permute-start.16
  64.7 1.7 %collective-permute-start.17 = (f16[4,48,256]{2,1,0:T(8,128)(2,1)S(1)}, f16[4,48,256]{2,1,0:T(8,128)(2,1)S(1)}, u32[]{:S(2)}, u32[]{:S(2)}) collective-permute-start(f16[4,48,256]{2,1,0:T(8,128)(2,1)S(1)} %pad_maximum_fusion.4), channel_id=1, source_target_pairs={{0,2},{1,3},{2,0},{3,1},{4,6},{5,7},{6,4},{7,5},{8,10},{9,11},{10,... | collective-permute-start | bytes 294920 | tf_op jit(solution)/shard_map/ppermute | solution.py:484
  66.5 1.4 %collective-permute-start.18 = (f16[4,48,256]{2,1,0:T(8,128)(2,1)S(1)}, f16[4,48,256]{2,1,0:T(8,128)(2,1)S(1)}, u32[]{:S(2)}, u32[]{:S(2)}) collective-permute-start(f16[4,48,256]{2,1,0:T(8,128)(2,1)S(1)} %pad_maximum_fusion.5), channel_id=1, source_target_pairs={{0,3},{1,0},{2,1},{3,2},{4,7},{5,4},{6,5},{7,6},{8,11},{9,8},{10,9... | collective-permute-start | bytes 294920 | tf_op jit(solution)/shard_map/ppermute | solution.py:484
  67.9 3.6 %collective-permute-done.16 = f16[4,48,256]{2,1,0:T(8,128)(2,1)S(1)} collective-permute-done((f16[4,48,256]{2,1,0:T(8,128)(2,1)S(1)}, f16[4,48,256]{2,1,0:T(8,128)(2,1)S(1)}, u32[]{:S(2)}, u32[]{:S(2)}) %collective-permute-start.16) | collective-permute-done | bytes 98336 | tf_op jit(solution)/shard_map/ppermute | solution.py:484
  71.5 1.3 %collective-permute-done.17 = f16[4,48,256]{2,1,0:T(8,128)(2,1)S(1)} collective-permute-done((f16[4,48,256]{2,1,0:T(8,128)(2,1)S(1)}, f16[4,48,256]{2,1,0:T(8,128)(2,1)S(1)}, u32[]{:S(2)}, u32[]{:S(2)}) %collective-permute-start.17) | collective-permute-done | bytes 98336 | tf_op jit(solution)/shard_map/ppermute | solution.py:484
  72.8 0.8 collective-permute-done.18
  73.6 1.2 %shard_map.121 = (f32[8,32,512]{2,1,0:T(8,128)S(1)}, f32[16,16,256]{2,1,0:T(8,128)S(1)}) custom-call(s32[2]{0:T(128)S(1)} %pad_add_fusion.place, bf16[2,512,512]{2,1,0:T(8,128)(2,1)S(1)} %copy-done.6, f32[3,8,32,512]{3,2,1,0:T(8,128)S(1)} %copy-done.2, f32[4,48,256]{2,1,0:T(8,128)S(1)} %maximum_convert_fusion.1.refs_0_, ...), custom_call_target="tpu_custom_call" | custom-call | flops 1073741824 | bytes 4194312 | tf_op jit(solution)/shard_map/pallas_call | solution.py:204
  74.9 1.5 %all-to-all-done.1 = f16[16,48,256]{2,1,0:T(8,128)(2,1)} async-done(((f16[16,48,256]{2,1,0:T(8,128)(2,1)}), f16[16,48,256]{2,1,0:T(8,128)(2,1)}, u32[]{:S(2)}, u32[]{:S(2)}) %all-to-all-start.1) | async-done | bytes 393248 | tf_op jit(solution)/shard_map/all_to_all | solution.py:488
  76.4 1.1 %convert_element_type.59.spectra = f32[16,48,256]{2,1,0:T(8,128)S(1)} convert(f16[16,48,256]{2,1,0:T(8,128)(2,1)} %all-to-all-done.1) | non-fusion elementwise | flops 196608 | bytes 1179648 | tf_op jit(solution)/shard_map/convert_element_type | solution.py:588
  77.5 1.9 %shard_map.122 = f32[3,8,32,512]{3,2,1,0:T(8,128)} custom-call(f32[16,48,256]{2,1,0:T(8,128)S(1)} %convert_element_type.59.spectra, bf16[2,512,512]{2,1,0:T(8,128)(2,1)S(1)} %copy-done.6, f32[3,8,32,512]{3,2,1,0:T(8,128)S(1)} %copy-done.2, f32[8,32,512]{2,1,0:T(8,128)S(1)} %get-tuple-element.59.updated, f32[16,16,256]{2,1,0:T(8,128)S(1)} %get-tuple-element.60.kept), custom_call_target="tpu_custom_call" | custom-call | flops 2147483648 | bytes 5767168 | tf_op jit(solution)/shard_map/pallas_call | solution.py:204
  (39 shorter events, 0.6 us)
Async XLA Ops:
  0.7 1.0 %copy-start = (bf16[8,32,512]{2,1,0:T(8,128)(2,1)S(1)}, bf16[8,32,512]{2,1,0:T(8,128)(2,1)}, u32[]{:S(2)}) copy-start(bf16[8,32,512]{2,1,0:T(8,128)(2,1)} %moving.1) | copy-start | bytes 786436
  1.7 0.7 copy-start.1
  3.0 7.7 %collective-permute-start = (bf16[272,128]{1,0:T(8,128)(2,1)S(1)}, bf16[272,128]{1,0:T(8,128)(2,1)S(1)}, u32[]{:S(2)}, u32[]{:S(2)}) collective-permute-start(bf16[272,128]{1,0:T(8,128)(2,1)S(1)} %get-tuple-element.33), channel_id=1, source_target_pairs={{0,4},{4,8},{8,12},{12,0},{1,5},{5,9},{9,13},{13,1},{2,6},{6,10},{... | collective-permute-start | bytes 208904 | tf_op jit(solution)/shard_map/ppermute | solution.py:484
  6.1 7.3 %collective-permute-start.1 = (bf16[272,128]{1,0:T(8,128)(2,1)S(1)}, bf16[272,128]{1,0:T(8,128)(2,1)S(1)}, u32[]{:S(2)}, u32[]{:S(2)}) collective-permute-start(bf16[272,128]{1,0:T(8,128)(2,1)S(1)} %get-tuple-element.34), channel_id=1, source_target_pairs={{0,8},{4,12},{8,0},{12,4},{1,9},{5,13},{9,1},{13,5},{2,10},{6,14},... | collective-permute-start | bytes 208904 | tf_op jit(solution)/shard_map/ppermute | solution.py:484
  8.7 4.9 %collective-permute-start.2 = (bf16[272,128]{1,0:T(8,128)(2,1)S(1)}, bf16[272,128]{1,0:T(8,128)(2,1)S(1)}, u32[]{:S(2)}, u32[]{:S(2)}) collective-permute-start(bf16[272,128]{1,0:T(8,128)(2,1)S(1)} %get-tuple-element.35), channel_id=1, source_target_pairs={{0,12},{4,0},{8,4},{12,8},{1,13},{5,1},{9,5},{13,9},{2,14},{6,2},{... | collective-permute-start | bytes 208904 | tf_op jit(solution)/shard_map/ppermute | solution.py:484
  13.5 5.6 %copy-start.3 = (f32[8,32,512]{2,1,0:T(8,128)S(1)}, f32[8,32,512]{2,1,0:T(8,128)}, u32[]{:S(2)}) copy-start(f32[8,32,512]{2,1,0:T(8,128)} %stiffness.1) | copy-start | bytes 1572868
  13.5 5.6 %copy-start.5 = (s32[8,32,4]{1,2,0:T(4,128)S(1)}, s32[8,32,4]{1,2,0:T(4,128)}, u32[]{:S(2)}) copy-start(s32[8,32,4]{1,2,0:T(4,128)} %param.15) | copy-start | bytes 12292
  14.9 7.2 %collective-permute-start.3 = (bf16[10,32,128]{2,1,0:T(8,128)(2,1)S(1)}, bf16[10,32,128]{2,1,0:T(8,128)(2,1)S(1)}, u32[]{:S(2)}, u32[]{:S(2)}) collective-permute-start(bf16[10,32,128]{2,1,0:T(8,128)(2,1)S(1)} %get-tuple-element.37), channel_id=1, source_target_pairs={{0,4},{4,8},{8,12},{12,0},{1,5},{5,9},{9,13},{13,1},{2,6},{6,10},{... | collective-permute-start | bytes 245768 | tf_op jit(solution)/shard_map/ppermute | solution.py:484
  16.7 7.7 %collective-permute-start.4 = (bf16[10,32,128]{2,1,0:T(8,128)(2,1)S(1)}, bf16[10,32,128]{2,1,0:T(8,128)(2,1)S(1)}, u32[]{:S(2)}, u32[]{:S(2)}) collective-permute-start(bf16[10,32,128]{2,1,0:T(8,128)(2,1)S(1)} %get-tuple-element.38), channel_id=1, source_target_pairs={{0,8},{4,12},{8,0},{12,4},{1,9},{5,13},{9,1},{13,5},{2,10},{6,14},... | collective-permute-start | bytes 245768 | tf_op jit(solution)/shard_map/ppermute | solution.py:484
  18.7 5.7 %collective-permute-start.5 = (bf16[10,32,128]{2,1,0:T(8,128)(2,1)S(1)}, bf16[10,32,128]{2,1,0:T(8,128)(2,1)S(1)}, u32[]{:S(2)}, u32[]{:S(2)}) collective-permute-start(bf16[10,32,128]{2,1,0:T(8,128)(2,1)S(1)} %get-tuple-element.39), channel_id=1, source_target_pairs={{0,12},{4,0},{8,4},{12,8},{1,13},{5,1},{9,5},{13,9},{2,14},{6,2},{... | collective-permute-start | bytes 245768 | tf_op jit(solution)/shard_map/ppermute | solution.py:484
  19.2 5.3 %copy-start.4 = (bf16[8,32,512]{2,1,0:T(8,128)(2,1)S(1)}, bf16[8,32,512]{2,1,0:T(8,128)(2,1)}, u32[]{:S(2)}) copy-start(bf16[8,32,512]{2,1,0:T(8,128)(2,1)} %refs_4_.2) | copy-start | bytes 786436
  19.2 5.3 %copy-start.7 = (bf16[2,512,512]{2,1,0:T(8,128)(2,1)S(1)}, bf16[2,512,512]{2,1,0:T(8,128)(2,1)}, u32[]{:S(2)}) copy-start(bf16[2,512,512]{2,1,0:T(8,128)(2,1)} %constant.15.clone.refs_6_.basis) | copy-start | bytes 3145732
  26.5 4.7 %collective-permute-start.12 = (f32[24,512]{1,0:T(8,128)S(1)}, f32[24,512]{1,0:T(8,128)S(1)}, u32[]{:S(2)}, u32[]{:S(2)}) collective-permute-start(f32[24,512]{1,0:T(8,128)S(1)} %get-tuple-element.49), channel_id=1, source_target_pairs={{1,0},{2,1},{3,2},{0,3},{5,4},{6,5},{7,6},{4,7},{9,8},{10,9},{11,1... | collective-permute-start | bytes 147464 | tf_op jit(solution)/shard_map/ppermute | solution.py:531
  27.4 10.8 %collective-permute-start.8 = (f16[4,48,256]{2,1,0:T(8,128)(2,1)S(1)}, f16[4,48,256]{2,1,0:T(8,128)(2,1)S(1)}, u32[]{:S(2)}, u32[]{:S(2)}) collective-permute-start(f16[4,48,256]{2,1,0:T(8,128)(2,1)S(1)} %get-tuple-element.62), channel_id=1, source_target_pairs={{0,12},{4,0},{8,4},{12,8},{1,13},{5,1},{9,5},{13,9},{2,14},{6,2},{... | collective-permute-start | bytes 294920 | tf_op jit(solution)/shard_map/ppermute | solution.py:484
  29.3 10.7 %collective-permute-start.7 = (f16[4,48,256]{2,1,0:T(8,128)(2,1)S(1)}, f16[4,48,256]{2,1,0:T(8,128)(2,1)S(1)}, u32[]{:S(2)}, u32[]{:S(2)}) collective-permute-start(f16[4,48,256]{2,1,0:T(8,128)(2,1)S(1)} %get-tuple-element.63), channel_id=1, source_target_pairs={{0,8},{4,12},{8,0},{12,4},{1,9},{5,13},{9,1},{13,5},{2,10},{6,14},... | collective-permute-start | bytes 294920 | tf_op jit(solution)/shard_map/ppermute | solution.py:484
  31.2 8.7 %collective-permute-start.6 = (f16[4,48,256]{2,1,0:T(8,128)(2,1)S(1)}, f16[4,48,256]{2,1,0:T(8,128)(2,1)S(1)}, u32[]{:S(2)}, u32[]{:S(2)}) collective-permute-start(f16[4,48,256]{2,1,0:T(8,128)(2,1)S(1)} %get-tuple-element.64), channel_id=1, source_target_pairs={{0,4},{4,8},{8,12},{12,0},{1,5},{5,9},{9,13},{13,1},{2,6},{6,10},{... | collective-permute-start | bytes 294920 | tf_op jit(solution)/shard_map/ppermute | solution.py:484
  32.8 18.6 %all-to-all-start = ((f16[16,48,256]{2,1,0:T(8,128)(2,1)}), f16[16,48,256]{2,1,0:T(8,128)(2,1)S(1)}, u32[]{:S(2)}, u32[]{:S(2)}) async-start(f16[16,48,256]{2,1,0:T(8,128)(2,1)} %convert_element_type.56), calls=%async_computation | async-start | bytes 786432 | tf_op jit(solution)/shard_map/all_to_all | solution.py:488
  40.0 8.5 %copy-start.8 = (bf16[4,256,256]{2,1,0:T(8,128)(2,1)S(1)}, bf16[4,256,256]{2,1,0:T(8,128)(2,1)}, u32[]{:S(2)}) copy-start(bf16[4,256,256]{2,1,0:T(8,128)(2,1)} %constant.16.clone.refs_4_.basis_z) | copy-start | bytes 1572868
  40.0 8.5 %copy-start.9 = (bf16[6,128,128]{2,1,0:T(8,128)(2,1)S(1)}, bf16[6,128,128]{2,1,0:T(8,128)(2,1)}, u32[]{:S(2)}) copy-start(bf16[6,128,128]{2,1,0:T(8,128)(2,1)} %constant.17.clone.refs_5_.basis_y) | copy-start | bytes 589828
  40.1 5.8 %collective-permute-start.9 = (f16[4,48,256]{2,1,0:T(8,128)(2,1)S(1)}, f16[4,48,256]{2,1,0:T(8,128)(2,1)S(1)}, u32[]{:S(2)}, u32[]{:S(2)}) collective-permute-start(f16[4,48,256]{2,1,0:T(8,128)(2,1)S(1)} %pad_maximum_fusion), channel_id=1, source_target_pairs={{0,1},{1,2},{2,3},{3,0},{4,5},{5,6},{6,7},{7,4},{8,9},{9,10},{10,1... | collective-permute-start | bytes 294920 | tf_op jit(solution)/shard_map/ppermute | solution.py:484
  40.2 6.4 %collective-permute-start.10 = (f16[4,48,256]{2,1,0:T(8,128)(2,1)S(1)}, f16[4,48,256]{2,1,0:T(8,128)(2,1)S(1)}, u32[]{:S(2)}, u32[]{:S(2)}) collective-permute-start(f16[4,48,256]{2,1,0:T(8,128)(2,1)S(1)} %pad_maximum_fusion.1), channel_id=1, source_target_pairs={{0,2},{1,3},{2,0},{3,1},{4,6},{5,7},{6,4},{7,5},{8,10},{9,11},{10,... | collective-permute-start | bytes 294920 | tf_op jit(solution)/shard_map/ppermute | solution.py:484
  41.5 7.0 %collective-permute-start.11 = (f16[4,48,256]{2,1,0:T(8,128)(2,1)S(1)}, f16[4,48,256]{2,1,0:T(8,128)(2,1)S(1)}, u32[]{:S(2)}, u32[]{:S(2)}) collective-permute-start(f16[4,48,256]{2,1,0:T(8,128)(2,1)S(1)} %pad_maximum_fusion.2), channel_id=1, source_target_pairs={{0,3},{1,0},{2,1},{3,2},{4,7},{5,4},{6,5},{7,6},{8,11},{9,8},{10,9... | collective-permute-start | bytes 294920 | tf_op jit(solution)/shard_map/ppermute | solution.py:484
  51.5 12.7 %collective-permute-start.15 = (f16[4,48,256]{2,1,0:T(8,128)(2,1)S(1)}, f16[4,48,256]{2,1,0:T(8,128)(2,1)S(1)}, u32[]{:S(2)}, u32[]{:S(2)}) collective-permute-start(f16[4,48,256]{2,1,0:T(8,128)(2,1)S(1)} %convert_element_type.63), channel_id=1, source_target_pairs={{0,12},{4,0},{8,4},{12,8},{1,13},{5,1},{9,5},{13,9},{2,14},{6,2},{... | collective-permute-start | bytes 294920 | tf_op jit(solution)/shard_map/ppermute | solution.py:484
  53.9 10.2 %collective-permute-start.14 = (f16[4,48,256]{2,1,0:T(8,128)(2,1)S(1)}, f16[4,48,256]{2,1,0:T(8,128)(2,1)S(1)}, u32[]{:S(2)}, u32[]{:S(2)}) collective-permute-start(f16[4,48,256]{2,1,0:T(8,128)(2,1)S(1)} %convert_element_type.62), channel_id=1, source_target_pairs={{0,8},{4,12},{8,0},{12,4},{1,9},{5,13},{9,1},{13,5},{2,10},{6,14},... | collective-permute-start | bytes 294920 | tf_op jit(solution)/shard_map/ppermute | solution.py:484
  53.9 10.3 %collective-permute-start.13 = (f16[4,48,256]{2,1,0:T(8,128)(2,1)S(1)}, f16[4,48,256]{2,1,0:T(8,128)(2,1)S(1)}, u32[]{:S(2)}, u32[]{:S(2)}) collective-permute-start(f16[4,48,256]{2,1,0:T(8,128)(2,1)S(1)} %convert_element_type.61), channel_id=1, source_target_pairs={{0,4},{4,8},{8,12},{12,0},{1,5},{5,9},{9,13},{13,1},{2,6},{6,10},{... | collective-permute-start | bytes 294920 | tf_op jit(solution)/shard_map/ppermute | solution.py:484
  58.9 14.7 %copy-start.2 = (f32[3,8,32,512]{3,2,1,0:T(8,128)S(1)}, f32[3,8,32,512]{3,2,1,0:T(8,128)}, u32[]{:S(2)}) copy-start(f32[3,8,32,512]{3,2,1,0:T(8,128)} %velocity.3) | copy-start | bytes 4718596
  58.9 14.7 %copy-start.6 = (bf16[2,512,512]{2,1,0:T(8,128)(2,1)S(1)}, bf16[2,512,512]{2,1,0:T(8,128)(2,1)}, u32[]{:S(2)}) copy-start(bf16[2,512,512]{2,1,0:T(8,128)(2,1)} %constant.18.clone.basis) | copy-start | bytes 3145732
  58.9 17.5 %all-to-all-start.1 = ((f16[16,48,256]{2,1,0:T(8,128)(2,1)}), f16[16,48,256]{2,1,0:T(8,128)(2,1)}, u32[]{:S(2)}, u32[]{:S(2)}) async-start(f16[16,48,256]{2,1,0:T(8,128)(2,1)} %convert_element_type.58), calls=%async_computation.1 | async-start | bytes 786432 | tf_op jit(solution)/shard_map/all_to_all | solution.py:488
  64.3 7.2 %collective-permute-start.16 = (f16[4,48,256]{2,1,0:T(8,128)(2,1)S(1)}, f16[4,48,256]{2,1,0:T(8,128)(2,1)S(1)}, u32[]{:S(2)}, u32[]{:S(2)}) collective-permute-start(f16[4,48,256]{2,1,0:T(8,128)(2,1)S(1)} %pad_maximum_fusion.3), channel_id=1, source_target_pairs={{0,1},{1,2},{2,3},{3,0},{4,5},{5,6},{6,7},{7,4},{8,9},{9,10},{10,1... | collective-permute-start | bytes 294920 | tf_op jit(solution)/shard_map/ppermute | solution.py:484
  64.7 8.1 %collective-permute-start.17 = (f16[4,48,256]{2,1,0:T(8,128)(2,1)S(1)}, f16[4,48,256]{2,1,0:T(8,128)(2,1)S(1)}, u32[]{:S(2)}, u32[]{:S(2)}) collective-permute-start(f16[4,48,256]{2,1,0:T(8,128)(2,1)S(1)} %pad_maximum_fusion.4), channel_id=1, source_target_pairs={{0,2},{1,3},{2,0},{3,1},{4,6},{5,7},{6,4},{7,5},{8,10},{9,11},{10,... | collective-permute-start | bytes 294920 | tf_op jit(solution)/shard_map/ppermute | solution.py:484
  66.5 7.1 %collective-permute-start.18 = (f16[4,48,256]{2,1,0:T(8,128)(2,1)S(1)}, f16[4,48,256]{2,1,0:T(8,128)(2,1)S(1)}, u32[]{:S(2)}, u32[]{:S(2)}) collective-permute-start(f16[4,48,256]{2,1,0:T(8,128)(2,1)S(1)} %pad_maximum_fusion.5), channel_id=1, source_target_pairs={{0,3},{1,0},{2,1},{3,2},{4,7},{5,4},{6,5},{7,6},{8,11},{9,8},{10,9... | collective-permute-start | bytes 294920 | tf_op jit(solution)/shard_map/ppermute | solution.py:484

commit v11 on v10

--- a/solution.py
+++ b/solution.py
@@ -186,6 +186,9 @@
     return wave * wave
 
 
+HOPS = (0, 2, 1, 3)
+
+
 def around(value, count):
     return lax.rem(value + 2 * count, count)
 
@@ -222,7 +225,7 @@
 def send_columns_kernel(slabs, place, moving, fetch, *sends):
     planes, rows, _ = moving.shape
     for step, send in enumerate(sends):
-        to = around(place[0] + step, slabs)
+        to = around(place[0] + HOPS[step], slabs)
         block = pl.ds(pl.multiple_of(to * BLOCK, BLOCK), BLOCK)
         for z in range(planes):
             send[z * rows : (z + 1) * rows] = moving[z, :, block]
@@ -238,7 +241,7 @@
     group = 4
 
     def name(other, plane):
-        number = (around(me - other, slabs) * planes).astype(jnp.float32) + float(plane)
+        number = (around(me - HOPS[other], slabs) * planes).astype(jnp.float32) + float(plane)
         return jnp.full((rows, BLOCK), number, jnp.float32).astype(jnp.bfloat16)
 
     for step in range(slabs):
@@ -255,14 +258,14 @@
                     values = received[other][plane * rows : (plane + 1) * rows]
                     own = name(other, plane)
                     found = [jnp.where(w == own, values, f) for w, f in zip(wanted, found)]
-            back = (slabs - step) % slabs
+            back = (slabs - HOPS[step]) % slabs
             for z in range(group):
                 own = start + z
-                sends[back][own + 1] = found[z]
+                sends[HOPS.index(back)][own + 1] = found[z]
                 if own == 0:
-                    sends[(back - 1) % slabs][planes + 1] = found[z]
+                    sends[HOPS.index((back - 1) % slabs)][planes + 1] = found[z]
                 if own == planes - 1:
-                    sends[(back + 1) % slabs][0] = found[z]
+                    sends[HOPS.index((back + 1) % slabs)][0] = found[z]
 
 
 def coefficient_kernel(stiffness, tissue, out):
@@ -285,7 +288,7 @@
     template, coefficient, basis, first, image, weight, spectra, kept, planes_of, wide = refs
     planes, rows, x_length = template.shape
     for step in range(slabs):
-        block = pl.ds(pl.multiple_of(around(place[0] - step, slabs) * BLOCK, BLOCK), BLOCK)
+        block = pl.ds(pl.multiple_of(around(place[0] - HOPS[step], slabs) * BLOCK, BLOCK), BLOCK)
         planes_of[:, :, block] = received[step][...].astype(jnp.float32)
     forces = [[], []]
     for z in range(planes):
@@ -451,9 +454,19 @@
             own = jnp.concatenate([spectra[:, part:, :], kept[...]], axis=1)
         else:
             own = spectra[:, :part, :]
-        result[a] = moved(own.reshape(devices * part, area), velocity[a + 1], basis)
-        leaving.append(pltpu.make_async_copy(result.at[a], out.at[a + 1], done.at[a + 1]))
-        leaving[-1].start()
+        high, low = split(own.reshape(devices * part, area).T)
+        planes, rows, x_length = velocity.shape[1:]
+        some = planes // 2
+        for k in range(2):
+            cells = slice(k * some * rows, (k + 1) * some * rows)
+            smoothed = times((high[cells], low[cells]), (basis[0], basis[1]), ((1,), (0,)))
+            own_planes = slice(k * some, (k + 1) * some)
+            step = velocity[a + 1, own_planes] - 32.0 * smoothed.reshape(some, rows, x_length)
+            result[a, own_planes] = 0.5 * step
+            there = out.at[a + 1, pl.ds(k * some, some)]
+            own_copy = pltpu.make_async_copy(result.at[a, pl.ds(k * some, some)], there, done.at[1 + 2 * a + k])
+            own_copy.start()
+            leaving.append(own_copy)
     for copy in leaving:
         copy.wait()
 
@@ -461,7 +474,7 @@
 def place_kernel(slabs, place, *refs):
     received, warped = refs[:slabs], refs[slabs]
     for step in range(slabs):
-        block = pl.ds(pl.multiple_of(around(place[0] - step, slabs) * BLOCK, BLOCK), BLOCK)
+        block = pl.ds(pl.multiple_of(around(place[0] - HOPS[step], slabs) * BLOCK, BLOCK), BLOCK)
         warped[:, :, block] = received[step][1:-1]
 
 
@@ -478,10 +491,10 @@
     def shape(dims, kind=f32):
         return jax.ShapeDtypeStruct(dims, kind)
 
-    def scatter(sends, axis):
+    def scatter(sends, axis, hops=(0, 1, 2, 3)):
         count = lax.axis_size(axis)
         return [sends[0]] + [
-            lax.ppermute(sends[d], axis, [(i, (i + d) % count) for i in range(count)]) for d in range(1, count)
+            lax.ppermute(sends[d], axis, [(i, (i + hops[d]) % count) for i in range(count)]) for d in range(1, count)
         ]
 
     def exchange(values):
@@ -500,10 +513,10 @@
         functools.partial(pick_kernel, slabs),
         [shape((planes + 2, rows, BLOCK), bf16)] * slabs,
         place,
-        *scatter(sends, "slab"),
+        *scatter(sends, "slab", HOPS),
         flops=1 << 30,
     )
-    received = scatter(sends, "slab")
+    received = scatter(sends, "slab", HOPS)
     basis_x = in_two(real_basis(x_length))
     basis_z = np.kron(real_basis(total_z), np.eye(8))
     basis_z = np.concatenate([in_two(basis_z), in_two(basis_z.T)])
@@ -590,7 +603,7 @@
         velocity,
         updated,
         kept,
-        scratch=[pltpu.VMEM((2,) + moving.shape, f32), pltpu.SemaphoreType.DMA((3,))],
+        scratch=[pltpu.VMEM((2,) + moving.shape, f32), pltpu.SemaphoreType.DMA((5,))],
         flops=2 << 30,
         stays=1,
     )
@@ -606,7 +619,7 @@
         and planes * slabs * 8 == 256
         and rows % 16 == 0
         and rows * subs == BLOCK
-        and subs == 4
+        and slabs == subs == len(HOPS)
         and x_length % (32 * slabs * subs) == 0
     )
     run = local_blocks if fits else local_general

time: 79.8 us -> 79.4 us (level)
  waiting for transfers between devices: 21.4 us -> 19 us
  starting transfers between devices: 36.8 us -> 38.9 us
    ppermute x18, starting transfers between devices: 25.3 us -> 28.7 us  [scatter(): lax.ppermute(sends[d], axis, [(i, (i + hops[d]) % count) for i in range(c...]
    ppermute x18, waiting for transfers between devices: 19.9 us -> 17.5 us  [scatter(): lax.ppermute(sends[d], axis, [(i, (i + hops[d]) % count) for i in range(c...]
  transfers between devices with their start and end apart: 21 -> 21, of which waited for: 13 -> 14; matrix products, arithmetic and copies ran while one was open for 3% -> 3% of each run, Pallas kernels for 11% -> 11%
where the time goes in v11:
time: 79.4 us; the launch traced here: 78.9 us
  starting transfers between devices  38.9 us (49%)
  waiting for transfers between devices  19 us (24%)
  Pallas kernels  14.8 us (19%)
  other arithmetic  3.32 us (4%)
  local copies, waits for them, and re-layouts  1.94 us (2%)
  between operations  0.97 us (1%)
    ppermute x18, starting transfers between devices, scatter(): lax.ppermute(sends[d], axis, [(i, (i + hops[d]) % count) for i in range(c...  28.7 us
    ppermute x18, waiting for transfers between devices, scatter(): lax.ppermute(sends[d], axis, [(i, (i + hops[d]) % count) for i in range(c...  17.5 us
    pallas_call x10, Pallas kernels, call(): pl.pallas_call(kernel, out_shape=out_shape, in_specs=places, out_specs=ja...  14.8 us
    all_to_all x2, starting transfers between devices, exchange(): lax.all_to_all(values, ('slab', 'sub'), split_axis=0, concat_axis=0, tile...  10.1 us
    unnamed x20, local copies, waits for them, and re-layouts  1.7 us
    convert_element_type x2, other arithmetic, local_blocks(): spectra = exchange(spectra.astype(f16))  1.62 us
  transfers between devices with their start and end apart: 21, of which 14 were waited for; matrix products, arithmetic and copies ran while one was open for 3% of the time, Pallas kernels for 11%

profile of v11, /device:TPU:0, one launch (start us, length us, event | category | flops | bytes accessed | tf_op | source)
XLA Modules:
  0.0 78.9 jit_solution(11289096831851518186)
XLA Ops:
  0.6 0.1 pad_add_fusion.place
  0.7 0.9 %copy-done = bf16[8,32,512]{2,1,0:T(8,128)(2,1)S(1)} copy-done((bf16[8,32,512]{2,1,0:T(8,128)(2,1)S(1)}, bf16[8,32,512]{2,1,0:T(8,128)(2,1)}, u32[]{:S(2)}) %copy-start) | copy-done | bytes 262168
  1.7 0.7 copy-done.1
  2.4 0.6 shard_map.113
  3.0 4.1 %collective-permute-start = (bf16[272,128]{1,0:T(8,128)(2,1)S(1)}, bf16[272,128]{1,0:T(8,128)(2,1)S(1)}, u32[]{:S(2)}, u32[]{:S(2)}) collective-permute-start(bf16[272,128]{1,0:T(8,128)(2,1)S(1)} %get-tuple-element.33), channel_id=1, source_target_pairs={{0,8},{4,12},{8,0},{12,4},{1,9},{5,13},{9,1},{13,5},{2,10},{6,14},... | collective-permute-start | bytes 208904 | tf_op jit(solution)/shard_map/ppermute | solution.py:497
  7.1 1.6 %collective-permute-start.1 = (bf16[272,128]{1,0:T(8,128)(2,1)S(1)}, bf16[272,128]{1,0:T(8,128)(2,1)S(1)}, u32[]{:S(2)}, u32[]{:S(2)}) collective-permute-start(bf16[272,128]{1,0:T(8,128)(2,1)S(1)} %get-tuple-element.34), channel_id=1, source_target_pairs={{0,4},{4,8},{8,12},{12,0},{1,5},{5,9},{9,13},{13,1},{2,6},{6,10},{... | collective-permute-start | bytes 208904 | tf_op jit(solution)/shard_map/ppermute | solution.py:497
  8.7 2.2 %collective-permute-start.2 = (bf16[272,128]{1,0:T(8,128)(2,1)S(1)}, bf16[272,128]{1,0:T(8,128)(2,1)S(1)}, u32[]{:S(2)}, u32[]{:S(2)}) collective-permute-start(bf16[272,128]{1,0:T(8,128)(2,1)S(1)} %get-tuple-element.35), channel_id=1, source_target_pairs={{0,12},{4,0},{8,4},{12,8},{1,13},{5,1},{9,5},{13,9},{2,14},{6,2},{... | collective-permute-start | bytes 208904 | tf_op jit(solution)/shard_map/ppermute | solution.py:497
  10.9 0.1 collective-permute-done.refs_1_
  11.0 2.5 %collective-permute-done.1.refs_2_ = bf16[272,128]{1,0:T(8,128)(2,1)S(1)} collective-permute-done((bf16[272,128]{1,0:T(8,128)(2,1)S(1)}, bf16[272,128]{1,0:T(8,128)(2,1)S(1)}, u32[]{:S(2)}, u32[]{:S(2)}) %collective-permute-start.1) | collective-permute-done | bytes 69664 | tf_op jit(solution)/shard_map/ppermute | solution.py:497
  13.4 0.3 collective-permute-done.2.refs_3_
  13.7 1.3 %shard_map.114 = (bf16[10,32,128]{2,1,0:T(8,128)(2,1)S(1)}, bf16[10,32,128]{2,1,0:T(8,128)(2,1)S(1)}, bf16[10,32,128]{2,1,0:T(8,128)(2,1)S(1)}, bf16[10,32,128]{2,1,0:T(8,128)(2,1)S(1)}) custom-call(s32[2]{0:T(128)S(1)} %pad_add_fusion.place, bf16[272,128]{1,0:T(8,128)(2,1)S(1)} %get-tuple-element.32.refs_0_, ...), custom_call_target="tpu_custom_call" | custom-call | flops 1073741824 | bytes 606216 | tf_op jit(solution)/shard_map/pallas_call | solution.py:207
  15.1 2.7 %collective-permute-start.3 = (bf16[10,32,128]{2,1,0:T(8,128)(2,1)S(1)}, bf16[10,32,128]{2,1,0:T(8,128)(2,1)S(1)}, u32[]{:S(2)}, u32[]{:S(2)}) collective-permute-start(bf16[10,32,128]{2,1,0:T(8,128)(2,1)S(1)} %get-tuple-element.37), channel_id=1, source_target_pairs={{0,8},{4,12},{8,0},{12,4},{1,9},{5,13},{9,1},{13,5},{2,10},{6,14},... | collective-permute-start | bytes 245768 | tf_op jit(solution)/shard_map/ppermute | solution.py:497
  17.8 1.3 %collective-permute-start.4 = (bf16[10,32,128]{2,1,0:T(8,128)(2,1)S(1)}, bf16[10,32,128]{2,1,0:T(8,128)(2,1)S(1)}, u32[]{:S(2)}, u32[]{:S(2)}) collective-permute-start(bf16[10,32,128]{2,1,0:T(8,128)(2,1)S(1)} %get-tuple-element.38), channel_id=1, source_target_pairs={{0,4},{4,8},{8,12},{12,0},{1,5},{5,9},{9,13},{13,1},{2,6},{6,10},{... | collective-permute-start | bytes 245768 | tf_op jit(solution)/shard_map/ppermute | solution.py:497
  19.1 2.5 %collective-permute-start.5 = (bf16[10,32,128]{2,1,0:T(8,128)(2,1)S(1)}, bf16[10,32,128]{2,1,0:T(8,128)(2,1)S(1)}, u32[]{:S(2)}, u32[]{:S(2)}) collective-permute-start(bf16[10,32,128]{2,1,0:T(8,128)(2,1)S(1)} %get-tuple-element.39), channel_id=1, source_target_pairs={{0,12},{4,0},{8,4},{12,8},{1,13},{5,1},{9,5},{13,9},{2,14},{6,2},{... | collective-permute-start | bytes 245768 | tf_op jit(solution)/shard_map/ppermute | solution.py:497
  21.6 0.3 shard_map.115.refs_5_
  22.0 1.2 %collective-permute-done.3.refs_1_ = bf16[10,32,128]{2,1,0:T(8,128)(2,1)S(1)} collective-permute-done((bf16[10,32,128]{2,1,0:T(8,128)(2,1)S(1)}, bf16[10,32,128]{2,1,0:T(8,128)(2,1)S(1)}, u32[]{:S(2)}, u32[]{:S(2)}) %collective-permute-start.3) | collective-permute-done | bytes 81952 | tf_op jit(solution)/shard_map/ppermute | solution.py:497
  23.2 1.0 %collective-permute-done.4.refs_2_ = bf16[10,32,128]{2,1,0:T(8,128)(2,1)S(1)} collective-permute-done((bf16[10,32,128]{2,1,0:T(8,128)(2,1)S(1)}, bf16[10,32,128]{2,1,0:T(8,128)(2,1)S(1)}, u32[]{:S(2)}, u32[]{:S(2)}) %collective-permute-start.4) | collective-permute-done | bytes 81952 | tf_op jit(solution)/shard_map/ppermute | solution.py:497
  24.2 0.4 collective-permute-done.5.refs_3_
  24.6 0.0 copy-done.7
  24.7 2.0 %shard_map.116 = (f32[24,512]{1,0:T(8,128)S(1)}, f32[8,32,512]{2,1,0:T(8,128)S(1)}, f32[8,32,512]{2,1,0:T(8,128)S(1)}, f32[4,4,48,256]{3,2,1,0:T(8,128)S(1)}, f32[16,16,256]{2,1,0:T(8,128)S(1)}) custom-call(s32[2]{0:T(128)S(1)} %pad_add_fusion.place, bf16[10,32,128]{2,1,0:T(8,128)(2,1)S(1)} %get-tuple-element.36.refs_0_, ...), custom_call_target="tpu_custom_call" | custom-call | flops 3221225472 | bytes 4309000 | tf_op jit(solution)/shard_map/pallas_call | solution.py:207
  26.7 0.1 convert_element_type.51
  26.7 0.1 collective-permute-start.12
  26.8 0.1 slice_bitcast_fusion
  26.9 3.3 %collective-permute-start.8 = (f16[4,48,256]{2,1,0:T(8,128)(2,1)S(1)}, f16[4,48,256]{2,1,0:T(8,128)(2,1)S(1)}, u32[]{:S(2)}, u32[]{:S(2)}) collective-permute-start(f16[4,48,256]{2,1,0:T(8,128)(2,1)S(1)} %get-tuple-element.62), channel_id=1, source_target_pairs={{0,12},{4,0},{8,4},{12,8},{1,13},{5,1},{9,5},{13,9},{2,14},{6,2},{... | collective-permute-start | bytes 294920 | tf_op jit(solution)/shard_map/ppermute | solution.py:497
  30.2 0.0 collective-permute-start.7
  30.2 0.6 collective-permute-start.6
  30.8 0.0 collective-permute-done.12.beyond
  30.8 0.7 shard_map.118
  31.5 0.8 %convert_element_type.56 = f16[16,48,256]{2,1,0:T(8,128)(2,1)} convert(f32[16,48,256]{2,1,0:T(8,128)S(1)} %shard_map.118) | non-fusion elementwise | flops 196608 | bytes 1179648 | tf_op jit(solution)/shard_map/convert_element_type | solution.py:560
  32.3 5.5 %all-to-all-start = ((f16[16,48,256]{2,1,0:T(8,128)(2,1)}), f16[16,48,256]{2,1,0:T(8,128)(2,1)S(1)}, u32[]{:S(2)}, u32[]{:S(2)}) async-start(f16[16,48,256]{2,1,0:T(8,128)(2,1)} %convert_element_type.56), calls=%async_computation | async-start | bytes 786432 | tf_op jit(solution)/shard_map/all_to_all | solution.py:501
  37.8 0.0 collective-permute-done.8
  37.9 2.1 %collective-permute-done.7 = f16[4,48,256]{2,1,0:T(8,128)(2,1)S(1)} collective-permute-done((f16[4,48,256]{2,1,0:T(8,128)(2,1)S(1)}, f16[4,48,256]{2,1,0:T(8,128)(2,1)S(1)}, u32[]{:S(2)}, u32[]{:S(2)}) %collective-permute-start.7) | collective-permute-done | bytes 98336 | tf_op jit(solution)/shard_map/ppermute | solution.py:497
  39.9 0.0 collective-permute-done.6
  40.1 0.1 collective-permute-start.9
  40.2 1.6 %collective-permute-start.10 = (f16[4,48,256]{2,1,0:T(8,128)(2,1)S(1)}, f16[4,48,256]{2,1,0:T(8,128)(2,1)S(1)}, u32[]{:S(2)}, u32[]{:S(2)}) collective-permute-start(f16[4,48,256]{2,1,0:T(8,128)(2,1)S(1)} %pad_maximum_fusion.1), channel_id=1, source_target_pairs={{0,2},{1,3},{2,0},{3,1},{4,6},{5,7},{6,4},{7,5},{8,10},{9,11},{10,... | collective-permute-start | bytes 294920 | tf_op jit(solution)/shard_map/ppermute | solution.py:497
  41.8 1.5 %collective-permute-start.11 = (f16[4,48,256]{2,1,0:T(8,128)(2,1)S(1)}, f16[4,48,256]{2,1,0:T(8,128)(2,1)S(1)}, u32[]{:S(2)}, u32[]{:S(2)}) collective-permute-start(f16[4,48,256]{2,1,0:T(8,128)(2,1)S(1)} %pad_maximum_fusion.2), channel_id=1, source_target_pairs={{0,3},{1,0},{2,1},{3,2},{4,7},{5,4},{6,5},{7,6},{8,11},{9,8},{10,9... | collective-permute-start | bytes 294920 | tf_op jit(solution)/shard_map/ppermute | solution.py:497
  43.3 1.3 %shard_map.119 = bf16[8,32,512]{2,1,0:T(8,128)(2,1)} custom-call(s32[2]{0:T(128)S(1)} %pad_add_fusion.place, bf16[10,32,128]{2,1,0:T(8,128)(2,1)S(1)} %get-tuple-element.36.refs_0_, bf16[10,32,128]{2,1,0:T(8,128)(2,1)S(1)} %collective-permute-done.3.refs_1_, bf16[10,32,128]{2,1,0:T(8,128)(2,1)S(1)} %collective-permute-done.4.refs_2_, ...), custom_call_target="tpu_custom_call" | custom-call | bytes 589832 | tf_op jit(solution)/shard_map/pallas_call | solution.py:207
  44.6 0.8 %collective-permute-done.9 = f16[4,48,256]{2,1,0:T(8,128)(2,1)S(1)} collective-permute-done((f16[4,48,256]{2,1,0:T(8,128)(2,1)S(1)}, f16[4,48,256]{2,1,0:T(8,128)(2,1)S(1)}, u32[]{:S(2)}, u32[]{:S(2)}) %collective-permute-start.9) | collective-permute-done | bytes 98336 | tf_op jit(solution)/shard_map/ppermute | solution.py:497
  45.5 1.1 %collective-permute-done.10 = f16[4,48,256]{2,1,0:T(8,128)(2,1)S(1)} collective-permute-done((f16[4,48,256]{2,1,0:T(8,128)(2,1)S(1)}, f16[4,48,256]{2,1,0:T(8,128)(2,1)S(1)}, u32[]{:S(2)}, u32[]{:S(2)}) %collective-permute-start.10) | collective-permute-done | bytes 98336 | tf_op jit(solution)/shard_map/ppermute | solution.py:497
  46.6 2.4 %collective-permute-done.11 = f16[4,48,256]{2,1,0:T(8,128)(2,1)S(1)} collective-permute-done((f16[4,48,256]{2,1,0:T(8,128)(2,1)S(1)}, f16[4,48,256]{2,1,0:T(8,128)(2,1)S(1)}, u32[]{:S(2)}, u32[]{:S(2)}) %collective-permute-start.11) | collective-permute-done | bytes 98336 | tf_op jit(solution)/shard_map/ppermute | solution.py:497
  49.0 2.8 %shard_map.117 = (f32[4,48,256]{2,1,0:T(8,128)S(1)}, f32[4,48,256]{2,1,0:T(8,128)S(1)}, f32[4,48,256]{2,1,0:T(8,128)S(1)}, f32[4,48,256]{2,1,0:T(8,128)S(1)}) custom-call(s32[2]{0:T(128)S(1)} %pad_add_fusion.place, f32[4,48,256]{2,1,0:T(8,128)S(1)} %maximum_convert_fusion.refs_0_, f32[4,48,256]{2,1,0:T(8,128)S(1)} %convert_element_type.53.refs_1_, ...), custom_call_target="tpu_custom_call" | custom-call | flops 2147483648 | bytes 2293768 | tf_op jit(solution)/shard_map/pallas_call | solution.py:207
  51.8 0.0 all-to-all-done
  51.9 1.6 %collective-permute-start.15 = (f16[4,48,256]{2,1,0:T(8,128)(2,1)S(1)}, f16[4,48,256]{2,1,0:T(8,128)(2,1)S(1)}, u32[]{:S(2)}, u32[]{:S(2)}) collective-permute-start(f16[4,48,256]{2,1,0:T(8,128)(2,1)S(1)} %convert_element_type.63), channel_id=1, source_target_pairs={{0,12},{4,0},{8,4},{12,8},{1,13},{5,1},{9,5},{13,9},{2,14},{6,2},{... | collective-permute-start | bytes 294920 | tf_op jit(solution)/shard_map/ppermute | solution.py:497
  53.6 0.1 collective-permute-start.14
  53.7 1.9 %collective-permute-start.13 = (f16[4,48,256]{2,1,0:T(8,128)(2,1)S(1)}, f16[4,48,256]{2,1,0:T(8,128)(2,1)S(1)}, u32[]{:S(2)}, u32[]{:S(2)}) collective-permute-start(f16[4,48,256]{2,1,0:T(8,128)(2,1)S(1)} %convert_element_type.61), channel_id=1, source_target_pairs={{0,4},{4,8},{8,12},{12,0},{1,5},{5,9},{9,13},{13,1},{2,6},{6,10},{... | collective-permute-start | bytes 294920 | tf_op jit(solution)/shard_map/ppermute | solution.py:497
  55.6 0.1 convert_element_type.57.spectra
  55.7 2.6 %shard_map.120 = f32[16,48,256]{2,1,0:T(8,128)S(1)} custom-call(s32[2]{0:T(128)S(1)} %pad_add_fusion.place, f32[16,48,256]{2,1,0:T(8,128)S(1)} %convert_element_type.57.spectra, bf16[4,256,256]{2,1,0:T(8,128)(2,1)S(1)} %copy-done.8, bf16[6,128,128]{2,1,0:T(8,128)(2,1)S(1)} %copy-done.9), custom_call_target="tpu_custom_call" | custom-call | flops 2147483648 | bytes 2293768 | tf_op jit(solution)/shard_map/pallas_call | solution.py:207
  58.3 0.8 %convert_element_type.58 = f16[16,48,256]{2,1,0:T(8,128)(2,1)} convert(f32[16,48,256]{2,1,0:T(8,128)S(1)} %shard_map.120) | non-fusion elementwise | flops 196608 | bytes 1179648 | tf_op jit(solution)/shard_map/convert_element_type | solution.py:584
  59.1 4.6 %all-to-all-start.1 = ((f16[16,48,256]{2,1,0:T(8,128)(2,1)}), f16[16,48,256]{2,1,0:T(8,128)(2,1)}, u32[]{:S(2)}, u32[]{:S(2)}) async-start(f16[16,48,256]{2,1,0:T(8,128)(2,1)} %convert_element_type.58), calls=%async_computation.1 | async-start | bytes 786432 | tf_op jit(solution)/shard_map/all_to_all | solution.py:501
  63.7 0.0 collective-permute-done.15
  63.8 0.0 collective-permute-done.14
  63.8 0.0 collective-permute-done.13
  63.9 0.4 collective-permute-start.16
  64.4 1.7 %collective-permute-start.17 = (f16[4,48,256]{2,1,0:T(8,128)(2,1)S(1)}, f16[4,48,256]{2,1,0:T(8,128)(2,1)S(1)}, u32[]{:S(2)}, u32[]{:S(2)}) collective-permute-start(f16[4,48,256]{2,1,0:T(8,128)(2,1)S(1)} %pad_maximum_fusion.4), channel_id=1, source_target_pairs={{0,2},{1,3},{2,0},{3,1},{4,6},{5,7},{6,4},{7,5},{8,10},{9,11},{10,... | collective-permute-start | bytes 294920 | tf_op jit(solution)/shard_map/ppermute | solution.py:497
  66.1 1.4 %collective-permute-start.18 = (f16[4,48,256]{2,1,0:T(8,128)(2,1)S(1)}, f16[4,48,256]{2,1,0:T(8,128)(2,1)S(1)}, u32[]{:S(2)}, u32[]{:S(2)}) collective-permute-start(f16[4,48,256]{2,1,0:T(8,128)(2,1)S(1)} %pad_maximum_fusion.5), channel_id=1, source_target_pairs={{0,3},{1,0},{2,1},{3,2},{4,7},{5,4},{6,5},{7,6},{8,11},{9,8},{10,9... | collective-permute-start | bytes 294920 | tf_op jit(solution)/shard_map/ppermute | solution.py:497
  67.5 3.6 %collective-permute-done.16 = f16[4,48,256]{2,1,0:T(8,128)(2,1)S(1)} collective-permute-done((f16[4,48,256]{2,1,0:T(8,128)(2,1)S(1)}, f16[4,48,256]{2,1,0:T(8,128)(2,1)S(1)}, u32[]{:S(2)}, u32[]{:S(2)}) %collective-permute-start.16) | collective-permute-done | bytes 98336 | tf_op jit(solution)/shard_map/ppermute | solution.py:497
  71.1 1.3 %collective-permute-done.17 = f16[4,48,256]{2,1,0:T(8,128)(2,1)S(1)} collective-permute-done((f16[4,48,256]{2,1,0:T(8,128)(2,1)S(1)}, f16[4,48,256]{2,1,0:T(8,128)(2,1)S(1)}, u32[]{:S(2)}, u32[]{:S(2)}) %collective-permute-start.17) | collective-permute-done | bytes 98336 | tf_op jit(solution)/shard_map/ppermute | solution.py:497
  72.4 0.8 collective-permute-done.18
  73.2 0.0 copy-done.2
  73.2 0.0 copy-done.6
  73.2 1.2 %shard_map.121 = (f32[8,32,512]{2,1,0:T(8,128)S(1)}, f32[16,16,256]{2,1,0:T(8,128)S(1)}) custom-call(s32[2]{0:T(128)S(1)} %pad_add_fusion.place, bf16[2,512,512]{2,1,0:T(8,128)(2,1)S(1)} %copy-done.6, f32[3,8,32,512]{3,2,1,0:T(8,128)S(1)} %copy-done.2, f32[4,48,256]{2,1,0:T(8,128)S(1)} %maximum_convert_fusion.1.refs_0_, ...), custom_call_target="tpu_custom_call" | custom-call | flops 1073741824 | bytes 4194312 | tf_op jit(solution)/shard_map/pallas_call | solution.py:207
  74.5 1.5 %all-to-all-done.1 = f16[16,48,256]{2,1,0:T(8,128)(2,1)} async-done(((f16[16,48,256]{2,1,0:T(8,128)(2,1)}), f16[16,48,256]{2,1,0:T(8,128)(2,1)}, u32[]{:S(2)}, u32[]{:S(2)}) %all-to-all-start.1) | async-done | bytes 393248 | tf_op jit(solution)/shard_map/all_to_all | solution.py:501
  76.0 1.1 %convert_element_type.59.spectra = f32[16,48,256]{2,1,0:T(8,128)S(1)} convert(f16[16,48,256]{2,1,0:T(8,128)(2,1)} %all-to-all-done.1) | non-fusion elementwise | flops 196608 | bytes 1179648 | tf_op jit(solution)/shard_map/convert_element_type | solution.py:601
  77.1 1.8 %shard_map.122 = f32[3,8,32,512]{3,2,1,0:T(8,128)} custom-call(f32[16,48,256]{2,1,0:T(8,128)S(1)} %convert_element_type.59.spectra, bf16[2,512,512]{2,1,0:T(8,128)(2,1)S(1)} %copy-done.6, f32[3,8,32,512]{3,2,1,0:T(8,128)S(1)} %copy-done.2, f32[8,32,512]{2,1,0:T(8,128)S(1)} %get-tuple-element.59.updated, f32[16,16,256]{2,1,0:T(8,128)S(1)} %get-tuple-element.60.kept), custom_call_target="tpu_custom_call" | custom-call | flops 2147483648 | bytes 5767168 | tf_op jit(solution)/shard_map/pallas_call | solution.py:207
  (39 shorter events, 0.6 us)
Async XLA Ops:
  0.7 1.0 %copy-start = (bf16[8,32,512]{2,1,0:T(8,128)(2,1)S(1)}, bf16[8,32,512]{2,1,0:T(8,128)(2,1)}, u32[]{:S(2)}) copy-start(bf16[8,32,512]{2,1,0:T(8,128)(2,1)} %moving.1) | copy-start | bytes 786436
  1.7 0.7 copy-start.1
  3.0 8.0 %collective-permute-start = (bf16[272,128]{1,0:T(8,128)(2,1)S(1)}, bf16[272,128]{1,0:T(8,128)(2,1)S(1)}, u32[]{:S(2)}, u32[]{:S(2)}) collective-permute-start(bf16[272,128]{1,0:T(8,128)(2,1)S(1)} %get-tuple-element.33), channel_id=1, source_target_pairs={{0,8},{4,12},{8,0},{12,4},{1,9},{5,13},{9,1},{13,5},{2,10},{6,14},... | collective-permute-start | bytes 208904 | tf_op jit(solution)/shard_map/ppermute | solution.py:497
  7.1 6.3 %collective-permute-start.1 = (bf16[272,128]{1,0:T(8,128)(2,1)S(1)}, bf16[272,128]{1,0:T(8,128)(2,1)S(1)}, u32[]{:S(2)}, u32[]{:S(2)}) collective-permute-start(bf16[272,128]{1,0:T(8,128)(2,1)S(1)} %get-tuple-element.34), channel_id=1, source_target_pairs={{0,4},{4,8},{8,12},{12,0},{1,5},{5,9},{9,13},{13,1},{2,6},{6,10},{... | collective-permute-start | bytes 208904 | tf_op jit(solution)/shard_map/ppermute | solution.py:497
  8.7 5.1 %collective-permute-start.2 = (bf16[272,128]{1,0:T(8,128)(2,1)S(1)}, bf16[272,128]{1,0:T(8,128)(2,1)S(1)}, u32[]{:S(2)}, u32[]{:S(2)}) collective-permute-start(bf16[272,128]{1,0:T(8,128)(2,1)S(1)} %get-tuple-element.35), channel_id=1, source_target_pairs={{0,12},{4,0},{8,4},{12,8},{1,13},{5,1},{9,5},{13,9},{2,14},{6,2},{... | collective-permute-start | bytes 208904 | tf_op jit(solution)/shard_map/ppermute | solution.py:497
  13.7 7.9 %copy-start.3 = (f32[8,32,512]{2,1,0:T(8,128)S(1)}, f32[8,32,512]{2,1,0:T(8,128)}, u32[]{:S(2)}) copy-start(f32[8,32,512]{2,1,0:T(8,128)} %stiffness.1) | copy-start | bytes 1572868
  13.7 7.9 %copy-start.5 = (s32[8,32,4]{1,2,0:T(4,128)S(1)}, s32[8,32,4]{1,2,0:T(4,128)}, u32[]{:S(2)}) copy-start(s32[8,32,4]{1,2,0:T(4,128)} %param.15) | copy-start | bytes 12292
  15.1 8.1 %collective-permute-start.3 = (bf16[10,32,128]{2,1,0:T(8,128)(2,1)S(1)}, bf16[10,32,128]{2,1,0:T(8,128)(2,1)S(1)}, u32[]{:S(2)}, u32[]{:S(2)}) collective-permute-start(bf16[10,32,128]{2,1,0:T(8,128)(2,1)S(1)} %get-tuple-element.37), channel_id=1, source_target_pairs={{0,8},{4,12},{8,0},{12,4},{1,9},{5,13},{9,1},{13,5},{2,10},{6,14},... | collective-permute-start | bytes 245768 | tf_op jit(solution)/shard_map/ppermute | solution.py:497
  17.8 6.4 %collective-permute-start.4 = (bf16[10,32,128]{2,1,0:T(8,128)(2,1)S(1)}, bf16[10,32,128]{2,1,0:T(8,128)(2,1)S(1)}, u32[]{:S(2)}, u32[]{:S(2)}) collective-permute-start(bf16[10,32,128]{2,1,0:T(8,128)(2,1)S(1)} %get-tuple-element.38), channel_id=1, source_target_pairs={{0,4},{4,8},{8,12},{12,0},{1,5},{5,9},{9,13},{13,1},{2,6},{6,10},{... | collective-permute-start | bytes 245768 | tf_op jit(solution)/shard_map/ppermute | solution.py:497
  19.1 5.5 %collective-permute-start.5 = (bf16[10,32,128]{2,1,0:T(8,128)(2,1)S(1)}, bf16[10,32,128]{2,1,0:T(8,128)(2,1)S(1)}, u32[]{:S(2)}, u32[]{:S(2)}) collective-permute-start(bf16[10,32,128]{2,1,0:T(8,128)(2,1)S(1)} %get-tuple-element.39), channel_id=1, source_target_pairs={{0,12},{4,0},{8,4},{12,8},{1,13},{5,1},{9,5},{13,9},{2,14},{6,2},{... | collective-permute-start | bytes 245768 | tf_op jit(solution)/shard_map/ppermute | solution.py:497
  21.6 3.0 %copy-start.4 = (bf16[8,32,512]{2,1,0:T(8,128)(2,1)S(1)}, bf16[8,32,512]{2,1,0:T(8,128)(2,1)}, u32[]{:S(2)}) copy-start(bf16[8,32,512]{2,1,0:T(8,128)(2,1)} %refs_4_.2) | copy-start | bytes 786436
  21.6 3.0 %copy-start.7 = (bf16[2,512,512]{2,1,0:T(8,128)(2,1)S(1)}, bf16[2,512,512]{2,1,0:T(8,128)(2,1)}, u32[]{:S(2)}) copy-start(bf16[2,512,512]{2,1,0:T(8,128)(2,1)} %constant.15.clone.refs_6_.basis) | copy-start | bytes 3145732
  26.7 4.1 %collective-permute-start.12 = (f32[24,512]{1,0:T(8,128)S(1)}, f32[24,512]{1,0:T(8,128)S(1)}, u32[]{:S(2)}, u32[]{:S(2)}) collective-permute-start(f32[24,512]{1,0:T(8,128)S(1)} %get-tuple-element.49), channel_id=1, source_target_pairs={{1,0},{2,1},{3,2},{0,3},{5,4},{6,5},{7,6},{4,7},{9,8},{10,9},{11,1... | collective-permute-start | bytes 147464 | tf_op jit(solution)/shard_map/ppermute | solution.py:544
  26.9 11.0 %collective-permute-start.8 = (f16[4,48,256]{2,1,0:T(8,128)(2,1)S(1)}, f16[4,48,256]{2,1,0:T(8,128)(2,1)S(1)}, u32[]{:S(2)}, u32[]{:S(2)}) collective-permute-start(f16[4,48,256]{2,1,0:T(8,128)(2,1)S(1)} %get-tuple-element.62), channel_id=1, source_target_pairs={{0,12},{4,0},{8,4},{12,8},{1,13},{5,1},{9,5},{13,9},{2,14},{6,2},{... | collective-permute-start | bytes 294920 | tf_op jit(solution)/shard_map/ppermute | solution.py:497
  30.2 9.8 %collective-permute-start.7 = (f16[4,48,256]{2,1,0:T(8,128)(2,1)S(1)}, f16[4,48,256]{2,1,0:T(8,128)(2,1)S(1)}, u32[]{:S(2)}, u32[]{:S(2)}) collective-permute-start(f16[4,48,256]{2,1,0:T(8,128)(2,1)S(1)} %get-tuple-element.63), channel_id=1, source_target_pairs={{0,8},{4,12},{8,0},{12,4},{1,9},{5,13},{9,1},{13,5},{2,10},{6,14},... | collective-permute-start | bytes 294920 | tf_op jit(solution)/shard_map/ppermute | solution.py:497
  30.2 9.8 %collective-permute-start.6 = (f16[4,48,256]{2,1,0:T(8,128)(2,1)S(1)}, f16[4,48,256]{2,1,0:T(8,128)(2,1)S(1)}, u32[]{:S(2)}, u32[]{:S(2)}) collective-permute-start(f16[4,48,256]{2,1,0:T(8,128)(2,1)S(1)} %get-tuple-element.64), channel_id=1, source_target_pairs={{0,4},{4,8},{8,12},{12,0},{1,5},{5,9},{9,13},{13,1},{2,6},{6,10},{... | collective-permute-start | bytes 294920 | tf_op jit(solution)/shard_map/ppermute | solution.py:497
  32.3 19.5 %all-to-all-start = ((f16[16,48,256]{2,1,0:T(8,128)(2,1)}), f16[16,48,256]{2,1,0:T(8,128)(2,1)S(1)}, u32[]{:S(2)}, u32[]{:S(2)}) async-start(f16[16,48,256]{2,1,0:T(8,128)(2,1)} %convert_element_type.56), calls=%async_computation | async-start | bytes 786432 | tf_op jit(solution)/shard_map/all_to_all | solution.py:501
  39.9 9.0 %copy-start.8 = (bf16[4,256,256]{2,1,0:T(8,128)(2,1)S(1)}, bf16[4,256,256]{2,1,0:T(8,128)(2,1)}, u32[]{:S(2)}) copy-start(bf16[4,256,256]{2,1,0:T(8,128)(2,1)} %constant.16.clone.refs_4_.basis_z) | copy-start | bytes 1572868
  39.9 9.0 %copy-start.9 = (bf16[6,128,128]{2,1,0:T(8,128)(2,1)S(1)}, bf16[6,128,128]{2,1,0:T(8,128)(2,1)}, u32[]{:S(2)}) copy-start(bf16[6,128,128]{2,1,0:T(8,128)(2,1)} %constant.17.clone.refs_5_.basis_y) | copy-start | bytes 589828
  40.1 5.4 %collective-permute-start.9 = (f16[4,48,256]{2,1,0:T(8,128)(2,1)S(1)}, f16[4,48,256]{2,1,0:T(8,128)(2,1)S(1)}, u32[]{:S(2)}, u32[]{:S(2)}) collective-permute-start(f16[4,48,256]{2,1,0:T(8,128)(2,1)S(1)} %pad_maximum_fusion), channel_id=1, source_target_pairs={{0,1},{1,2},{2,3},{3,0},{4,5},{5,6},{6,7},{7,4},{8,9},{9,10},{10,1... | collective-permute-start | bytes 294920 | tf_op jit(solution)/shard_map/ppermute | solution.py:497
  40.2 6.3 %collective-permute-start.10 = (f16[4,48,256]{2,1,0:T(8,128)(2,1)S(1)}, f16[4,48,256]{2,1,0:T(8,128)(2,1)S(1)}, u32[]{:S(2)}, u32[]{:S(2)}) collective-permute-start(f16[4,48,256]{2,1,0:T(8,128)(2,1)S(1)} %pad_maximum_fusion.1), channel_id=1, source_target_pairs={{0,2},{1,3},{2,0},{3,1},{4,6},{5,7},{6,4},{7,5},{8,10},{9,11},{10,... | collective-permute-start | bytes 294920 | tf_op jit(solution)/shard_map/ppermute | solution.py:497
  41.8 7.1 %collective-permute-start.11 = (f16[4,48,256]{2,1,0:T(8,128)(2,1)S(1)}, f16[4,48,256]{2,1,0:T(8,128)(2,1)S(1)}, u32[]{:S(2)}, u32[]{:S(2)}) collective-permute-start(f16[4,48,256]{2,1,0:T(8,128)(2,1)S(1)} %pad_maximum_fusion.2), channel_id=1, source_target_pairs={{0,3},{1,0},{2,1},{3,2},{4,7},{5,4},{6,5},{7,6},{8,11},{9,8},{10,9... | collective-permute-start | bytes 294920 | tf_op jit(solution)/shard_map/ppermute | solution.py:497
  51.9 11.8 %collective-permute-start.15 = (f16[4,48,256]{2,1,0:T(8,128)(2,1)S(1)}, f16[4,48,256]{2,1,0:T(8,128)(2,1)S(1)}, u32[]{:S(2)}, u32[]{:S(2)}) collective-permute-start(f16[4,48,256]{2,1,0:T(8,128)(2,1)S(1)} %convert_element_type.63), channel_id=1, source_target_pairs={{0,12},{4,0},{8,4},{12,8},{1,13},{5,1},{9,5},{13,9},{2,14},{6,2},{... | collective-permute-start | bytes 294920 | tf_op jit(solution)/shard_map/ppermute | solution.py:497
  53.6 10.2 %collective-permute-start.14 = (f16[4,48,256]{2,1,0:T(8,128)(2,1)S(1)}, f16[4,48,256]{2,1,0:T(8,128)(2,1)S(1)}, u32[]{:S(2)}, u32[]{:S(2)}) collective-permute-start(f16[4,48,256]{2,1,0:T(8,128)(2,1)S(1)} %convert_element_type.62), channel_id=1, source_target_pairs={{0,8},{4,12},{8,0},{12,4},{1,9},{5,13},{9,1},{13,5},{2,10},{6,14},... | collective-permute-start | bytes 294920 | tf_op jit(solution)/shard_map/ppermute | solution.py:497
  53.7 10.2 %collective-permute-start.13 = (f16[4,48,256]{2,1,0:T(8,128)(2,1)S(1)}, f16[4,48,256]{2,1,0:T(8,128)(2,1)S(1)}, u32[]{:S(2)}, u32[]{:S(2)}) collective-permute-start(f16[4,48,256]{2,1,0:T(8,128)(2,1)S(1)} %convert_element_type.61), channel_id=1, source_target_pairs={{0,4},{4,8},{8,12},{12,0},{1,5},{5,9},{9,13},{13,1},{2,6},{6,10},{... | collective-permute-start | bytes 294920 | tf_op jit(solution)/shard_map/ppermute | solution.py:497
  59.1 14.1 %copy-start.2 = (f32[3,8,32,512]{3,2,1,0:T(8,128)S(1)}, f32[3,8,32,512]{3,2,1,0:T(8,128)}, u32[]{:S(2)}) copy-start(f32[3,8,32,512]{3,2,1,0:T(8,128)} %velocity.3) | copy-start | bytes 4718596
  59.1 14.1 %copy-start.6 = (bf16[2,512,512]{2,1,0:T(8,128)(2,1)S(1)}, bf16[2,512,512]{2,1,0:T(8,128)(2,1)}, u32[]{:S(2)}) copy-start(bf16[2,512,512]{2,1,0:T(8,128)(2,1)} %constant.18.clone.basis) | copy-start | bytes 3145732
  59.1 16.9 %all-to-all-start.1 = ((f16[16,48,256]{2,1,0:T(8,128)(2,1)}), f16[16,48,256]{2,1,0:T(8,128)(2,1)}, u32[]{:S(2)}, u32[]{:S(2)}) async-start(f16[16,48,256]{2,1,0:T(8,128)(2,1)} %convert_element_type.58), calls=%async_computation.1 | async-start | bytes 786432 | tf_op jit(solution)/shard_map/all_to_all | solution.py:501
  63.9 7.2 %collective-permute-start.16 = (f16[4,48,256]{2,1,0:T(8,128)(2,1)S(1)}, f16[4,48,256]{2,1,0:T(8,128)(2,1)S(1)}, u32[]{:S(2)}, u32[]{:S(2)}) collective-permute-start(f16[4,48,256]{2,1,0:T(8,128)(2,1)S(1)} %pad_maximum_fusion.3), channel_id=1, source_target_pairs={{0,1},{1,2},{2,3},{3,0},{4,5},{5,6},{6,7},{7,4},{8,9},{9,10},{10,1... | collective-permute-start | bytes 294920 | tf_op jit(solution)/shard_map/ppermute | solution.py:497
  64.4 8.1 %collective-permute-start.17 = (f16[4,48,256]{2,1,0:T(8,128)(2,1)S(1)}, f16[4,48,256]{2,1,0:T(8,128)(2,1)S(1)}, u32[]{:S(2)}, u32[]{:S(2)}) collective-permute-start(f16[4,48,256]{2,1,0:T(8,128)(2,1)S(1)} %pad_maximum_fusion.4), channel_id=1, source_target_pairs={{0,2},{1,3},{2,0},{3,1},{4,6},{5,7},{6,4},{7,5},{8,10},{9,11},{10,... | collective-permute-start | bytes 294920 | tf_op jit(solution)/shard_map/ppermute | solution.py:497
  66.1 7.1 %collective-permute-start.18 = (f16[4,48,256]{2,1,0:T(8,128)(2,1)S(1)}, f16[4,48,256]{2,1,0:T(8,128)(2,1)S(1)}, u32[]{:S(2)}, u32[]{:S(2)}) collective-permute-start(f16[4,48,256]{2,1,0:T(8,128)(2,1)S(1)} %pad_maximum_fusion.5), channel_id=1, source_target_pairs={{0,3},{1,0},{2,1},{3,2},{4,7},{5,4},{6,5},{7,6},{8,11},{9,8},{10,9... | collective-permute-start | bytes 294920 | tf_op jit(solution)/shard_map/ppermute | solution.py:497

commit v12 on v11

--- a/solution.py
+++ b/solution.py
@@ -285,7 +285,7 @@
 
 def force_zx_kernel(slabs, subs, place, *refs):
     received, refs = refs[:slabs], refs[slabs:]
-    template, coefficient, basis, first, image, weight, spectra, kept, planes_of, wide = refs
+    template, coefficient, basis, upper, first, image, weight, spectra, planes_of, wide, wide_x = refs
     planes, rows, x_length = template.shape
     for step in range(slabs):
         block = pl.ds(pl.multiple_of(around(place[0] - HOPS[step], slabs) * BLOCK, BLOCK), BLOCK)
@@ -301,24 +301,21 @@
         first[2 * planes + z : 2 * planes + z + 1] = own[0:1]
         forces[0].append(own * (planes_of[z + 2] - planes_of[z]))
         forces[1].append(own * (pltpu.roll(here, x_length - 1, 1) - pltpu.roll(here, 1, 1)))
-    for a in range(2):
-        force = split(jnp.concatenate(forces[a], axis=0))
-        wide[a] = times((basis[0], basis[1]), force, ((1,), (1,)))
+    wide[...] = times((basis[0], basis[1]), split(jnp.concatenate(forces[0], axis=0)), ((1,), (1,)))
+    wide_x[...] = times((upper[0], upper[1]), split(jnp.concatenate(forces[1], axis=0)), ((1,), (1,)))
     part = x_length // (slabs * subs)
-    cut = kept.shape[1]
+    rest = spectra.shape[2] - part
     for d in range(slabs):
         for e in range(subs):
-            start = (around(place[0] + d, slabs) * subs + around(place[1] + e, subs)) * part
-            spectra[d, e, :part] = wide[0, pl.ds(pl.multiple_of(start, part), part), :]
-            spectra[d, e, part:] = wide[1, pl.ds(pl.multiple_of(start + cut, 8), part - cut), :]
-    for k in range(slabs * subs):
-        kept[k] = wide[1, k * part : k * part + cut, :]
-
-
-def force_y_kernel(beyond, image, weight, basis, kept, spectra):
+            index = around(place[0] + d, slabs) * subs + around(place[1] + e, subs)
+            spectra[d, e, :part] = wide[pl.ds(pl.multiple_of(index * part, part), part), :]
+            spectra[d, e, part:] = wide_x[pl.ds(pl.multiple_of(index * rest, rest), rest), :]
+
+
+def force_y_kernel(beyond, image, weight, basis, lower, spectra):
     planes, rows, x_length = image.shape
     row = lax.broadcasted_iota(jnp.int32, (rows, x_length), 0)
-    force = []
+    force, along_x = [], []
     for z in range(planes):
         here = image[z]
         after = jnp.where(row == rows - 2, beyond[z : z + 1, :], pltpu.roll(here, rows - 2, 0))
@@ -326,11 +323,13 @@
         own = pltpu.roll(weight[z], rows - 1, 0)
         own = jnp.where(row == rows - 1, beyond[2 * planes + z : 2 * planes + z + 1, :], own)
         force.append(own * (after - here))
+        along_x.append(weight[z] * (pltpu.roll(here, x_length - 1, 1) - pltpu.roll(here, 1, 1)))
     devices = spectra.shape[0]
     part = x_length // devices
     spectrum = times((basis[0], basis[1]), split(jnp.concatenate(force, axis=0)), ((1,), (1,)))
     spectra[:, :part, :] = spectrum.reshape(devices, part, planes * rows)
-    spectra[:, part:, :] = kept[...]
+    spectrum = times((lower[0], lower[1]), split(jnp.concatenate(along_x, axis=0)), ((1,), (1,)))
+    spectra[:, part:, :] = spectrum.reshape(devices, -1, planes * rows)
 
 
 def swap_blocks(values):
@@ -524,21 +523,23 @@
     basis_y = np.concatenate([in_two(b) for b in (basis_y.T, basis_y, np.roll(basis_y.T, -1, 0))])
     cut = part // 2
     with_z, with_y = 2 * part - cut, part + cut
-    first, image, weight, chain, kept = call(
+    by_part = basis_x.reshape(2, devices, part, x_length)
+    lower, upper = (h.reshape(2, -1, x_length) for h in (by_part[:, :, :cut], by_part[:, :, cut:]))
+    first, image, weight, chain = call(
         functools.partial(force_zx_kernel, slabs, subs),
         [
             shape((3 * planes, x_length)),
             shape(moving.shape),
             shape(moving.shape),
             shape((slabs, subs, with_z, area)),
-            shape((devices, cut, area)),
         ],
         place,
         *received,
         template,
         coefficient,
         basis_x,
-        scratch=[pltpu.VMEM((planes + 2, rows, x_length), f32), pltpu.VMEM((2, x_length, area), f32)],
+        upper,
+        scratch=[pltpu.VMEM((planes + 2, rows, x_length), f32), pltpu.VMEM((x_length, area), f32), pltpu.VMEM((devices * (part - cut), area), f32)],
         flops=3 << 30,
     )
     beyond = lax.ppermute(first, "sub", [((i + 1) % subs, i) for i in range(subs)])
@@ -554,7 +555,7 @@
         image,
         weight,
         basis_x,
-        kept,
+        lower,
         flops=2 << 30,
     )
     spectra = exchange(spectra.astype(f16))

time: 79.4 us -> 79.3 us (level)
    unnamed x20 -> x24, local copies, waits for them, and re-layouts: 1.7 us -> 1.71 us
  transfers between devices with their start and end apart: 21 -> 21, of which waited for: 14 -> 15; matrix products, arithmetic and copies ran while one was open for 3% -> 3% of each run, Pallas kernels for 11% -> 12%
where the time goes in v12:
time: 79.3 us; the launch traced here: 78.9 us
  starting transfers between devices  39.2 us (49%)
  waiting for transfers between devices  18.6 us (23%)
  Pallas kernels  14.8 us (19%)
  other arithmetic  3.32 us (4%)
  local copies, waits for them, and re-layouts  1.95 us (2%)
  between operations  0.98 us (1%)
    ppermute x18, starting transfers between devices, scatter(): lax.ppermute(sends[d], axis, [(i, (i + hops[d]) % count) for i in range(c...  28.8 us
    ppermute x18, waiting for transfers between devices, scatter(): lax.ppermute(sends[d], axis, [(i, (i + hops[d]) % count) for i in range(c...  17.1 us
    pallas_call x10, Pallas kernels, call(): pl.pallas_call(kernel, out_shape=out_shape, in_specs=places, out_specs=ja...  14.8 us
    all_to_all x2, starting transfers between devices, exchange(): lax.all_to_all(values, ('slab', 'sub'), split_axis=0, concat_axis=0, tile...  10.3 us
    unnamed x24, local copies, waits for them, and re-layouts  1.71 us
    convert_element_type x2, other arithmetic, local_blocks(): spectra = exchange(spectra.astype(f16))  1.62 us
  transfers between devices with their start and end apart: 21, of which 15 were waited for; matrix products, arithmetic and copies ran while one was open for 3% of the time, Pallas kernels for 12%

profile of v12, /device:TPU:0, one launch (start us, length us, event | category | flops | bytes accessed | tf_op | source)
XLA Modules:
  0.0 78.9 jit_solution(10737038903368016122)
XLA Ops:
  0.6 0.1 pad_add_fusion.place
  0.7 0.9 %copy-done = bf16[8,32,512]{2,1,0:T(8,128)(2,1)S(1)} copy-done((bf16[8,32,512]{2,1,0:T(8,128)(2,1)S(1)}, bf16[8,32,512]{2,1,0:T(8,128)(2,1)}, u32[]{:S(2)}) %copy-start) | copy-done | bytes 262168
  1.7 0.7 copy-done.1
  2.4 0.6 shard_map.131
  3.0 4.1 %collective-permute-start = (bf16[272,128]{1,0:T(8,128)(2,1)S(1)}, bf16[272,128]{1,0:T(8,128)(2,1)S(1)}, u32[]{:S(2)}, u32[]{:S(2)}) collective-permute-start(bf16[272,128]{1,0:T(8,128)(2,1)S(1)} %get-tuple-element.32), channel_id=1, source_target_pairs={{0,8},{4,12},{8,0},{12,4},{1,9},{5,13},{9,1},{13,5},{2,10},{6,14},... | collective-permute-start | bytes 208904 | tf_op jit(solution)/shard_map/ppermute | solution.py:496
  7.1 1.6 %collective-permute-start.1 = (bf16[272,128]{1,0:T(8,128)(2,1)S(1)}, bf16[272,128]{1,0:T(8,128)(2,1)S(1)}, u32[]{:S(2)}, u32[]{:S(2)}) collective-permute-start(bf16[272,128]{1,0:T(8,128)(2,1)S(1)} %get-tuple-element.33), channel_id=1, source_target_pairs={{0,4},{4,8},{8,12},{12,0},{1,5},{5,9},{9,13},{13,1},{2,6},{6,10},{... | collective-permute-start | bytes 208904 | tf_op jit(solution)/shard_map/ppermute | solution.py:496
  8.7 2.2 %collective-permute-start.2 = (bf16[272,128]{1,0:T(8,128)(2,1)S(1)}, bf16[272,128]{1,0:T(8,128)(2,1)S(1)}, u32[]{:S(2)}, u32[]{:S(2)}) collective-permute-start(bf16[272,128]{1,0:T(8,128)(2,1)S(1)} %get-tuple-element.34), channel_id=1, source_target_pairs={{0,12},{4,0},{8,4},{12,8},{1,13},{5,1},{9,5},{13,9},{2,14},{6,2},{... | collective-permute-start | bytes 208904 | tf_op jit(solution)/shard_map/ppermute | solution.py:496
  10.9 0.1 collective-permute-done.refs_1_
  11.0 2.5 %collective-permute-done.1.refs_2_ = bf16[272,128]{1,0:T(8,128)(2,1)S(1)} collective-permute-done((bf16[272,128]{1,0:T(8,128)(2,1)S(1)}, bf16[272,128]{1,0:T(8,128)(2,1)S(1)}, u32[]{:S(2)}, u32[]{:S(2)}) %collective-permute-start.1) | collective-permute-done | bytes 69664 | tf_op jit(solution)/shard_map/ppermute | solution.py:496
  13.4 0.3 collective-permute-done.2.refs_3_
  13.7 1.3 %shard_map.132 = (bf16[10,32,128]{2,1,0:T(8,128)(2,1)S(1)}, bf16[10,32,128]{2,1,0:T(8,128)(2,1)S(1)}, bf16[10,32,128]{2,1,0:T(8,128)(2,1)S(1)}, bf16[10,32,128]{2,1,0:T(8,128)(2,1)S(1)}) custom-call(s32[2]{0:T(128)S(1)} %pad_add_fusion.place, bf16[272,128]{1,0:T(8,128)(2,1)S(1)} %get-tuple-element.31.refs_0_, ...), custom_call_target="tpu_custom_call" | custom-call | flops 1073741824 | bytes 606216 | tf_op jit(solution)/shard_map/pallas_call | solution.py:207
  15.1 2.7 %collective-permute-start.3 = (bf16[10,32,128]{2,1,0:T(8,128)(2,1)S(1)}, bf16[10,32,128]{2,1,0:T(8,128)(2,1)S(1)}, u32[]{:S(2)}, u32[]{:S(2)}) collective-permute-start(bf16[10,32,128]{2,1,0:T(8,128)(2,1)S(1)} %get-tuple-element.36), channel_id=1, source_target_pairs={{0,8},{4,12},{8,0},{12,4},{1,9},{5,13},{9,1},{13,5},{2,10},{6,14},... | collective-permute-start | bytes 245768 | tf_op jit(solution)/shard_map/ppermute | solution.py:496
  17.8 1.3 %collective-permute-start.4 = (bf16[10,32,128]{2,1,0:T(8,128)(2,1)S(1)}, bf16[10,32,128]{2,1,0:T(8,128)(2,1)S(1)}, u32[]{:S(2)}, u32[]{:S(2)}) collective-permute-start(bf16[10,32,128]{2,1,0:T(8,128)(2,1)S(1)} %get-tuple-element.37), channel_id=1, source_target_pairs={{0,4},{4,8},{8,12},{12,0},{1,5},{5,9},{9,13},{13,1},{2,6},{6,10},{... | collective-permute-start | bytes 245768 | tf_op jit(solution)/shard_map/ppermute | solution.py:496
  19.1 2.5 %collective-permute-start.5 = (bf16[10,32,128]{2,1,0:T(8,128)(2,1)S(1)}, bf16[10,32,128]{2,1,0:T(8,128)(2,1)S(1)}, u32[]{:S(2)}, u32[]{:S(2)}) collective-permute-start(bf16[10,32,128]{2,1,0:T(8,128)(2,1)S(1)} %get-tuple-element.38), channel_id=1, source_target_pairs={{0,12},{4,0},{8,4},{12,8},{1,13},{5,1},{9,5},{13,9},{2,14},{6,2},{... | collective-permute-start | bytes 245768 | tf_op jit(solution)/shard_map/ppermute | solution.py:496
  21.6 0.0 copy-done.5
  21.6 0.0 copy-start.10
  21.7 0.3 shard_map.133.refs_5_
  22.0 1.2 %collective-permute-done.3.refs_1_ = bf16[10,32,128]{2,1,0:T(8,128)(2,1)S(1)} collective-permute-done((bf16[10,32,128]{2,1,0:T(8,128)(2,1)S(1)}, bf16[10,32,128]{2,1,0:T(8,128)(2,1)S(1)}, u32[]{:S(2)}, u32[]{:S(2)}) %collective-permute-start.3) | collective-permute-done | bytes 81952 | tf_op jit(solution)/shard_map/ppermute | solution.py:496
  23.2 1.0 %collective-permute-done.4.refs_2_ = bf16[10,32,128]{2,1,0:T(8,128)(2,1)S(1)} collective-permute-done((bf16[10,32,128]{2,1,0:T(8,128)(2,1)S(1)}, bf16[10,32,128]{2,1,0:T(8,128)(2,1)S(1)}, u32[]{:S(2)}, u32[]{:S(2)}) %collective-permute-start.4) | collective-permute-done | bytes 81952 | tf_op jit(solution)/shard_map/ppermute | solution.py:496
  24.2 0.4 collective-permute-done.5.refs_3_
  24.7 1.7 %shard_map.134 = (f32[24,512]{1,0:T(8,128)S(1)}, f32[8,32,512]{2,1,0:T(8,128)S(1)}, f32[8,32,512]{2,1,0:T(8,128)S(1)}, f32[4,4,48,256]{3,2,1,0:T(8,128)S(1)}) custom-call(s32[2]{0:T(128)S(1)} %pad_add_fusion.place, bf16[10,32,128]{2,1,0:T(8,128)(2,1)S(1)} %get-tuple-element.35.refs_0_, bf16[10,32,128]{2,1,0:T(8,128)(2,1)S(1)} %collective-permute-done.3.refs_1_, ...), custom_call_target="tpu_custom_call" | custom-call | flops 3221225472 | bytes 4571144 | tf_op jit(solution)/shard_map/pallas_call | solution.py:207
  26.4 0.0 copy-start.9
  26.4 0.1 convert_element_type.51
  26.4 0.1 collective-permute-start.12
  26.5 0.1 slice_bitcast_fusion
  26.6 3.3 %collective-permute-start.8 = (f16[4,48,256]{2,1,0:T(8,128)(2,1)S(1)}, f16[4,48,256]{2,1,0:T(8,128)(2,1)S(1)}, u32[]{:S(2)}, u32[]{:S(2)}) collective-permute-start(f16[4,48,256]{2,1,0:T(8,128)(2,1)S(1)} %get-tuple-element.60), channel_id=1, source_target_pairs={{0,12},{4,0},{8,4},{12,8},{1,13},{5,1},{9,5},{13,9},{2,14},{6,2},{... | collective-permute-start | bytes 294920 | tf_op jit(solution)/shard_map/ppermute | solution.py:496
  29.9 0.0 collective-permute-start.7
  29.9 0.6 collective-permute-start.6
  30.5 0.0 collective-permute-done.12.beyond
  30.5 1.0 %shard_map.136 = f32[16,48,256]{2,1,0:T(8,128)S(1)} custom-call(f32[24,512]{1,0:T(8,128)S(1)} %collective-permute-done.12.beyond, f32[8,32,512]{2,1,0:T(8,128)S(1)} %get-tuple-element.49.image, f32[8,32,512]{2,1,0:T(8,128)S(1)} %get-tuple-element.50.weight, bf16[2,512,512]{2,1,0:T(8,128)(2,1)S(1)} %copy-done.7, bf16[2,256,512]{2,1,0:T(8,128)(2,1)S(1)} %copy-done.9), custom_call_target="tpu_custom_call" | custom-call | flops 2147483648 | bytes 3457024 | tf_op jit(solution)/shard_map/pallas_call | solution.py:207
  31.5 0.8 %convert_element_type.56 = f16[16,48,256]{2,1,0:T(8,128)(2,1)} convert(f32[16,48,256]{2,1,0:T(8,128)S(1)} %shard_map.136) | non-fusion elementwise | flops 196608 | bytes 1179648 | tf_op jit(solution)/shard_map/convert_element_type | solution.py:561
  32.3 5.5 %all-to-all-start = ((f16[16,48,256]{2,1,0:T(8,128)(2,1)}), f16[16,48,256]{2,1,0:T(8,128)(2,1)S(1)}, u32[]{:S(2)}, u32[]{:S(2)}) async-start(f16[16,48,256]{2,1,0:T(8,128)(2,1)} %convert_element_type.56), calls=%async_computation | async-start | bytes 786432 | tf_op jit(solution)/shard_map/all_to_all | solution.py:500
  37.8 0.0 collective-permute-done.8
  37.8 1.8 %collective-permute-done.7 = f16[4,48,256]{2,1,0:T(8,128)(2,1)S(1)} collective-permute-done((f16[4,48,256]{2,1,0:T(8,128)(2,1)S(1)}, f16[4,48,256]{2,1,0:T(8,128)(2,1)S(1)}, u32[]{:S(2)}, u32[]{:S(2)}) %collective-permute-start.7) | collective-permute-done | bytes 98336 | tf_op jit(solution)/shard_map/ppermute | solution.py:496
  39.6 0.0 collective-permute-done.6
  39.8 0.1 collective-permute-start.9
  39.9 1.6 %collective-permute-start.10 = (f16[4,48,256]{2,1,0:T(8,128)(2,1)S(1)}, f16[4,48,256]{2,1,0:T(8,128)(2,1)S(1)}, u32[]{:S(2)}, u32[]{:S(2)}) collective-permute-start(f16[4,48,256]{2,1,0:T(8,128)(2,1)S(1)} %pad_maximum_fusion.1), channel_id=1, source_target_pairs={{0,2},{1,3},{2,0},{3,1},{4,6},{5,7},{6,4},{7,5},{8,10},{9,11},{10,... | collective-permute-start | bytes 294920 | tf_op jit(solution)/shard_map/ppermute | solution.py:496
  41.5 1.5 %collective-permute-start.11 = (f16[4,48,256]{2,1,0:T(8,128)(2,1)S(1)}, f16[4,48,256]{2,1,0:T(8,128)(2,1)S(1)}, u32[]{:S(2)}, u32[]{:S(2)}) collective-permute-start(f16[4,48,256]{2,1,0:T(8,128)(2,1)S(1)} %pad_maximum_fusion.2), channel_id=1, source_target_pairs={{0,3},{1,0},{2,1},{3,2},{4,7},{5,4},{6,5},{7,6},{8,11},{9,8},{10,9... | collective-permute-start | bytes 294920 | tf_op jit(solution)/shard_map/ppermute | solution.py:496
  43.0 1.3 %shard_map.137 = bf16[8,32,512]{2,1,0:T(8,128)(2,1)} custom-call(s32[2]{0:T(128)S(1)} %pad_add_fusion.place, bf16[10,32,128]{2,1,0:T(8,128)(2,1)S(1)} %get-tuple-element.35.refs_0_, bf16[10,32,128]{2,1,0:T(8,128)(2,1)S(1)} %collective-permute-done.3.refs_1_, bf16[10,32,128]{2,1,0:T(8,128)(2,1)S(1)} %collective-permute-done.4.refs_2_, ...), custom_call_target="tpu_custom_call" | custom-call | bytes 589832 | tf_op jit(solution)/shard_map/pallas_call | solution.py:207
  44.3 1.2 %collective-permute-done.9 = f16[4,48,256]{2,1,0:T(8,128)(2,1)S(1)} collective-permute-done((f16[4,48,256]{2,1,0:T(8,128)(2,1)S(1)}, f16[4,48,256]{2,1,0:T(8,128)(2,1)S(1)}, u32[]{:S(2)}, u32[]{:S(2)}) %collective-permute-start.9) | collective-permute-done | bytes 98336 | tf_op jit(solution)/shard_map/ppermute | solution.py:496
  45.5 0.8 %collective-permute-done.10 = f16[4,48,256]{2,1,0:T(8,128)(2,1)S(1)} collective-permute-done((f16[4,48,256]{2,1,0:T(8,128)(2,1)S(1)}, f16[4,48,256]{2,1,0:T(8,128)(2,1)S(1)}, u32[]{:S(2)}, u32[]{:S(2)}) %collective-permute-start.10) | collective-permute-done | bytes 98336 | tf_op jit(solution)/shard_map/ppermute | solution.py:496
  46.3 2.1 %collective-permute-done.11 = f16[4,48,256]{2,1,0:T(8,128)(2,1)S(1)} collective-permute-done((f16[4,48,256]{2,1,0:T(8,128)(2,1)S(1)}, f16[4,48,256]{2,1,0:T(8,128)(2,1)S(1)}, u32[]{:S(2)}, u32[]{:S(2)}) %collective-permute-start.11) | collective-permute-done | bytes 98336 | tf_op jit(solution)/shard_map/ppermute | solution.py:496
  48.5 2.8 %shard_map.135 = (f32[4,48,256]{2,1,0:T(8,128)S(1)}, f32[4,48,256]{2,1,0:T(8,128)S(1)}, f32[4,48,256]{2,1,0:T(8,128)S(1)}, f32[4,48,256]{2,1,0:T(8,128)S(1)}) custom-call(s32[2]{0:T(128)S(1)} %pad_add_fusion.place, f32[4,48,256]{2,1,0:T(8,128)S(1)} %maximum_convert_fusion.refs_0_, f32[4,48,256]{2,1,0:T(8,128)S(1)} %convert_element_type.53.refs_1_, ...), custom_call_target="tpu_custom_call" | custom-call | flops 2147483648 | bytes 2293768 | tf_op jit(solution)/shard_map/pallas_call | solution.py:207
  51.3 0.0 all-to-all-done
  51.4 2.1 %collective-permute-start.15 = (f16[4,48,256]{2,1,0:T(8,128)(2,1)S(1)}, f16[4,48,256]{2,1,0:T(8,128)(2,1)S(1)}, u32[]{:S(2)}, u32[]{:S(2)}) collective-permute-start(f16[4,48,256]{2,1,0:T(8,128)(2,1)S(1)} %convert_element_type.63), channel_id=1, source_target_pairs={{0,12},{4,0},{8,4},{12,8},{1,13},{5,1},{9,5},{13,9},{2,14},{6,2},{... | collective-permute-start | bytes 294920 | tf_op jit(solution)/shard_map/ppermute | solution.py:496
  53.5 0.0 collective-permute-start.14
  53.5 1.8 %collective-permute-start.13 = (f16[4,48,256]{2,1,0:T(8,128)(2,1)S(1)}, f16[4,48,256]{2,1,0:T(8,128)(2,1)S(1)}, u32[]{:S(2)}, u32[]{:S(2)}) collective-permute-start(f16[4,48,256]{2,1,0:T(8,128)(2,1)S(1)} %convert_element_type.61), channel_id=1, source_target_pairs={{0,4},{4,8},{8,12},{12,0},{1,5},{5,9},{9,13},{13,1},{2,6},{6,10},{... | collective-permute-start | bytes 294920 | tf_op jit(solution)/shard_map/ppermute | solution.py:496
  55.3 0.1 convert_element_type.57.spectra
  55.4 2.6 %shard_map.138 = f32[16,48,256]{2,1,0:T(8,128)S(1)} custom-call(s32[2]{0:T(128)S(1)} %pad_add_fusion.place, f32[16,48,256]{2,1,0:T(8,128)S(1)} %convert_element_type.57.spectra, bf16[4,256,256]{2,1,0:T(8,128)(2,1)S(1)} %copy-done.8, bf16[6,128,128]{2,1,0:T(8,128)(2,1)S(1)} %copy-done.11), custom_call_target="tpu_custom_call" | custom-call | flops 2147483648 | bytes 2293768 | tf_op jit(solution)/shard_map/pallas_call | solution.py:207
  58.0 0.8 %convert_element_type.58 = f16[16,48,256]{2,1,0:T(8,128)(2,1)} convert(f32[16,48,256]{2,1,0:T(8,128)S(1)} %shard_map.138) | non-fusion elementwise | flops 196608 | bytes 1179648 | tf_op jit(solution)/shard_map/convert_element_type | solution.py:585
  58.8 4.9 %all-to-all-start.1 = ((f16[16,48,256]{2,1,0:T(8,128)(2,1)}), f16[16,48,256]{2,1,0:T(8,128)(2,1)}, u32[]{:S(2)}, u32[]{:S(2)}) async-start(f16[16,48,256]{2,1,0:T(8,128)(2,1)} %convert_element_type.58), calls=%async_computation.1 | async-start | bytes 786432 | tf_op jit(solution)/shard_map/all_to_all | solution.py:500
  63.7 0.0 collective-permute-done.15
  63.7 0.1 collective-permute-done.14
  63.9 0.0 collective-permute-done.13
  64.0 0.3 collective-permute-start.16
  64.3 1.7 %collective-permute-start.17 = (f16[4,48,256]{2,1,0:T(8,128)(2,1)S(1)}, f16[4,48,256]{2,1,0:T(8,128)(2,1)S(1)}, u32[]{:S(2)}, u32[]{:S(2)}) collective-permute-start(f16[4,48,256]{2,1,0:T(8,128)(2,1)S(1)} %pad_maximum_fusion.4), channel_id=1, source_target_pairs={{0,2},{1,3},{2,0},{3,1},{4,6},{5,7},{6,4},{7,5},{8,10},{9,11},{10,... | collective-permute-start | bytes 294920 | tf_op jit(solution)/shard_map/ppermute | solution.py:496
  66.1 1.4 %collective-permute-start.18 = (f16[4,48,256]{2,1,0:T(8,128)(2,1)S(1)}, f16[4,48,256]{2,1,0:T(8,128)(2,1)S(1)}, u32[]{:S(2)}, u32[]{:S(2)}) collective-permute-start(f16[4,48,256]{2,1,0:T(8,128)(2,1)S(1)} %pad_maximum_fusion.5), channel_id=1, source_target_pairs={{0,3},{1,0},{2,1},{3,2},{4,7},{5,4},{6,5},{7,6},{8,11},{9,8},{10,9... | collective-permute-start | bytes 294920 | tf_op jit(solution)/shard_map/ppermute | solution.py:496
  67.5 3.6 %collective-permute-done.16 = f16[4,48,256]{2,1,0:T(8,128)(2,1)S(1)} collective-permute-done((f16[4,48,256]{2,1,0:T(8,128)(2,1)S(1)}, f16[4,48,256]{2,1,0:T(8,128)(2,1)S(1)}, u32[]{:S(2)}, u32[]{:S(2)}) %collective-permute-start.16) | collective-permute-done | bytes 98336 | tf_op jit(solution)/shard_map/ppermute | solution.py:496
  71.1 1.3 %collective-permute-done.17 = f16[4,48,256]{2,1,0:T(8,128)(2,1)S(1)} collective-permute-done((f16[4,48,256]{2,1,0:T(8,128)(2,1)S(1)}, f16[4,48,256]{2,1,0:T(8,128)(2,1)S(1)}, u32[]{:S(2)}, u32[]{:S(2)}) %collective-permute-start.17) | collective-permute-done | bytes 98336 | tf_op jit(solution)/shard_map/ppermute | solution.py:496
  72.4 0.8 collective-permute-done.18
  73.2 1.2 %shard_map.139 = (f32[8,32,512]{2,1,0:T(8,128)S(1)}, f32[16,16,256]{2,1,0:T(8,128)S(1)}) custom-call(s32[2]{0:T(128)S(1)} %pad_add_fusion.place, bf16[2,512,512]{2,1,0:T(8,128)(2,1)S(1)} %copy-done.6, f32[3,8,32,512]{3,2,1,0:T(8,128)S(1)} %copy-done.2, f32[4,48,256]{2,1,0:T(8,128)S(1)} %maximum_convert_fusion.1.refs_0_, ...), custom_call_target="tpu_custom_call" | custom-call | flops 1073741824 | bytes 4194312 | tf_op jit(solution)/shard_map/pallas_call | solution.py:207
  74.4 1.5 %all-to-all-done.1 = f16[16,48,256]{2,1,0:T(8,128)(2,1)} async-done(((f16[16,48,256]{2,1,0:T(8,128)(2,1)}), f16[16,48,256]{2,1,0:T(8,128)(2,1)}, u32[]{:S(2)}, u32[]{:S(2)}) %all-to-all-start.1) | async-done | bytes 393248 | tf_op jit(solution)/shard_map/all_to_all | solution.py:500
  76.0 1.1 %convert_element_type.59.spectra = f32[16,48,256]{2,1,0:T(8,128)S(1)} convert(f16[16,48,256]{2,1,0:T(8,128)(2,1)} %all-to-all-done.1) | non-fusion elementwise | flops 196608 | bytes 1179648 | tf_op jit(solution)/shard_map/convert_element_type | solution.py:602
  77.0 1.8 %shard_map.140 = f32[3,8,32,512]{3,2,1,0:T(8,128)} custom-call(f32[16,48,256]{2,1,0:T(8,128)S(1)} %convert_element_type.59.spectra, bf16[2,512,512]{2,1,0:T(8,128)(2,1)S(1)} %copy-done.6, f32[3,8,32,512]{3,2,1,0:T(8,128)S(1)} %copy-done.2, f32[8,32,512]{2,1,0:T(8,128)S(1)} %get-tuple-element.57.updated, f32[16,16,256]{2,1,0:T(8,128)S(1)} %get-tuple-element.58.kept), custom_call_target="tpu_custom_call" | custom-call | flops 2147483648 | bytes 5767168 | tf_op jit(solution)/shard_map/pallas_call | solution.py:207
  (43 shorter events, 0.6 us)
Async XLA Ops:
  0.7 1.0 %copy-start = (bf16[8,32,512]{2,1,0:T(8,128)(2,1)S(1)}, bf16[8,32,512]{2,1,0:T(8,128)(2,1)}, u32[]{:S(2)}) copy-start(bf16[8,32,512]{2,1,0:T(8,128)(2,1)} %moving.1) | copy-start | bytes 786436
  1.7 0.7 copy-start.1
  3.0 8.0 %collective-permute-start = (bf16[272,128]{1,0:T(8,128)(2,1)S(1)}, bf16[272,128]{1,0:T(8,128)(2,1)S(1)}, u32[]{:S(2)}, u32[]{:S(2)}) collective-permute-start(bf16[272,128]{1,0:T(8,128)(2,1)S(1)} %get-tuple-element.32), channel_id=1, source_target_pairs={{0,8},{4,12},{8,0},{12,4},{1,9},{5,13},{9,1},{13,5},{2,10},{6,14},... | collective-permute-start | bytes 208904 | tf_op jit(solution)/shard_map/ppermute | solution.py:496
  7.1 6.3 %collective-permute-start.1 = (bf16[272,128]{1,0:T(8,128)(2,1)S(1)}, bf16[272,128]{1,0:T(8,128)(2,1)S(1)}, u32[]{:S(2)}, u32[]{:S(2)}) collective-permute-start(bf16[272,128]{1,0:T(8,128)(2,1)S(1)} %get-tuple-element.33), channel_id=1, source_target_pairs={{0,4},{4,8},{8,12},{12,0},{1,5},{5,9},{9,13},{13,1},{2,6},{6,10},{... | collective-permute-start | bytes 208904 | tf_op jit(solution)/shard_map/ppermute | solution.py:496
  8.7 5.1 %collective-permute-start.2 = (bf16[272,128]{1,0:T(8,128)(2,1)S(1)}, bf16[272,128]{1,0:T(8,128)(2,1)S(1)}, u32[]{:S(2)}, u32[]{:S(2)}) collective-permute-start(bf16[272,128]{1,0:T(8,128)(2,1)S(1)} %get-tuple-element.34), channel_id=1, source_target_pairs={{0,12},{4,0},{8,4},{12,8},{1,13},{5,1},{9,5},{13,9},{2,14},{6,2},{... | collective-permute-start | bytes 208904 | tf_op jit(solution)/shard_map/ppermute | solution.py:496
  13.7 7.9 %copy-start.3 = (f32[8,32,512]{2,1,0:T(8,128)S(1)}, f32[8,32,512]{2,1,0:T(8,128)}, u32[]{:S(2)}) copy-start(f32[8,32,512]{2,1,0:T(8,128)} %stiffness.1) | copy-start | bytes 1572868
  13.7 7.9 %copy-start.5 = (s32[8,32,4]{1,2,0:T(4,128)S(1)}, s32[8,32,4]{1,2,0:T(4,128)}, u32[]{:S(2)}) copy-start(s32[8,32,4]{1,2,0:T(4,128)} %param.17) | copy-start | bytes 12292
  15.1 8.1 %collective-permute-start.3 = (bf16[10,32,128]{2,1,0:T(8,128)(2,1)S(1)}, bf16[10,32,128]{2,1,0:T(8,128)(2,1)S(1)}, u32[]{:S(2)}, u32[]{:S(2)}) collective-permute-start(bf16[10,32,128]{2,1,0:T(8,128)(2,1)S(1)} %get-tuple-element.36), channel_id=1, source_target_pairs={{0,8},{4,12},{8,0},{12,4},{1,9},{5,13},{9,1},{13,5},{2,10},{6,14},... | collective-permute-start | bytes 245768 | tf_op jit(solution)/shard_map/ppermute | solution.py:496
  17.8 6.4 %collective-permute-start.4 = (bf16[10,32,128]{2,1,0:T(8,128)(2,1)S(1)}, bf16[10,32,128]{2,1,0:T(8,128)(2,1)S(1)}, u32[]{:S(2)}, u32[]{:S(2)}) collective-permute-start(bf16[10,32,128]{2,1,0:T(8,128)(2,1)S(1)} %get-tuple-element.37), channel_id=1, source_target_pairs={{0,4},{4,8},{8,12},{12,0},{1,5},{5,9},{9,13},{13,1},{2,6},{6,10},{... | collective-permute-start | bytes 245768 | tf_op jit(solution)/shard_map/ppermute | solution.py:496
  19.1 5.5 %collective-permute-start.5 = (bf16[10,32,128]{2,1,0:T(8,128)(2,1)S(1)}, bf16[10,32,128]{2,1,0:T(8,128)(2,1)S(1)}, u32[]{:S(2)}, u32[]{:S(2)}) collective-permute-start(bf16[10,32,128]{2,1,0:T(8,128)(2,1)S(1)} %get-tuple-element.38), channel_id=1, source_target_pairs={{0,12},{4,0},{8,4},{12,8},{1,13},{5,1},{9,5},{13,9},{2,14},{6,2},{... | collective-permute-start | bytes 245768 | tf_op jit(solution)/shard_map/ppermute | solution.py:496
  21.6 3.0 %copy-start.4 = (bf16[8,32,512]{2,1,0:T(8,128)(2,1)S(1)}, bf16[8,32,512]{2,1,0:T(8,128)(2,1)}, u32[]{:S(2)}) copy-start(bf16[8,32,512]{2,1,0:T(8,128)(2,1)} %refs_4_.2) | copy-start | bytes 786436
  21.6 3.0 %copy-start.7 = (bf16[2,512,512]{2,1,0:T(8,128)(2,1)S(1)}, bf16[2,512,512]{2,1,0:T(8,128)(2,1)}, u32[]{:S(2)}) copy-start(bf16[2,512,512]{2,1,0:T(8,128)(2,1)} %constant.19.clone.refs_6_.basis) | copy-start | bytes 3145732
  21.6 3.0 %copy-start.10 = (bf16[2,256,512]{2,1,0:T(8,128)(2,1)S(1)}, bf16[2,256,512]{2,1,0:T(8,128)(2,1)}, u32[]{:S(2)}) copy-start(bf16[2,256,512]{2,1,0:T(8,128)(2,1)} %constant.20.clone.refs_7_) | copy-start | bytes 1572868
  26.4 4.2 %copy-start.9 = (bf16[2,256,512]{2,1,0:T(8,128)(2,1)S(1)}, bf16[2,256,512]{2,1,0:T(8,128)(2,1)}, u32[]{:S(2)}) copy-start(bf16[2,256,512]{2,1,0:T(8,128)(2,1)} %constant.21.clone.lower) | copy-start | bytes 1572868
  26.4 4.1 %collective-permute-start.12 = (f32[24,512]{1,0:T(8,128)S(1)}, f32[24,512]{1,0:T(8,128)S(1)}, u32[]{:S(2)}, u32[]{:S(2)}) collective-permute-start(f32[24,512]{1,0:T(8,128)S(1)} %get-tuple-element.48), channel_id=1, source_target_pairs={{1,0},{2,1},{3,2},{0,3},{5,4},{6,5},{7,6},{4,7},{9,8},{10,9},{11,1... | collective-permute-start | bytes 147464 | tf_op jit(solution)/shard_map/ppermute | solution.py:545
  26.6 11.2 %collective-permute-start.8 = (f16[4,48,256]{2,1,0:T(8,128)(2,1)S(1)}, f16[4,48,256]{2,1,0:T(8,128)(2,1)S(1)}, u32[]{:S(2)}, u32[]{:S(2)}) collective-permute-start(f16[4,48,256]{2,1,0:T(8,128)(2,1)S(1)} %get-tuple-element.60), channel_id=1, source_target_pairs={{0,12},{4,0},{8,4},{12,8},{1,13},{5,1},{9,5},{13,9},{2,14},{6,2},{... | collective-permute-start | bytes 294920 | tf_op jit(solution)/shard_map/ppermute | solution.py:496
  29.9 9.8 %collective-permute-start.7 = (f16[4,48,256]{2,1,0:T(8,128)(2,1)S(1)}, f16[4,48,256]{2,1,0:T(8,128)(2,1)S(1)}, u32[]{:S(2)}, u32[]{:S(2)}) collective-permute-start(f16[4,48,256]{2,1,0:T(8,128)(2,1)S(1)} %get-tuple-element.61), channel_id=1, source_target_pairs={{0,8},{4,12},{8,0},{12,4},{1,9},{5,13},{9,1},{13,5},{2,10},{6,14},... | collective-permute-start | bytes 294920 | tf_op jit(solution)/shard_map/ppermute | solution.py:496
  29.9 9.8 %collective-permute-start.6 = (f16[4,48,256]{2,1,0:T(8,128)(2,1)S(1)}, f16[4,48,256]{2,1,0:T(8,128)(2,1)S(1)}, u32[]{:S(2)}, u32[]{:S(2)}) collective-permute-start(f16[4,48,256]{2,1,0:T(8,128)(2,1)S(1)} %get-tuple-element.62), channel_id=1, source_target_pairs={{0,4},{4,8},{8,12},{12,0},{1,5},{5,9},{9,13},{13,1},{2,6},{6,10},{... | collective-permute-start | bytes 294920 | tf_op jit(solution)/shard_map/ppermute | solution.py:496
  32.3 19.0 %all-to-all-start = ((f16[16,48,256]{2,1,0:T(8,128)(2,1)}), f16[16,48,256]{2,1,0:T(8,128)(2,1)S(1)}, u32[]{:S(2)}, u32[]{:S(2)}) async-start(f16[16,48,256]{2,1,0:T(8,128)(2,1)} %convert_element_type.56), calls=%async_computation | async-start | bytes 786432 | tf_op jit(solution)/shard_map/all_to_all | solution.py:500
  39.6 8.8 %copy-start.8 = (bf16[4,256,256]{2,1,0:T(8,128)(2,1)S(1)}, bf16[4,256,256]{2,1,0:T(8,128)(2,1)}, u32[]{:S(2)}) copy-start(bf16[4,256,256]{2,1,0:T(8,128)(2,1)} %constant.22.clone.refs_4_.basis_z) | copy-start | bytes 1572868
  39.6 8.8 %copy-start.11 = (bf16[6,128,128]{2,1,0:T(8,128)(2,1)S(1)}, bf16[6,128,128]{2,1,0:T(8,128)(2,1)}, u32[]{:S(2)}) copy-start(bf16[6,128,128]{2,1,0:T(8,128)(2,1)} %constant.23.clone.refs_5_.basis_y) | copy-start | bytes 589828
  39.8 5.7 %collective-permute-start.9 = (f16[4,48,256]{2,1,0:T(8,128)(2,1)S(1)}, f16[4,48,256]{2,1,0:T(8,128)(2,1)S(1)}, u32[]{:S(2)}, u32[]{:S(2)}) collective-permute-start(f16[4,48,256]{2,1,0:T(8,128)(2,1)S(1)} %pad_maximum_fusion), channel_id=1, source_target_pairs={{0,1},{1,2},{2,3},{3,0},{4,5},{5,6},{6,7},{7,4},{8,9},{9,10},{10,1... | collective-permute-start | bytes 294920 | tf_op jit(solution)/shard_map/ppermute | solution.py:496
  39.9 6.4 %collective-permute-start.10 = (f16[4,48,256]{2,1,0:T(8,128)(2,1)S(1)}, f16[4,48,256]{2,1,0:T(8,128)(2,1)S(1)}, u32[]{:S(2)}, u32[]{:S(2)}) collective-permute-start(f16[4,48,256]{2,1,0:T(8,128)(2,1)S(1)} %pad_maximum_fusion.1), channel_id=1, source_target_pairs={{0,2},{1,3},{2,0},{3,1},{4,6},{5,7},{6,4},{7,5},{8,10},{9,11},{10,... | collective-permute-start | bytes 294920 | tf_op jit(solution)/shard_map/ppermute | solution.py:496
  41.5 6.9 %collective-permute-start.11 = (f16[4,48,256]{2,1,0:T(8,128)(2,1)S(1)}, f16[4,48,256]{2,1,0:T(8,128)(2,1)S(1)}, u32[]{:S(2)}, u32[]{:S(2)}) collective-permute-start(f16[4,48,256]{2,1,0:T(8,128)(2,1)S(1)} %pad_maximum_fusion.2), channel_id=1, source_target_pairs={{0,3},{1,0},{2,1},{3,2},{4,7},{5,4},{6,5},{7,6},{8,11},{9,8},{10,9... | collective-permute-start | bytes 294920 | tf_op jit(solution)/shard_map/ppermute | solution.py:496
  51.4 12.3 %collective-permute-start.15 = (f16[4,48,256]{2,1,0:T(8,128)(2,1)S(1)}, f16[4,48,256]{2,1,0:T(8,128)(2,1)S(1)}, u32[]{:S(2)}, u32[]{:S(2)}) collective-permute-start(f16[4,48,256]{2,1,0:T(8,128)(2,1)S(1)} %convert_element_type.63), channel_id=1, source_target_pairs={{0,12},{4,0},{8,4},{12,8},{1,13},{5,1},{9,5},{13,9},{2,14},{6,2},{... | collective-permute-start | bytes 294920 | tf_op jit(solution)/shard_map/ppermute | solution.py:496
  53.5 10.4 %collective-permute-start.14 = (f16[4,48,256]{2,1,0:T(8,128)(2,1)S(1)}, f16[4,48,256]{2,1,0:T(8,128)(2,1)S(1)}, u32[]{:S(2)}, u32[]{:S(2)}) collective-permute-start(f16[4,48,256]{2,1,0:T(8,128)(2,1)S(1)} %convert_element_type.62), channel_id=1, source_target_pairs={{0,8},{4,12},{8,0},{12,4},{1,9},{5,13},{9,1},{13,5},{2,10},{6,14},... | collective-permute-start | bytes 294920 | tf_op jit(solution)/shard_map/ppermute | solution.py:496
  53.5 10.4 %collective-permute-start.13 = (f16[4,48,256]{2,1,0:T(8,128)(2,1)S(1)}, f16[4,48,256]{2,1,0:T(8,128)(2,1)S(1)}, u32[]{:S(2)}, u32[]{:S(2)}) collective-permute-start(f16[4,48,256]{2,1,0:T(8,128)(2,1)S(1)} %convert_element_type.61), channel_id=1, source_target_pairs={{0,4},{4,8},{8,12},{12,0},{1,5},{5,9},{9,13},{13,1},{2,6},{6,10},{... | collective-permute-start | bytes 294920 | tf_op jit(solution)/shard_map/ppermute | solution.py:496
  58.8 14.3 %copy-start.2 = (f32[3,8,32,512]{3,2,1,0:T(8,128)S(1)}, f32[3,8,32,512]{3,2,1,0:T(8,128)}, u32[]{:S(2)}) copy-start(f32[3,8,32,512]{3,2,1,0:T(8,128)} %velocity.3) | copy-start | bytes 4718596
  58.8 14.3 %copy-start.6 = (bf16[2,512,512]{2,1,0:T(8,128)(2,1)S(1)}, bf16[2,512,512]{2,1,0:T(8,128)(2,1)}, u32[]{:S(2)}) copy-start(bf16[2,512,512]{2,1,0:T(8,128)(2,1)} %constant.24.clone.basis) | copy-start | bytes 3145732
  58.8 17.1 %all-to-all-start.1 = ((f16[16,48,256]{2,1,0:T(8,128)(2,1)}), f16[16,48,256]{2,1,0:T(8,128)(2,1)}, u32[]{:S(2)}, u32[]{:S(2)}) async-start(f16[16,48,256]{2,1,0:T(8,128)(2,1)} %convert_element_type.58), calls=%async_computation.1 | async-start | bytes 786432 | tf_op jit(solution)/shard_map/all_to_all | solution.py:500
  64.0 7.1 %collective-permute-start.16 = (f16[4,48,256]{2,1,0:T(8,128)(2,1)S(1)}, f16[4,48,256]{2,1,0:T(8,128)(2,1)S(1)}, u32[]{:S(2)}, u32[]{:S(2)}) collective-permute-start(f16[4,48,256]{2,1,0:T(8,128)(2,1)S(1)} %pad_maximum_fusion.3), channel_id=1, source_target_pairs={{0,1},{1,2},{2,3},{3,0},{4,5},{5,6},{6,7},{7,4},{8,9},{9,10},{10,1... | collective-permute-start | bytes 294920 | tf_op jit(solution)/shard_map/ppermute | solution.py:496
  64.3 8.1 %collective-permute-start.17 = (f16[4,48,256]{2,1,0:T(8,128)(2,1)S(1)}, f16[4,48,256]{2,1,0:T(8,128)(2,1)S(1)}, u32[]{:S(2)}, u32[]{:S(2)}) collective-permute-start(f16[4,48,256]{2,1,0:T(8,128)(2,1)S(1)} %pad_maximum_fusion.4), channel_id=1, source_target_pairs={{0,2},{1,3},{2,0},{3,1},{4,6},{5,7},{6,4},{7,5},{8,10},{9,11},{10,... | collective-permute-start | bytes 294920 | tf_op jit(solution)/shard_map/ppermute | solution.py:496
  66.1 7.1 %collective-permute-start.18 = (f16[4,48,256]{2,1,0:T(8,128)(2,1)S(1)}, f16[4,48,256]{2,1,0:T(8,128)(2,1)S(1)}, u32[]{:S(2)}, u32[]{:S(2)}) collective-permute-start(f16[4,48,256]{2,1,0:T(8,128)(2,1)S(1)} %pad_maximum_fusion.5), channel_id=1, source_target_pairs={{0,3},{1,0},{2,1},{3,2},{4,7},{5,4},{6,5},{7,6},{8,11},{9,8},{10,9... | collective-permute-start | bytes 294920 | tf_op jit(solution)/shard_map/ppermute | solution.py:496

commit v13 on v11

--- a/solution.py
+++ b/solution.py
@@ -543,7 +543,8 @@
     )
     beyond = lax.ppermute(first, "sub", [((i + 1) % subs, i) for i in range(subs)])
     chain = chain.astype(f16)
-    chain = scatter([chain[d] for d in range(slabs)], "slab")
+    chain = scatter([chain[d] for d in HOPS], "slab", HOPS)
+    chain = [chain[HOPS.index(d)] for d in range(slabs)]
     later, *chain = lax.optimization_barrier((place, *chain))
     warped = call(functools.partial(place_kernel, slabs), shape(moving.shape, bf16), later, *received)
     chain = scatter([jnp.stack([r[e] for r in chain]) for e in range(subs)], "sub")
@@ -569,7 +570,8 @@
         flops=2 << 30,
     )
     chain, spectra, warped = lax.optimization_barrier((chain, spectra, warped))
-    chain = scatter([r.astype(f16) for r in chain], "slab")
+    chain = scatter([chain[d].astype(f16) for d in HOPS], "slab", HOPS)
+    chain = [chain[HOPS.index(d)] for d in range(slabs)]
     chain = scatter([jnp.stack([r[e] for r in chain]) for e in range(subs)], "sub")
     spectra = call(
         functools.partial(solve_yx_kernel, subs, x_length),

time: 79.4 us -> 79.4 us (level)
  no operation moved by 1% of the time
where the time goes in v13:
time: 79.4 us; the launch traced here: 78.9 us
  starting transfers between devices  38.9 us (49%)
  waiting for transfers between devices  19 us (24%)
  Pallas kernels  14.8 us (19%)
  other arithmetic  3.32 us (4%)
  local copies, waits for them, and re-layouts  1.94 us (2%)
  between operations  0.97 us (1%)
    ppermute x18, starting transfers between devices, scatter(): lax.ppermute(sends[d], axis, [(i, (i + hops[d]) % count) for i in range(c...  28.7 us
    ppermute x18, waiting for transfers between devices, scatter(): lax.ppermute(sends[d], axis, [(i, (i + hops[d]) % count) for i in range(c...  17.5 us
    pallas_call x10, Pallas kernels, call(): pl.pallas_call(kernel, out_shape=out_shape, in_specs=places, out_specs=ja...  14.8 us
    all_to_all x2, starting transfers between devices, exchange(): lax.all_to_all(values, ('slab', 'sub'), split_axis=0, concat_axis=0, tile...  10.1 us
    unnamed x20, local copies, waits for them, and re-layouts  1.7 us
    convert_element_type x2, other arithmetic, local_blocks(): spectra = exchange(spectra.astype(f16))  1.62 us
  transfers between devices with their start and end apart: 21, of which 14 were waited for; matrix products, arithmetic and copies ran while one was open for 3% of the time, Pallas kernels for 11%

profile of v13, /device:TPU:0, one launch (start us, length us, event | category | flops | bytes accessed | tf_op | source)
XLA Modules:
  0.0 78.9 jit_solution(11289096831851518186)
XLA Ops:
  0.6 0.1 pad_add_fusion.place
  0.7 0.9 %copy-done = bf16[8,32,512]{2,1,0:T(8,128)(2,1)S(1)} copy-done((bf16[8,32,512]{2,1,0:T(8,128)(2,1)S(1)}, bf16[8,32,512]{2,1,0:T(8,128)(2,1)}, u32[]{:S(2)}) %copy-start) | copy-done | bytes 262168
  1.7 0.7 copy-done.1
  2.4 0.6 shard_map.113
  3.0 4.1 %collective-permute-start = (bf16[272,128]{1,0:T(8,128)(2,1)S(1)}, bf16[272,128]{1,0:T(8,128)(2,1)S(1)}, u32[]{:S(2)}, u32[]{:S(2)}) collective-permute-start(bf16[272,128]{1,0:T(8,128)(2,1)S(1)} %get-tuple-element.33), channel_id=1, source_target_pairs={{0,8},{4,12},{8,0},{12,4},{1,9},{5,13},{9,1},{13,5},{2,10},{6,14},... | collective-permute-start | bytes 208904 | tf_op jit(solution)/shard_map/ppermute | solution.py:497
  7.1 1.6 %collective-permute-start.1 = (bf16[272,128]{1,0:T(8,128)(2,1)S(1)}, bf16[272,128]{1,0:T(8,128)(2,1)S(1)}, u32[]{:S(2)}, u32[]{:S(2)}) collective-permute-start(bf16[272,128]{1,0:T(8,128)(2,1)S(1)} %get-tuple-element.34), channel_id=1, source_target_pairs={{0,4},{4,8},{8,12},{12,0},{1,5},{5,9},{9,13},{13,1},{2,6},{6,10},{... | collective-permute-start | bytes 208904 | tf_op jit(solution)/shard_map/ppermute | solution.py:497
  8.7 2.2 %collective-permute-start.2 = (bf16[272,128]{1,0:T(8,128)(2,1)S(1)}, bf16[272,128]{1,0:T(8,128)(2,1)S(1)}, u32[]{:S(2)}, u32[]{:S(2)}) collective-permute-start(bf16[272,128]{1,0:T(8,128)(2,1)S(1)} %get-tuple-element.35), channel_id=1, source_target_pairs={{0,12},{4,0},{8,4},{12,8},{1,13},{5,1},{9,5},{13,9},{2,14},{6,2},{... | collective-permute-start | bytes 208904 | tf_op jit(solution)/shard_map/ppermute | solution.py:497
  10.9 0.1 collective-permute-done.refs_1_
  11.0 2.5 %collective-permute-done.1.refs_2_ = bf16[272,128]{1,0:T(8,128)(2,1)S(1)} collective-permute-done((bf16[272,128]{1,0:T(8,128)(2,1)S(1)}, bf16[272,128]{1,0:T(8,128)(2,1)S(1)}, u32[]{:S(2)}, u32[]{:S(2)}) %collective-permute-start.1) | collective-permute-done | bytes 69664 | tf_op jit(solution)/shard_map/ppermute | solution.py:497
  13.4 0.3 collective-permute-done.2.refs_3_
  13.7 1.3 %shard_map.114 = (bf16[10,32,128]{2,1,0:T(8,128)(2,1)S(1)}, bf16[10,32,128]{2,1,0:T(8,128)(2,1)S(1)}, bf16[10,32,128]{2,1,0:T(8,128)(2,1)S(1)}, bf16[10,32,128]{2,1,0:T(8,128)(2,1)S(1)}) custom-call(s32[2]{0:T(128)S(1)} %pad_add_fusion.place, bf16[272,128]{1,0:T(8,128)(2,1)S(1)} %get-tuple-element.32.refs_0_, ...), custom_call_target="tpu_custom_call" | custom-call | flops 1073741824 | bytes 606216 | tf_op jit(solution)/shard_map/pallas_call | solution.py:207
  15.1 2.7 %collective-permute-start.3 = (bf16[10,32,128]{2,1,0:T(8,128)(2,1)S(1)}, bf16[10,32,128]{2,1,0:T(8,128)(2,1)S(1)}, u32[]{:S(2)}, u32[]{:S(2)}) collective-permute-start(bf16[10,32,128]{2,1,0:T(8,128)(2,1)S(1)} %get-tuple-element.37), channel_id=1, source_target_pairs={{0,8},{4,12},{8,0},{12,4},{1,9},{5,13},{9,1},{13,5},{2,10},{6,14},... | collective-permute-start | bytes 245768 | tf_op jit(solution)/shard_map/ppermute | solution.py:497
  17.8 1.3 %collective-permute-start.4 = (bf16[10,32,128]{2,1,0:T(8,128)(2,1)S(1)}, bf16[10,32,128]{2,1,0:T(8,128)(2,1)S(1)}, u32[]{:S(2)}, u32[]{:S(2)}) collective-permute-start(bf16[10,32,128]{2,1,0:T(8,128)(2,1)S(1)} %get-tuple-element.38), channel_id=1, source_target_pairs={{0,4},{4,8},{8,12},{12,0},{1,5},{5,9},{9,13},{13,1},{2,6},{6,10},{... | collective-permute-start | bytes 245768 | tf_op jit(solution)/shard_map/ppermute | solution.py:497
  19.1 2.5 %collective-permute-start.5 = (bf16[10,32,128]{2,1,0:T(8,128)(2,1)S(1)}, bf16[10,32,128]{2,1,0:T(8,128)(2,1)S(1)}, u32[]{:S(2)}, u32[]{:S(2)}) collective-permute-start(bf16[10,32,128]{2,1,0:T(8,128)(2,1)S(1)} %get-tuple-element.39), channel_id=1, source_target_pairs={{0,12},{4,0},{8,4},{12,8},{1,13},{5,1},{9,5},{13,9},{2,14},{6,2},{... | collective-permute-start | bytes 245768 | tf_op jit(solution)/shard_map/ppermute | solution.py:497
  21.6 0.3 shard_map.115.refs_5_
  22.0 1.2 %collective-permute-done.3.refs_1_ = bf16[10,32,128]{2,1,0:T(8,128)(2,1)S(1)} collective-permute-done((bf16[10,32,128]{2,1,0:T(8,128)(2,1)S(1)}, bf16[10,32,128]{2,1,0:T(8,128)(2,1)S(1)}, u32[]{:S(2)}, u32[]{:S(2)}) %collective-permute-start.3) | collective-permute-done | bytes 81952 | tf_op jit(solution)/shard_map/ppermute | solution.py:497
  23.2 1.0 %collective-permute-done.4.refs_2_ = bf16[10,32,128]{2,1,0:T(8,128)(2,1)S(1)} collective-permute-done((bf16[10,32,128]{2,1,0:T(8,128)(2,1)S(1)}, bf16[10,32,128]{2,1,0:T(8,128)(2,1)S(1)}, u32[]{:S(2)}, u32[]{:S(2)}) %collective-permute-start.4) | collective-permute-done | bytes 81952 | tf_op jit(solution)/shard_map/ppermute | solution.py:497
  24.2 0.4 collective-permute-done.5.refs_3_
  24.6 0.0 copy-done.7
  24.7 2.0 %shard_map.116 = (f32[24,512]{1,0:T(8,128)S(1)}, f32[8,32,512]{2,1,0:T(8,128)S(1)}, f32[8,32,512]{2,1,0:T(8,128)S(1)}, f32[4,4,48,256]{3,2,1,0:T(8,128)S(1)}, f32[16,16,256]{2,1,0:T(8,128)S(1)}) custom-call(s32[2]{0:T(128)S(1)} %pad_add_fusion.place, bf16[10,32,128]{2,1,0:T(8,128)(2,1)S(1)} %get-tuple-element.36.refs_0_, ...), custom_call_target="tpu_custom_call" | custom-call | flops 3221225472 | bytes 4309000 | tf_op jit(solution)/shard_map/pallas_call | solution.py:207
  26.7 0.1 convert_element_type.51
  26.7 0.1 collective-permute-start.12
  26.8 0.1 slice_bitcast_fusion
  26.9 3.3 %collective-permute-start.8 = (f16[4,48,256]{2,1,0:T(8,128)(2,1)S(1)}, f16[4,48,256]{2,1,0:T(8,128)(2,1)S(1)}, u32[]{:S(2)}, u32[]{:S(2)}) collective-permute-start(f16[4,48,256]{2,1,0:T(8,128)(2,1)S(1)} %get-tuple-element.62), channel_id=1, source_target_pairs={{0,12},{4,0},{8,4},{12,8},{1,13},{5,1},{9,5},{13,9},{2,14},{6,2},{... | collective-permute-start | bytes 294920 | tf_op jit(solution)/shard_map/ppermute | solution.py:497
  30.2 0.0 collective-permute-start.7
  30.2 0.6 collective-permute-start.6
  30.8 0.0 collective-permute-done.12.beyond
  30.8 0.7 shard_map.118
  31.5 0.8 %convert_element_type.56 = f16[16,48,256]{2,1,0:T(8,128)(2,1)} convert(f32[16,48,256]{2,1,0:T(8,128)S(1)} %shard_map.118) | non-fusion elementwise | flops 196608 | bytes 1179648 | tf_op jit(solution)/shard_map/convert_element_type | solution.py:561
  32.3 5.5 %all-to-all-start = ((f16[16,48,256]{2,1,0:T(8,128)(2,1)}), f16[16,48,256]{2,1,0:T(8,128)(2,1)S(1)}, u32[]{:S(2)}, u32[]{:S(2)}) async-start(f16[16,48,256]{2,1,0:T(8,128)(2,1)} %convert_element_type.56), calls=%async_computation | async-start | bytes 786432 | tf_op jit(solution)/shard_map/all_to_all | solution.py:501
  37.8 0.0 collective-permute-done.8
  37.9 2.1 %collective-permute-done.7 = f16[4,48,256]{2,1,0:T(8,128)(2,1)S(1)} collective-permute-done((f16[4,48,256]{2,1,0:T(8,128)(2,1)S(1)}, f16[4,48,256]{2,1,0:T(8,128)(2,1)S(1)}, u32[]{:S(2)}, u32[]{:S(2)}) %collective-permute-start.7) | collective-permute-done | bytes 98336 | tf_op jit(solution)/shard_map/ppermute | solution.py:497
  39.9 0.0 collective-permute-done.6
  40.1 0.1 collective-permute-start.9
  40.2 1.6 %collective-permute-start.10 = (f16[4,48,256]{2,1,0:T(8,128)(2,1)S(1)}, f16[4,48,256]{2,1,0:T(8,128)(2,1)S(1)}, u32[]{:S(2)}, u32[]{:S(2)}) collective-permute-start(f16[4,48,256]{2,1,0:T(8,128)(2,1)S(1)} %pad_maximum_fusion.1), channel_id=1, source_target_pairs={{0,2},{1,3},{2,0},{3,1},{4,6},{5,7},{6,4},{7,5},{8,10},{9,11},{10,... | collective-permute-start | bytes 294920 | tf_op jit(solution)/shard_map/ppermute | solution.py:497
  41.8 1.5 %collective-permute-start.11 = (f16[4,48,256]{2,1,0:T(8,128)(2,1)S(1)}, f16[4,48,256]{2,1,0:T(8,128)(2,1)S(1)}, u32[]{:S(2)}, u32[]{:S(2)}) collective-permute-start(f16[4,48,256]{2,1,0:T(8,128)(2,1)S(1)} %pad_maximum_fusion.2), channel_id=1, source_target_pairs={{0,3},{1,0},{2,1},{3,2},{4,7},{5,4},{6,5},{7,6},{8,11},{9,8},{10,9... | collective-permute-start | bytes 294920 | tf_op jit(solution)/shard_map/ppermute | solution.py:497
  43.3 1.3 %shard_map.119 = bf16[8,32,512]{2,1,0:T(8,128)(2,1)} custom-call(s32[2]{0:T(128)S(1)} %pad_add_fusion.place, bf16[10,32,128]{2,1,0:T(8,128)(2,1)S(1)} %get-tuple-element.36.refs_0_, bf16[10,32,128]{2,1,0:T(8,128)(2,1)S(1)} %collective-permute-done.3.refs_1_, bf16[10,32,128]{2,1,0:T(8,128)(2,1)S(1)} %collective-permute-done.4.refs_2_, ...), custom_call_target="tpu_custom_call" | custom-call | bytes 589832 | tf_op jit(solution)/shard_map/pallas_call | solution.py:207
  44.6 0.8 %collective-permute-done.9 = f16[4,48,256]{2,1,0:T(8,128)(2,1)S(1)} collective-permute-done((f16[4,48,256]{2,1,0:T(8,128)(2,1)S(1)}, f16[4,48,256]{2,1,0:T(8,128)(2,1)S(1)}, u32[]{:S(2)}, u32[]{:S(2)}) %collective-permute-start.9) | collective-permute-done | bytes 98336 | tf_op jit(solution)/shard_map/ppermute | solution.py:497
  45.5 1.1 %collective-permute-done.10 = f16[4,48,256]{2,1,0:T(8,128)(2,1)S(1)} collective-permute-done((f16[4,48,256]{2,1,0:T(8,128)(2,1)S(1)}, f16[4,48,256]{2,1,0:T(8,128)(2,1)S(1)}, u32[]{:S(2)}, u32[]{:S(2)}) %collective-permute-start.10) | collective-permute-done | bytes 98336 | tf_op jit(solution)/shard_map/ppermute | solution.py:497
  46.6 2.4 %collective-permute-done.11 = f16[4,48,256]{2,1,0:T(8,128)(2,1)S(1)} collective-permute-done((f16[4,48,256]{2,1,0:T(8,128)(2,1)S(1)}, f16[4,48,256]{2,1,0:T(8,128)(2,1)S(1)}, u32[]{:S(2)}, u32[]{:S(2)}) %collective-permute-start.11) | collective-permute-done | bytes 98336 | tf_op jit(solution)/shard_map/ppermute | solution.py:497
  49.0 2.8 %shard_map.117 = (f32[4,48,256]{2,1,0:T(8,128)S(1)}, f32[4,48,256]{2,1,0:T(8,128)S(1)}, f32[4,48,256]{2,1,0:T(8,128)S(1)}, f32[4,48,256]{2,1,0:T(8,128)S(1)}) custom-call(s32[2]{0:T(128)S(1)} %pad_add_fusion.place, f32[4,48,256]{2,1,0:T(8,128)S(1)} %maximum_convert_fusion.refs_0_, f32[4,48,256]{2,1,0:T(8,128)S(1)} %convert_element_type.53.refs_1_, ...), custom_call_target="tpu_custom_call" | custom-call | flops 2147483648 | bytes 2293768 | tf_op jit(solution)/shard_map/pallas_call | solution.py:207
  51.8 0.0 all-to-all-done
  51.9 1.6 %collective-permute-start.15 = (f16[4,48,256]{2,1,0:T(8,128)(2,1)S(1)}, f16[4,48,256]{2,1,0:T(8,128)(2,1)S(1)}, u32[]{:S(2)}, u32[]{:S(2)}) collective-permute-start(f16[4,48,256]{2,1,0:T(8,128)(2,1)S(1)} %convert_element_type.63), channel_id=1, source_target_pairs={{0,12},{4,0},{8,4},{12,8},{1,13},{5,1},{9,5},{13,9},{2,14},{6,2},{... | collective-permute-start | bytes 294920 | tf_op jit(solution)/shard_map/ppermute | solution.py:497
  53.6 0.1 collective-permute-start.14
  53.7 1.9 %collective-permute-start.13 = (f16[4,48,256]{2,1,0:T(8,128)(2,1)S(1)}, f16[4,48,256]{2,1,0:T(8,128)(2,1)S(1)}, u32[]{:S(2)}, u32[]{:S(2)}) collective-permute-start(f16[4,48,256]{2,1,0:T(8,128)(2,1)S(1)} %convert_element_type.61), channel_id=1, source_target_pairs={{0,4},{4,8},{8,12},{12,0},{1,5},{5,9},{9,13},{13,1},{2,6},{6,10},{... | collective-permute-start | bytes 294920 | tf_op jit(solution)/shard_map/ppermute | solution.py:497
  55.6 0.1 convert_element_type.57.spectra
  55.7 2.6 %shard_map.120 = f32[16,48,256]{2,1,0:T(8,128)S(1)} custom-call(s32[2]{0:T(128)S(1)} %pad_add_fusion.place, f32[16,48,256]{2,1,0:T(8,128)S(1)} %convert_element_type.57.spectra, bf16[4,256,256]{2,1,0:T(8,128)(2,1)S(1)} %copy-done.8, bf16[6,128,128]{2,1,0:T(8,128)(2,1)S(1)} %copy-done.9), custom_call_target="tpu_custom_call" | custom-call | flops 2147483648 | bytes 2293768 | tf_op jit(solution)/shard_map/pallas_call | solution.py:207
  58.3 0.8 %convert_element_type.58 = f16[16,48,256]{2,1,0:T(8,128)(2,1)} convert(f32[16,48,256]{2,1,0:T(8,128)S(1)} %shard_map.120) | non-fusion elementwise | flops 196608 | bytes 1179648 | tf_op jit(solution)/shard_map/convert_element_type | solution.py:586
  59.1 4.6 %all-to-all-start.1 = ((f16[16,48,256]{2,1,0:T(8,128)(2,1)}), f16[16,48,256]{2,1,0:T(8,128)(2,1)}, u32[]{:S(2)}, u32[]{:S(2)}) async-start(f16[16,48,256]{2,1,0:T(8,128)(2,1)} %convert_element_type.58), calls=%async_computation.1 | async-start | bytes 786432 | tf_op jit(solution)/shard_map/all_to_all | solution.py:501
  63.7 0.0 collective-permute-done.15
  63.8 0.0 collective-permute-done.14
  63.8 0.0 collective-permute-done.13
  63.9 0.4 collective-permute-start.16
  64.4 1.7 %collective-permute-start.17 = (f16[4,48,256]{2,1,0:T(8,128)(2,1)S(1)}, f16[4,48,256]{2,1,0:T(8,128)(2,1)S(1)}, u32[]{:S(2)}, u32[]{:S(2)}) collective-permute-start(f16[4,48,256]{2,1,0:T(8,128)(2,1)S(1)} %pad_maximum_fusion.4), channel_id=1, source_target_pairs={{0,2},{1,3},{2,0},{3,1},{4,6},{5,7},{6,4},{7,5},{8,10},{9,11},{10,... | collective-permute-start | bytes 294920 | tf_op jit(solution)/shard_map/ppermute | solution.py:497
  66.1 1.4 %collective-permute-start.18 = (f16[4,48,256]{2,1,0:T(8,128)(2,1)S(1)}, f16[4,48,256]{2,1,0:T(8,128)(2,1)S(1)}, u32[]{:S(2)}, u32[]{:S(2)}) collective-permute-start(f16[4,48,256]{2,1,0:T(8,128)(2,1)S(1)} %pad_maximum_fusion.5), channel_id=1, source_target_pairs={{0,3},{1,0},{2,1},{3,2},{4,7},{5,4},{6,5},{7,6},{8,11},{9,8},{10,9... | collective-permute-start | bytes 294920 | tf_op jit(solution)/shard_map/ppermute | solution.py:497
  67.5 3.6 %collective-permute-done.16 = f16[4,48,256]{2,1,0:T(8,128)(2,1)S(1)} collective-permute-done((f16[4,48,256]{2,1,0:T(8,128)(2,1)S(1)}, f16[4,48,256]{2,1,0:T(8,128)(2,1)S(1)}, u32[]{:S(2)}, u32[]{:S(2)}) %collective-permute-start.16) | collective-permute-done | bytes 98336 | tf_op jit(solution)/shard_map/ppermute | solution.py:497
  71.1 1.3 %collective-permute-done.17 = f16[4,48,256]{2,1,0:T(8,128)(2,1)S(1)} collective-permute-done((f16[4,48,256]{2,1,0:T(8,128)(2,1)S(1)}, f16[4,48,256]{2,1,0:T(8,128)(2,1)S(1)}, u32[]{:S(2)}, u32[]{:S(2)}) %collective-permute-start.17) | collective-permute-done | bytes 98336 | tf_op jit(solution)/shard_map/ppermute | solution.py:497
  72.4 0.8 collective-permute-done.18
  73.2 0.0 copy-done.2
  73.2 0.0 copy-done.6
  73.2 1.2 %shard_map.121 = (f32[8,32,512]{2,1,0:T(8,128)S(1)}, f32[16,16,256]{2,1,0:T(8,128)S(1)}) custom-call(s32[2]{0:T(128)S(1)} %pad_add_fusion.place, bf16[2,512,512]{2,1,0:T(8,128)(2,1)S(1)} %copy-done.6, f32[3,8,32,512]{3,2,1,0:T(8,128)S(1)} %copy-done.2, f32[4,48,256]{2,1,0:T(8,128)S(1)} %maximum_convert_fusion.1.refs_0_, ...), custom_call_target="tpu_custom_call" | custom-call | flops 1073741824 | bytes 4194312 | tf_op jit(solution)/shard_map/pallas_call | solution.py:207
  74.5 1.5 %all-to-all-done.1 = f16[16,48,256]{2,1,0:T(8,128)(2,1)} async-done(((f16[16,48,256]{2,1,0:T(8,128)(2,1)}), f16[16,48,256]{2,1,0:T(8,128)(2,1)}, u32[]{:S(2)}, u32[]{:S(2)}) %all-to-all-start.1) | async-done | bytes 393248 | tf_op jit(solution)/shard_map/all_to_all | solution.py:501
  76.0 1.1 %convert_element_type.59.spectra = f32[16,48,256]{2,1,0:T(8,128)S(1)} convert(f16[16,48,256]{2,1,0:T(8,128)(2,1)} %all-to-all-done.1) | non-fusion elementwise | flops 196608 | bytes 1179648 | tf_op jit(solution)/shard_map/convert_element_type | solution.py:603
  77.1 1.8 %shard_map.122 = f32[3,8,32,512]{3,2,1,0:T(8,128)} custom-call(f32[16,48,256]{2,1,0:T(8,128)S(1)} %convert_element_type.59.spectra, bf16[2,512,512]{2,1,0:T(8,128)(2,1)S(1)} %copy-done.6, f32[3,8,32,512]{3,2,1,0:T(8,128)S(1)} %copy-done.2, f32[8,32,512]{2,1,0:T(8,128)S(1)} %get-tuple-element.59.updated, f32[16,16,256]{2,1,0:T(8,128)S(1)} %get-tuple-element.60.kept), custom_call_target="tpu_custom_call" | custom-call | flops 2147483648 | bytes 5767168 | tf_op jit(solution)/shard_map/pallas_call | solution.py:207
  (39 shorter events, 0.6 us)
Async XLA Ops:
  0.7 1.0 %copy-start = (bf16[8,32,512]{2,1,0:T(8,128)(2,1)S(1)}, bf16[8,32,512]{2,1,0:T(8,128)(2,1)}, u32[]{:S(2)}) copy-start(bf16[8,32,512]{2,1,0:T(8,128)(2,1)} %moving.1) | copy-start | bytes 786436
  1.7 0.7 copy-start.1
  3.0 8.0 %collective-permute-start = (bf16[272,128]{1,0:T(8,128)(2,1)S(1)}, bf16[272,128]{1,0:T(8,128)(2,1)S(1)}, u32[]{:S(2)}, u32[]{:S(2)}) collective-permute-start(bf16[272,128]{1,0:T(8,128)(2,1)S(1)} %get-tuple-element.33), channel_id=1, source_target_pairs={{0,8},{4,12},{8,0},{12,4},{1,9},{5,13},{9,1},{13,5},{2,10},{6,14},... | collective-permute-start | bytes 208904 | tf_op jit(solution)/shard_map/ppermute | solution.py:497
  7.1 6.3 %collective-permute-start.1 = (bf16[272,128]{1,0:T(8,128)(2,1)S(1)}, bf16[272,128]{1,0:T(8,128)(2,1)S(1)}, u32[]{:S(2)}, u32[]{:S(2)}) collective-permute-start(bf16[272,128]{1,0:T(8,128)(2,1)S(1)} %get-tuple-element.34), channel_id=1, source_target_pairs={{0,4},{4,8},{8,12},{12,0},{1,5},{5,9},{9,13},{13,1},{2,6},{6,10},{... | collective-permute-start | bytes 208904 | tf_op jit(solution)/shard_map/ppermute | solution.py:497
  8.7 5.1 %collective-permute-start.2 = (bf16[272,128]{1,0:T(8,128)(2,1)S(1)}, bf16[272,128]{1,0:T(8,128)(2,1)S(1)}, u32[]{:S(2)}, u32[]{:S(2)}) collective-permute-start(bf16[272,128]{1,0:T(8,128)(2,1)S(1)} %get-tuple-element.35), channel_id=1, source_target_pairs={{0,12},{4,0},{8,4},{12,8},{1,13},{5,1},{9,5},{13,9},{2,14},{6,2},{... | collective-permute-start | bytes 208904 | tf_op jit(solution)/shard_map/ppermute | solution.py:497
  13.7 7.9 %copy-start.3 = (f32[8,32,512]{2,1,0:T(8,128)S(1)}, f32[8,32,512]{2,1,0:T(8,128)}, u32[]{:S(2)}) copy-start(f32[8,32,512]{2,1,0:T(8,128)} %stiffness.1) | copy-start | bytes 1572868
  13.7 7.9 %copy-start.5 = (s32[8,32,4]{1,2,0:T(4,128)S(1)}, s32[8,32,4]{1,2,0:T(4,128)}, u32[]{:S(2)}) copy-start(s32[8,32,4]{1,2,0:T(4,128)} %param.15) | copy-start | bytes 12292
  15.1 8.1 %collective-permute-start.3 = (bf16[10,32,128]{2,1,0:T(8,128)(2,1)S(1)}, bf16[10,32,128]{2,1,0:T(8,128)(2,1)S(1)}, u32[]{:S(2)}, u32[]{:S(2)}) collective-permute-start(bf16[10,32,128]{2,1,0:T(8,128)(2,1)S(1)} %get-tuple-element.37), channel_id=1, source_target_pairs={{0,8},{4,12},{8,0},{12,4},{1,9},{5,13},{9,1},{13,5},{2,10},{6,14},... | collective-permute-start | bytes 245768 | tf_op jit(solution)/shard_map/ppermute | solution.py:497
  17.8 6.4 %collective-permute-start.4 = (bf16[10,32,128]{2,1,0:T(8,128)(2,1)S(1)}, bf16[10,32,128]{2,1,0:T(8,128)(2,1)S(1)}, u32[]{:S(2)}, u32[]{:S(2)}) collective-permute-start(bf16[10,32,128]{2,1,0:T(8,128)(2,1)S(1)} %get-tuple-element.38), channel_id=1, source_target_pairs={{0,4},{4,8},{8,12},{12,0},{1,5},{5,9},{9,13},{13,1},{2,6},{6,10},{... | collective-permute-start | bytes 245768 | tf_op jit(solution)/shard_map/ppermute | solution.py:497
  19.1 5.5 %collective-permute-start.5 = (bf16[10,32,128]{2,1,0:T(8,128)(2,1)S(1)}, bf16[10,32,128]{2,1,0:T(8,128)(2,1)S(1)}, u32[]{:S(2)}, u32[]{:S(2)}) collective-permute-start(bf16[10,32,128]{2,1,0:T(8,128)(2,1)S(1)} %get-tuple-element.39), channel_id=1, source_target_pairs={{0,12},{4,0},{8,4},{12,8},{1,13},{5,1},{9,5},{13,9},{2,14},{6,2},{... | collective-permute-start | bytes 245768 | tf_op jit(solution)/shard_map/ppermute | solution.py:497
  21.6 3.0 %copy-start.4 = (bf16[8,32,512]{2,1,0:T(8,128)(2,1)S(1)}, bf16[8,32,512]{2,1,0:T(8,128)(2,1)}, u32[]{:S(2)}) copy-start(bf16[8,32,512]{2,1,0:T(8,128)(2,1)} %refs_4_.2) | copy-start | bytes 786436
  21.6 3.0 %copy-start.7 = (bf16[2,512,512]{2,1,0:T(8,128)(2,1)S(1)}, bf16[2,512,512]{2,1,0:T(8,128)(2,1)}, u32[]{:S(2)}) copy-start(bf16[2,512,512]{2,1,0:T(8,128)(2,1)} %constant.15.clone.refs_6_.basis) | copy-start | bytes 3145732
  26.7 4.1 %collective-permute-start.12 = (f32[24,512]{1,0:T(8,128)S(1)}, f32[24,512]{1,0:T(8,128)S(1)}, u32[]{:S(2)}, u32[]{:S(2)}) collective-permute-start(f32[24,512]{1,0:T(8,128)S(1)} %get-tuple-element.49), channel_id=1, source_target_pairs={{1,0},{2,1},{3,2},{0,3},{5,4},{6,5},{7,6},{4,7},{9,8},{10,9},{11,1... | collective-permute-start | bytes 147464 | tf_op jit(solution)/shard_map/ppermute | solution.py:544
  26.9 11.0 %collective-permute-start.8 = (f16[4,48,256]{2,1,0:T(8,128)(2,1)S(1)}, f16[4,48,256]{2,1,0:T(8,128)(2,1)S(1)}, u32[]{:S(2)}, u32[]{:S(2)}) collective-permute-start(f16[4,48,256]{2,1,0:T(8,128)(2,1)S(1)} %get-tuple-element.62), channel_id=1, source_target_pairs={{0,12},{4,0},{8,4},{12,8},{1,13},{5,1},{9,5},{13,9},{2,14},{6,2},{... | collective-permute-start | bytes 294920 | tf_op jit(solution)/shard_map/ppermute | solution.py:497
  30.2 9.8 %collective-permute-start.7 = (f16[4,48,256]{2,1,0:T(8,128)(2,1)S(1)}, f16[4,48,256]{2,1,0:T(8,128)(2,1)S(1)}, u32[]{:S(2)}, u32[]{:S(2)}) collective-permute-start(f16[4,48,256]{2,1,0:T(8,128)(2,1)S(1)} %get-tuple-element.63), channel_id=1, source_target_pairs={{0,8},{4,12},{8,0},{12,4},{1,9},{5,13},{9,1},{13,5},{2,10},{6,14},... | collective-permute-start | bytes 294920 | tf_op jit(solution)/shard_map/ppermute | solution.py:497
  30.2 9.8 %collective-permute-start.6 = (f16[4,48,256]{2,1,0:T(8,128)(2,1)S(1)}, f16[4,48,256]{2,1,0:T(8,128)(2,1)S(1)}, u32[]{:S(2)}, u32[]{:S(2)}) collective-permute-start(f16[4,48,256]{2,1,0:T(8,128)(2,1)S(1)} %get-tuple-element.64), channel_id=1, source_target_pairs={{0,4},{4,8},{8,12},{12,0},{1,5},{5,9},{9,13},{13,1},{2,6},{6,10},{... | collective-permute-start | bytes 294920 | tf_op jit(solution)/shard_map/ppermute | solution.py:497
  32.3 19.5 %all-to-all-start = ((f16[16,48,256]{2,1,0:T(8,128)(2,1)}), f16[16,48,256]{2,1,0:T(8,128)(2,1)S(1)}, u32[]{:S(2)}, u32[]{:S(2)}) async-start(f16[16,48,256]{2,1,0:T(8,128)(2,1)} %convert_element_type.56), calls=%async_computation | async-start | bytes 786432 | tf_op jit(solution)/shard_map/all_to_all | solution.py:501
  39.9 9.0 %copy-start.8 = (bf16[4,256,256]{2,1,0:T(8,128)(2,1)S(1)}, bf16[4,256,256]{2,1,0:T(8,128)(2,1)}, u32[]{:S(2)}) copy-start(bf16[4,256,256]{2,1,0:T(8,128)(2,1)} %constant.16.clone.refs_4_.basis_z) | copy-start | bytes 1572868
  39.9 9.0 %copy-start.9 = (bf16[6,128,128]{2,1,0:T(8,128)(2,1)S(1)}, bf16[6,128,128]{2,1,0:T(8,128)(2,1)}, u32[]{:S(2)}) copy-start(bf16[6,128,128]{2,1,0:T(8,128)(2,1)} %constant.17.clone.refs_5_.basis_y) | copy-start | bytes 589828
  40.1 5.4 %collective-permute-start.9 = (f16[4,48,256]{2,1,0:T(8,128)(2,1)S(1)}, f16[4,48,256]{2,1,0:T(8,128)(2,1)S(1)}, u32[]{:S(2)}, u32[]{:S(2)}) collective-permute-start(f16[4,48,256]{2,1,0:T(8,128)(2,1)S(1)} %pad_maximum_fusion), channel_id=1, source_target_pairs={{0,1},{1,2},{2,3},{3,0},{4,5},{5,6},{6,7},{7,4},{8,9},{9,10},{10,1... | collective-permute-start | bytes 294920 | tf_op jit(solution)/shard_map/ppermute | solution.py:497
  40.2 6.3 %collective-permute-start.10 = (f16[4,48,256]{2,1,0:T(8,128)(2,1)S(1)}, f16[4,48,256]{2,1,0:T(8,128)(2,1)S(1)}, u32[]{:S(2)}, u32[]{:S(2)}) collective-permute-start(f16[4,48,256]{2,1,0:T(8,128)(2,1)S(1)} %pad_maximum_fusion.1), channel_id=1, source_target_pairs={{0,2},{1,3},{2,0},{3,1},{4,6},{5,7},{6,4},{7,5},{8,10},{9,11},{10,... | collective-permute-start | bytes 294920 | tf_op jit(solution)/shard_map/ppermute | solution.py:497
  41.8 7.1 %collective-permute-start.11 = (f16[4,48,256]{2,1,0:T(8,128)(2,1)S(1)}, f16[4,48,256]{2,1,0:T(8,128)(2,1)S(1)}, u32[]{:S(2)}, u32[]{:S(2)}) collective-permute-start(f16[4,48,256]{2,1,0:T(8,128)(2,1)S(1)} %pad_maximum_fusion.2), channel_id=1, source_target_pairs={{0,3},{1,0},{2,1},{3,2},{4,7},{5,4},{6,5},{7,6},{8,11},{9,8},{10,9... | collective-permute-start | bytes 294920 | tf_op jit(solution)/shard_map/ppermute | solution.py:497
  51.9 11.8 %collective-permute-start.15 = (f16[4,48,256]{2,1,0:T(8,128)(2,1)S(1)}, f16[4,48,256]{2,1,0:T(8,128)(2,1)S(1)}, u32[]{:S(2)}, u32[]{:S(2)}) collective-permute-start(f16[4,48,256]{2,1,0:T(8,128)(2,1)S(1)} %convert_element_type.63), channel_id=1, source_target_pairs={{0,12},{4,0},{8,4},{12,8},{1,13},{5,1},{9,5},{13,9},{2,14},{6,2},{... | collective-permute-start | bytes 294920 | tf_op jit(solution)/shard_map/ppermute | solution.py:497
  53.6 10.2 %collective-permute-start.14 = (f16[4,48,256]{2,1,0:T(8,128)(2,1)S(1)}, f16[4,48,256]{2,1,0:T(8,128)(2,1)S(1)}, u32[]{:S(2)}, u32[]{:S(2)}) collective-permute-start(f16[4,48,256]{2,1,0:T(8,128)(2,1)S(1)} %convert_element_type.62), channel_id=1, source_target_pairs={{0,8},{4,12},{8,0},{12,4},{1,9},{5,13},{9,1},{13,5},{2,10},{6,14},... | collective-permute-start | bytes 294920 | tf_op jit(solution)/shard_map/ppermute | solution.py:497
  53.7 10.2 %collective-permute-start.13 = (f16[4,48,256]{2,1,0:T(8,128)(2,1)S(1)}, f16[4,48,256]{2,1,0:T(8,128)(2,1)S(1)}, u32[]{:S(2)}, u32[]{:S(2)}) collective-permute-start(f16[4,48,256]{2,1,0:T(8,128)(2,1)S(1)} %convert_element_type.61), channel_id=1, source_target_pairs={{0,4},{4,8},{8,12},{12,0},{1,5},{5,9},{9,13},{13,1},{2,6},{6,10},{... | collective-permute-start | bytes 294920 | tf_op jit(solution)/shard_map/ppermute | solution.py:497
  59.1 14.1 %copy-start.2 = (f32[3,8,32,512]{3,2,1,0:T(8,128)S(1)}, f32[3,8,32,512]{3,2,1,0:T(8,128)}, u32[]{:S(2)}) copy-start(f32[3,8,32,512]{3,2,1,0:T(8,128)} %velocity.3) | copy-start | bytes 4718596
  59.1 14.1 %copy-start.6 = (bf16[2,512,512]{2,1,0:T(8,128)(2,1)S(1)}, bf16[2,512,512]{2,1,0:T(8,128)(2,1)}, u32[]{:S(2)}) copy-start(bf16[2,512,512]{2,1,0:T(8,128)(2,1)} %constant.18.clone.basis) | copy-start | bytes 3145732
  59.1 16.9 %all-to-all-start.1 = ((f16[16,48,256]{2,1,0:T(8,128)(2,1)}), f16[16,48,256]{2,1,0:T(8,128)(2,1)}, u32[]{:S(2)}, u32[]{:S(2)}) async-start(f16[16,48,256]{2,1,0:T(8,128)(2,1)} %convert_element_type.58), calls=%async_computation.1 | async-start | bytes 786432 | tf_op jit(solution)/shard_map/all_to_all | solution.py:501
  63.9 7.2 %collective-permute-start.16 = (f16[4,48,256]{2,1,0:T(8,128)(2,1)S(1)}, f16[4,48,256]{2,1,0:T(8,128)(2,1)S(1)}, u32[]{:S(2)}, u32[]{:S(2)}) collective-permute-start(f16[4,48,256]{2,1,0:T(8,128)(2,1)S(1)} %pad_maximum_fusion.3), channel_id=1, source_target_pairs={{0,1},{1,2},{2,3},{3,0},{4,5},{5,6},{6,7},{7,4},{8,9},{9,10},{10,1... | collective-permute-start | bytes 294920 | tf_op jit(solution)/shard_map/ppermute | solution.py:497
  64.4 8.1 %collective-permute-start.17 = (f16[4,48,256]{2,1,0:T(8,128)(2,1)S(1)}, f16[4,48,256]{2,1,0:T(8,128)(2,1)S(1)}, u32[]{:S(2)}, u32[]{:S(2)}) collective-permute-start(f16[4,48,256]{2,1,0:T(8,128)(2,1)S(1)} %pad_maximum_fusion.4), channel_id=1, source_target_pairs={{0,2},{1,3},{2,0},{3,1},{4,6},{5,7},{6,4},{7,5},{8,10},{9,11},{10,... | collective-permute-start | bytes 294920 | tf_op jit(solution)/shard_map/ppermute | solution.py:497
  66.1 7.1 %collective-permute-start.18 = (f16[4,48,256]{2,1,0:T(8,128)(2,1)S(1)}, f16[4,48,256]{2,1,0:T(8,128)(2,1)S(1)}, u32[]{:S(2)}, u32[]{:S(2)}) collective-permute-start(f16[4,48,256]{2,1,0:T(8,128)(2,1)S(1)} %pad_maximum_fusion.5), channel_id=1, source_target_pairs={{0,3},{1,0},{2,1},{3,2},{4,7},{5,4},{6,5},{7,6},{8,11},{9,8},{10,9... | collective-permute-start | bytes 294920 | tf_op jit(solution)/shard_map/ppermute | solution.py:497

commit v14 on v11

--- a/solution.py
+++ b/solution.py
@@ -186,7 +186,7 @@
     return wave * wave
 
 
-HOPS = (0, 2, 1, 3)
+HOPS = (0, 2, 3, 1)
 
 
 def around(value, count):

time: 79.4 us -> 79.3 us (level)
  starting transfers between devices: 38.9 us -> 34.3 us
  waiting for transfers between devices: 19 us -> 23.5 us
    ppermute x18, waiting for transfers between devices: 17.5 us -> 21.7 us  [scatter(): lax.ppermute(sends[d], axis, [(i, (i + hops[d]) % count) for i in range(c...]
    ppermute x18, starting transfers between devices: 28.7 us -> 25.7 us  [scatter(): lax.ppermute(sends[d], axis, [(i, (i + hops[d]) % count) for i in range(c...]
    all_to_all x2, starting transfers between devices: 10.1 us -> 8.52 us  [exchange(): lax.all_to_all(values, ('slab', 'sub'), split_axis=0, concat_axis=0, tile...]
  transfers between devices with their start and end apart: 21 -> 21, of which waited for: 14 -> 13; matrix products, arithmetic and copies ran while one was open for 3% -> 3% of each run, Pallas kernels for 11% -> 11%
where the time goes in v14:
time: 79.3 us; the launch traced here: 78.9 us
  starting transfers between devices  34.3 us (43%)
  waiting for transfers between devices  23.5 us (30%)
  Pallas kernels  14.8 us (19%)
  other arithmetic  3.32 us (4%)
  local copies, waits for them, and re-layouts  1.94 us (2%)
  between operations  0.98 us (1%)
    ppermute x18, starting transfers between devices, scatter(): lax.ppermute(sends[d], axis, [(i, (i + hops[d]) % count) for i in range(c...  25.7 us
    ppermute x18, waiting for transfers between devices, scatter(): lax.ppermute(sends[d], axis, [(i, (i + hops[d]) % count) for i in range(c...  21.7 us
    pallas_call x10, Pallas kernels, call(): pl.pallas_call(kernel, out_shape=out_shape, in_specs=places, out_specs=ja...  14.8 us
    all_to_all x2, starting transfers between devices, exchange(): lax.all_to_all(values, ('slab', 'sub'), split_axis=0, concat_axis=0, tile...  8.52 us
    all_to_all x2, waiting for transfers between devices, exchange(): lax.all_to_all(values, ('slab', 'sub'), split_axis=0, concat_axis=0, tile...  1.82 us
    unnamed x20, local copies, waits for them, and re-layouts  1.7 us
    convert_element_type x2, other arithmetic, local_blocks(): spectra = exchange(spectra.astype(f16))  1.62 us
  transfers between devices with their start and end apart: 21, of which 13 were waited for; matrix products, arithmetic and copies ran while one was open for 3% of the time, Pallas kernels for 11%

profile of v14, /device:TPU:0, one launch (start us, length us, event | category | flops | bytes accessed | tf_op | source)
XLA Modules:
  0.0 78.9 jit_solution(12693463102860290242)
XLA Ops:
  0.6 0.1 pad_add_fusion.place
  0.7 0.9 %copy-done = bf16[8,32,512]{2,1,0:T(8,128)(2,1)S(1)} copy-done((bf16[8,32,512]{2,1,0:T(8,128)(2,1)S(1)}, bf16[8,32,512]{2,1,0:T(8,128)(2,1)}, u32[]{:S(2)}) %copy-start) | copy-done | bytes 262168
  1.7 0.7 copy-done.1
  2.4 0.6 shard_map.113
  3.0 4.1 %collective-permute-start = (bf16[272,128]{1,0:T(8,128)(2,1)S(1)}, bf16[272,128]{1,0:T(8,128)(2,1)S(1)}, u32[]{:S(2)}, u32[]{:S(2)}) collective-permute-start(bf16[272,128]{1,0:T(8,128)(2,1)S(1)} %get-tuple-element.33), channel_id=1, source_target_pairs={{0,8},{4,12},{8,0},{12,4},{1,9},{5,13},{9,1},{13,5},{2,10},{6,14},... | collective-permute-start | bytes 208904 | tf_op jit(solution)/shard_map/ppermute | solution.py:497
  7.1 1.3 %collective-permute-start.1 = (bf16[272,128]{1,0:T(8,128)(2,1)S(1)}, bf16[272,128]{1,0:T(8,128)(2,1)S(1)}, u32[]{:S(2)}, u32[]{:S(2)}) collective-permute-start(bf16[272,128]{1,0:T(8,128)(2,1)S(1)} %get-tuple-element.34), channel_id=1, source_target_pairs={{0,12},{4,0},{8,4},{12,8},{1,13},{5,1},{9,5},{13,9},{2,14},{6,2},{... | collective-permute-start | bytes 208904 | tf_op jit(solution)/shard_map/ppermute | solution.py:497
  8.4 0.7 collective-permute-start.2
  9.1 1.1 %collective-permute-done.refs_1_ = bf16[272,128]{1,0:T(8,128)(2,1)S(1)} collective-permute-done((bf16[272,128]{1,0:T(8,128)(2,1)S(1)}, bf16[272,128]{1,0:T(8,128)(2,1)S(1)}, u32[]{:S(2)}, u32[]{:S(2)}) %collective-permute-start) | collective-permute-done | bytes 69664 | tf_op jit(solution)/shard_map/ppermute | solution.py:497
  10.3 1.1 %collective-permute-done.1.refs_2_ = bf16[272,128]{1,0:T(8,128)(2,1)S(1)} collective-permute-done((bf16[272,128]{1,0:T(8,128)(2,1)S(1)}, bf16[272,128]{1,0:T(8,128)(2,1)S(1)}, u32[]{:S(2)}, u32[]{:S(2)}) %collective-permute-start.1) | collective-permute-done | bytes 69664 | tf_op jit(solution)/shard_map/ppermute | solution.py:497
  11.4 3.1 %collective-permute-done.2.refs_3_ = bf16[272,128]{1,0:T(8,128)(2,1)S(1)} collective-permute-done((bf16[272,128]{1,0:T(8,128)(2,1)S(1)}, bf16[272,128]{1,0:T(8,128)(2,1)S(1)}, u32[]{:S(2)}, u32[]{:S(2)}) %collective-permute-start.2) | collective-permute-done | bytes 69664 | tf_op jit(solution)/shard_map/ppermute | solution.py:497
  14.6 1.3 %shard_map.114 = (bf16[10,32,128]{2,1,0:T(8,128)(2,1)S(1)}, bf16[10,32,128]{2,1,0:T(8,128)(2,1)S(1)}, bf16[10,32,128]{2,1,0:T(8,128)(2,1)S(1)}, bf16[10,32,128]{2,1,0:T(8,128)(2,1)S(1)}) custom-call(s32[2]{0:T(128)S(1)} %pad_add_fusion.place, bf16[272,128]{1,0:T(8,128)(2,1)S(1)} %get-tuple-element.32.refs_0_, ...), custom_call_target="tpu_custom_call" | custom-call | flops 1073741824 | bytes 606216 | tf_op jit(solution)/shard_map/pallas_call | solution.py:207
  15.9 1.9 %collective-permute-start.3 = (bf16[10,32,128]{2,1,0:T(8,128)(2,1)S(1)}, bf16[10,32,128]{2,1,0:T(8,128)(2,1)S(1)}, u32[]{:S(2)}, u32[]{:S(2)}) collective-permute-start(bf16[10,32,128]{2,1,0:T(8,128)(2,1)S(1)} %get-tuple-element.37), channel_id=1, source_target_pairs={{0,8},{4,12},{8,0},{12,4},{1,9},{5,13},{9,1},{13,5},{2,10},{6,14},... | collective-permute-start | bytes 245768 | tf_op jit(solution)/shard_map/ppermute | solution.py:497
  17.8 0.4 collective-permute-start.4
  18.2 1.6 %collective-permute-start.5 = (bf16[10,32,128]{2,1,0:T(8,128)(2,1)S(1)}, bf16[10,32,128]{2,1,0:T(8,128)(2,1)S(1)}, u32[]{:S(2)}, u32[]{:S(2)}) collective-permute-start(bf16[10,32,128]{2,1,0:T(8,128)(2,1)S(1)} %get-tuple-element.39), channel_id=1, source_target_pairs={{0,4},{4,8},{8,12},{12,0},{1,5},{5,9},{9,13},{13,1},{2,6},{6,10},{... | collective-permute-start | bytes 245768 | tf_op jit(solution)/shard_map/ppermute | solution.py:497
  19.8 0.0 copy-done.5
  19.8 0.3 shard_map.115.refs_5_
  20.2 4.4 %collective-permute-done.3.refs_1_ = bf16[10,32,128]{2,1,0:T(8,128)(2,1)S(1)} collective-permute-done((bf16[10,32,128]{2,1,0:T(8,128)(2,1)S(1)}, bf16[10,32,128]{2,1,0:T(8,128)(2,1)S(1)}, u32[]{:S(2)}, u32[]{:S(2)}) %collective-permute-start.3) | collective-permute-done | bytes 81952 | tf_op jit(solution)/shard_map/ppermute | solution.py:497
  24.6 0.1 collective-permute-done.4.refs_2_
  24.7 0.0 collective-permute-done.5.refs_3_
  24.7 2.0 %shard_map.116 = (f32[24,512]{1,0:T(8,128)S(1)}, f32[8,32,512]{2,1,0:T(8,128)S(1)}, f32[8,32,512]{2,1,0:T(8,128)S(1)}, f32[4,4,48,256]{3,2,1,0:T(8,128)S(1)}, f32[16,16,256]{2,1,0:T(8,128)S(1)}) custom-call(s32[2]{0:T(128)S(1)} %pad_add_fusion.place, bf16[10,32,128]{2,1,0:T(8,128)(2,1)S(1)} %get-tuple-element.36.refs_0_, ...), custom_call_target="tpu_custom_call" | custom-call | flops 3221225472 | bytes 4309000 | tf_op jit(solution)/shard_map/pallas_call | solution.py:207
  26.7 0.1 convert_element_type.51
  26.8 0.1 collective-permute-start.12
  26.8 0.1 slice_bitcast_fusion
  26.9 2.6 %collective-permute-start.8 = (f16[4,48,256]{2,1,0:T(8,128)(2,1)S(1)}, f16[4,48,256]{2,1,0:T(8,128)(2,1)S(1)}, u32[]{:S(2)}, u32[]{:S(2)}) collective-permute-start(f16[4,48,256]{2,1,0:T(8,128)(2,1)S(1)} %get-tuple-element.62), channel_id=1, source_target_pairs={{0,12},{4,0},{8,4},{12,8},{1,13},{5,1},{9,5},{13,9},{2,14},{6,2},{... | collective-permute-start | bytes 294920 | tf_op jit(solution)/shard_map/ppermute | solution.py:497
  29.5 0.6 collective-permute-start.7
  30.1 1.7 %collective-permute-start.6 = (f16[4,48,256]{2,1,0:T(8,128)(2,1)S(1)}, f16[4,48,256]{2,1,0:T(8,128)(2,1)S(1)}, u32[]{:S(2)}, u32[]{:S(2)}) collective-permute-start(f16[4,48,256]{2,1,0:T(8,128)(2,1)S(1)} %get-tuple-element.64), channel_id=1, source_target_pairs={{0,4},{4,8},{8,12},{12,0},{1,5},{5,9},{9,13},{13,1},{2,6},{6,10},{... | collective-permute-start | bytes 294920 | tf_op jit(solution)/shard_map/ppermute | solution.py:497
  31.9 0.0 collective-permute-done.12.beyond
  31.9 0.7 shard_map.118
  32.6 0.8 %convert_element_type.56 = f16[16,48,256]{2,1,0:T(8,128)(2,1)} convert(f32[16,48,256]{2,1,0:T(8,128)S(1)} %shard_map.118) | non-fusion elementwise | flops 196608 | bytes 1179648 | tf_op jit(solution)/shard_map/convert_element_type | solution.py:560
  33.4 4.1 %all-to-all-start = ((f16[16,48,256]{2,1,0:T(8,128)(2,1)}), f16[16,48,256]{2,1,0:T(8,128)(2,1)S(1)}, u32[]{:S(2)}, u32[]{:S(2)}) async-start(f16[16,48,256]{2,1,0:T(8,128)(2,1)} %convert_element_type.56), calls=%async_computation | async-start | bytes 786432 | tf_op jit(solution)/shard_map/all_to_all | solution.py:501
  37.5 0.0 collective-permute-done.8
  37.5 2.1 %collective-permute-done.7 = f16[4,48,256]{2,1,0:T(8,128)(2,1)S(1)} collective-permute-done((f16[4,48,256]{2,1,0:T(8,128)(2,1)S(1)}, f16[4,48,256]{2,1,0:T(8,128)(2,1)S(1)}, u32[]{:S(2)}, u32[]{:S(2)}) %collective-permute-start.7) | collective-permute-done | bytes 98336 | tf_op jit(solution)/shard_map/ppermute | solution.py:497
  39.6 0.0 collective-permute-done.6
  39.7 0.1 collective-permute-start.9
  39.8 1.6 %collective-permute-start.10 = (f16[4,48,256]{2,1,0:T(8,128)(2,1)S(1)}, f16[4,48,256]{2,1,0:T(8,128)(2,1)S(1)}, u32[]{:S(2)}, u32[]{:S(2)}) collective-permute-start(f16[4,48,256]{2,1,0:T(8,128)(2,1)S(1)} %pad_maximum_fusion.1), channel_id=1, source_target_pairs={{0,2},{1,3},{2,0},{3,1},{4,6},{5,7},{6,4},{7,5},{8,10},{9,11},{10,... | collective-permute-start | bytes 294920 | tf_op jit(solution)/shard_map/ppermute | solution.py:497
  41.4 1.5 %collective-permute-start.11 = (f16[4,48,256]{2,1,0:T(8,128)(2,1)S(1)}, f16[4,48,256]{2,1,0:T(8,128)(2,1)S(1)}, u32[]{:S(2)}, u32[]{:S(2)}) collective-permute-start(f16[4,48,256]{2,1,0:T(8,128)(2,1)S(1)} %pad_maximum_fusion.2), channel_id=1, source_target_pairs={{0,3},{1,0},{2,1},{3,2},{4,7},{5,4},{6,5},{7,6},{8,11},{9,8},{10,9... | collective-permute-start | bytes 294920 | tf_op jit(solution)/shard_map/ppermute | solution.py:497
  42.9 1.3 %shard_map.119 = bf16[8,32,512]{2,1,0:T(8,128)(2,1)} custom-call(s32[2]{0:T(128)S(1)} %pad_add_fusion.place, bf16[10,32,128]{2,1,0:T(8,128)(2,1)S(1)} %get-tuple-element.36.refs_0_, bf16[10,32,128]{2,1,0:T(8,128)(2,1)S(1)} %collective-permute-done.3.refs_1_, bf16[10,32,128]{2,1,0:T(8,128)(2,1)S(1)} %collective-permute-done.4.refs_2_, ...), custom_call_target="tpu_custom_call" | custom-call | bytes 589832 | tf_op jit(solution)/shard_map/pallas_call | solution.py:207
  44.3 0.9 %collective-permute-done.9 = f16[4,48,256]{2,1,0:T(8,128)(2,1)S(1)} collective-permute-done((f16[4,48,256]{2,1,0:T(8,128)(2,1)S(1)}, f16[4,48,256]{2,1,0:T(8,128)(2,1)S(1)}, u32[]{:S(2)}, u32[]{:S(2)}) %collective-permute-start.9) | collective-permute-done | bytes 98336 | tf_op jit(solution)/shard_map/ppermute | solution.py:497
  45.1 1.0 %collective-permute-done.10 = f16[4,48,256]{2,1,0:T(8,128)(2,1)S(1)} collective-permute-done((f16[4,48,256]{2,1,0:T(8,128)(2,1)S(1)}, f16[4,48,256]{2,1,0:T(8,128)(2,1)S(1)}, u32[]{:S(2)}, u32[]{:S(2)}) %collective-permute-start.10) | collective-permute-done | bytes 98336 | tf_op jit(solution)/shard_map/ppermute | solution.py:497
  46.2 2.4 %collective-permute-done.11 = f16[4,48,256]{2,1,0:T(8,128)(2,1)S(1)} collective-permute-done((f16[4,48,256]{2,1,0:T(8,128)(2,1)S(1)}, f16[4,48,256]{2,1,0:T(8,128)(2,1)S(1)}, u32[]{:S(2)}, u32[]{:S(2)}) %collective-permute-start.11) | collective-permute-done | bytes 98336 | tf_op jit(solution)/shard_map/ppermute | solution.py:497
  48.6 0.0 copy-done.8
  48.6 0.0 copy-done.9
  48.6 2.8 %shard_map.117 = (f32[4,48,256]{2,1,0:T(8,128)S(1)}, f32[4,48,256]{2,1,0:T(8,128)S(1)}, f32[4,48,256]{2,1,0:T(8,128)S(1)}, f32[4,48,256]{2,1,0:T(8,128)S(1)}) custom-call(s32[2]{0:T(128)S(1)} %pad_add_fusion.place, f32[4,48,256]{2,1,0:T(8,128)S(1)} %maximum_convert_fusion.refs_0_, f32[4,48,256]{2,1,0:T(8,128)S(1)} %convert_element_type.53.refs_1_, ...), custom_call_target="tpu_custom_call" | custom-call | flops 2147483648 | bytes 2293768 | tf_op jit(solution)/shard_map/pallas_call | solution.py:207
  51.4 0.0 all-to-all-done
  51.5 1.6 %collective-permute-start.15 = (f16[4,48,256]{2,1,0:T(8,128)(2,1)S(1)}, f16[4,48,256]{2,1,0:T(8,128)(2,1)S(1)}, u32[]{:S(2)}, u32[]{:S(2)}) collective-permute-start(f16[4,48,256]{2,1,0:T(8,128)(2,1)S(1)} %convert_element_type.63), channel_id=1, source_target_pairs={{0,12},{4,0},{8,4},{12,8},{1,13},{5,1},{9,5},{13,9},{2,14},{6,2},{... | collective-permute-start | bytes 294920 | tf_op jit(solution)/shard_map/ppermute | solution.py:497
  53.2 0.7 collective-permute-start.14
  53.8 1.9 %collective-permute-start.13 = (f16[4,48,256]{2,1,0:T(8,128)(2,1)S(1)}, f16[4,48,256]{2,1,0:T(8,128)(2,1)S(1)}, u32[]{:S(2)}, u32[]{:S(2)}) collective-permute-start(f16[4,48,256]{2,1,0:T(8,128)(2,1)S(1)} %convert_element_type.61), channel_id=1, source_target_pairs={{0,4},{4,8},{8,12},{12,0},{1,5},{5,9},{9,13},{13,1},{2,6},{6,10},{... | collective-permute-start | bytes 294920 | tf_op jit(solution)/shard_map/ppermute | solution.py:497
  55.8 0.1 convert_element_type.57.spectra
  55.9 2.6 %shard_map.120 = f32[16,48,256]{2,1,0:T(8,128)S(1)} custom-call(s32[2]{0:T(128)S(1)} %pad_add_fusion.place, f32[16,48,256]{2,1,0:T(8,128)S(1)} %convert_element_type.57.spectra, bf16[4,256,256]{2,1,0:T(8,128)(2,1)S(1)} %copy-done.8, bf16[6,128,128]{2,1,0:T(8,128)(2,1)S(1)} %copy-done.9), custom_call_target="tpu_custom_call" | custom-call | flops 2147483648 | bytes 2293768 | tf_op jit(solution)/shard_map/pallas_call | solution.py:207
  58.5 0.8 %convert_element_type.58 = f16[16,48,256]{2,1,0:T(8,128)(2,1)} convert(f32[16,48,256]{2,1,0:T(8,128)S(1)} %shard_map.120) | non-fusion elementwise | flops 196608 | bytes 1179648 | tf_op jit(solution)/shard_map/convert_element_type | solution.py:584
  59.3 4.5 %all-to-all-start.1 = ((f16[16,48,256]{2,1,0:T(8,128)(2,1)}), f16[16,48,256]{2,1,0:T(8,128)(2,1)}, u32[]{:S(2)}, u32[]{:S(2)}) async-start(f16[16,48,256]{2,1,0:T(8,128)(2,1)} %convert_element_type.58), calls=%async_computation.1 | async-start | bytes 786432 | tf_op jit(solution)/shard_map/all_to_all | solution.py:501
  63.8 0.0 collective-permute-done.15
  63.8 0.0 collective-permute-done.14
  63.9 0.0 collective-permute-done.13
  63.9 0.3 collective-permute-start.16
  64.3 1.7 %collective-permute-start.17 = (f16[4,48,256]{2,1,0:T(8,128)(2,1)S(1)}, f16[4,48,256]{2,1,0:T(8,128)(2,1)S(1)}, u32[]{:S(2)}, u32[]{:S(2)}) collective-permute-start(f16[4,48,256]{2,1,0:T(8,128)(2,1)S(1)} %pad_maximum_fusion.4), channel_id=1, source_target_pairs={{0,2},{1,3},{2,0},{3,1},{4,6},{5,7},{6,4},{7,5},{8,10},{9,11},{10,... | collective-permute-start | bytes 294920 | tf_op jit(solution)/shard_map/ppermute | solution.py:497
  66.0 1.4 %collective-permute-start.18 = (f16[4,48,256]{2,1,0:T(8,128)(2,1)S(1)}, f16[4,48,256]{2,1,0:T(8,128)(2,1)S(1)}, u32[]{:S(2)}, u32[]{:S(2)}) collective-permute-start(f16[4,48,256]{2,1,0:T(8,128)(2,1)S(1)} %pad_maximum_fusion.5), channel_id=1, source_target_pairs={{0,3},{1,0},{2,1},{3,2},{4,7},{5,4},{6,5},{7,6},{8,11},{9,8},{10,9... | collective-permute-start | bytes 294920 | tf_op jit(solution)/shard_map/ppermute | solution.py:497
  67.4 3.6 %collective-permute-done.16 = f16[4,48,256]{2,1,0:T(8,128)(2,1)S(1)} collective-permute-done((f16[4,48,256]{2,1,0:T(8,128)(2,1)S(1)}, f16[4,48,256]{2,1,0:T(8,128)(2,1)S(1)}, u32[]{:S(2)}, u32[]{:S(2)}) %collective-permute-start.16) | collective-permute-done | bytes 98336 | tf_op jit(solution)/shard_map/ppermute | solution.py:497
  71.0 1.3 %collective-permute-done.17 = f16[4,48,256]{2,1,0:T(8,128)(2,1)S(1)} collective-permute-done((f16[4,48,256]{2,1,0:T(8,128)(2,1)S(1)}, f16[4,48,256]{2,1,0:T(8,128)(2,1)S(1)}, u32[]{:S(2)}, u32[]{:S(2)}) %collective-permute-start.17) | collective-permute-done | bytes 98336 | tf_op jit(solution)/shard_map/ppermute | solution.py:497
  72.3 0.5 collective-permute-done.18
  72.9 1.2 %shard_map.121 = (f32[8,32,512]{2,1,0:T(8,128)S(1)}, f32[16,16,256]{2,1,0:T(8,128)S(1)}) custom-call(s32[2]{0:T(128)S(1)} %pad_add_fusion.place, bf16[2,512,512]{2,1,0:T(8,128)(2,1)S(1)} %copy-done.6, f32[3,8,32,512]{3,2,1,0:T(8,128)S(1)} %copy-done.2, f32[4,48,256]{2,1,0:T(8,128)S(1)} %maximum_convert_fusion.1.refs_0_, ...), custom_call_target="tpu_custom_call" | custom-call | flops 1073741824 | bytes 4194312 | tf_op jit(solution)/shard_map/pallas_call | solution.py:207
  74.2 1.8 %all-to-all-done.1 = f16[16,48,256]{2,1,0:T(8,128)(2,1)} async-done(((f16[16,48,256]{2,1,0:T(8,128)(2,1)}), f16[16,48,256]{2,1,0:T(8,128)(2,1)}, u32[]{:S(2)}, u32[]{:S(2)}) %all-to-all-start.1) | async-done | bytes 393248 | tf_op jit(solution)/shard_map/all_to_all | solution.py:501
  76.0 1.1 %convert_element_type.59.spectra = f32[16,48,256]{2,1,0:T(8,128)S(1)} convert(f16[16,48,256]{2,1,0:T(8,128)(2,1)} %all-to-all-done.1) | non-fusion elementwise | flops 196608 | bytes 1179648 | tf_op jit(solution)/shard_map/convert_element_type | solution.py:601
  77.1 1.8 %shard_map.122 = f32[3,8,32,512]{3,2,1,0:T(8,128)} custom-call(f32[16,48,256]{2,1,0:T(8,128)S(1)} %convert_element_type.59.spectra, bf16[2,512,512]{2,1,0:T(8,128)(2,1)S(1)} %copy-done.6, f32[3,8,32,512]{3,2,1,0:T(8,128)S(1)} %copy-done.2, f32[8,32,512]{2,1,0:T(8,128)S(1)} %get-tuple-element.59.updated, f32[16,16,256]{2,1,0:T(8,128)S(1)} %get-tuple-element.60.kept), custom_call_target="tpu_custom_call" | custom-call | flops 2147483648 | bytes 5767168 | tf_op jit(solution)/shard_map/pallas_call | solution.py:207
  (39 shorter events, 0.6 us)
Async XLA Ops:
  0.7 1.0 %copy-start = (bf16[8,32,512]{2,1,0:T(8,128)(2,1)S(1)}, bf16[8,32,512]{2,1,0:T(8,128)(2,1)}, u32[]{:S(2)}) copy-start(bf16[8,32,512]{2,1,0:T(8,128)(2,1)} %moving.1) | copy-start | bytes 786436
  1.7 0.7 copy-start.1
  3.0 7.3 %collective-permute-start = (bf16[272,128]{1,0:T(8,128)(2,1)S(1)}, bf16[272,128]{1,0:T(8,128)(2,1)S(1)}, u32[]{:S(2)}, u32[]{:S(2)}) collective-permute-start(bf16[272,128]{1,0:T(8,128)(2,1)S(1)} %get-tuple-element.33), channel_id=1, source_target_pairs={{0,8},{4,12},{8,0},{12,4},{1,9},{5,13},{9,1},{13,5},{2,10},{6,14},... | collective-permute-start | bytes 208904 | tf_op jit(solution)/shard_map/ppermute | solution.py:497
  7.1 4.3 %collective-permute-start.1 = (bf16[272,128]{1,0:T(8,128)(2,1)S(1)}, bf16[272,128]{1,0:T(8,128)(2,1)S(1)}, u32[]{:S(2)}, u32[]{:S(2)}) collective-permute-start(bf16[272,128]{1,0:T(8,128)(2,1)S(1)} %get-tuple-element.34), channel_id=1, source_target_pairs={{0,12},{4,0},{8,4},{12,8},{1,13},{5,1},{9,5},{13,9},{2,14},{6,2},{... | collective-permute-start | bytes 208904 | tf_op jit(solution)/shard_map/ppermute | solution.py:497
  8.4 6.1 %collective-permute-start.2 = (bf16[272,128]{1,0:T(8,128)(2,1)S(1)}, bf16[272,128]{1,0:T(8,128)(2,1)S(1)}, u32[]{:S(2)}, u32[]{:S(2)}) collective-permute-start(bf16[272,128]{1,0:T(8,128)(2,1)S(1)} %get-tuple-element.35), channel_id=1, source_target_pairs={{0,4},{4,8},{8,12},{12,0},{1,5},{5,9},{9,13},{13,1},{2,6},{6,10},{... | collective-permute-start | bytes 208904 | tf_op jit(solution)/shard_map/ppermute | solution.py:497
  14.6 5.3 %copy-start.3 = (f32[8,32,512]{2,1,0:T(8,128)S(1)}, f32[8,32,512]{2,1,0:T(8,128)}, u32[]{:S(2)}) copy-start(f32[8,32,512]{2,1,0:T(8,128)} %stiffness.1) | copy-start | bytes 1572868
  14.6 5.3 %copy-start.5 = (s32[8,32,4]{1,2,0:T(4,128)S(1)}, s32[8,32,4]{1,2,0:T(4,128)}, u32[]{:S(2)}) copy-start(s32[8,32,4]{1,2,0:T(4,128)} %param.15) | copy-start | bytes 12292
  15.9 8.7 %collective-permute-start.3 = (bf16[10,32,128]{2,1,0:T(8,128)(2,1)S(1)}, bf16[10,32,128]{2,1,0:T(8,128)(2,1)S(1)}, u32[]{:S(2)}, u32[]{:S(2)}) collective-permute-start(bf16[10,32,128]{2,1,0:T(8,128)(2,1)S(1)} %get-tuple-element.37), channel_id=1, source_target_pairs={{0,8},{4,12},{8,0},{12,4},{1,9},{5,13},{9,1},{13,5},{2,10},{6,14},... | collective-permute-start | bytes 245768 | tf_op jit(solution)/shard_map/ppermute | solution.py:497
  17.8 6.9 %collective-permute-start.4 = (bf16[10,32,128]{2,1,0:T(8,128)(2,1)S(1)}, bf16[10,32,128]{2,1,0:T(8,128)(2,1)S(1)}, u32[]{:S(2)}, u32[]{:S(2)}) collective-permute-start(bf16[10,32,128]{2,1,0:T(8,128)(2,1)S(1)} %get-tuple-element.38), channel_id=1, source_target_pairs={{0,12},{4,0},{8,4},{12,8},{1,13},{5,1},{9,5},{13,9},{2,14},{6,2},{... | collective-permute-start | bytes 245768 | tf_op jit(solution)/shard_map/ppermute | solution.py:497
  18.2 6.4 %collective-permute-start.5 = (bf16[10,32,128]{2,1,0:T(8,128)(2,1)S(1)}, bf16[10,32,128]{2,1,0:T(8,128)(2,1)S(1)}, u32[]{:S(2)}, u32[]{:S(2)}) collective-permute-start(bf16[10,32,128]{2,1,0:T(8,128)(2,1)S(1)} %get-tuple-element.39), channel_id=1, source_target_pairs={{0,4},{4,8},{8,12},{12,0},{1,5},{5,9},{9,13},{13,1},{2,6},{6,10},{... | collective-permute-start | bytes 245768 | tf_op jit(solution)/shard_map/ppermute | solution.py:497
  19.8 4.9 %copy-start.4 = (bf16[8,32,512]{2,1,0:T(8,128)(2,1)S(1)}, bf16[8,32,512]{2,1,0:T(8,128)(2,1)}, u32[]{:S(2)}) copy-start(bf16[8,32,512]{2,1,0:T(8,128)(2,1)} %refs_4_.2) | copy-start | bytes 786436
  19.8 4.9 %copy-start.7 = (bf16[2,512,512]{2,1,0:T(8,128)(2,1)S(1)}, bf16[2,512,512]{2,1,0:T(8,128)(2,1)}, u32[]{:S(2)}) copy-start(bf16[2,512,512]{2,1,0:T(8,128)(2,1)} %constant.15.clone.refs_6_.basis) | copy-start | bytes 3145732
  26.8 5.1 %collective-permute-start.12 = (f32[24,512]{1,0:T(8,128)S(1)}, f32[24,512]{1,0:T(8,128)S(1)}, u32[]{:S(2)}, u32[]{:S(2)}) collective-permute-start(f32[24,512]{1,0:T(8,128)S(1)} %get-tuple-element.49), channel_id=1, source_target_pairs={{1,0},{2,1},{3,2},{0,3},{5,4},{6,5},{7,6},{4,7},{9,8},{10,9},{11,1... | collective-permute-start | bytes 147464 | tf_op jit(solution)/shard_map/ppermute | solution.py:544
  26.9 10.5 %collective-permute-start.8 = (f16[4,48,256]{2,1,0:T(8,128)(2,1)S(1)}, f16[4,48,256]{2,1,0:T(8,128)(2,1)S(1)}, u32[]{:S(2)}, u32[]{:S(2)}) collective-permute-start(f16[4,48,256]{2,1,0:T(8,128)(2,1)S(1)} %get-tuple-element.62), channel_id=1, source_target_pairs={{0,12},{4,0},{8,4},{12,8},{1,13},{5,1},{9,5},{13,9},{2,14},{6,2},{... | collective-permute-start | bytes 294920 | tf_op jit(solution)/shard_map/ppermute | solution.py:497
  29.5 10.0 %collective-permute-start.7 = (f16[4,48,256]{2,1,0:T(8,128)(2,1)S(1)}, f16[4,48,256]{2,1,0:T(8,128)(2,1)S(1)}, u32[]{:S(2)}, u32[]{:S(2)}) collective-permute-start(f16[4,48,256]{2,1,0:T(8,128)(2,1)S(1)} %get-tuple-element.63), channel_id=1, source_target_pairs={{0,8},{4,12},{8,0},{12,4},{1,9},{5,13},{9,1},{13,5},{2,10},{6,14},... | collective-permute-start | bytes 294920 | tf_op jit(solution)/shard_map/ppermute | solution.py:497
  30.1 9.4 %collective-permute-start.6 = (f16[4,48,256]{2,1,0:T(8,128)(2,1)S(1)}, f16[4,48,256]{2,1,0:T(8,128)(2,1)S(1)}, u32[]{:S(2)}, u32[]{:S(2)}) collective-permute-start(f16[4,48,256]{2,1,0:T(8,128)(2,1)S(1)} %get-tuple-element.64), channel_id=1, source_target_pairs={{0,4},{4,8},{8,12},{12,0},{1,5},{5,9},{9,13},{13,1},{2,6},{6,10},{... | collective-permute-start | bytes 294920 | tf_op jit(solution)/shard_map/ppermute | solution.py:497
  33.4 18.0 %all-to-all-start = ((f16[16,48,256]{2,1,0:T(8,128)(2,1)}), f16[16,48,256]{2,1,0:T(8,128)(2,1)S(1)}, u32[]{:S(2)}, u32[]{:S(2)}) async-start(f16[16,48,256]{2,1,0:T(8,128)(2,1)} %convert_element_type.56), calls=%async_computation | async-start | bytes 786432 | tf_op jit(solution)/shard_map/all_to_all | solution.py:501
  39.6 9.0 %copy-start.8 = (bf16[4,256,256]{2,1,0:T(8,128)(2,1)S(1)}, bf16[4,256,256]{2,1,0:T(8,128)(2,1)}, u32[]{:S(2)}) copy-start(bf16[4,256,256]{2,1,0:T(8,128)(2,1)} %constant.16.clone.refs_4_.basis_z) | copy-start | bytes 1572868
  39.6 9.0 %copy-start.9 = (bf16[6,128,128]{2,1,0:T(8,128)(2,1)S(1)}, bf16[6,128,128]{2,1,0:T(8,128)(2,1)}, u32[]{:S(2)}) copy-start(bf16[6,128,128]{2,1,0:T(8,128)(2,1)} %constant.17.clone.refs_5_.basis_y) | copy-start | bytes 589828
  39.7 5.4 %collective-permute-start.9 = (f16[4,48,256]{2,1,0:T(8,128)(2,1)S(1)}, f16[4,48,256]{2,1,0:T(8,128)(2,1)S(1)}, u32[]{:S(2)}, u32[]{:S(2)}) collective-permute-start(f16[4,48,256]{2,1,0:T(8,128)(2,1)S(1)} %pad_maximum_fusion), channel_id=1, source_target_pairs={{0,1},{1,2},{2,3},{3,0},{4,5},{5,6},{6,7},{7,4},{8,9},{9,10},{10,1... | collective-permute-start | bytes 294920 | tf_op jit(solution)/shard_map/ppermute | solution.py:497
  39.8 6.3 %collective-permute-start.10 = (f16[4,48,256]{2,1,0:T(8,128)(2,1)S(1)}, f16[4,48,256]{2,1,0:T(8,128)(2,1)S(1)}, u32[]{:S(2)}, u32[]{:S(2)}) collective-permute-start(f16[4,48,256]{2,1,0:T(8,128)(2,1)S(1)} %pad_maximum_fusion.1), channel_id=1, source_target_pairs={{0,2},{1,3},{2,0},{3,1},{4,6},{5,7},{6,4},{7,5},{8,10},{9,11},{10,... | collective-permute-start | bytes 294920 | tf_op jit(solution)/shard_map/ppermute | solution.py:497
  41.4 7.1 %collective-permute-start.11 = (f16[4,48,256]{2,1,0:T(8,128)(2,1)S(1)}, f16[4,48,256]{2,1,0:T(8,128)(2,1)S(1)}, u32[]{:S(2)}, u32[]{:S(2)}) collective-permute-start(f16[4,48,256]{2,1,0:T(8,128)(2,1)S(1)} %pad_maximum_fusion.2), channel_id=1, source_target_pairs={{0,3},{1,0},{2,1},{3,2},{4,7},{5,4},{6,5},{7,6},{8,11},{9,8},{10,9... | collective-permute-start | bytes 294920 | tf_op jit(solution)/shard_map/ppermute | solution.py:497
  51.5 12.2 %collective-permute-start.15 = (f16[4,48,256]{2,1,0:T(8,128)(2,1)S(1)}, f16[4,48,256]{2,1,0:T(8,128)(2,1)S(1)}, u32[]{:S(2)}, u32[]{:S(2)}) collective-permute-start(f16[4,48,256]{2,1,0:T(8,128)(2,1)S(1)} %convert_element_type.63), channel_id=1, source_target_pairs={{0,12},{4,0},{8,4},{12,8},{1,13},{5,1},{9,5},{13,9},{2,14},{6,2},{... | collective-permute-start | bytes 294920 | tf_op jit(solution)/shard_map/ppermute | solution.py:497
  53.2 10.7 %collective-permute-start.14 = (f16[4,48,256]{2,1,0:T(8,128)(2,1)S(1)}, f16[4,48,256]{2,1,0:T(8,128)(2,1)S(1)}, u32[]{:S(2)}, u32[]{:S(2)}) collective-permute-start(f16[4,48,256]{2,1,0:T(8,128)(2,1)S(1)} %convert_element_type.62), channel_id=1, source_target_pairs={{0,8},{4,12},{8,0},{12,4},{1,9},{5,13},{9,1},{13,5},{2,10},{6,14},... | collective-permute-start | bytes 294920 | tf_op jit(solution)/shard_map/ppermute | solution.py:497
  53.8 10.0 %collective-permute-start.13 = (f16[4,48,256]{2,1,0:T(8,128)(2,1)S(1)}, f16[4,48,256]{2,1,0:T(8,128)(2,1)S(1)}, u32[]{:S(2)}, u32[]{:S(2)}) collective-permute-start(f16[4,48,256]{2,1,0:T(8,128)(2,1)S(1)} %convert_element_type.61), channel_id=1, source_target_pairs={{0,4},{4,8},{8,12},{12,0},{1,5},{5,9},{9,13},{13,1},{2,6},{6,10},{... | collective-permute-start | bytes 294920 | tf_op jit(solution)/shard_map/ppermute | solution.py:497
  59.3 13.6 %copy-start.2 = (f32[3,8,32,512]{3,2,1,0:T(8,128)S(1)}, f32[3,8,32,512]{3,2,1,0:T(8,128)}, u32[]{:S(2)}) copy-start(f32[3,8,32,512]{3,2,1,0:T(8,128)} %velocity.3) | copy-start | bytes 4718596
  59.3 13.6 %copy-start.6 = (bf16[2,512,512]{2,1,0:T(8,128)(2,1)S(1)}, bf16[2,512,512]{2,1,0:T(8,128)(2,1)}, u32[]{:S(2)}) copy-start(bf16[2,512,512]{2,1,0:T(8,128)(2,1)} %constant.18.clone.basis) | copy-start | bytes 3145732
  59.3 16.7 %all-to-all-start.1 = ((f16[16,48,256]{2,1,0:T(8,128)(2,1)}), f16[16,48,256]{2,1,0:T(8,128)(2,1)}, u32[]{:S(2)}, u32[]{:S(2)}) async-start(f16[16,48,256]{2,1,0:T(8,128)(2,1)} %convert_element_type.58), calls=%async_computation.1 | async-start | bytes 786432 | tf_op jit(solution)/shard_map/all_to_all | solution.py:501
  63.9 7.1 %collective-permute-start.16 = (f16[4,48,256]{2,1,0:T(8,128)(2,1)S(1)}, f16[4,48,256]{2,1,0:T(8,128)(2,1)S(1)}, u32[]{:S(2)}, u32[]{:S(2)}) collective-permute-start(f16[4,48,256]{2,1,0:T(8,128)(2,1)S(1)} %pad_maximum_fusion.3), channel_id=1, source_target_pairs={{0,1},{1,2},{2,3},{3,0},{4,5},{5,6},{6,7},{7,4},{8,9},{9,10},{10,1... | collective-permute-start | bytes 294920 | tf_op jit(solution)/shard_map/ppermute | solution.py:497
  64.3 8.1 %collective-permute-start.17 = (f16[4,48,256]{2,1,0:T(8,128)(2,1)S(1)}, f16[4,48,256]{2,1,0:T(8,128)(2,1)S(1)}, u32[]{:S(2)}, u32[]{:S(2)}) collective-permute-start(f16[4,48,256]{2,1,0:T(8,128)(2,1)S(1)} %pad_maximum_fusion.4), channel_id=1, source_target_pairs={{0,2},{1,3},{2,0},{3,1},{4,6},{5,7},{6,4},{7,5},{8,10},{9,11},{10,... | collective-permute-start | bytes 294920 | tf_op jit(solution)/shard_map/ppermute | solution.py:497
  66.0 6.8 %collective-permute-start.18 = (f16[4,48,256]{2,1,0:T(8,128)(2,1)S(1)}, f16[4,48,256]{2,1,0:T(8,128)(2,1)S(1)}, u32[]{:S(2)}, u32[]{:S(2)}) collective-permute-start(f16[4,48,256]{2,1,0:T(8,128)(2,1)S(1)} %pad_maximum_fusion.5), channel_id=1, source_target_pairs={{0,3},{1,0},{2,1},{3,2},{4,7},{5,4},{6,5},{7,6},{8,11},{9,8},{10,9... | collective-permute-start | bytes 294920 | tf_op jit(solution)/shard_map/ppermute | solution.py:497
